TPU v7x, 32 devices: a whole 2x2x4 slice. The times are simulated.
32 devices in a mesh: gx: 2 (over x), gy: 4 (over y, core), gz: 4 (over z).
Axes of the slice: x: 2, y: 2, z: 4, core: 2. Of those that a mesh axis runs over, the one named last changes fastest.
Arguments:
- residual_in: float32 [2, 4, 4, 128, 768], P('gx', 'gy', 'gz'), as said below
- schur: float32 [2, 4, 4, 768, 768], P('gx', 'gy', 'gz'), as said below
- modes: float32 [2, 4, 4, 6, 768], P('gx', 'gy', 'gz'), may hold values from -0.875 to 0.875
- coarse_inv: float32 [2, 4, 24, 24], P('gx', 'gy', 'gz'), as said below
Outputs:
- multipliers: float32 [2, 4, 4, 128, 768], P('gx', 'gy', 'gz')
- residual: float32 [2, 4, 4, 128, 768], P('gx', 'gy', 'gz')
Inputs may be any that keep to these rules, and one draw needn't show every extreme that they name: `residual_in`: each multiplier has the same value on both sides of its face. `schur`: every subdomain's matrix is symmetric positive definite. `coarse_inv`: every coarse block is symmetric positive definite.
All inputs are finite; a program needn't handle non-finite values.
Results may differ from a plain program's by a relative error of at most 0.0003.
Values sent between devices are 32-bit elements; how exact they have to be, the bound alone decides.
No kernel may reach another device: no remote copies, remote signals or barrier semaphores. Data moves between devices by JAX's collectives and lax.ppermute only.
A program may use at most 64 MiB of HBM per device.

v0:
```python
import jax
import jax.numpy as jnp
from jax import lax
from jax.sharding import PartitionSpec as P

ITERS = 4


def with_halo(x, sides, width):
    for axis, dim in sides:
        devices, length = (lax.axis_size(axis), x.shape[dim])
        up = [(i, (i + 1) % devices) for i in range(devices)]
        down = [(j, i) for i, j in up]
        last = lax.slice_in_dim(x, length - width, length, axis=dim)
        initial = lax.slice_in_dim(x, 0, width, axis=dim)
        before = lax.ppermute(last, axis, up)
        after = lax.ppermute(initial, axis, down)
        x = jnp.concatenate([before, x, after], axis=dim)
    return x


def assemble(values, face):
    parts = []
    pair_x = jnp.stack([values[:, 0:face], values[:, face : 2 * face]])
    ext_x = with_halo(pair_x, (("gx", 0),), 1)
    parts.append(pair_x[0] - ext_x[0])
    parts.append(ext_x[3] - pair_x[1])
    pair_y = jnp.stack([values[:, 2 * face : 3 * face], values[:, 3 * face : 4 * face]])
    ext_y = with_halo(pair_y, (("gy", 0),), 1)
    parts.append(pair_y[0] - ext_y[0])
    parts.append(ext_y[3] - pair_y[1])
    pair_z = jnp.stack([values[:, 4 * face : 5 * face], values[:, 5 * face : 6 * face]])
    ext_z = with_halo(pair_z, (("gz", 0),), 1)
    parts.append(pair_z[0] - ext_z[0])
    parts.append(ext_z[3] - pair_z[1])
    return jnp.concatenate(parts, axis=1)


def global_sums(first, second):
    return lax.psum((first, second), ("gx", "gy", "gz"))


def body(residual_in, schur, modes, coarse_inv):
    resid = residual_in[0, 0, 0]
    matrix = schur[0, 0, 0]
    mode_rows = modes[0, 0, 0]
    coarse_rows = coarse_inv[0, 0]
    face = resid.shape[1] // 6
    sign = jnp.repeat(jnp.array([1.0, -1.0, 1.0, -1.0, 1.0, -1.0], dtype=jnp.float32), face)

    def operate(field):
        u = sign * field
        loads = jnp.einsum("mj,rj->mr", mode_rows, u, precision=lax.Precision.HIGHEST)
        amp = jnp.dot(
            coarse_rows,
            lax.all_gather(loads, "gz", axis=0, tiled=True),
            precision=lax.Precision.HIGHEST,
            preferred_element_type=jnp.float32,
        )
        local = jnp.einsum(
            "rj,ij->ri",
            u,
            matrix,
            precision=lax.Precision.HIGHEST,
            preferred_element_type=jnp.float32,
        )
        coarse_term = jnp.einsum("mr,mj->rj", amp, mode_rows, precision=lax.Precision.HIGHEST)
        values = local + coarse_term
        image = assemble(values, face)
        part_norm = 0.5 * jnp.sum(field * field, axis=1)
        part_curv = 0.5 * jnp.sum(field * image, axis=1)
        norm_sum, curv_sum = global_sums(part_norm, part_curv)
        return (image, norm_sum, curv_sum)

    mult = jnp.zeros_like(resid)
    image, norm_now, curv = operate(resid)
    alpha = norm_now / curv
    direction = resid
    along = image
    for step in range(ITERS):
        mult = mult + alpha[:, None] * direction
        resid = resid - alpha[:, None] * along
        if step + 1 < ITERS:
            image, norm_next, curv = operate(resid)
            ratio = norm_next / norm_now
            alpha = norm_next / (curv - ratio * norm_next / alpha)
            direction = resid + ratio[:, None] * direction
            along = image + ratio[:, None] * along
            norm_now = norm_next
    return (mult[None, None, None], resid[None, None, None])


def solution(mesh):
    return jax.shard_map(
        body,
        mesh=mesh,
        in_specs=(
            P("gx", "gy", "gz", None, None),
            P("gx", "gy", "gz", None, None),
            P("gx", "gy", "gz", None, None),
            P("gx", "gy", "gz", None),
        ),
        out_specs=(P("gx", "gy", "gz", None, None), P("gx", "gy", "gz", None, None)),
        check_vma=False,
    )
```

profile of v0, /device:TPU:0, one launch (start us, length us, event | category | flops | bytes accessed | tf_op | source)
XLA Modules:
  0.0 336.9 jit_solution(1675158672934289230)
XLA Ops:
  2.9 14.8 %all-gather = f32[4,6,128]{2,1,0:T(8,128)S(1)} all-gather(f32[1,6,128]{2,1,0:T(8,128)S(1)} %convolution_bitcast_fusion.3), channel_id=1, replica_groups=mesh['gx'=2,'gy'=4,'gz'=4] {'gz'}, dimensions={0}, use_global_device_ids=true | all-gather | bytes 15360 | tf_op jit(solution)/shard_map/all_gather | solution.py:56
  17.8 3.5 %fusion.6 = f32[128,768]{1,0:T(8,128)S(1)} fusion(f32[1,1,1,768,768]{4,3,2,1,0:T(8,128)S(1)} %copy-done, f32[1,1,1,128,768]{4,3,2,1,0:T(8,128)} %param.5, f32[768]{0:T(1024)S(1)} %broadcast_bitcast_fusion), kind=kOutput, calls=%fused_computation.6 | convolution fusion | flops 906067968 | bytes 3148800 | tf_op jit(solution)/shard_map/rj,ij->ri/dot_general | solution.py:60
  23.5 2.8 collective-permute-done
  27.9 2.8 collective-permute-done.1
  30.8 3.7 %collective-permute-done.2 = f32[1,128,128]{2,1,0:T(8,128)S(1)} collective-permute-done((f32[1,128,128]{2,1,0:T(8,128)S(1)}, f32[1,128,128]{2,1,0:T(8,128)S(1)}, u32[]{:S(2)}, u32[]{:S(2)}) %collective-permute-start.2) | collective-permute-done | bytes 65568 | tf_op jit(solution)/shard_map/ppermute | solution.py:16
  38.1 4.5 %collective-permute-done.4 = f32[1,128,128]{2,1,0:T(8,128)S(1)} collective-permute-done((f32[1,128,128]{2,1,0:T(8,128)S(1)}, f32[1,128,128]{2,1,0:T(8,128)S(1)}, u32[]{:S(2)}, u32[]{:S(2)}) %collective-permute-start.4) | collective-permute-done | bytes 65568 | tf_op jit(solution)/shard_map/ppermute | solution.py:16
  44.2 2.9 collective-permute-done.5
  48.5 40.0 %all-reduce.3 = (f32[128]{0:T(128)S(1)}, f32[128]{0:T(128)}) all-reduce(f32[128]{0:T(128)} %get-tuple-element.59, f32[128]{0:T(128)S(1)} %get-tuple-element.58), channel_id=1, replica_groups=mesh['gx'=2,'gy'=4,'gz'=4] {'gx','gy','gz'}, use_global_device_ids=true, to_apply=%region_1.0 | all-reduce | flops 256 | bytes 2048 | tf_op jit(solution)/shard_map/psum | solution.py:40
  92.8 3.3 fusion.4
  96.1 14.3 %all-gather.1 = f32[4,6,128]{2,1,0:T(8,128)} all-gather(f32[1,6,128]{2,1,0:T(8,128)S(1)} %convolution_bitcast_fusion.2), channel_id=1, replica_groups=mesh['gx'=2,'gy'=4,'gz'=4] {'gz'}, dimensions={0}, use_global_device_ids=true | all-gather | bytes 15360 | tf_op jit(solution)/shard_map/all_gather | solution.py:56
  114.1 2.3 collective-permute-start.6
  118.8 3.5 %collective-permute-done.7 = f32[1,128,128]{2,1,0:T(8,128)S(1)} collective-permute-done((f32[1,128,128]{2,1,0:T(8,128)S(1)}, f32[1,128,128]{2,1,0:T(8,128)S(1)}, u32[]{:S(2)}, u32[]{:S(2)}) %collective-permute-start.7) | collective-permute-done | bytes 65568 | tf_op jit(solution)/shard_map/ppermute | solution.py:17
  126.6 37.6 %all-reduce.2 = (f32[128]{0:T(128)S(1)}, f32[128]{0:T(128)S(1)}) all-reduce(f32[128]{0:T(128)S(1)} %broadcast_multiply_fusion.5, f32[128]{0:T(128)S(1)} %broadcast_multiply_fusion.4), channel_id=1, replica_groups=mesh['gx'=2,'gy'=4,'gz'=4] {'gx','gy','gz'}, use_global_device_ids=true, to_apply=%region_5.0 | all-reduce | flops 256 | bytes 2048 | tf_op jit(solution)/shard_map/psum | solution.py:40
  173.8 3.3 fusion.2
  177.1 14.5 %all-gather.2 = f32[4,6,128]{2,1,0:T(8,128)} all-gather(f32[1,6,128]{2,1,0:T(8,128)S(1)} %convolution_bitcast_fusion.1), channel_id=1, replica_groups=mesh['gx'=2,'gy'=4,'gz'=4] {'gz'}, dimensions={0}, use_global_device_ids=true | all-gather | bytes 15360 | tf_op jit(solution)/shard_map/all_gather | solution.py:56
  195.5 2.3 collective-permute-start.12
  200.7 3.6 %collective-permute-done.13 = f32[1,128,128]{2,1,0:T(8,128)S(1)} collective-permute-done((f32[1,128,128]{2,1,0:T(8,128)S(1)}, f32[1,128,128]{2,1,0:T(8,128)S(1)}, u32[]{:S(2)}, u32[]{:S(2)}) %collective-permute-start.13) | collective-permute-done | bytes 65568 | tf_op jit(solution)/shard_map/ppermute | solution.py:17
  208.6 38.5 %all-reduce.1 = (f32[128]{0:T(128)}, f32[128]{0:T(128)}) all-reduce(f32[128]{0:T(128)} %broadcast_multiply_fusion.3, f32[128]{0:T(128)S(1)} %broadcast_multiply_fusion.2), channel_id=1, replica_groups=mesh['gx'=2,'gy'=4,'gz'=4] {'gx','gy','gz'}, use_global_device_ids=true, to_apply=%region_9.0 | all-reduce | flops 256 | bytes 2048 | tf_op jit(solution)/shard_map/psum | solution.py:40
  255.7 3.3 fusion
  259.0 14.4 %all-gather.3 = f32[4,6,128]{2,1,0:T(8,128)} all-gather(f32[1,6,128]{2,1,0:T(8,128)S(1)} %convolution_bitcast_fusion), channel_id=1, replica_groups=mesh['gx'=2,'gy'=4,'gz'=4] {'gz'}, dimensions={0}, use_global_device_ids=true | all-gather | bytes 15360 | tf_op jit(solution)/shard_map/all_gather | solution.py:56
  277.2 2.3 collective-permute-start.18
  282.4 3.6 %collective-permute-done.19 = f32[1,128,128]{2,1,0:T(8,128)S(1)} collective-permute-done((f32[1,128,128]{2,1,0:T(8,128)S(1)}, f32[1,128,128]{2,1,0:T(8,128)S(1)}, u32[]{:S(2)}, u32[]{:S(2)}) %collective-permute-start.19) | collective-permute-done | bytes 65568 | tf_op jit(solution)/shard_map/ppermute | solution.py:17
  290.8 37.9 %all-reduce = (f32[128]{0:T(128)}, f32[128]{0:T(128)}) all-reduce(f32[128]{0:T(128)} %broadcast_multiply_fusion.1, f32[128]{0:T(128)} %broadcast_multiply_fusion), channel_id=1, replica_groups=mesh['gx'=2,'gy'=4,'gz'=4] {'gx','gy','gz'}, use_global_device_ids=true, to_apply=%region_13.0 | all-reduce | flops 256 | bytes 2048 | tf_op jit(solution)/shard_map/psum | solution.py:40
  334.7 2.2 multiply_subtract_fusion
  (218 shorter events, 73.7 us)
Async XLA Ops:
  22.0 4.3 %collective-permute-start = (f32[1,128,128]{2,1,0:T(8,128)S(1)}, f32[1,128,128]{2,1,0:T(8,128)S(1)}, u32[]{:S(2)}, u32[]{:S(2)}) collective-permute-start(f32[1,128,128]{2,1,0:T(8,128)S(1)} %slice_bitcast_fusion.22), channel_id=1, source_target_pairs={{0,16},{16,0},{1,17},{17,1},{2,18},{18,2},{3,19},{19,3},{4,20},{20... | collective-permute-start | bytes 196616 | tf_op jit(solution)/shard_map/ppermute | solution.py:16
  26.3 4.3 %collective-permute-start.1 = (f32[1,128,128]{2,1,0:T(8,128)S(1)}, f32[1,128,128]{2,1,0:T(8,128)S(1)}, u32[]{:S(2)}, u32[]{:S(2)}) collective-permute-start(f32[1,128,128]{2,1,0:T(8,128)S(1)} %get-tuple-element.57), channel_id=1, source_target_pairs={{16,0},{0,16},{17,1},{1,17},{18,2},{2,18},{19,3},{3,19},{20,4},{4,... | collective-permute-start | bytes 196616 | tf_op jit(solution)/shard_map/ppermute | solution.py:17
  30.7 3.7 %collective-permute-start.2 = (f32[1,128,128]{2,1,0:T(8,128)S(1)}, f32[1,128,128]{2,1,0:T(8,128)S(1)}, u32[]{:S(2)}, u32[]{:S(2)}) collective-permute-start(f32[1,128,128]{2,1,0:T(8,128)S(1)} %get-tuple-element.55), channel_id=1, source_target_pairs={{0,4},{4,8},{8,12},{12,0},{1,5},{5,9},{9,13},{13,1},{2,6},{6,10},{... | collective-permute-start | bytes 196616 | tf_op jit(solution)/shard_map/ppermute | solution.py:16
  34.4 2.0 collective-permute-start.3
  36.4 6.1 %collective-permute-start.4 = (f32[1,128,128]{2,1,0:T(8,128)S(1)}, f32[1,128,128]{2,1,0:T(8,128)S(1)}, u32[]{:S(2)}, u32[]{:S(2)}) collective-permute-start(f32[1,128,128]{2,1,0:T(8,128)S(1)} %get-tuple-element.51), channel_id=1, source_target_pairs={{0,1},{1,2},{2,3},{3,0},{4,5},{5,6},{6,7},{7,4},{8,9},{9,10},{10,1... | collective-permute-start | bytes 196616 | tf_op jit(solution)/shard_map/ppermute | solution.py:16
  42.5 4.6 %collective-permute-start.5 = (f32[1,128,128]{2,1,0:T(8,128)S(1)}, f32[1,128,128]{2,1,0:T(8,128)S(1)}, u32[]{:S(2)}, u32[]{:S(2)}) collective-permute-start(f32[1,128,128]{2,1,0:T(8,128)S(1)} %get-tuple-element.49), channel_id=1, source_target_pairs={{1,0},{2,1},{3,2},{0,3},{5,4},{6,5},{7,6},{4,7},{9,8},{10,9},{11,1... | collective-permute-start | bytes 196616 | tf_op jit(solution)/shard_map/ppermute | solution.py:17
  114.1 4.6 %collective-permute-start.6 = (f32[1,128,128]{2,1,0:T(8,128)S(1)}, f32[1,128,128]{2,1,0:T(8,128)S(1)}, u32[]{:S(2)}, u32[]{:S(2)}) collective-permute-start(f32[1,128,128]{2,1,0:T(8,128)S(1)} %get-tuple-element.47), channel_id=1, source_target_pairs={{0,16},{16,0},{1,17},{17,1},{2,18},{18,2},{3,19},{19,3},{4,20},{20... | collective-permute-start | bytes 196616 | tf_op jit(solution)/shard_map/ppermute | solution.py:16
  116.5 8.0 %collective-permute-start.11 = (f32[1,128,128]{2,1,0:T(8,128)S(1)}, f32[1,128,128]{2,1,0:T(8,128)S(1)}, u32[]{:S(2)}, u32[]{:S(2)}) collective-permute-start(f32[1,128,128]{2,1,0:T(8,128)S(1)} %get-tuple-element.42), channel_id=1, source_target_pairs={{1,0},{2,1},{3,2},{0,3},{5,4},{6,5},{7,6},{4,7},{9,8},{10,9},{11,1... | collective-permute-start | bytes 196616 | tf_op jit(solution)/shard_map/ppermute | solution.py:17
  118.0 4.3 %collective-permute-start.7 = (f32[1,128,128]{2,1,0:T(8,128)S(1)}, f32[1,128,128]{2,1,0:T(8,128)S(1)}, u32[]{:S(2)}, u32[]{:S(2)}) collective-permute-start(f32[1,128,128]{2,1,0:T(8,128)S(1)} %get-tuple-element.43), channel_id=1, source_target_pairs={{16,0},{0,16},{17,1},{1,17},{18,2},{2,18},{19,3},{3,19},{20,4},{4,... | collective-permute-start | bytes 196616 | tf_op jit(solution)/shard_map/ppermute | solution.py:17
  118.1 5.2 %collective-permute-start.9 = (f32[1,128,128]{2,1,0:T(8,128)S(1)}, f32[1,128,128]{2,1,0:T(8,128)S(1)}, u32[]{:S(2)}, u32[]{:S(2)}) collective-permute-start(f32[1,128,128]{2,1,0:T(8,128)S(1)} %get-tuple-element.44), channel_id=1, source_target_pairs={{4,0},{8,4},{12,8},{0,12},{5,1},{9,5},{13,9},{1,13},{6,2},{10,6},{... | collective-permute-start | bytes 196616 | tf_op jit(solution)/shard_map/ppermute | solution.py:17
  118.1 6.3 %collective-permute-start.10 = (f32[1,128,128]{2,1,0:T(8,128)S(1)}, f32[1,128,128]{2,1,0:T(8,128)S(1)}, u32[]{:S(2)}, u32[]{:S(2)}) collective-permute-start(f32[1,128,128]{2,1,0:T(8,128)S(1)} %get-tuple-element.45), channel_id=1, source_target_pairs={{0,1},{1,2},{2,3},{3,0},{4,5},{5,6},{6,7},{7,4},{8,9},{9,10},{10,1... | collective-permute-start | bytes 196616 | tf_op jit(solution)/shard_map/ppermute | solution.py:16
  118.7 4.5 %collective-permute-start.8 = (f32[1,128,128]{2,1,0:T(8,128)S(1)}, f32[1,128,128]{2,1,0:T(8,128)S(1)}, u32[]{:S(2)}, u32[]{:S(2)}) collective-permute-start(f32[1,128,128]{2,1,0:T(8,128)S(1)} %get-tuple-element.46), channel_id=1, source_target_pairs={{0,4},{4,8},{8,12},{12,0},{1,5},{5,9},{9,13},{13,1},{2,6},{6,10},{... | collective-permute-start | bytes 196616 | tf_op jit(solution)/shard_map/ppermute | solution.py:16
  195.5 4.6 %collective-permute-start.12 = (f32[1,128,128]{2,1,0:T(8,128)S(1)}, f32[1,128,128]{2,1,0:T(8,128)S(1)}, u32[]{:S(2)}, u32[]{:S(2)}) collective-permute-start(f32[1,128,128]{2,1,0:T(8,128)S(1)} %get-tuple-element.41), channel_id=1, source_target_pairs={{0,16},{16,0},{1,17},{17,1},{2,18},{18,2},{3,19},{19,3},{4,20},{20... | collective-permute-start | bytes 196616 | tf_op jit(solution)/shard_map/ppermute | solution.py:16
  197.8 8.6 %collective-permute-start.17 = (f32[1,128,128]{2,1,0:T(8,128)S(1)}, f32[1,128,128]{2,1,0:T(8,128)S(1)}, u32[]{:S(2)}, u32[]{:S(2)}) collective-permute-start(f32[1,128,128]{2,1,0:T(8,128)S(1)} %get-tuple-element.36), channel_id=1, source_target_pairs={{1,0},{2,1},{3,2},{0,3},{5,4},{6,5},{7,6},{4,7},{9,8},{10,9},{11,1... | collective-permute-start | bytes 196616 | tf_op jit(solution)/shard_map/ppermute | solution.py:17
  200.0 4.3 %collective-permute-start.13 = (f32[1,128,128]{2,1,0:T(8,128)S(1)}, f32[1,128,128]{2,1,0:T(8,128)S(1)}, u32[]{:S(2)}, u32[]{:S(2)}) collective-permute-start(f32[1,128,128]{2,1,0:T(8,128)S(1)} %get-tuple-element.37), channel_id=1, source_target_pairs={{16,0},{0,16},{17,1},{1,17},{18,2},{2,18},{19,3},{3,19},{20,4},{4,... | collective-permute-start | bytes 196616 | tf_op jit(solution)/shard_map/ppermute | solution.py:17
  200.1 4.7 %collective-permute-start.15 = (f32[1,128,128]{2,1,0:T(8,128)S(1)}, f32[1,128,128]{2,1,0:T(8,128)S(1)}, u32[]{:S(2)}, u32[]{:S(2)}) collective-permute-start(f32[1,128,128]{2,1,0:T(8,128)S(1)} %get-tuple-element.38), channel_id=1, source_target_pairs={{4,0},{8,4},{12,8},{0,12},{5,1},{9,5},{13,9},{1,13},{6,2},{10,6},{... | collective-permute-start | bytes 196616 | tf_op jit(solution)/shard_map/ppermute | solution.py:17
  200.1 6.3 %collective-permute-start.16 = (f32[1,128,128]{2,1,0:T(8,128)S(1)}, f32[1,128,128]{2,1,0:T(8,128)S(1)}, u32[]{:S(2)}, u32[]{:S(2)}) collective-permute-start(f32[1,128,128]{2,1,0:T(8,128)S(1)} %get-tuple-element.39), channel_id=1, source_target_pairs={{0,1},{1,2},{2,3},{3,0},{4,5},{5,6},{6,7},{7,4},{8,9},{9,10},{10,1... | collective-permute-start | bytes 196616 | tf_op jit(solution)/shard_map/ppermute | solution.py:16
  200.1 4.7 %collective-permute-start.14 = (f32[1,128,128]{2,1,0:T(8,128)S(1)}, f32[1,128,128]{2,1,0:T(8,128)S(1)}, u32[]{:S(2)}, u32[]{:S(2)}) collective-permute-start(f32[1,128,128]{2,1,0:T(8,128)S(1)} %get-tuple-element.40), channel_id=1, source_target_pairs={{0,4},{4,8},{8,12},{12,0},{1,5},{5,9},{9,13},{13,1},{2,6},{6,10},{... | collective-permute-start | bytes 196616 | tf_op jit(solution)/shard_map/ppermute | solution.py:16
  277.2 4.6 %collective-permute-start.18 = (f32[1,128,128]{2,1,0:T(8,128)S(1)}, f32[1,128,128]{2,1,0:T(8,128)S(1)}, u32[]{:S(2)}, u32[]{:S(2)}) collective-permute-start(f32[1,128,128]{2,1,0:T(8,128)S(1)} %get-tuple-element.35), channel_id=1, source_target_pairs={{0,16},{16,0},{1,17},{17,1},{2,18},{18,2},{3,19},{19,3},{4,20},{20... | collective-permute-start | bytes 196616 | tf_op jit(solution)/shard_map/ppermute | solution.py:16
  279.6 8.6 %collective-permute-start.23 = (f32[1,128,128]{2,1,0:T(8,128)S(1)}, f32[1,128,128]{2,1,0:T(8,128)S(1)}, u32[]{:S(2)}, u32[]{:S(2)}) collective-permute-start(f32[1,128,128]{2,1,0:T(8,128)S(1)} %get-tuple-element.30), channel_id=1, source_target_pairs={{1,0},{2,1},{3,2},{0,3},{5,4},{6,5},{7,6},{4,7},{9,8},{10,9},{11,1... | collective-permute-start | bytes 196616 | tf_op jit(solution)/shard_map/ppermute | solution.py:17
  281.8 4.3 %collective-permute-start.19 = (f32[1,128,128]{2,1,0:T(8,128)S(1)}, f32[1,128,128]{2,1,0:T(8,128)S(1)}, u32[]{:S(2)}, u32[]{:S(2)}) collective-permute-start(f32[1,128,128]{2,1,0:T(8,128)S(1)} %get-tuple-element.31), channel_id=1, source_target_pairs={{16,0},{0,16},{17,1},{1,17},{18,2},{2,18},{19,3},{3,19},{20,4},{4,... | collective-permute-start | bytes 196616 | tf_op jit(solution)/shard_map/ppermute | solution.py:17
  281.8 4.9 %collective-permute-start.21 = (f32[1,128,128]{2,1,0:T(8,128)S(1)}, f32[1,128,128]{2,1,0:T(8,128)S(1)}, u32[]{:S(2)}, u32[]{:S(2)}) collective-permute-start(f32[1,128,128]{2,1,0:T(8,128)S(1)} %get-tuple-element.32), channel_id=1, source_target_pairs={{4,0},{8,4},{12,8},{0,12},{5,1},{9,5},{13,9},{1,13},{6,2},{10,6},{... | collective-permute-start | bytes 196616 | tf_op jit(solution)/shard_map/ppermute | solution.py:17
  281.8 6.3 %collective-permute-start.22 = (f32[1,128,128]{2,1,0:T(8,128)S(1)}, f32[1,128,128]{2,1,0:T(8,128)S(1)}, u32[]{:S(2)}, u32[]{:S(2)}) collective-permute-start(f32[1,128,128]{2,1,0:T(8,128)S(1)} %get-tuple-element.33), channel_id=1, source_target_pairs={{0,1},{1,2},{2,3},{3,0},{4,5},{5,6},{6,7},{7,4},{8,9},{9,10},{10,1... | collective-permute-start | bytes 196616 | tf_op jit(solution)/shard_map/ppermute | solution.py:16
  281.9 4.9 %collective-permute-start.20 = (f32[1,128,128]{2,1,0:T(8,128)S(1)}, f32[1,128,128]{2,1,0:T(8,128)S(1)}, u32[]{:S(2)}, u32[]{:S(2)}) collective-permute-start(f32[1,128,128]{2,1,0:T(8,128)S(1)} %get-tuple-element.34), channel_id=1, source_target_pairs={{0,4},{4,8},{8,12},{12,0},{1,5},{5,9},{9,13},{13,1},{2,6},{6,10},{... | collective-permute-start | bytes 196616 | tf_op jit(solution)/shard_map/ppermute | solution.py:16
  (47 other events, 560.6 us)
where the time goes:
time: 340 us; the launch traced here: 337 us
  blocking collectives  212 us (62%)
  waiting for transfers between devices  35.5 us (10%)
  other arithmetic  32.2 us (9%)
  matrix products  25.6 us (8%)
  starting transfers between devices  21.3 us (6%)
  local copies, waits for them, and re-layouts  9 us (3%)
    psum x4, blocking collectives, global_sums(): return lax.psum((first, second), ('gx', 'gy', 'gz'))  154 us
    all_gather x4, blocking collectives, operate(): lax.all_gather(loads, 'gz', axis=0, tiled=True)  57.9 us
    ppermute x12, waiting for transfers between devices, with_halo(): after = lax.ppermute(initial, axis, down)  18.3 us
    ppermute x12, waiting for transfers between devices, with_halo(): before = lax.ppermute(last, axis, up)  17.2 us
    unnamed x40, other arithmetic  13.5 us
    dot_general x4, matrix products, operate(): jnp.einsum('rj,ij->ri', u, matrix, precision=lax.Precision.HIGHEST, prefe...  13.4 us
    ppermute x12, starting transfers between devices, with_halo(): before = lax.ppermute(last, axis, up)  11.9 us
    ppermute x12, starting transfers between devices, with_halo(): after = lax.ppermute(initial, axis, down)  9.42 us
  transfers between devices with their start and end apart: 24, of which 16 were waited for; matrix products, arithmetic and copies ran while one was open for 0% of the time, Pallas kernels for 0%

commit v1 on v0

v1 whole, which is shorter than its diff:
```python
import functools

import jax
import jax.numpy as jnp
from jax import lax
from jax.experimental import pallas as pl
from jax.experimental.pallas import tpu as pltpu
from jax.sharding import PartitionSpec as P

F32 = jnp.float32
BF16 = jnp.bfloat16
HI = lax.Precision.HIGHEST
MODE_PAD = 8
DOT_PAD = 8


def call(kernel, outs, *args, flops=0):
    nbytes = sum(a.size * a.dtype.itemsize for a in args)
    nbytes += sum(o.size * o.dtype.itemsize for o in outs)
    return pl.pallas_call(
        kernel,
        out_shape=outs,
        in_specs=[pl.BlockSpec(memory_space=pltpu.VMEM)] * len(args),
        out_specs=[pl.BlockSpec(memory_space=pltpu.VMEM)] * len(outs),
        compiler_params=pltpu.CompilerParams(vmem_limit_bytes=24 * 1024 * 1024),
        cost_estimate=pl.CostEstimate(flops=flops, bytes_accessed=nbytes, transcendentals=0),
    )(*args)


def sds(shape, dtype=F32):
    return jax.ShapeDtypeStruct(shape, dtype)


def split(x):
    high = x.astype(BF16)
    return high, (x - high.astype(F32)).astype(BF16)


def split3(x):
    high = x.astype(BF16)
    rest = x - high.astype(F32)
    mid = rest.astype(BF16)
    return high, mid, (rest - mid.astype(F32)).astype(BF16)


def half_dot(a, b):
    return 0.5 * jnp.sum(a * b, axis=0, keepdims=True)


def publish(vec, modes, u2_ref, g_ref):
    high, low = split(vec)
    cols = vec.shape[1]
    u2_ref[:, :cols] = high
    u2_ref[:, cols:] = low
    g_ref[0:MODE_PAD, :] = jnp.dot(modes, vec, precision=HI, preferred_element_type=F32)


def start_kernel(face, resid_ref, modes_ref, vec_ref, u2_ref, g_ref, mt_ref):
    for f in range(6):
        part = resid_ref[:, f * face:(f + 1) * face].T
        vec_ref[f * face:(f + 1) * face, :] = part if f % 2 == 0 else -part
    modes = modes_ref[...]
    publish(vec_ref[...], modes, u2_ref, g_ref)
    high, mid, low = split3(modes.T)
    mt_ref[...] = jnp.concatenate([high, high, mid, mid, high, low], axis=1)


def multiply(s_high_ref, s_low_ref, u2_ref, y_ref):
    rows, cols = y_ref.shape
    u2 = u2_ref[...]
    step = 256
    for i in range(0, rows, step):
        both = jnp.dot(s_high_ref[i:i + step, :], u2, preferred_element_type=F32)
        both += jnp.dot(s_low_ref[i:i + step, :], u2, preferred_element_type=F32)
        y_ref[i:i + step, :] = both[:, :cols] + both[:, cols:]


def first_product_kernel(schur_ref, u2_ref, y_ref, s_high_ref, s_low_ref):
    high, low = split(schur_ref[...])
    s_high_ref[...] = high
    s_low_ref[...] = low
    multiply(s_high_ref, s_low_ref, u2_ref, y_ref)


def product_kernel(s_high_ref, s_low_ref, u2_ref, y_ref):
    multiply(s_high_ref, s_low_ref, u2_ref, y_ref)


def product_dots_a_kernel(s_high_ref, s_low_ref, u2_ref, r0_ref, w0_ref, y_ref, d_ref):
    multiply(s_high_ref, s_low_ref, u2_ref, y_ref)
    r0, w0 = r0_ref[...], w0_ref[...]
    d_ref[...] = jnp.zeros_like(d_ref)
    d_ref[0:1, :] = half_dot(r0, r0)
    d_ref[1:2, :] = half_dot(r0, w0)
    d_ref[2:3, :] = half_dot(w0, w0)


def product_dots_b_kernel(s_high_ref, s_low_ref, u2_ref, r2_ref, w2_ref, s1_ref, z1_ref, y_ref, d_ref):
    multiply(s_high_ref, s_low_ref, u2_ref, y_ref)
    r2, w2, s1, z1 = r2_ref[...], w2_ref[...], s1_ref[...], z1_ref[...]
    d_ref[...] = jnp.zeros_like(d_ref)
    d_ref[0:1, :] = half_dot(r2, r2)
    d_ref[1:2, :] = half_dot(r2, w2)
    d_ref[2:3, :] = half_dot(w2, w2)
    d_ref[3:4, :] = half_dot(w2, s1)
    d_ref[4:5, :] = half_dot(s1, s1)
    d_ref[7:8, :] = half_dot(s1, z1)


def coarse(y_ref, mt_ref, c_ref, g_refs):
    if len(g_refs) == 1:
        loads = g_refs[0][...]
    else:
        loads = jnp.concatenate([ref[0:MODE_PAD, :] for ref in g_refs], axis=0)
    amp = jnp.dot(c_ref[...], loads, precision=HI, preferred_element_type=F32)
    high, mid, low = split3(amp)
    pieces = jnp.concatenate([high, mid, high, mid, low, high], axis=0)
    return y_ref[...] + jnp.dot(mt_ref[...], pieces, preferred_element_type=F32)


def value_kernel(face, n_col, n_dots, send_sums, *refs):
    y_ref, mt_ref, c_ref = refs[:3]
    g_refs = refs[3:3 + n_col]
    rest = refs[3 + n_col:]
    vecs, rest = rest[:len(n_dots)], rest[len(n_dots):]
    if n_dots:
        d_in, rest = rest[0], rest[1:]
    xb, ym, yp, zm, zp = rest[:5]
    value = coarse(y_ref, mt_ref, c_ref, g_refs)
    xb[0:2 * face, :] = value[0:2 * face]
    ym[0:face, :] = value[2 * face:3 * face]
    yp[0:face, :] = value[3 * face:4 * face]
    zm[...] = value[4 * face:5 * face]
    zp[...] = value[5 * face:6 * face]
    if n_dots:
        for ref, at in ((xb, 2 * face), (ym, face), (yp, face)):
            ref[at:at + DOT_PAD, :] = d_in[...]
        for vec, row in zip(vecs, n_dots):
            dot = jnp.sum(vec[...] * value, axis=0, keepdims=True)
            for ref, at in ((xb, 2 * face), (ym, face), (yp, face)):
                ref[at + row:at + row + 1, :] = dot
    if send_sums:
        total = g_refs[0][MODE_PAD:MODE_PAD + DOT_PAD, :]
        for ref in g_refs[1:]:
            total = total + ref[MODE_PAD:MODE_PAD + DOT_PAD, :]
        rest[5][...] = total


def assemble(face, own, got):
    xb, ym, yp, zm, zp = own
    gxb, gyl, gyh, gzl, gzh = got
    f = face
    return jnp.concatenate([
        xb[0:f, :] - gxb[f:2 * f, :],
        xb[f:2 * f, :] - gxb[0:f, :],
        ym[0:f, :] - gyl[0:f, :],
        yp[0:f, :] - gyh[0:f, :],
        zm[...] - gzl[...],
        zp[...] - gzh[...],
    ], axis=0)


def near_sum(face, own, got):
    xb, ym = own[0], own[1]
    gxb, gyl, gyh = got[0], got[1], got[2]
    f = face
    total = xb[2 * f:2 * f + DOT_PAD, :] + gxb[2 * f:2 * f + DOT_PAD, :]
    return total + (gyl[f:f + DOT_PAD, :] + gyh[f:f + DOT_PAD, :])


def image_kernel(face, with_sums, *refs):
    own, got = refs[0:5], refs[5:10]
    modes_ref, vec_ref, u2_ref, g_ref = refs[10:14]
    vec = assemble(face, own, got)
    vec_ref[...] = vec
    publish(vec, modes_ref[...], u2_ref, g_ref)
    if with_sums:
        g_ref[MODE_PAD:MODE_PAD + DOT_PAD, :] = near_sum(face, own, got)


def two_steps(m):
    m0, m1, m2, m3 = (m[i:i + 1, :] for i in range(4))
    alpha0 = m0 / m1
    norm1 = alpha0 * alpha0 * m2 - m0
    curv1 = m1 - 2.0 * alpha0 * m2 + alpha0 * alpha0 * m3
    beta1 = norm1 / m0
    alpha1 = norm1 / (curv1 - beta1 * norm1 / alpha0)
    return alpha0, norm1, beta1, alpha1


def middle_kernel(face, *refs):
    own, got = refs[0:5], refs[5:10]
    sums_refs, (r0_ref, w0_ref, b2_ref, modes_ref), outs = refs[10:12], refs[12:16], refs[16:]
    r2_ref, w2_ref, p1_ref, s1_ref, z1_ref, m2_ref, k_ref, u2_ref, g_ref = outs
    b3 = assemble(face, own, got)
    alpha0, norm1, beta1, alpha1 = two_steps(sums_refs[0][...] + sums_refs[1][...])
    r0, w0, b2 = r0_ref[...], w0_ref[...], b2_ref[...]
    r1 = r0 - alpha0 * w0
    w1 = w0 - alpha0 * b2
    p1 = r1 + beta1 * r0
    s1 = w1 + beta1 * w0
    z1 = (b2 - alpha0 * b3) + beta1 * b2
    w2 = w1 - alpha1 * z1
    r2_ref[...] = r1 - alpha1 * s1
    w2_ref[...] = w2
    p1_ref[...] = p1
    s1_ref[...] = s1
    z1_ref[...] = z1
    m2_ref[...] = alpha0 * r0 + alpha1 * p1
    k_ref[...] = jnp.zeros_like(k_ref)
    k_ref[0:1, :] = norm1
    k_ref[1:2, :] = alpha1
    publish(w2, modes_ref[...], u2_ref, g_ref)


def near_sum_kernel(face, *refs):
    refs[-1][...] = near_sum(face, (refs[0], refs[1]), refs[2:5])


def add_kernel(*refs):
    total = refs[0][...]
    for ref in refs[1:-1]:
        total = total + ref[...]
    refs[-1][...] = total


def last_kernel(face, *refs):
    own, got = refs[0:5], refs[5:10]
    sums_refs, (r2_ref, w2_ref, p1_ref, s1_ref, z1_ref, m2_ref, k_ref) = refs[10:12], refs[12:19]
    mult_ref, resid_ref = refs[19:]
    d = sums_refs[0][...] + sums_refs[1][...]
    rr, rw, ww, ws, ss, wc, sc, sz = (d[i:i + 1, :] for i in range(8))
    norm1, alpha1 = k_ref[0:1, :], k_ref[1:2, :]
    beta2 = rr / norm1
    alpha2 = rr / (rw - beta2 * rr / alpha1)
    norm3 = alpha2 * alpha2 * (ww + 2.0 * beta2 * ws + beta2 * beta2 * ss) - rr
    curv3 = rw - 2.0 * alpha2 * (ww + beta2 * ws)
    curv3 = curv3 + alpha2 * alpha2 * (wc + 2.0 * beta2 * sc + beta2 * beta2 * sz)
    beta3 = norm3 / rr
    alpha3 = norm3 / (curv3 - beta3 * norm3 / alpha2)
    c3 = assemble(face, own, got)
    r2, w2, p1, s1 = r2_ref[...], w2_ref[...], p1_ref[...], s1_ref[...]
    p2 = r2 + beta2 * p1
    s2 = w2 + beta2 * s1
    r3 = r2 - alpha2 * s2
    w3 = w2 - alpha2 * (c3 + beta2 * z1_ref[...])
    p3 = r3 + beta3 * p2
    s3 = w3 + beta3 * s2
    mult = m2_ref[...] + alpha2 * p2 + alpha3 * p3
    resid = r3 - alpha3 * s3
    for f in range(6):
        at = slice(f * face, (f + 1) * face)
        sign = 1.0 if f % 2 == 0 else -1.0
        mult_ref[:, at] = sign * mult[at, :].T
        resid_ref[:, at] = sign * resid[at, :].T


def body(sizes, residual_in, schur, modes, coarse_inv):
    nx, ny, nz = sizes
    resid = residual_in[0, 0, 0]
    matrix = schur[0, 0, 0]
    mode_rows = modes[0, 0, 0]
    loads, width = resid.shape
    face = width // 6
    n_modes = mode_rows.shape[0]
    mode_rows = jnp.pad(mode_rows, ((0, MODE_PAD - n_modes), (0, 0)))
    near = (nx, ny, nz) == (2, 4, 4)

    def shift(x, axis, by):
        n = lax.axis_size(axis)
        return lax.ppermute(x, axis, [(i, (i + by) % n) for i in range(n)])

    blocks = coarse_inv[0, 0].reshape(n_modes, nz, n_modes)
    if nz <= 4:
        turned = jnp.concatenate([blocks[:, ::-1]] * 2, axis=1)
        blocks = lax.dynamic_slice_in_dim(turned, nz - 1 - lax.axis_index("gz"), nz, axis=1)
    pad = MODE_PAD - n_modes
    c_rows = jnp.pad(blocks, ((0, pad), (0, 0), (0, pad))).reshape(MODE_PAD, nz * MODE_PAD)

    def column(msg):
        if nz <= 4:
            return [msg] + [shift(msg, "gz", s) for s in range(1, nz)]
        return [lax.all_gather(msg, "gz", axis=0, tiled=True)]

    def exchange(own):
        xb, ym, yp, zm, zp = own
        if nx == 2:
            gxb = shift(xb, "gx", 1)
        else:
            low, high, dots = xb[:face], xb[face:2 * face], xb[2 * face:]
            gxb = jnp.concatenate([shift(low, "gx", -1), shift(high, "gx", 1), dots], axis=0)
        gyl, gyh = shift(yp, "gy", 1), shift(ym, "gy", -1)
        return (gxb, gyl, gyh, shift(zp, "gz", 1), shift(zm, "gz", -1))

    def far(x):
        pairs = []
        for i in range(nx):
            for j in range(ny):
                pairs.append((i * ny + j, (i + 1) % nx * ny + (j + 2) % ny))
        return lax.ppermute(x, ("gx", "gy"), pairs)

    vec = sds((width, loads))
    u2 = sds((width, 2 * loads), BF16)
    half = sds((width, width), BF16)
    g_msg = sds((MODE_PAD, loads))
    d_msg = sds((DOT_PAD, loads))
    flops = 2 * width * width * 2 * loads * 2

    def faces(extra):
        return [sds((2 * face + extra, loads)), sds((face + extra, loads)), sds((face + extra, loads)), sds((face, loads)), sds((face, loads))]

    def value(y, col, vecs=(), rows=(), d_in=None, send_sums=False):
        outs = faces(DOT_PAD if rows else 0) + ([d_msg] if send_sums else [])
        extra = list(vecs) + ([d_in] if rows else [])
        kern = functools.partial(value_kernel, face, len(col), rows, send_sums)
        res = call(kern, outs, y, mt, c_rows, *col, *extra, flops=2 * width * loads * 24)
        return res[:5], res[5:]

    def total_dots(own, got):
        return lax.psum(own[0][2 * face:], ("gx", "gy", "gz"))

    r0, v2, g, mt = call(
        functools.partial(start_kernel, face),
        [vec, u2, g_msg, sds((width, 6 * MODE_PAD), BF16)], resid, mode_rows)
    col = column(g)
    y, s_high, s_low = call(first_product_kernel, [vec, half, half], matrix, v2, flops=flops)
    own, _ = value(y, col)
    got = exchange(own)

    w0, v2, g = call(functools.partial(image_kernel, face, False), [vec, u2, g_msg], *own, *got, mode_rows)
    col = column(g)
    y, d = call(product_dots_a_kernel, [vec, d_msg], s_high, s_low, v2, r0, w0, flops=flops)
    own, _ = value(y, col, [w0], (3,), d)
    got = exchange(own)

    if near:
        gd_msg = sds((MODE_PAD + DOT_PAD, loads))
        b2, v2, g = call(functools.partial(image_kernel, face, True), [vec, u2, gd_msg], *own, *got, mode_rows)
    else:
        sums = total_dots(own, got)
        b2, v2, g = call(functools.partial(image_kernel, face, False), [vec, u2, g_msg], *own, *got, mode_rows)
    col = column(g)
    y, = call(product_kernel, [vec], s_high, s_low, v2, flops=flops)
    own, part = value(y, col, send_sums=near)
    got = exchange(own)
    pair = (part[0], far(part[0])) if near else (sums, jnp.zeros_like(sums))

    r2, w2, p1, s1, z1, m2, k, v2, g = call(
        functools.partial(middle_kernel, face),
        [vec] * 6 + [d_msg, u2, g_msg], *own, *got, *pair, r0, w0, b2, mode_rows)
    col = column(g)
    y, d = call(product_dots_b_kernel, [vec, d_msg], s_high, s_low, v2, r2, w2, s1, z1, flops=flops)
    own, _ = value(y, col, [w2, s1], (5, 6), d)
    got = exchange(own)

    if near:
        part, = call(functools.partial(near_sum_kernel, face), [d_msg], own[0], own[1], *got[:3])
        part, = call(add_kernel, [d_msg], *column(part))
        pair = (part, far(part))
    else:
        sums = total_dots(own, got)
        pair = (sums, jnp.zeros_like(sums))
    out = sds((loads, width))
    mult, final = call(
        functools.partial(last_kernel, face), [out, out],
        *own, *got, *pair, r2, w2, p1, s1, z1, m2, k)
    return (mult[None, None, None], final[None, None, None])


def solution(mesh):
    spec = P("gx", "gy", "gz", None, None)
    sizes = tuple(mesh.shape[axis] for axis in ("gx", "gy", "gz"))
    return jax.shard_map(
        functools.partial(body, sizes),
        mesh=mesh,
        in_specs=(spec, spec, spec, P("gx", "gy", "gz", None)),
        out_specs=(spec, spec),
        check_vma=False,
    )
```

time: 340 us -> 89.1 us (0.26)
  blocking collectives: 212 us -> 0 us
  other arithmetic: 32.2 us -> 0.72 us
  matrix products: 25.6 us -> 0 us
  starting transfers between devices: 21.3 us -> 35.9 us
  Pallas kernels: 0 us -> 7.77 us
  local copies, waits for them, and re-layouts: 9 us -> 5.32 us
    psum x4 -> x0, blocking collectives: 154 us -> none  [global_sums(): return lax.psum((first, second), ('gx', 'gy', 'gz'))]
    all_gather x4 -> x0, blocking collectives: 57.9 us -> none  [operate(): lax.all_gather(loads, 'gz', axis=0, tiled=True)]
    dot_general x16 -> x0, matrix products: 25.6 us -> none  [the longest x4 13.4 us: operate(): jnp.einsum('rj,ij->ri', u, matrix, precision=lax.Precision.HIGHEST, prefe...]
    ppermute x24 -> x37, starting transfers between devices: 21.3 us -> 35.9 us  [the longest x35 33.2 us: shift(): return lax.ppermute(x, axis, [(i, (i + by) % n) for i in range(n)])]
    unnamed x40 -> x1, other arithmetic: 13.5 us -> 0.7 us
    pallas_call x0 -> x15, Pallas kernels: none -> 7.77 us  [call(): pl.pallas_call(kernel, out_shape=outs, in_specs=[pl.BlockSpec(memory_spac...]
    sub x3 -> x0, other arithmetic: 4.45 us -> none  [body(): resid = resid - alpha[:, None] * along]
    concatenate x8 -> x1, other arithmetic: 4.17 us -> 0.02 us  [body(): turned = jnp.concatenate([blocks[:, ::-1]] * 2, axis=1)]
  transfers between devices with their start and end apart: 24 -> 37, of which waited for: 16 -> 23; matrix products, arithmetic and copies ran while one was open for 0% -> 1% of each run, Pallas kernels for 0% -> 4%
where the time goes in v1:
time: 89.1 us; the launch traced here: 88.8 us
  waiting for transfers between devices  38.3 us (43%)
  starting transfers between devices  35.9 us (40%)
  Pallas kernels  7.77 us (9%)
  local copies, waits for them, and re-layouts  5.32 us (6%)
    ppermute x35, waiting for transfers between devices, shift(): return lax.ppermute(x, axis, [(i, (i + by) % n) for i in range(n)])  33.6 us
    ppermute x35, starting transfers between devices, shift(): return lax.ppermute(x, axis, [(i, (i + by) % n) for i in range(n)])  33.2 us
    pallas_call x15, Pallas kernels, call(): pl.pallas_call(kernel, out_shape=outs, in_specs=[pl.BlockSpec(memory_spac...  7.77 us
    unnamed x9, local copies, waits for them, and re-layouts  5.11 us
    ppermute x2, waiting for transfers between devices, far(): return lax.ppermute(x, ('gx', 'gy'), pairs)  4.75 us
    ppermute x2, starting transfers between devices, far(): return lax.ppermute(x, ('gx', 'gy'), pairs)  2.64 us
  transfers between devices with their start and end apart: 37, of which 23 were waited for; matrix products, arithmetic and copies ran while one was open for 1% of the time, Pallas kernels for 4%

profile of v1, /device:TPU:0, one launch (start us, length us, event | category | flops | bytes accessed | tf_op | source)
XLA Modules:
  0.0 88.8 jit_solution(9527495145076859305)
XLA Ops:
  3.7 5.0 %collective-permute-start.2 = (f32[8,128]{1,0:T(8,128)S(1)}, f32[8,128]{1,0:T(8,128)S(1)}, u32[]{:S(2)}, u32[]{:S(2)}) collective-permute-start(f32[8,128]{1,0:T(8,128)S(1)} %get-tuple-element.56.refs_3_), channel_id=1, source_target_pairs={{0,3},{1,0},{2,1},{3,2},{4,7},{5,4},{6,5},{7,6},{8,11},{9,8},{10,9... | collective-permute-start | bytes 12296 | tf_op jit(solution)/shard_map/ppermute | solution.py:271
  10.6 1.7 %copy-done = f32[1,1,1,768,768]{4,3,2,1,0:T(8,128)S(1)} copy-done((f32[1,1,1,768,768]{4,3,2,1,0:T(8,128)S(1)}, f32[1,1,1,768,768]{4,3,2,1,0:T(8,128)}, u32[]{:S(2)}) %copy-start) | copy-done | bytes 2359320
  14.5 1.6 %collective-permute-start.3 = (f32[256,128]{1,0:T(8,128)S(1)}, f32[256,128]{1,0:T(8,128)S(1)}, u32[]{:S(2)}, u32[]{:S(2)}) collective-permute-start(f32[256,128]{1,0:T(8,128)S(1)} %get-tuple-element.57.refs_0_), channel_id=1, source_target_pairs={{0,16},{16,0},{1,17},{17,1},{2,18},{18,2},{3,19},{19,3},{4,20},{20... | collective-permute-start | bytes 393224 | tf_op jit(solution)/shard_map/ppermute | solution.py:271
  16.6 2.8 %collective-permute-start.7 = (f32[128,128]{1,0:T(8,128)S(1)}, f32[128,128]{1,0:T(8,128)S(1)}, u32[]{:S(2)}, u32[]{:S(2)}) collective-permute-start(f32[128,128]{1,0:T(8,128)S(1)} %get-tuple-element.60.refs_3_), channel_id=1, source_target_pairs={{0,3},{1,0},{2,1},{3,2},{4,7},{5,4},{6,5},{7,6},{8,11},{9,8},{10,9... | collective-permute-start | bytes 196616 | tf_op jit(solution)/shard_map/ppermute | solution.py:271
  20.4 1.3 %collective-permute-done.7.refs_9_ = f32[128,128]{1,0:T(8,128)S(1)} collective-permute-done((f32[128,128]{1,0:T(8,128)S(1)}, f32[128,128]{1,0:T(8,128)S(1)}, u32[]{:S(2)}, u32[]{:S(2)}) %collective-permute-start.7) | collective-permute-done | bytes 65568 | tf_op jit(solution)/shard_map/ppermute | solution.py:271
  21.7 4.3 %collective-permute-done.6.refs_8_ = f32[128,128]{1,0:T(8,128)S(1)} collective-permute-done((f32[128,128]{1,0:T(8,128)S(1)}, f32[128,128]{1,0:T(8,128)S(1)}, u32[]{:S(2)}, u32[]{:S(2)}) %collective-permute-start.6) | collective-permute-done | bytes 65568 | tf_op jit(solution)/shard_map/ppermute | solution.py:271
  27.5 1.6 %collective-permute-start.8 = (f32[8,128]{1,0:T(8,128)S(1)}, f32[8,128]{1,0:T(8,128)S(1)}, u32[]{:S(2)}, u32[]{:S(2)}) collective-permute-start(f32[8,128]{1,0:T(8,128)S(1)} %get-tuple-element.66.refs_3_), channel_id=1, source_target_pairs={{0,1},{1,2},{2,3},{3,0},{4,5},{5,6},{6,7},{7,4},{8,9},{9,10},{10,1... | collective-permute-start | bytes 12296 | tf_op jit(solution)/shard_map/ppermute | solution.py:271
  31.1 1.8 %collective-permute-done.8.refs_4_ = f32[8,128]{1,0:T(8,128)S(1)} collective-permute-done((f32[8,128]{1,0:T(8,128)S(1)}, f32[8,128]{1,0:T(8,128)S(1)}, u32[]{:S(2)}, u32[]{:S(2)}) %collective-permute-start.8) | collective-permute-done | bytes 4128 | tf_op jit(solution)/shard_map/ppermute | solution.py:271
  34.4 1.6 %collective-permute-start.15 = (f32[128,128]{1,0:T(8,128)S(1)}, f32[128,128]{1,0:T(8,128)S(1)}, u32[]{:S(2)}, u32[]{:S(2)}) collective-permute-start(f32[128,128]{1,0:T(8,128)S(1)} %get-tuple-element.71.refs_3_), channel_id=1, source_target_pairs={{0,3},{1,0},{2,1},{3,2},{4,7},{5,4},{6,5},{7,6},{8,11},{9,8},{10,9... | collective-permute-start | bytes 196616 | tf_op jit(solution)/shard_map/ppermute | solution.py:271
  36.4 2.5 %collective-permute-done.15.refs_9_ = f32[128,128]{1,0:T(8,128)S(1)} collective-permute-done((f32[128,128]{1,0:T(8,128)S(1)}, f32[128,128]{1,0:T(8,128)S(1)}, u32[]{:S(2)}, u32[]{:S(2)}) %collective-permute-start.15) | collective-permute-done | bytes 65568 | tf_op jit(solution)/shard_map/ppermute | solution.py:271
  38.9 3.1 %collective-permute-done.14.refs_8_ = f32[128,128]{1,0:T(8,128)S(1)} collective-permute-done((f32[128,128]{1,0:T(8,128)S(1)}, f32[128,128]{1,0:T(8,128)S(1)}, u32[]{:S(2)}, u32[]{:S(2)}) %collective-permute-start.14) | collective-permute-done | bytes 65568 | tf_op jit(solution)/shard_map/ppermute | solution.py:271
  46.0 1.6 %collective-permute-done.17.refs_5_ = f32[16,128]{1,0:T(8,128)S(1)} collective-permute-done((f32[16,128]{1,0:T(8,128)S(1)}, f32[16,128]{1,0:T(8,128)S(1)}, u32[]{:S(2)}, u32[]{:S(2)}) %collective-permute-start.17) | collective-permute-done | bytes 8224 | tf_op jit(solution)/shard_map/ppermute | solution.py:271
  47.6 1.6 %collective-permute-done.16.refs_4_ = f32[16,128]{1,0:T(8,128)S(1)} collective-permute-done((f32[16,128]{1,0:T(8,128)S(1)}, f32[16,128]{1,0:T(8,128)S(1)}, u32[]{:S(2)}, u32[]{:S(2)}) %collective-permute-start.16) | collective-permute-done | bytes 8224 | tf_op jit(solution)/shard_map/ppermute | solution.py:271
  49.6 1.6 %collective-permute-start.19 = (f32[256,128]{1,0:T(8,128)S(1)}, f32[256,128]{1,0:T(8,128)S(1)}, u32[]{:S(2)}, u32[]{:S(2)}) collective-permute-start(f32[256,128]{1,0:T(8,128)S(1)} %get-tuple-element.75.refs_0_), channel_id=1, source_target_pairs={{0,16},{16,0},{1,17},{17,1},{2,18},{18,2},{3,19},{19,3},{4,20},{20... | collective-permute-start | bytes 393224 | tf_op jit(solution)/shard_map/ppermute | solution.py:271
  53.9 1.8 %collective-permute-done.24.refs_11_ = f32[8,128]{1,0:T(8,128)S(1)} collective-permute-done((f32[8,128]{1,0:T(8,128)S(1)}, f32[8,128]{1,0:T(8,128)S(1)}, u32[]{:S(2)}, u32[]{:S(2)}) %collective-permute-start.24) | collective-permute-done | bytes 4128 | tf_op jit(solution)/shard_map/ppermute | solution.py:300
  57.2 4.6 %collective-permute-done.22.refs_8_ = f32[128,128]{1,0:T(8,128)S(1)} collective-permute-done((f32[128,128]{1,0:T(8,128)S(1)}, f32[128,128]{1,0:T(8,128)S(1)}, u32[]{:S(2)}, u32[]{:S(2)}) %collective-permute-start.22) | collective-permute-done | bytes 65568 | tf_op jit(solution)/shard_map/ppermute | solution.py:271
  62.6 1.9 %collective-permute-start.25 = (f32[8,128]{1,0:T(8,128)S(1)}, f32[8,128]{1,0:T(8,128)S(1)}, u32[]{:S(2)}, u32[]{:S(2)}) collective-permute-start(f32[8,128]{1,0:T(8,128)S(1)} %get-tuple-element.88.refs_3_), channel_id=1, source_target_pairs={{0,1},{1,2},{2,3},{3,0},{4,5},{5,6},{6,7},{7,4},{8,9},{9,10},{10,1... | collective-permute-start | bytes 12296 | tf_op jit(solution)/shard_map/ppermute | solution.py:271
  67.1 1.4 %collective-permute-done.25.refs_4_ = f32[8,128]{1,0:T(8,128)S(1)} collective-permute-done((f32[8,128]{1,0:T(8,128)S(1)}, f32[8,128]{1,0:T(8,128)S(1)}, u32[]{:S(2)}, u32[]{:S(2)}) %collective-permute-start.25) | collective-permute-done | bytes 4128 | tf_op jit(solution)/shard_map/ppermute | solution.py:271
  70.0 1.7 %collective-permute-start.30 = (f32[136,128]{1,0:T(8,128)S(1)}, f32[136,128]{1,0:T(8,128)S(1)}, u32[]{:S(2)}, u32[]{:S(2)}) collective-permute-start(f32[136,128]{1,0:T(8,128)S(1)} %get-tuple-element.91.refs_1_), channel_id=1, source_target_pairs={{0,12},{4,0},{8,4},{12,8},{1,13},{5,1},{9,5},{13,9},{2,14},{6,2},{... | collective-permute-start | bytes 208904 | tf_op jit(solution)/shard_map/ppermute | solution.py:271
  71.7 2.0 %collective-permute-start.32 = (f32[128,128]{1,0:T(8,128)S(1)}, f32[128,128]{1,0:T(8,128)S(1)}, u32[]{:S(2)}, u32[]{:S(2)}) collective-permute-start(f32[128,128]{1,0:T(8,128)S(1)} %get-tuple-element.93.refs_3_), channel_id=1, source_target_pairs={{0,3},{1,0},{2,1},{3,2},{4,7},{5,4},{6,5},{7,6},{8,11},{9,8},{10,9... | collective-permute-start | bytes 196616 | tf_op jit(solution)/shard_map/ppermute | solution.py:271
  74.0 3.6 %collective-permute-start.35 = (f32[8,128]{1,0:T(8,128)S(1)}, f32[8,128]{1,0:T(8,128)S(1)}, u32[]{:S(2)}, u32[]{:S(2)}) collective-permute-start(f32[8,128]{1,0:T(8,128)S(1)} %shard_map.71.refs_0_), channel_id=1, source_target_pairs={{0,3},{1,0},{2,1},{3,2},{4,7},{5,4},{6,5},{7,6},{8,11},{9,8},{10,9... | collective-permute-start | bytes 12296 | tf_op jit(solution)/shard_map/ppermute | solution.py:271
  78.9 3.2 %collective-permute-done.34.refs_2_ = f32[8,128]{1,0:T(8,128)S(1)} collective-permute-done((f32[8,128]{1,0:T(8,128)S(1)}, f32[8,128]{1,0:T(8,128)S(1)}, u32[]{:S(2)}, u32[]{:S(2)}) %collective-permute-start.34) | collective-permute-done | bytes 4128 | tf_op jit(solution)/shard_map/ppermute | solution.py:271
  83.0 1.6 %collective-permute-start.36 = (f32[8,128]{1,0:T(8,128)S(1)}, f32[8,128]{1,0:T(8,128)S(1)}, u32[]{:S(2)}, u32[]{:S(2)}) collective-permute-start(f32[8,128]{1,0:T(8,128)S(1)} %shard_map.72.refs_10_), channel_id=1, source_target_pairs={{0,24},{4,28},{8,16},{12,20},{16,8},{20,12},{24,0},{28,4},{1,25},{... | collective-permute-start | bytes 12296 | tf_op jit(solution)/shard_map/ppermute | solution.py:300
  84.6 2.9 %collective-permute-done.36.refs_11_ = f32[8,128]{1,0:T(8,128)S(1)} collective-permute-done((f32[8,128]{1,0:T(8,128)S(1)}, f32[8,128]{1,0:T(8,128)S(1)}, u32[]{:S(2)}, u32[]{:S(2)}) %collective-permute-start.36) | collective-permute-done | bytes 4128 | tf_op jit(solution)/shard_map/ppermute | solution.py:300
  (81 shorter events, 31.1 us)
Async XLA Ops:
  3.7 10.5 %collective-permute-start.2 = (f32[8,128]{1,0:T(8,128)S(1)}, f32[8,128]{1,0:T(8,128)S(1)}, u32[]{:S(2)}, u32[]{:S(2)}) collective-permute-start(f32[8,128]{1,0:T(8,128)S(1)} %get-tuple-element.56.refs_3_), channel_id=1, source_target_pairs={{0,3},{1,0},{2,1},{3,2},{4,7},{5,4},{6,5},{7,6},{8,11},{9,8},{10,9... | collective-permute-start | bytes 12296 | tf_op jit(solution)/shard_map/ppermute | solution.py:271
  8.7 5.4 %collective-permute-start.1 = (f32[8,128]{1,0:T(8,128)S(1)}, f32[8,128]{1,0:T(8,128)S(1)}, u32[]{:S(2)}, u32[]{:S(2)}) collective-permute-start(f32[8,128]{1,0:T(8,128)S(1)} %get-tuple-element.56.refs_3_), channel_id=1, source_target_pairs={{0,2},{1,3},{2,0},{3,1},{4,6},{5,7},{6,4},{7,5},{8,10},{9,11},{10,... | collective-permute-start | bytes 12296 | tf_op jit(solution)/shard_map/ppermute | solution.py:271
  8.7 5.4 %collective-permute-start = (f32[8,128]{1,0:T(8,128)S(1)}, f32[8,128]{1,0:T(8,128)S(1)}, u32[]{:S(2)}, u32[]{:S(2)}) collective-permute-start(f32[8,128]{1,0:T(8,128)S(1)} %get-tuple-element.56.refs_3_), channel_id=1, source_target_pairs={{0,1},{1,2},{2,3},{3,0},{4,5},{5,6},{6,7},{7,4},{8,9},{9,10},{10,1... | collective-permute-start | bytes 12296 | tf_op jit(solution)/shard_map/ppermute | solution.py:271
  14.5 11.5 %collective-permute-start.3 = (f32[256,128]{1,0:T(8,128)S(1)}, f32[256,128]{1,0:T(8,128)S(1)}, u32[]{:S(2)}, u32[]{:S(2)}) collective-permute-start(f32[256,128]{1,0:T(8,128)S(1)} %get-tuple-element.57.refs_0_), channel_id=1, source_target_pairs={{0,16},{16,0},{1,17},{17,1},{2,18},{18,2},{3,19},{19,3},{4,20},{20... | collective-permute-start | bytes 393224 | tf_op jit(solution)/shard_map/ppermute | solution.py:271
  16.6 5.1 %collective-permute-start.7 = (f32[128,128]{1,0:T(8,128)S(1)}, f32[128,128]{1,0:T(8,128)S(1)}, u32[]{:S(2)}, u32[]{:S(2)}) collective-permute-start(f32[128,128]{1,0:T(8,128)S(1)} %get-tuple-element.60.refs_3_), channel_id=1, source_target_pairs={{0,3},{1,0},{2,1},{3,2},{4,7},{5,4},{6,5},{7,6},{8,11},{9,8},{10,9... | collective-permute-start | bytes 196616 | tf_op jit(solution)/shard_map/ppermute | solution.py:271
  19.4 6.6 %collective-permute-start.6 = (f32[128,128]{1,0:T(8,128)S(1)}, f32[128,128]{1,0:T(8,128)S(1)}, u32[]{:S(2)}, u32[]{:S(2)}) collective-permute-start(f32[128,128]{1,0:T(8,128)S(1)} %get-tuple-element.61.refs_4_), channel_id=1, source_target_pairs={{0,1},{1,2},{2,3},{3,0},{4,5},{5,6},{6,7},{7,4},{8,9},{9,10},{10,1... | collective-permute-start | bytes 196616 | tf_op jit(solution)/shard_map/ppermute | solution.py:271
  27.5 5.4 %collective-permute-start.8 = (f32[8,128]{1,0:T(8,128)S(1)}, f32[8,128]{1,0:T(8,128)S(1)}, u32[]{:S(2)}, u32[]{:S(2)}) collective-permute-start(f32[8,128]{1,0:T(8,128)S(1)} %get-tuple-element.66.refs_3_), channel_id=1, source_target_pairs={{0,1},{1,2},{2,3},{3,0},{4,5},{5,6},{6,7},{7,4},{8,9},{9,10},{10,1... | collective-permute-start | bytes 12296 | tf_op jit(solution)/shard_map/ppermute | solution.py:271
  33.3 8.7 %collective-permute-start.11 = (f32[264,128]{1,0:T(8,128)S(1)}, f32[264,128]{1,0:T(8,128)S(1)}, u32[]{:S(2)}, u32[]{:S(2)}) collective-permute-start(f32[264,128]{1,0:T(8,128)S(1)} %get-tuple-element.68.refs_0_), channel_id=1, source_target_pairs={{0,16},{16,0},{1,17},{17,1},{2,18},{18,2},{3,19},{19,3},{4,20},{20... | collective-permute-start | bytes 405512 | tf_op jit(solution)/shard_map/ppermute | solution.py:271
  33.9 8.1 %collective-permute-start.13 = (f32[136,128]{1,0:T(8,128)S(1)}, f32[136,128]{1,0:T(8,128)S(1)}, u32[]{:S(2)}, u32[]{:S(2)}) collective-permute-start(f32[136,128]{1,0:T(8,128)S(1)} %get-tuple-element.69.refs_1_), channel_id=1, source_target_pairs={{0,12},{4,0},{8,4},{12,8},{1,13},{5,1},{9,5},{13,9},{2,14},{6,2},{... | collective-permute-start | bytes 208904 | tf_op jit(solution)/shard_map/ppermute | solution.py:271
  33.9 8.1 %collective-permute-start.12 = (f32[136,128]{1,0:T(8,128)S(1)}, f32[136,128]{1,0:T(8,128)S(1)}, u32[]{:S(2)}, u32[]{:S(2)}) collective-permute-start(f32[136,128]{1,0:T(8,128)S(1)} %get-tuple-element.70.refs_2_), channel_id=1, source_target_pairs={{0,4},{4,8},{8,12},{12,0},{1,5},{5,9},{9,13},{13,1},{2,6},{6,10},{... | collective-permute-start | bytes 208904 | tf_op jit(solution)/shard_map/ppermute | solution.py:271
  34.4 4.6 %collective-permute-start.15 = (f32[128,128]{1,0:T(8,128)S(1)}, f32[128,128]{1,0:T(8,128)S(1)}, u32[]{:S(2)}, u32[]{:S(2)}) collective-permute-start(f32[128,128]{1,0:T(8,128)S(1)} %get-tuple-element.71.refs_3_), channel_id=1, source_target_pairs={{0,3},{1,0},{2,1},{3,2},{4,7},{5,4},{6,5},{7,6},{8,11},{9,8},{10,9... | collective-permute-start | bytes 196616 | tf_op jit(solution)/shard_map/ppermute | solution.py:271
  35.9 6.1 %collective-permute-start.14 = (f32[128,128]{1,0:T(8,128)S(1)}, f32[128,128]{1,0:T(8,128)S(1)}, u32[]{:S(2)}, u32[]{:S(2)}) collective-permute-start(f32[128,128]{1,0:T(8,128)S(1)} %get-tuple-element.72.refs_4_), channel_id=1, source_target_pairs={{0,1},{1,2},{2,3},{3,0},{4,5},{5,6},{6,7},{7,4},{8,9},{9,10},{10,1... | collective-permute-start | bytes 196616 | tf_op jit(solution)/shard_map/ppermute | solution.py:271
  43.0 4.5 %collective-permute-start.17 = (f32[16,128]{1,0:T(8,128)S(1)}, f32[16,128]{1,0:T(8,128)S(1)}, u32[]{:S(2)}, u32[]{:S(2)}) collective-permute-start(f32[16,128]{1,0:T(8,128)S(1)} %get-tuple-element.74.refs_3_), channel_id=1, source_target_pairs={{0,2},{1,3},{2,0},{3,1},{4,6},{5,7},{6,4},{7,5},{8,10},{9,11},{10,... | collective-permute-start | bytes 24584 | tf_op jit(solution)/shard_map/ppermute | solution.py:271
  43.8 5.4 %collective-permute-start.16 = (f32[16,128]{1,0:T(8,128)S(1)}, f32[16,128]{1,0:T(8,128)S(1)}, u32[]{:S(2)}, u32[]{:S(2)}) collective-permute-start(f32[16,128]{1,0:T(8,128)S(1)} %get-tuple-element.74.refs_3_), channel_id=1, source_target_pairs={{0,1},{1,2},{2,3},{3,0},{4,5},{5,6},{6,7},{7,4},{8,9},{9,10},{10,1... | collective-permute-start | bytes 24584 | tf_op jit(solution)/shard_map/ppermute | solution.py:271
  49.6 12.3 %collective-permute-start.19 = (f32[256,128]{1,0:T(8,128)S(1)}, f32[256,128]{1,0:T(8,128)S(1)}, u32[]{:S(2)}, u32[]{:S(2)}) collective-permute-start(f32[256,128]{1,0:T(8,128)S(1)} %get-tuple-element.75.refs_0_), channel_id=1, source_target_pairs={{0,16},{16,0},{1,17},{17,1},{2,18},{18,2},{3,19},{19,3},{4,20},{20... | collective-permute-start | bytes 393224 | tf_op jit(solution)/shard_map/ppermute | solution.py:271
  51.1 4.6 %collective-permute-start.24 = (f32[8,128]{1,0:T(8,128)S(1)}, f32[8,128]{1,0:T(8,128)S(1)}, u32[]{:S(2)}, u32[]{:S(2)}) collective-permute-start(f32[8,128]{1,0:T(8,128)S(1)} %get-tuple-element.80.refs_10_), channel_id=1, source_target_pairs={{0,24},{4,28},{8,16},{12,20},{16,8},{20,12},{24,0},{28,4},{1,25},{... | collective-permute-start | bytes 12296 | tf_op jit(solution)/shard_map/ppermute | solution.py:300
  55.7 6.1 %collective-permute-start.22 = (f32[128,128]{1,0:T(8,128)S(1)}, f32[128,128]{1,0:T(8,128)S(1)}, u32[]{:S(2)}, u32[]{:S(2)}) collective-permute-start(f32[128,128]{1,0:T(8,128)S(1)} %get-tuple-element.79.refs_4_), channel_id=1, source_target_pairs={{0,1},{1,2},{2,3},{3,0},{4,5},{5,6},{6,7},{7,4},{8,9},{9,10},{10,1... | collective-permute-start | bytes 196616 | tf_op jit(solution)/shard_map/ppermute | solution.py:271
  62.5 4.6 %collective-permute-start.26 = (f32[8,128]{1,0:T(8,128)S(1)}, f32[8,128]{1,0:T(8,128)S(1)}, u32[]{:S(2)}, u32[]{:S(2)}) collective-permute-start(f32[8,128]{1,0:T(8,128)S(1)} %get-tuple-element.88.refs_3_), channel_id=1, source_target_pairs={{0,2},{1,3},{2,0},{3,1},{4,6},{5,7},{6,4},{7,5},{8,10},{9,11},{10,... | collective-permute-start | bytes 12296 | tf_op jit(solution)/shard_map/ppermute | solution.py:271
  62.6 5.9 %collective-permute-start.25 = (f32[8,128]{1,0:T(8,128)S(1)}, f32[8,128]{1,0:T(8,128)S(1)}, u32[]{:S(2)}, u32[]{:S(2)}) collective-permute-start(f32[8,128]{1,0:T(8,128)S(1)} %get-tuple-element.88.refs_3_), channel_id=1, source_target_pairs={{0,1},{1,2},{2,3},{3,0},{4,5},{5,6},{6,7},{7,4},{8,9},{9,10},{10,1... | collective-permute-start | bytes 12296 | tf_op jit(solution)/shard_map/ppermute | solution.py:271
  68.9 5.1 %collective-permute-start.28 = (f32[264,128]{1,0:T(8,128)S(1)}, f32[264,128]{1,0:T(8,128)S(1)}, u32[]{:S(2)}, u32[]{:S(2)}) collective-permute-start(f32[264,128]{1,0:T(8,128)S(1)} %get-tuple-element.90.refs_0_), channel_id=1, source_target_pairs={{0,16},{16,0},{1,17},{17,1},{2,18},{18,2},{3,19},{19,3},{4,20},{20... | collective-permute-start | bytes 405512 | tf_op jit(solution)/shard_map/ppermute | solution.py:271
  71.7 12.9 %collective-permute-start.32 = (f32[128,128]{1,0:T(8,128)S(1)}, f32[128,128]{1,0:T(8,128)S(1)}, u32[]{:S(2)}, u32[]{:S(2)}) collective-permute-start(f32[128,128]{1,0:T(8,128)S(1)} %get-tuple-element.93.refs_3_), channel_id=1, source_target_pairs={{0,3},{1,0},{2,1},{3,2},{4,7},{5,4},{6,5},{7,6},{8,11},{9,8},{10,9... | collective-permute-start | bytes 196616 | tf_op jit(solution)/shard_map/ppermute | solution.py:271
  73.7 10.9 %collective-permute-start.31 = (f32[128,128]{1,0:T(8,128)S(1)}, f32[128,128]{1,0:T(8,128)S(1)}, u32[]{:S(2)}, u32[]{:S(2)}) collective-permute-start(f32[128,128]{1,0:T(8,128)S(1)} %get-tuple-element.94.refs_4_), channel_id=1, source_target_pairs={{0,1},{1,2},{2,3},{3,0},{4,5},{5,6},{6,7},{7,4},{8,9},{9,10},{10,1... | collective-permute-start | bytes 196616 | tf_op jit(solution)/shard_map/ppermute | solution.py:271
  74.0 4.9 %collective-permute-start.35 = (f32[8,128]{1,0:T(8,128)S(1)}, f32[8,128]{1,0:T(8,128)S(1)}, u32[]{:S(2)}, u32[]{:S(2)}) collective-permute-start(f32[8,128]{1,0:T(8,128)S(1)} %shard_map.71.refs_0_), channel_id=1, source_target_pairs={{0,3},{1,0},{2,1},{3,2},{4,7},{5,4},{6,5},{7,6},{8,11},{9,8},{10,9... | collective-permute-start | bytes 12296 | tf_op jit(solution)/shard_map/ppermute | solution.py:271
  77.6 5.4 %collective-permute-start.33 = (f32[8,128]{1,0:T(8,128)S(1)}, f32[8,128]{1,0:T(8,128)S(1)}, u32[]{:S(2)}, u32[]{:S(2)}) collective-permute-start(f32[8,128]{1,0:T(8,128)S(1)} %shard_map.71.refs_0_), channel_id=1, source_target_pairs={{0,1},{1,2},{2,3},{3,0},{4,5},{5,6},{6,7},{7,4},{8,9},{9,10},{10,1... | collective-permute-start | bytes 12296 | tf_op jit(solution)/shard_map/ppermute | solution.py:271
  (17 other events, 56.2 us)

commit v2 on v0

v2 whole, which is shorter than its diff:
```python
import functools

import jax
import jax.numpy as jnp
from jax import lax
from jax.experimental import pallas as pl
from jax.experimental.pallas import tpu as pltpu
from jax.sharding import PartitionSpec as P

F32 = jnp.float32
BF16 = jnp.bfloat16
HI = lax.Precision.HIGHEST
PAD = 8
ORDER = (0, -1, 1, 2)
VMEM_LIMIT = 24 * 1024 * 1024


def sds(shape, dtype=F32):
    return jax.ShapeDtypeStruct(shape, dtype)


def call(kernel, ins, outs, flops=0):
    names_in, names_out = list(ins), list(outs)
    nbytes = sum(a.size * a.dtype.itemsize for a in list(ins.values()) + list(outs.values()))

    def run(*refs):
        n = len(names_in)
        kernel(dict(zip(names_in, refs[:n])), dict(zip(names_out, refs[n:])))

    vmem = pl.BlockSpec(memory_space=pltpu.VMEM)
    res = pl.pallas_call(
        run,
        out_shape=[outs[n] for n in names_out],
        in_specs=[vmem] * len(names_in),
        out_specs=[vmem] * len(names_out),
        compiler_params=pltpu.CompilerParams(vmem_limit_bytes=VMEM_LIMIT),
        cost_estimate=pl.CostEstimate(flops=flops, bytes_accessed=nbytes, transcendentals=0),
    )(*[ins[n] for n in names_in])
    return dict(zip(names_out, res))


def split(x):
    high = x.astype(BF16)
    return high, (x - high.astype(F32)).astype(BF16)


def split3(x):
    high = x.astype(BF16)
    rest = x - high.astype(F32)
    mid = rest.astype(BF16)
    return high, mid, (rest - mid.astype(F32)).astype(BF16)


def mode_pieces(modes):
    high, mid, low = split3(modes.T)
    return jnp.concatenate([high, high, mid, mid, high, low], axis=1)


def amp_pieces(amp):
    high, mid, low = split3(amp)
    return jnp.concatenate([high, mid, high, mid, low, high], axis=0)


def dot32(a, b):
    return jnp.dot(a, b, precision=HI, preferred_element_type=F32)


def dot16(a, b):
    return jnp.dot(a, b, preferred_element_type=F32)


def col_sum(x):
    return jnp.sum(x, axis=0, keepdims=True)


def half_dot(a, b):
    return 0.5 * col_sum(a * b)


def row(x, i):
    return x[i:i + 1, :]


def multiply(face, high, low, vec, at):
    cols = vec.shape[1] // 2
    both = dot16(high, vec) + dot16(low, vec)
    return both[:, :cols] + both[:, cols:]


def send_product(face, part, y, o):
    if part < 2:
        o["y"][2 * part * face:2 * (part + 1) * face, :] = y
    else:
        o["zm"][0:face, :] = y[0:face]
        o["zp"][0:face, :] = y[face:]


def send_rows(face, rows, at, o):
    n = rows.shape[0]
    for name, start in (("zm", face), ("zp", face), ("z2", 0)):
        o[name][start + at:start + at + n, :] = rows


def product(face, vec, i, o, want_dot):
    cols = vec.shape[1]
    halves = jnp.concatenate(split(vec), axis=1)
    total = None
    for part in range(3):
        at = slice(2 * part * face, 2 * (part + 1) * face)
        y = multiply(face, i["s_high"][at, :], i["s_low"][at, :], halves, at)
        send_product(face, part, y, o)
        if want_dot:
            dot = col_sum(vec[at] * y)
            total = dot if total is None else total + dot
    send_rows(face, dot32(i["modes"][...], vec), 0, o)
    return total


def stack_rows(rows, cols):
    zero = jnp.zeros((1, cols), F32)
    return jnp.concatenate(list(rows) + [zero] * (PAD - len(rows)), axis=0)


def first_kernel(face, nz, n_modes, turn, resid_hbm, schur_hbm, modes_hbm, coarse_hbm, *refs):
    names = ["r0", "s_high", "s_low", "modes", "mt", "c_own", "y", "zm", "zp", "z2"]
    o = dict(zip(names, refs[:len(names)]))
    resid, schur, mode_rows, coarse, sems = refs[len(names):]
    two = 2 * face
    copies = [
        pltpu.make_async_copy(modes_hbm, mode_rows, sems.at[0]),
        pltpu.make_async_copy(resid_hbm, resid, sems.at[1]),
        pltpu.make_async_copy(coarse_hbm, coarse, sems.at[2]),
    ]
    for part in range(3):
        at = pl.ds(part * two, two)
        copies.append(pltpu.make_async_copy(schur_hbm.at[at, :], schur.at[at, :], sems.at[3 + part]))
    for copy in copies:
        copy.start()

    copies[0].wait()
    modes = jnp.concatenate([mode_rows[m] for m in range(n_modes)], axis=0)
    modes = jnp.concatenate([modes, jnp.zeros((PAD - n_modes, modes.shape[1]), F32)], axis=0)
    o["modes"][...] = modes
    o["mt"][...] = mode_pieces(modes)

    copies[1].wait()
    for f in range(6):
        part = resid[:, f * face:(f + 1) * face].T
        o["r0"][f * face:(f + 1) * face, :] = part if f % 2 == 0 else -part
    r0 = o["r0"][...]
    cols = r0.shape[1]
    send_rows(face, dot32(modes, r0), 0, o)

    copies[2].wait()
    rows = jnp.concatenate([coarse[m] for m in range(n_modes)], axis=0)
    rows = jnp.concatenate([rows, jnp.zeros((PAD - n_modes, rows.shape[1]), F32)], axis=0)
    wide = nz * PAD
    source = lax.broadcasted_iota(jnp.int32, (nz * n_modes, wide), 0)
    place = lax.broadcasted_iota(jnp.int32, (nz * n_modes, wide), 1)
    block, mode = place // PAD, place % PAD

    def ordered(holder):
        if holder is None:
            device = block
        else:
            offset = jnp.zeros_like(block)
            for at, by in enumerate(ORDER):
                offset = jnp.where(block == at, by, offset)
            device = (holder + offset + 2 * nz) % nz
        pick = jnp.where((source == device * n_modes + mode) & (mode < n_modes), 1.0, 0.0)
        return dot32(rows, pick)

    if turn:
        me = lax.axis_index("gz")
        o["c_own"][...] = ordered(me)
        for name, by, start in (("zm", -1, face + 3 * PAD), ("zp", 1, face + 3 * PAD), ("z2", 2, 2 * PAD)):
            o[name][start:start + PAD, :] = jnp.zeros((PAD, cols), F32)
            o[name][start:start + PAD, 0:wide] = ordered(me + by)
    else:
        o["c_own"][...] = ordered(None)
    o["zm"][face + 2 * PAD:face + 3 * PAD, :] = modes[:, 4 * face:5 * face]
    o["zp"][face + 2 * PAD:face + 3 * PAD, :] = modes[:, 5 * face:6 * face]

    halves = jnp.concatenate(split(r0), axis=1)
    curv = jnp.zeros((1, cols), F32)
    for part in range(3):
        at = slice(part * two, (part + 1) * two)
        copies[3 + part].wait()
        high, low = split(schur[at, :])
        o["s_high"][at, :] = high
        o["s_low"][at, :] = low
        y = multiply(face, high, low, halves, at)
        send_product(face, part, y, o)
        curv = curv + col_sum(r0[at] * y)
    send_rows(face, stack_rows([half_dot(r0, r0), curv], cols), PAD, o)


def column_rows(face, i, at):
    return [i["zm"][face + at:face + at + PAD, :], i["gzl"][face + at:face + at + PAD, :],
            i["gzh"][face + at:face + at + PAD, :], i["gz2"][at:at + PAD, :]]


def value_kernel(face, stage, i, o):
    gathered = "g_all" in i
    loads = i["g_all"][...] if gathered else jnp.concatenate(column_rows(face, i, 0), axis=0)
    if stage == 0:
        low = mode_pieces(i["gzl"][face + 2 * PAD:face + 3 * PAD, :])
        high = mode_pieces(i["gzh"][face + 2 * PAD:face + 3 * PAD, :])
        o["mt_low"][...] = low
        o["mt_high"][...] = high
        if gathered:
            coarse = i["c_all"][...]
        else:
            wide = i["c_own"].shape[1]
            at = face + 3 * PAD
            coarse = jnp.concatenate([
                i["c_own"][...], i["gzl"][at:at + PAD, 0:wide], i["gzh"][at:at + PAD, 0:wide],
                i["gz2"][2 * PAD:3 * PAD, 0:wide]], axis=0)
            o["c_all"][...] = coarse
    else:
        low, high, coarse = i["mt_low"][...], i["mt_high"][...], i["c_all"][...]
    amp = dot32(coarse, loads)
    own = amp_pieces(amp[0:PAD])
    mt = i["mt"]
    xy = i["y"][...] + dot16(mt[0:4 * face, :], own)
    z_low = i["zm"][0:face, :] + dot16(mt[4 * face:5 * face, :], own)
    z_low = z_low - (i["gzl"][0:face, :] + dot16(low, amp_pieces(amp[PAD:2 * PAD])))
    z_high = i["zp"][0:face, :] + dot16(mt[5 * face:6 * face, :], own)
    z_high = z_high - (i["gzh"][0:face, :] + dot16(high, amp_pieces(amp[2 * PAD:3 * PAD])))
    cols = loads.shape[1]

    if stage != 2:
        if gathered:
            dots = i["d_all"][...]
            quad = col_sum(loads * amp[3 * PAD:])
        else:
            parts = column_rows(face, i, PAD)
            dots = (parts[0] + parts[1]) + (parts[2] + parts[3])
            quad = col_sum(loads * amp)
        at = {0: 1, 1: 1, 3: 5}[stage]
        dots = jnp.concatenate([dots[0:at], row(dots, at) + quad, dots[at + 1:]], axis=0)
    if stage == 1:
        sums = i["sum_near"][...] + i["sum_far"][...]
        alpha0 = row(sums, 0) / row(sums, 1)
        ratio = alpha0 / row(i["scale"], 0)
        o["known"][...] = stack_rows([row(sums, 0), row(sums, 1), alpha0], cols)
        dots = dots * (ratio * ratio)
        xy, z_low, z_high = xy * ratio, z_low * ratio, z_high * ratio
    o["z"][0:face, :] = z_low
    o["z"][face:, :] = z_high
    o["xb"][0:2 * face, :] = xy[0:2 * face]
    o["ym"][0:face, :] = xy[2 * face:3 * face]
    o["yp"][0:face, :] = xy[3 * face:]
    if stage != 2:
        o["xb"][2 * face:, :] = dots
        o["ym"][face:, :] = dots
        o["yp"][face:, :] = dots


def assemble(face, i):
    f = face
    return jnp.concatenate([
        i["xb"][0:f, :] - i["gxb"][f:2 * f, :],
        i["xb"][f:2 * f, :] - i["gxb"][0:f, :],
        i["ym"][0:f, :] - i["gyl"][0:f, :],
        i["yp"][0:f, :] - i["gyh"][0:f, :],
        i["z"][...],
    ], axis=0)


def near_sum(face, i):
    f = face
    total = i["xb"][2 * f:2 * f + PAD, :] + i["gxb"][2 * f:2 * f + PAD, :]
    return total + (i["gyl"][f:f + PAD, :] + i["gyh"][f:f + PAD, :])


def second_kernel(face, i, o):
    w0 = assemble(face, i)
    o["w0"][...] = w0
    own = i["xb"][2 * face:2 * face + PAD, :]
    scale = row(own, 0) / row(own, 1)
    cols = w0.shape[1]
    o["scale"][...] = stack_rows([scale], cols)
    if "near" in o:
        o["near"][...] = near_sum(face, i)
    vec = scale * w0
    curv = product(face, vec, i, o, True)
    send_rows(face, stack_rows([half_dot(vec, vec), curv], cols), PAD, o)


def third_kernel(face, i, o):
    q = assemble(face, i)
    w1 = i["w0"][...] - q
    o["q"][...] = q
    o["w1"][...] = w1
    if "near" in o:
        o["near"][...] = near_sum(face, i)
    product(face, row(i["known"], 2) * w1, i, o, False)


def fourth_kernel(face, i, o):
    b = assemble(face, i)
    m0, m1, alpha0 = (row(i["known"], k) for k in range(3))
    sums = i["sum_near"][...] + i["sum_far"][...]
    m2, m3 = row(sums, 0), row(sums, 1)
    norm1 = m2 - m0
    curv1 = m1 - 2.0 * (m2 / alpha0) + m3
    beta1 = norm1 / m0
    alpha1 = norm1 / (curv1 - beta1 * norm1 / alpha0)
    r0, w0, w1, q = i["r0"][...], i["w0"][...], i["w1"][...], i["q"][...]
    ratio = alpha1 / alpha0
    r1 = r0 - alpha0 * w0
    p1 = r1 + beta1 * r0
    s1 = alpha1 * (w1 + beta1 * w0)
    r2 = r1 - s1
    z1 = ratio * (b + beta1 * q)
    w2 = w1 - z1
    vec = alpha1 * w2
    cols = w2.shape[1]
    o["r2"][...] = r2
    o["w2"][...] = vec
    o["p1"][...] = p1
    o["s1"][...] = s1
    o["z1"][...] = z1
    o["m2"][...] = alpha0 * r0 + alpha1 * p1
    o["known"][...] = stack_rows([norm1, alpha1], cols)
    curv = product(face, vec, i, o, True)
    send_rows(face, stack_rows([
        half_dot(r2, r2), half_dot(r2, w2), half_dot(vec, vec), half_dot(vec, s1),
        half_dot(s1, s1), curv, half_dot(z1, vec), half_dot(s1, z1)], cols), PAD, o)


def near_kernel(face, i, o):
    o["near"][...] = near_sum(face, i)


def last_kernel(face, i, o):
    d = i["sum_near"][...] + i["sum_far"][...]
    rr, rw, ww, ws, ss, wc, sc, sz = (row(d, k) for k in range(8))
    norm1, alpha1 = row(i["known"], 0), row(i["known"], 1)
    beta2 = rr / norm1
    alpha2 = rr / (rw - beta2 * rr / alpha1)
    ratio = alpha2 / alpha1
    ratio2 = ratio * ratio
    norm3 = ratio2 * (ww + 2.0 * beta2 * ws + beta2 * beta2 * ss) - rr
    curv3 = rw - 2.0 * (ratio2 / alpha2) * (ww + beta2 * ws)
    curv3 = curv3 + ratio2 * (wc + 2.0 * beta2 * sc + beta2 * beta2 * sz)
    beta3 = norm3 / rr
    alpha3 = norm3 / (curv3 - beta3 * norm3 / alpha2)
    c3 = assemble(face, i)
    w2, s1 = i["w2"][...], i["s1"][...]
    p2 = i["r2"][...] + beta2 * i["p1"][...]
    s2 = w2 + beta2 * s1
    r3 = i["r2"][...] - ratio * s2
    w3 = w2 / alpha1 - ratio * (c3 + beta2 * i["z1"][...])
    mult = i["m2"][...] + alpha2 * p2 + alpha3 * (r3 + beta3 * p2)
    resid = r3 - alpha3 * (w3 + (beta3 / alpha1) * s2)
    for f in range(6):
        at = slice(f * face, (f + 1) * face)
        sign = 1.0 if f % 2 == 0 else -1.0
        o["mult"][:, at] = sign * mult[at, :].T
        o["resid"][:, at] = sign * resid[at, :].T


def body(sizes, residual_in, schur, modes, coarse_inv):
    nx, ny, nz = sizes
    resid = residual_in[0, 0, 0]
    matrix = schur[0, 0, 0]
    loads, width = resid.shape
    face = width // 6
    n_modes = modes.shape[3]
    mode_rows = modes.reshape(n_modes, 1, width)
    coarse_rows = coarse_inv.reshape(n_modes, 1, nz * n_modes)
    small = (nx, ny, nz) == (2, 4, 4)

    def shift(x, axis, by):
        n = lax.axis_size(axis)
        return lax.ppermute(x, axis, [(k, (k + by) % n) for k in range(n)])

    def far(x):
        pairs = []
        for a in range(nx):
            for b in range(ny):
                pairs.append((a * ny + b, (a + 1) % nx * ny + (b + 2) % ny))
        return lax.ppermute(x, ("gx", "gy"), pairs)

    def total(x):
        return dict(sum_near=lax.psum(x, ("gx", "gy")), sum_far=jnp.zeros_like(x))

    vec = sds((width, loads))
    rows = sds((PAD, loads))
    half = sds((width, width), BF16)
    flops = 2 * width * width * 2 * loads * 2

    def z_out(extra):
        return dict(y=sds((4 * face, loads)), zm=sds((face + PAD + extra, loads)),
                    zp=sds((face + PAD + extra, loads)), z2=sds((PAD + min(extra, 2 * PAD), loads)))

    def z_exchange(a, with_dots):
        got = dict(zm=a["zm"], zp=a["zp"], y=a["y"], gzl=shift(a["zp"], "gz", 1), gzh=shift(a["zm"], "gz", -1))
        if small:
            got["gz2"] = shift(a["z2"], "gz", 2)
        else:
            got["g_all"] = lax.all_gather(a["z2"][0:PAD], "gz", axis=0, tiled=True)
            if with_dots:
                got["d_all"] = lax.psum(a["z2"][PAD:2 * PAD], "gz")
        return got

    def value(stage, ins):
        extra = 0 if stage == 2 else PAD
        outs = dict(z=sds((2 * face, loads)), xb=sds((2 * face + extra, loads)),
                    ym=sds((face + extra, loads)), yp=sds((face + extra, loads)))
        if stage == 0:
            outs.update(mt_low=sds((face, 6 * PAD), BF16), mt_high=sds((face, 6 * PAD), BF16))
            if small:
                outs["c_all"] = sds((nz * PAD, nz * PAD))
        if stage == 1:
            outs["known"] = rows
        return call(functools.partial(value_kernel, face, stage), ins, outs, flops=2 * width * loads * 48)

    def xy_exchange(v):
        got = {name: v[name] for name in ("z", "xb", "ym", "yp")}
        if nx == 2:
            got["gxb"] = shift(v["xb"], "gx", 1)
        else:
            low, high, rest = v["xb"][:face], v["xb"][face:2 * face], v["xb"][2 * face:]
            got["gxb"] = jnp.concatenate([shift(low, "gx", -1), shift(high, "gx", 1), rest], axis=0)
        got["gyl"] = shift(v["yp"], "gy", 1)
        got["gyh"] = shift(v["ym"], "gy", -1)
        return got

    near = dict(near=rows) if small else {}

    hbm = pl.BlockSpec(memory_space=pltpu.HBM)
    vmem = pl.BlockSpec(memory_space=pltpu.VMEM)
    outs = dict(r0=vec, s_high=half, s_low=half, modes=sds((PAD, width)), mt=sds((width, 6 * PAD), BF16),
                c_own=sds((PAD, nz * PAD)), **z_out(3 * PAD))
    res = pl.pallas_call(
        functools.partial(first_kernel, face, nz, n_modes, small),
        out_shape=list(outs.values()),
        in_specs=[hbm] * 4,
        out_specs=[vmem] * len(outs),
        scratch_shapes=[
            pltpu.VMEM(resid.shape, F32), pltpu.VMEM(matrix.shape, F32),
            pltpu.VMEM(mode_rows.shape, F32), pltpu.VMEM(coarse_rows.shape, F32),
            pltpu.SemaphoreType.DMA((6,)),
        ],
        compiler_params=pltpu.CompilerParams(vmem_limit_bytes=VMEM_LIMIT),
        cost_estimate=pl.CostEstimate(flops=flops, bytes_accessed=4 * matrix.size, transcendentals=0),
    )(resid, matrix, mode_rows, coarse_rows)
    a = dict(zip(outs, res))
    r0, mt = a["r0"], a["mt"]
    fixed = dict(s_high=a["s_high"], s_low=a["s_low"], modes=a["modes"])
    ins = dict(z_exchange(a, True), mt=mt)
    if small:
        ins["c_own"] = a["c_own"]
    else:
        c_own = a["c_own"]
        ins["c_all"] = jnp.concatenate([
            c_own, shift(c_own, "gz", 1), shift(c_own, "gz", -1),
            lax.all_gather(c_own, "gz", axis=0, tiled=True)], axis=0)
    v = value(0, ins)
    column = dict(mt=mt, mt_low=v["mt_low"], mt_high=v["mt_high"], c_all=v["c_all"] if small else ins["c_all"])
    x = xy_exchange(v)

    a = call(functools.partial(second_kernel, face), dict(x, **fixed),
             dict(w0=vec, scale=rows, **near, **z_out(PAD)), flops=flops)
    w0 = a["w0"]
    sums = dict(sum_near=a["near"], sum_far=far(a["near"])) if small else total(v["xb"][2 * face:])
    v = value(1, dict(z_exchange(a, True), **column, **sums, scale=a["scale"]))
    known = v["known"]
    x = xy_exchange(v)

    a = call(functools.partial(third_kernel, face), dict(x, **fixed, w0=w0, known=known),
             dict(q=vec, w1=vec, **near, **z_out(0)), flops=flops)
    sums = dict(sum_near=a["near"], sum_far=far(a["near"])) if small else total(v["xb"][2 * face:])
    q, w1 = a["q"], a["w1"]
    v = value(2, dict(z_exchange(a, False), **column))
    x = xy_exchange(v)

    names = ("r2", "w2", "p1", "s1", "z1", "m2")
    a = call(functools.partial(fourth_kernel, face),
             dict(x, **fixed, **sums, known=known, r0=r0, w0=w0, w1=w1, q=q),
             dict({name: vec for name in names}, known=rows, **z_out(PAD)), flops=flops)
    v = value(3, dict(z_exchange(a, True), **column))
    x = xy_exchange(v)
    if small:
        part = call(functools.partial(near_kernel, face), {name: x[name] for name in ("xb", "gxb", "gyl", "gyh")}, near)["near"]
        sums = dict(sum_near=part, sum_far=far(part))
    else:
        sums = total(v["xb"][2 * face:])
    out = sds((loads, width))
    res = call(functools.partial(last_kernel, face),
               dict(x, **sums, known=a["known"], **{name: a[name] for name in names}),
               dict(mult=out, resid=out))
    return (res["mult"][None, None, None], res["resid"][None, None, None])


def solution(mesh):
    spec = P("gx", "gy", "gz", None, None)
    sizes = tuple(mesh.shape[axis] for axis in ("gx", "gy", "gz"))
    return jax.shard_map(
        functools.partial(body, sizes),
        mesh=mesh,
        in_specs=(spec, spec, spec, P("gx", "gy", "gz", None)),
        out_specs=(spec, spec),
        check_vma=False,
    )
```

time: 340 us -> 77.4 us (0.23)
  blocking collectives: 212 us -> 0 us
  other arithmetic: 32.2 us -> 0 us
  matrix products: 25.6 us -> 0 us
  Pallas kernels: 0 us -> 9.07 us
  starting transfers between devices: 21.3 us -> 27.2 us
  local copies, waits for them, and re-layouts: 9 us -> 4.06 us
    psum x4 -> x0, blocking collectives: 154 us -> none  [global_sums(): return lax.psum((first, second), ('gx', 'gy', 'gz'))]
    all_gather x4 -> x0, blocking collectives: 57.9 us -> none  [operate(): lax.all_gather(loads, 'gz', axis=0, tiled=True)]
    dot_general x16 -> x0, matrix products: 25.6 us -> none  [the longest x4 13.4 us: operate(): jnp.einsum('rj,ij->ri', u, matrix, precision=lax.Precision.HIGHEST, prefe...]
    unnamed x40 -> x0, other arithmetic: 13.5 us -> none
    pallas_call x0 -> x10, Pallas kernels: none -> 9.07 us  [the longest x9 6.13 us: call(): pl.pallas_call(run, out_shape=[outs[n] for n in names_out], in_specs=[vme...]
    ppermute x24 -> x27, starting transfers between devices: 21.3 us -> 27.2 us  [the longest x24 22.7 us: shift(): return lax.ppermute(x, axis, [(k, (k + by) % n) for k in range(n)])]
    sub x3 -> x0, other arithmetic: 4.45 us -> none  [body(): resid = resid - alpha[:, None] * along]
    concatenate x8 -> x0, other arithmetic: 4.17 us -> none  [assemble(): return jnp.concatenate(parts, axis=1)]
  transfers between devices with their start and end apart: 24 -> 27, of which waited for: 16 -> 16; matrix products, arithmetic and copies ran while one was open for 0% -> 0% of each run, Pallas kernels for 0% -> 0%
where the time goes in v2:
time: 77.4 us; the launch traced here: 77.1 us
  waiting for transfers between devices  36 us (47%)
  starting transfers between devices  27.2 us (35%)
  Pallas kernels  9.07 us (12%)
  local copies, waits for them, and re-layouts  4.06 us (5%)
    ppermute x24, waiting for transfers between devices, shift(): return lax.ppermute(x, axis, [(k, (k + by) % n) for k in range(n)])  27 us
    ppermute x24, starting transfers between devices, shift(): return lax.ppermute(x, axis, [(k, (k + by) % n) for k in range(n)])  22.7 us
    ppermute x3, waiting for transfers between devices, far(): return lax.ppermute(x, ('gx', 'gy'), pairs)  9.04 us
    pallas_call x9, Pallas kernels, call(): pl.pallas_call(run, out_shape=[outs[n] for n in names_out], in_specs=[vme...  6.13 us
    ppermute x3, starting transfers between devices, far(): return lax.ppermute(x, ('gx', 'gy'), pairs)  4.54 us
    unnamed x8, local copies, waits for them, and re-layouts  4.06 us
    pallas_call x1, Pallas kernels, body(): pl.pallas_call(functools.partial(first_kernel, face, nz, n_modes, small),...  2.95 us
  transfers between devices with their start and end apart: 27, of which 16 were waited for; matrix products, arithmetic and copies ran while one was open for 0% of the time, Pallas kernels for 0%

profile of v2, /device:TPU:0, one launch (start us, length us, event | category | flops | bytes accessed | tf_op | source)
XLA Modules:
  0.0 77.1 jit_solution(10264862553869305988)
XLA Ops:
  0.6 1.7 %copy-done = f32[1,1,1,768,768]{4,3,2,1,0:T(8,128)S(1)} copy-done((f32[1,1,1,768,768]{4,3,2,1,0:T(8,128)S(1)}, f32[1,1,1,768,768]{4,3,2,1,0:T(8,128)}, u32[]{:S(2)}) %copy-start) | copy-done | bytes 2359320
  4.7 2.9 %shard_map.59 = (f32[768,128]{1,0:T(8,128)S(1)}, bf16[768,768]{1,0:T(8,128)(2,1)S(1)}, bf16[768,768]{1,0:T(8,128)(2,1)S(1)}, f32[8,768]{1,0:T(8,128)S(1)}, bf16[...) custom-call(f32[128,768]{1,0:T(8,128)S(1)} %bitcast.7, ...), custom_call_target="tpu_custom_call" | custom-call | flops 603979776 | bytes 2359296 | tf_op jit(solution)/shard_map/pallas_call | solution.py:438
  7.7 5.1 %collective-permute-start.1 = (f32[160,128]{1,0:T(8,128)S(1)}, f32[160,128]{1,0:T(8,128)S(1)}, u32[]{:S(2)}, u32[]{:S(2)}) collective-permute-start(f32[160,128]{1,0:T(8,128)S(1)} %get-tuple-element.59.refs_0_), channel_id=1, source_target_pairs={{0,3},{1,0},{2,1},{3,2},{4,7},{5,4},{6,5},{7,6},{8,11},{9,8},{10,9... | collective-permute-start | bytes 245768 | tf_op jit(solution)/shard_map/ppermute | solution.py:378
  13.8 4.1 %collective-permute-done.2.refs_5_ = f32[24,128]{1,0:T(8,128)S(1)} collective-permute-done((f32[24,128]{1,0:T(8,128)S(1)}, f32[24,128]{1,0:T(8,128)S(1)}, u32[]{:S(2)}, u32[]{:S(2)}) %collective-permute-start.2) | collective-permute-done | bytes 12320 | tf_op jit(solution)/shard_map/ppermute | solution.py:378
  19.4 1.6 %collective-permute-start.3 = (f32[264,128]{1,0:T(8,128)S(1)}, f32[264,128]{1,0:T(8,128)S(1)}, u32[]{:S(2)}, u32[]{:S(2)}) collective-permute-start(f32[264,128]{1,0:T(8,128)S(1)} %get-tuple-element.66.refs_1_), channel_id=1, source_target_pairs={{0,16},{16,0},{1,17},{17,1},{2,18},{18,2},{3,19},{19,3},{4,20},{20... | collective-permute-start | bytes 405512 | tf_op jit(solution)/shard_map/ppermute | solution.py:378
  21.5 1.4 %collective-permute-done.5.refs_6_ = f32[136,128]{1,0:T(8,128)S(1)} collective-permute-done((f32[136,128]{1,0:T(8,128)S(1)}, f32[136,128]{1,0:T(8,128)S(1)}, u32[]{:S(2)}, u32[]{:S(2)}) %collective-permute-start.5) | collective-permute-done | bytes 69664 | tf_op jit(solution)/shard_map/ppermute | solution.py:378
  22.9 2.5 %collective-permute-done.4.refs_5_ = f32[136,128]{1,0:T(8,128)S(1)} collective-permute-done((f32[136,128]{1,0:T(8,128)S(1)}, f32[136,128]{1,0:T(8,128)S(1)}, u32[]{:S(2)}, u32[]{:S(2)}) %collective-permute-start.4) | collective-permute-done | bytes 69664 | tf_op jit(solution)/shard_map/ppermute | solution.py:378
  26.4 2.2 %collective-permute-start.7 = (f32[144,128]{1,0:T(8,128)S(1)}, f32[144,128]{1,0:T(8,128)S(1)}, u32[]{:S(2)}, u32[]{:S(2)}) collective-permute-start(f32[144,128]{1,0:T(8,128)S(1)} %get-tuple-element.72.refs_0_), channel_id=1, source_target_pairs={{0,3},{1,0},{2,1},{3,2},{4,7},{5,4},{6,5},{7,6},{8,11},{9,8},{10,9... | collective-permute-start | bytes 221192 | tf_op jit(solution)/shard_map/ppermute | solution.py:378
  29.3 1.6 %collective-permute-start.9 = (f32[8,128]{1,0:T(8,128)S(1)}, f32[8,128]{1,0:T(8,128)S(1)}, u32[]{:S(2)}, u32[]{:S(2)}) collective-permute-start(f32[8,128]{1,0:T(8,128)S(1)} %get-tuple-element.79.refs_10_), channel_id=1, source_target_pairs={{0,24},{4,28},{8,16},{12,20},{16,8},{20,12},{24,0},{28,4},{1,25},{... | collective-permute-start | bytes 12296 | tf_op jit(solution)/shard_map/ppermute | solution.py:385
  30.9 3.0 %collective-permute-done.9.refs_11_ = f32[8,128]{1,0:T(8,128)S(1)} collective-permute-done((f32[8,128]{1,0:T(8,128)S(1)}, f32[8,128]{1,0:T(8,128)S(1)}, u32[]{:S(2)}, u32[]{:S(2)}) %collective-permute-start.9) | collective-permute-done | bytes 4128 | tf_op jit(solution)/shard_map/ppermute | solution.py:385
  36.3 1.4 %collective-permute-done.12.refs_6_ = f32[136,128]{1,0:T(8,128)S(1)} collective-permute-done((f32[136,128]{1,0:T(8,128)S(1)}, f32[136,128]{1,0:T(8,128)S(1)}, u32[]{:S(2)}, u32[]{:S(2)}) %collective-permute-start.12) | collective-permute-done | bytes 69664 | tf_op jit(solution)/shard_map/ppermute | solution.py:378
  37.8 2.5 %collective-permute-done.11.refs_5_ = f32[136,128]{1,0:T(8,128)S(1)} collective-permute-done((f32[136,128]{1,0:T(8,128)S(1)}, f32[136,128]{1,0:T(8,128)S(1)}, u32[]{:S(2)}, u32[]{:S(2)}) %collective-permute-start.11) | collective-permute-done | bytes 69664 | tf_op jit(solution)/shard_map/ppermute | solution.py:378
  41.2 2.3 %collective-permute-start.14 = (f32[136,128]{1,0:T(8,128)S(1)}, f32[136,128]{1,0:T(8,128)S(1)}, u32[]{:S(2)}, u32[]{:S(2)}) collective-permute-start(f32[136,128]{1,0:T(8,128)S(1)} %get-tuple-element.87.refs_0_), channel_id=1, source_target_pairs={{0,3},{1,0},{2,1},{3,2},{4,7},{5,4},{6,5},{7,6},{8,11},{9,8},{10,9... | collective-permute-start | bytes 208904 | tf_op jit(solution)/shard_map/ppermute | solution.py:378
  44.1 1.4 %collective-permute-start.15 = (f32[8,128]{1,0:T(8,128)S(1)}, f32[8,128]{1,0:T(8,128)S(1)}, u32[]{:S(2)}, u32[]{:S(2)}) collective-permute-start(f32[8,128]{1,0:T(8,128)S(1)} %get-tuple-element.90), channel_id=1, source_target_pairs={{0,2},{1,3},{2,0},{3,1},{4,6},{5,7},{6,4},{7,5},{8,10},{9,11},{10,... | collective-permute-start | bytes 12296 | tf_op jit(solution)/shard_map/ppermute | solution.py:378
  45.5 3.2 %collective-permute-done.15.refs_5_ = f32[8,128]{1,0:T(8,128)S(1)} collective-permute-done((f32[8,128]{1,0:T(8,128)S(1)}, f32[8,128]{1,0:T(8,128)S(1)}, u32[]{:S(2)}, u32[]{:S(2)}) %collective-permute-start.15) | collective-permute-done | bytes 4128 | tf_op jit(solution)/shard_map/ppermute | solution.py:378
  51.5 1.4 %collective-permute-start.19 = (f32[8,128]{1,0:T(8,128)S(1)}, f32[8,128]{1,0:T(8,128)S(1)}, u32[]{:S(2)}, u32[]{:S(2)}) collective-permute-start(f32[8,128]{1,0:T(8,128)S(1)} %get-tuple-element.95.refs_10_), channel_id=1, source_target_pairs={{0,24},{4,28},{8,16},{12,20},{16,8},{20,12},{24,0},{28,4},{1,25},{... | collective-permute-start | bytes 12296 | tf_op jit(solution)/shard_map/ppermute | solution.py:385
  52.9 3.1 %collective-permute-done.19.refs_11_ = f32[8,128]{1,0:T(8,128)S(1)} collective-permute-done((f32[8,128]{1,0:T(8,128)S(1)}, f32[8,128]{1,0:T(8,128)S(1)}, u32[]{:S(2)}, u32[]{:S(2)}) %collective-permute-start.19) | collective-permute-done | bytes 4128 | tf_op jit(solution)/shard_map/ppermute | solution.py:385
  57.3 2.3 %collective-permute-start.21 = (f32[144,128]{1,0:T(8,128)S(1)}, f32[144,128]{1,0:T(8,128)S(1)}, u32[]{:S(2)}, u32[]{:S(2)}) collective-permute-start(f32[144,128]{1,0:T(8,128)S(1)} %get-tuple-element.99.refs_0_), channel_id=1, source_target_pairs={{0,3},{1,0},{2,1},{3,2},{4,7},{5,4},{6,5},{7,6},{8,11},{9,8},{10,9... | collective-permute-start | bytes 221192 | tf_op jit(solution)/shard_map/ppermute | solution.py:378
  60.2 4.1 %collective-permute-done.22.refs_5_ = f32[16,128]{1,0:T(8,128)S(1)} collective-permute-done((f32[16,128]{1,0:T(8,128)S(1)}, f32[16,128]{1,0:T(8,128)S(1)}, u32[]{:S(2)}, u32[]{:S(2)}) %collective-permute-start.22) | collective-permute-done | bytes 8224 | tf_op jit(solution)/shard_map/ppermute | solution.py:378
  64.4 1.4 %collective-permute-done.20.refs_3_ = f32[144,128]{1,0:T(8,128)S(1)} collective-permute-done((f32[144,128]{1,0:T(8,128)S(1)}, f32[144,128]{1,0:T(8,128)S(1)}, u32[]{:S(2)}, u32[]{:S(2)}) %collective-permute-start.20) | collective-permute-done | bytes 73760 | tf_op jit(solution)/shard_map/ppermute | solution.py:378
  67.9 1.8 %collective-permute-done.25.refs_3_.refs_6_ = f32[136,128]{1,0:T(8,128)S(1)} collective-permute-done((f32[136,128]{1,0:T(8,128)S(1)}, f32[136,128]{1,0:T(8,128)S(1)}, u32[]{:S(2)}, u32[]{:S(2)}) %collective-permute-start.25) | collective-permute-done | bytes 69664 | tf_op jit(solution)/shard_map/ppermute | solution.py:378
  69.7 1.6 %collective-permute-done.24.refs_2_.refs_5_ = f32[136,128]{1,0:T(8,128)S(1)} collective-permute-done((f32[136,128]{1,0:T(8,128)S(1)}, f32[136,128]{1,0:T(8,128)S(1)}, u32[]{:S(2)}, u32[]{:S(2)}) %collective-permute-start.24) | collective-permute-done | bytes 69664 | tf_op jit(solution)/shard_map/ppermute | solution.py:378
  71.2 1.6 %collective-permute-start.26 = (f32[8,128]{1,0:T(8,128)S(1)}, f32[8,128]{1,0:T(8,128)S(1)}, u32[]{:S(2)}, u32[]{:S(2)}) collective-permute-start(f32[8,128]{1,0:T(8,128)S(1)} %shard_map.67.refs_7_), channel_id=1, source_target_pairs={{0,24},{4,28},{8,16},{12,20},{16,8},{20,12},{24,0},{28,4},{1,25},{... | collective-permute-start | bytes 12296 | tf_op jit(solution)/shard_map/ppermute | solution.py:385
  72.8 3.0 %collective-permute-done.26.refs_8_ = f32[8,128]{1,0:T(8,128)S(1)} collective-permute-done((f32[8,128]{1,0:T(8,128)S(1)}, f32[8,128]{1,0:T(8,128)S(1)}, u32[]{:S(2)}, u32[]{:S(2)}) %collective-permute-start.26) | collective-permute-done | bytes 4128 | tf_op jit(solution)/shard_map/ppermute | solution.py:385
  (48 shorter events, 19.4 us)
Async XLA Ops:
  7.7 10.2 %collective-permute-start.1 = (f32[160,128]{1,0:T(8,128)S(1)}, f32[160,128]{1,0:T(8,128)S(1)}, u32[]{:S(2)}, u32[]{:S(2)}) collective-permute-start(f32[160,128]{1,0:T(8,128)S(1)} %get-tuple-element.59.refs_0_), channel_id=1, source_target_pairs={{0,3},{1,0},{2,1},{3,2},{4,7},{5,4},{6,5},{7,6},{8,11},{9,8},{10,9... | collective-permute-start | bytes 245768 | tf_op jit(solution)/shard_map/ppermute | solution.py:378
  12.8 6.2 %collective-permute-start = (f32[160,128]{1,0:T(8,128)S(1)}, f32[160,128]{1,0:T(8,128)S(1)}, u32[]{:S(2)}, u32[]{:S(2)}) collective-permute-start(f32[160,128]{1,0:T(8,128)S(1)} %get-tuple-element.60.refs_1_), channel_id=1, source_target_pairs={{0,1},{1,2},{2,3},{3,0},{4,5},{5,6},{6,7},{7,4},{8,9},{9,10},{10,1... | collective-permute-start | bytes 245768 | tf_op jit(solution)/shard_map/ppermute | solution.py:378
  12.8 5.1 %collective-permute-start.2 = (f32[24,128]{1,0:T(8,128)S(1)}, f32[24,128]{1,0:T(8,128)S(1)}, u32[]{:S(2)}, u32[]{:S(2)}) collective-permute-start(f32[24,128]{1,0:T(8,128)S(1)} %get-tuple-element.62), channel_id=1, source_target_pairs={{0,2},{1,3},{2,0},{3,1},{4,6},{5,7},{6,4},{7,5},{8,10},{9,11},{10,... | collective-permute-start | bytes 36872 | tf_op jit(solution)/shard_map/ppermute | solution.py:378
  19.4 6.0 %collective-permute-start.3 = (f32[264,128]{1,0:T(8,128)S(1)}, f32[264,128]{1,0:T(8,128)S(1)}, u32[]{:S(2)}, u32[]{:S(2)}) collective-permute-start(f32[264,128]{1,0:T(8,128)S(1)} %get-tuple-element.66.refs_1_), channel_id=1, source_target_pairs={{0,16},{16,0},{1,17},{17,1},{2,18},{18,2},{3,19},{19,3},{4,20},{20... | collective-permute-start | bytes 405512 | tf_op jit(solution)/shard_map/ppermute | solution.py:378
  21.0 4.4 %collective-permute-start.4 = (f32[136,128]{1,0:T(8,128)S(1)}, f32[136,128]{1,0:T(8,128)S(1)}, u32[]{:S(2)}, u32[]{:S(2)}) collective-permute-start(f32[136,128]{1,0:T(8,128)S(1)} %get-tuple-element.68.refs_3_), channel_id=1, source_target_pairs={{0,4},{4,8},{8,12},{12,0},{1,5},{5,9},{9,13},{13,1},{2,6},{6,10},{... | collective-permute-start | bytes 208904 | tf_op jit(solution)/shard_map/ppermute | solution.py:378
  26.4 7.5 %collective-permute-start.7 = (f32[144,128]{1,0:T(8,128)S(1)}, f32[144,128]{1,0:T(8,128)S(1)}, u32[]{:S(2)}, u32[]{:S(2)}) collective-permute-start(f32[144,128]{1,0:T(8,128)S(1)} %get-tuple-element.72.refs_0_), channel_id=1, source_target_pairs={{0,3},{1,0},{2,1},{3,2},{4,7},{5,4},{6,5},{7,6},{8,11},{9,8},{10,9... | collective-permute-start | bytes 221192 | tf_op jit(solution)/shard_map/ppermute | solution.py:378
  28.6 6.2 %collective-permute-start.6 = (f32[144,128]{1,0:T(8,128)S(1)}, f32[144,128]{1,0:T(8,128)S(1)}, u32[]{:S(2)}, u32[]{:S(2)}) collective-permute-start(f32[144,128]{1,0:T(8,128)S(1)} %get-tuple-element.73.refs_1_), channel_id=1, source_target_pairs={{0,1},{1,2},{2,3},{3,0},{4,5},{5,6},{6,7},{7,4},{8,9},{9,10},{10,1... | collective-permute-start | bytes 221192 | tf_op jit(solution)/shard_map/ppermute | solution.py:378
  28.6 5.2 %collective-permute-start.8 = (f32[16,128]{1,0:T(8,128)S(1)}, f32[16,128]{1,0:T(8,128)S(1)}, u32[]{:S(2)}, u32[]{:S(2)}) collective-permute-start(f32[16,128]{1,0:T(8,128)S(1)} %get-tuple-element.75), channel_id=1, source_target_pairs={{0,2},{1,3},{2,0},{3,1},{4,6},{5,7},{6,4},{7,5},{8,10},{9,11},{10,... | collective-permute-start | bytes 24584 | tf_op jit(solution)/shard_map/ppermute | solution.py:378
  29.3 4.5 %collective-permute-start.9 = (f32[8,128]{1,0:T(8,128)S(1)}, f32[8,128]{1,0:T(8,128)S(1)}, u32[]{:S(2)}, u32[]{:S(2)}) collective-permute-start(f32[8,128]{1,0:T(8,128)S(1)} %get-tuple-element.79.refs_10_), channel_id=1, source_target_pairs={{0,24},{4,28},{8,16},{12,20},{16,8},{20,12},{24,0},{28,4},{1,25},{... | collective-permute-start | bytes 12296 | tf_op jit(solution)/shard_map/ppermute | solution.py:385
  35.2 5.1 %collective-permute-start.10 = (f32[264,128]{1,0:T(8,128)S(1)}, f32[264,128]{1,0:T(8,128)S(1)}, u32[]{:S(2)}, u32[]{:S(2)}) collective-permute-start(f32[264,128]{1,0:T(8,128)S(1)} %get-tuple-element.82.refs_1_), channel_id=1, source_target_pairs={{0,16},{16,0},{1,17},{17,1},{2,18},{18,2},{3,19},{19,3},{4,20},{20... | collective-permute-start | bytes 405512 | tf_op jit(solution)/shard_map/ppermute | solution.py:378
  35.8 4.4 %collective-permute-start.11 = (f32[136,128]{1,0:T(8,128)S(1)}, f32[136,128]{1,0:T(8,128)S(1)}, u32[]{:S(2)}, u32[]{:S(2)}) collective-permute-start(f32[136,128]{1,0:T(8,128)S(1)} %get-tuple-element.84.refs_3_), channel_id=1, source_target_pairs={{0,4},{4,8},{8,12},{12,0},{1,5},{5,9},{9,13},{13,1},{2,6},{6,10},{... | collective-permute-start | bytes 208904 | tf_op jit(solution)/shard_map/ppermute | solution.py:378
  41.2 7.4 %collective-permute-start.14 = (f32[136,128]{1,0:T(8,128)S(1)}, f32[136,128]{1,0:T(8,128)S(1)}, u32[]{:S(2)}, u32[]{:S(2)}) collective-permute-start(f32[136,128]{1,0:T(8,128)S(1)} %get-tuple-element.87.refs_0_), channel_id=1, source_target_pairs={{0,3},{1,0},{2,1},{3,2},{4,7},{5,4},{6,5},{7,6},{8,11},{9,8},{10,9... | collective-permute-start | bytes 208904 | tf_op jit(solution)/shard_map/ppermute | solution.py:378
  43.5 6.1 %collective-permute-start.13 = (f32[136,128]{1,0:T(8,128)S(1)}, f32[136,128]{1,0:T(8,128)S(1)}, u32[]{:S(2)}, u32[]{:S(2)}) collective-permute-start(f32[136,128]{1,0:T(8,128)S(1)} %get-tuple-element.88.refs_1_), channel_id=1, source_target_pairs={{0,1},{1,2},{2,3},{3,0},{4,5},{5,6},{6,7},{7,4},{8,9},{9,10},{10,1... | collective-permute-start | bytes 208904 | tf_op jit(solution)/shard_map/ppermute | solution.py:378
  44.1 4.6 %collective-permute-start.15 = (f32[8,128]{1,0:T(8,128)S(1)}, f32[8,128]{1,0:T(8,128)S(1)}, u32[]{:S(2)}, u32[]{:S(2)}) collective-permute-start(f32[8,128]{1,0:T(8,128)S(1)} %get-tuple-element.90), channel_id=1, source_target_pairs={{0,2},{1,3},{2,0},{3,1},{4,6},{5,7},{6,4},{7,5},{8,10},{9,11},{10,... | collective-permute-start | bytes 12296 | tf_op jit(solution)/shard_map/ppermute | solution.py:378
  50.0 6.0 %collective-permute-start.16 = (f32[256,128]{1,0:T(8,128)S(1)}, f32[256,128]{1,0:T(8,128)S(1)}, u32[]{:S(2)}, u32[]{:S(2)}) collective-permute-start(f32[256,128]{1,0:T(8,128)S(1)} %get-tuple-element.92.refs_1_), channel_id=1, source_target_pairs={{0,16},{16,0},{1,17},{17,1},{2,18},{18,2},{3,19},{19,3},{4,20},{20... | collective-permute-start | bytes 393224 | tf_op jit(solution)/shard_map/ppermute | solution.py:378
  50.9 5.0 %collective-permute-start.18 = (f32[128,128]{1,0:T(8,128)S(1)}, f32[128,128]{1,0:T(8,128)S(1)}, u32[]{:S(2)}, u32[]{:S(2)}) collective-permute-start(f32[128,128]{1,0:T(8,128)S(1)} %get-tuple-element.93.refs_2_), channel_id=1, source_target_pairs={{0,12},{4,0},{8,4},{12,8},{1,13},{5,1},{9,5},{13,9},{2,14},{6,2},{... | collective-permute-start | bytes 196616 | tf_op jit(solution)/shard_map/ppermute | solution.py:378
  51.0 5.0 %collective-permute-start.17 = (f32[128,128]{1,0:T(8,128)S(1)}, f32[128,128]{1,0:T(8,128)S(1)}, u32[]{:S(2)}, u32[]{:S(2)}) collective-permute-start(f32[128,128]{1,0:T(8,128)S(1)} %get-tuple-element.94.refs_3_), channel_id=1, source_target_pairs={{0,4},{4,8},{8,12},{12,0},{1,5},{5,9},{9,13},{13,1},{2,6},{6,10},{... | collective-permute-start | bytes 196616 | tf_op jit(solution)/shard_map/ppermute | solution.py:378
  51.5 4.5 %collective-permute-start.19 = (f32[8,128]{1,0:T(8,128)S(1)}, f32[8,128]{1,0:T(8,128)S(1)}, u32[]{:S(2)}, u32[]{:S(2)}) collective-permute-start(f32[8,128]{1,0:T(8,128)S(1)} %get-tuple-element.95.refs_10_), channel_id=1, source_target_pairs={{0,24},{4,28},{8,16},{12,20},{16,8},{20,12},{24,0},{28,4},{1,25},{... | collective-permute-start | bytes 12296 | tf_op jit(solution)/shard_map/ppermute | solution.py:385
  57.3 7.0 %collective-permute-start.21 = (f32[144,128]{1,0:T(8,128)S(1)}, f32[144,128]{1,0:T(8,128)S(1)}, u32[]{:S(2)}, u32[]{:S(2)}) collective-permute-start(f32[144,128]{1,0:T(8,128)S(1)} %get-tuple-element.99.refs_0_), channel_id=1, source_target_pairs={{0,3},{1,0},{2,1},{3,2},{4,7},{5,4},{6,5},{7,6},{8,11},{9,8},{10,9... | collective-permute-start | bytes 221192 | tf_op jit(solution)/shard_map/ppermute | solution.py:378
  59.6 6.2 %collective-permute-start.20 = (f32[144,128]{1,0:T(8,128)S(1)}, f32[144,128]{1,0:T(8,128)S(1)}, u32[]{:S(2)}, u32[]{:S(2)}) collective-permute-start(f32[144,128]{1,0:T(8,128)S(1)} %get-tuple-element.100.refs_1_), channel_id=1, source_target_pairs={{0,1},{1,2},{2,3},{3,0},{4,5},{5,6},{6,7},{7,4},{8,9},{9,10},{10,1... | collective-permute-start | bytes 221192 | tf_op jit(solution)/shard_map/ppermute | solution.py:378
  59.6 4.7 %collective-permute-start.22 = (f32[16,128]{1,0:T(8,128)S(1)}, f32[16,128]{1,0:T(8,128)S(1)}, u32[]{:S(2)}, u32[]{:S(2)}) collective-permute-start(f32[16,128]{1,0:T(8,128)S(1)} %get-tuple-element.102), channel_id=1, source_target_pairs={{0,2},{1,3},{2,0},{3,1},{4,6},{5,7},{6,4},{7,5},{8,10},{9,11},{10,... | collective-permute-start | bytes 24584 | tf_op jit(solution)/shard_map/ppermute | solution.py:378
  66.2 5.1 %collective-permute-start.23 = (f32[264,128]{1,0:T(8,128)S(1)}, f32[264,128]{1,0:T(8,128)S(1)}, u32[]{:S(2)}, u32[]{:S(2)}) collective-permute-start(f32[264,128]{1,0:T(8,128)S(1)} %get-tuple-element.104.refs_0_.refs_1_), channel_id=1, source_target_pairs={{0,16},{16,0},{1,17},{17,1},{2,18},{18,2},{3,19},{19,3},{4,20},{20... | collective-permute-start | bytes 405512 | tf_op jit(solution)/shard_map/ppermute | solution.py:378
  67.4 3.9 %collective-permute-start.24 = (f32[136,128]{1,0:T(8,128)S(1)}, f32[136,128]{1,0:T(8,128)S(1)}, u32[]{:S(2)}, u32[]{:S(2)}) collective-permute-start(f32[136,128]{1,0:T(8,128)S(1)} %get-tuple-element.106.refs_3_), channel_id=1, source_target_pairs={{0,4},{4,8},{8,12},{12,0},{1,5},{5,9},{9,13},{13,1},{2,6},{6,10},{... | collective-permute-start | bytes 208904 | tf_op jit(solution)/shard_map/ppermute | solution.py:378
  71.2 4.6 %collective-permute-start.26 = (f32[8,128]{1,0:T(8,128)S(1)}, f32[8,128]{1,0:T(8,128)S(1)}, u32[]{:S(2)}, u32[]{:S(2)}) collective-permute-start(f32[8,128]{1,0:T(8,128)S(1)} %shard_map.67.refs_7_), channel_id=1, source_target_pairs={{0,24},{4,28},{8,16},{12,20},{16,8},{20,12},{24,0},{28,4},{1,25},{... | collective-permute-start | bytes 12296 | tf_op jit(solution)/shard_map/ppermute | solution.py:385
  (7 other events, 10.3 us)

commit v3 on v2

--- a/solution.py
+++ b/solution.py
@@ -11,7 +11,6 @@
 BF16 = jnp.bfloat16
 HI = lax.Precision.HIGHEST
 PAD = 8
-ORDER = (0, -1, 1, 2)
 VMEM_LIMIT = 24 * 1024 * 1024
 
 
@@ -81,7 +80,17 @@
     return x[i:i + 1, :]
 
 
-def multiply(face, high, low, vec, at):
+def face_places(face):
+    places, signs = [], []
+    for k, axis in enumerate(("gx", "gy", "gz")):
+        odd = lax.rem(lax.axis_index(axis), 2)
+        for high in (1 - odd, odd):
+            places.append(pl.multiple_of((2 * k + high) * face, face))
+            signs.append((1 - 2 * high).astype(F32))
+    return places, signs
+
+
+def multiply(high, low, vec):
     cols = vec.shape[1] // 2
     both = dot16(high, vec) + dot16(low, vec)
     return both[:, :cols] + both[:, cols:]
@@ -91,13 +100,13 @@
     if part < 2:
         o["y"][2 * part * face:2 * (part + 1) * face, :] = y
     else:
-        o["zm"][0:face, :] = y[0:face]
-        o["zp"][0:face, :] = y[face:]
+        o["za"][0:face, :] = y[0:face]
+        o["zb"][0:face, :] = y[face:]
 
 
 def send_rows(face, rows, at, o):
     n = rows.shape[0]
-    for name, start in (("zm", face), ("zp", face), ("z2", 0)):
+    for name, start in (("za", face), ("zb", face), ("z2", 0)):
         o[name][start + at:start + at + n, :] = rows
 
 
@@ -107,7 +116,7 @@
     total = None
     for part in range(3):
         at = slice(2 * part * face, 2 * (part + 1) * face)
-        y = multiply(face, i["s_high"][at, :], i["s_low"][at, :], halves, at)
+        y = multiply(i["s_high"][at, :], i["s_low"][at, :], halves)
         send_product(face, part, y, o)
         if want_dot:
             dot = col_sum(vec[at] * y)
@@ -122,31 +131,33 @@
 
 
 def first_kernel(face, nz, n_modes, turn, resid_hbm, schur_hbm, modes_hbm, coarse_hbm, *refs):
-    names = ["r0", "s_high", "s_low", "modes", "mt", "c_own", "y", "zm", "zp", "z2"]
+    names = ["r0", "s_high", "s_low", "modes", "mt", "c_own", "y", "za", "zb", "z2"]
     o = dict(zip(names, refs[:len(names)]))
     resid, schur, mode_rows, coarse, sems = refs[len(names):]
     two = 2 * face
+    places, signs = face_places(face)
     copies = [
         pltpu.make_async_copy(modes_hbm, mode_rows, sems.at[0]),
         pltpu.make_async_copy(resid_hbm, resid, sems.at[1]),
         pltpu.make_async_copy(coarse_hbm, coarse, sems.at[2]),
     ]
-    for part in range(3):
-        at = pl.ds(part * two, two)
-        copies.append(pltpu.make_async_copy(schur_hbm.at[at, :], schur.at[at, :], sems.at[3 + part]))
+    for f in range(6):
+        at = pl.ds(f * face, face)
+        copies.append(pltpu.make_async_copy(schur_hbm.at[pl.ds(places[f], face), :], schur.at[at, :], sems.at[3 + f]))
     for copy in copies:
         copy.start()
 
     copies[0].wait()
-    modes = jnp.concatenate([mode_rows[m] for m in range(n_modes)], axis=0)
+    modes = jnp.concatenate([
+        jnp.concatenate([mode_rows[m, :, pl.ds(at, face)] for at in places], axis=1)
+        for m in range(n_modes)], axis=0)
     modes = jnp.concatenate([modes, jnp.zeros((PAD - n_modes, modes.shape[1]), F32)], axis=0)
     o["modes"][...] = modes
     o["mt"][...] = mode_pieces(modes)
 
     copies[1].wait()
     for f in range(6):
-        part = resid[:, f * face:(f + 1) * face].T
-        o["r0"][f * face:(f + 1) * face, :] = part if f % 2 == 0 else -part
+        o["r0"][f * face:(f + 1) * face, :] = signs[f] * resid[:, pl.ds(places[f], face)].T
     r0 = o["r0"][...]
     cols = r0.shape[1]
     send_rows(face, dot32(modes, r0), 0, o)
@@ -159,74 +170,74 @@
     place = lax.broadcasted_iota(jnp.int32, (nz * n_modes, wide), 1)
     block, mode = place // PAD, place % PAD
 
-    def ordered(holder):
-        if holder is None:
-            device = block
-        else:
-            offset = jnp.zeros_like(block)
-            for at, by in enumerate(ORDER):
-                offset = jnp.where(block == at, by, offset)
-            device = (holder + offset + 2 * nz) % nz
+    def ordered(device):
         pick = jnp.where((source == device * n_modes + mode) & (mode < n_modes), 1.0, 0.0)
         return dot32(rows, pick)
 
+    def held_by(holder, side):
+        offset = jnp.where(block == 1, side, jnp.where(block == 2, -side, 2 * (block // 3)))
+        return ordered((holder + offset + 2 * nz) % nz)
+
     if turn:
         me = lax.axis_index("gz")
-        o["c_own"][...] = ordered(me)
-        for name, by, start in (("zm", -1, face + 3 * PAD), ("zp", 1, face + 3 * PAD), ("z2", 2, 2 * PAD)):
+        side = 1 - 2 * lax.rem(me, 2)
+        o["c_own"][...] = held_by(me, side)
+        sent = (("za", me + side, -side, face + 3 * PAD), ("zb", me - side, -side, face + 3 * PAD), ("z2", me + 2, side, 2 * PAD))
+        for name, holder, holder_side, start in sent:
             o[name][start:start + PAD, :] = jnp.zeros((PAD, cols), F32)
-            o[name][start:start + PAD, 0:wide] = ordered(me + by)
+            o[name][start:start + PAD, 0:wide] = held_by(holder, holder_side)
     else:
-        o["c_own"][...] = ordered(None)
-    o["zm"][face + 2 * PAD:face + 3 * PAD, :] = modes[:, 4 * face:5 * face]
-    o["zp"][face + 2 * PAD:face + 3 * PAD, :] = modes[:, 5 * face:6 * face]
+        o["c_own"][...] = ordered(block)
+    o["za"][face + 2 * PAD:face + 3 * PAD, :] = modes[:, 4 * face:5 * face]
+    o["zb"][face + 2 * PAD:face + 3 * PAD, :] = modes[:, 5 * face:6 * face]
 
     halves = jnp.concatenate(split(r0), axis=1)
     curv = jnp.zeros((1, cols), F32)
     for part in range(3):
         at = slice(part * two, (part + 1) * two)
-        copies[3 + part].wait()
-        high, low = split(schur[at, :])
+        copies[3 + 2 * part].wait()
+        copies[4 + 2 * part].wait()
+        high, low = split(jnp.concatenate([schur[at, pl.ds(start, face)] for start in places], axis=1))
         o["s_high"][at, :] = high
         o["s_low"][at, :] = low
-        y = multiply(face, high, low, halves, at)
+        y = multiply(high, low, halves)
         send_product(face, part, y, o)
         curv = curv + col_sum(r0[at] * y)
     send_rows(face, stack_rows([half_dot(r0, r0), curv], cols), PAD, o)
 
 
 def column_rows(face, i, at):
-    return [i["zm"][face + at:face + at + PAD, :], i["gzl"][face + at:face + at + PAD, :],
-            i["gzh"][face + at:face + at + PAD, :], i["gz2"][at:at + PAD, :]]
+    return [i["za"][face + at:face + at + PAD, :], i["gza"][face + at:face + at + PAD, :],
+            i["gzb"][face + at:face + at + PAD, :], i["gz2"][at:at + PAD, :]]
 
 
 def value_kernel(face, stage, i, o):
     gathered = "g_all" in i
     loads = i["g_all"][...] if gathered else jnp.concatenate(column_rows(face, i, 0), axis=0)
     if stage == 0:
-        low = mode_pieces(i["gzl"][face + 2 * PAD:face + 3 * PAD, :])
-        high = mode_pieces(i["gzh"][face + 2 * PAD:face + 3 * PAD, :])
-        o["mt_low"][...] = low
-        o["mt_high"][...] = high
+        mt_a = mode_pieces(i["gza"][face + 2 * PAD:face + 3 * PAD, :])
+        mt_b = mode_pieces(i["gzb"][face + 2 * PAD:face + 3 * PAD, :])
+        o["mt_a"][...] = mt_a
+        o["mt_b"][...] = mt_b
         if gathered:
             coarse = i["c_all"][...]
         else:
             wide = i["c_own"].shape[1]
             at = face + 3 * PAD
             coarse = jnp.concatenate([
-                i["c_own"][...], i["gzl"][at:at + PAD, 0:wide], i["gzh"][at:at + PAD, 0:wide],
+                i["c_own"][...], i["gza"][at:at + PAD, 0:wide], i["gzb"][at:at + PAD, 0:wide],
                 i["gz2"][2 * PAD:3 * PAD, 0:wide]], axis=0)
             o["c_all"][...] = coarse
     else:
-        low, high, coarse = i["mt_low"][...], i["mt_high"][...], i["c_all"][...]
+        mt_a, mt_b, coarse = i["mt_a"][...], i["mt_b"][...], i["c_all"][...]
     amp = dot32(coarse, loads)
     own = amp_pieces(amp[0:PAD])
     mt = i["mt"]
     xy = i["y"][...] + dot16(mt[0:4 * face, :], own)
-    z_low = i["zm"][0:face, :] + dot16(mt[4 * face:5 * face, :], own)
-    z_low = z_low - (i["gzl"][0:face, :] + dot16(low, amp_pieces(amp[PAD:2 * PAD])))
-    z_high = i["zp"][0:face, :] + dot16(mt[5 * face:6 * face, :], own)
-    z_high = z_high - (i["gzh"][0:face, :] + dot16(high, amp_pieces(amp[2 * PAD:3 * PAD])))
+    z_a = i["za"][0:face, :] + dot16(mt[4 * face:5 * face, :], own)
+    z_a = z_a - (i["gza"][0:face, :] + dot16(mt_a, amp_pieces(amp[PAD:2 * PAD])))
+    z_b = i["zb"][0:face, :] + dot16(mt[5 * face:6 * face, :], own)
+    z_b = z_b - (i["gzb"][0:face, :] + dot16(mt_b, amp_pieces(amp[2 * PAD:3 * PAD])))
     cols = loads.shape[1]
 
     if stage != 2:
@@ -245,39 +256,40 @@
         ratio = alpha0 / row(i["scale"], 0)
         o["known"][...] = stack_rows([row(sums, 0), row(sums, 1), alpha0], cols)
         dots = dots * (ratio * ratio)
-        xy, z_low, z_high = xy * ratio, z_low * ratio, z_high * ratio
-    o["z"][0:face, :] = z_low
-    o["z"][face:, :] = z_high
-    o["xb"][0:2 * face, :] = xy[0:2 * face]
-    o["ym"][0:face, :] = xy[2 * face:3 * face]
-    o["yp"][0:face, :] = xy[3 * face:]
-    if stage != 2:
-        o["xb"][2 * face:, :] = dots
-        o["ym"][face:, :] = dots
-        o["yp"][face:, :] = dots
+        xy, z_a, z_b = xy * ratio, z_a * ratio, z_b * ratio
+    o["z"][0:face, :] = z_a
+    o["z"][face:, :] = z_b
+    o["xab"][0:2 * face, :] = xy[0:2 * face]
+    o["ya"][0:face, :] = xy[2 * face:3 * face]
+    o["yb"][0:face, :] = xy[3 * face:]
+    if stage == 3:
+        o["dots"][...] = dots
+    elif stage != 2:
+        o["xab"][2 * face:, :] = dots
+        o["ya"][face:, :] = dots
+        o["yb"][face:, :] = dots
 
 
 def assemble(face, i):
     f = face
     return jnp.concatenate([
-        i["xb"][0:f, :] - i["gxb"][f:2 * f, :],
-        i["xb"][f:2 * f, :] - i["gxb"][0:f, :],
-        i["ym"][0:f, :] - i["gyl"][0:f, :],
-        i["yp"][0:f, :] - i["gyh"][0:f, :],
+        i["xab"][0:2 * f, :] - i["gxab"][0:2 * f, :],
+        i["ya"][0:f, :] - i["gya"][0:f, :],
+        i["yb"][0:f, :] - i["gyb"][0:f, :],
         i["z"][...],
     ], axis=0)
 
 
 def near_sum(face, i):
     f = face
-    total = i["xb"][2 * f:2 * f + PAD, :] + i["gxb"][2 * f:2 * f + PAD, :]
-    return total + (i["gyl"][f:f + PAD, :] + i["gyh"][f:f + PAD, :])
+    total = i["xab"][2 * f:2 * f + PAD, :] + i["gxab"][2 * f:2 * f + PAD, :]
+    return total + (i["gya"][f:f + PAD, :] + i["gyb"][f:f + PAD, :])
 
 
 def second_kernel(face, i, o):
     w0 = assemble(face, i)
     o["w0"][...] = w0
-    own = i["xb"][2 * face:2 * face + PAD, :]
+    own = i["xab"][2 * face:2 * face + PAD, :]
     scale = row(own, 0) / row(own, 1)
     cols = w0.shape[1]
     o["scale"][...] = stack_rows([scale], cols)
@@ -330,12 +342,19 @@
         half_dot(s1, s1), curv, half_dot(z1, vec), half_dot(s1, z1)], cols), PAD, o)
 
 
-def near_kernel(face, i, o):
-    o["near"][...] = near_sum(face, i)
+def pair_kernel(face, i, o):
+    total = i["dots"][...] + i["gdots"][...]
+    o["pair"][...] = total
+    for name in ("ya", "yb"):
+        o[name][0:face, :] = i[name][...]
+        o[name][face:, :] = total
 
 
 def last_kernel(face, i, o):
-    d = i["sum_near"][...] + i["sum_far"][...]
+    if "sum" in i:
+        d = i["sum"][...]
+    else:
+        d = (i["pair"][...] + i["gpair"][...]) + (i["gya"][face:, :] + i["gyb"][face:, :])
     rr, rw, ww, ws, ss, wc, sc, sz = (row(d, k) for k in range(8))
     norm1, alpha1 = row(i["known"], 0), row(i["known"], 1)
     beta2 = rr / norm1
@@ -355,11 +374,11 @@
     w3 = w2 / alpha1 - ratio * (c3 + beta2 * i["z1"][...])
     mult = i["m2"][...] + alpha2 * p2 + alpha3 * (r3 + beta3 * p2)
     resid = r3 - alpha3 * (w3 + (beta3 / alpha1) * s2)
+    places, signs = face_places(face)
     for f in range(6):
         at = slice(f * face, (f + 1) * face)
-        sign = 1.0 if f % 2 == 0 else -1.0
-        o["mult"][:, at] = sign * mult[at, :].T
-        o["resid"][:, at] = sign * resid[at, :].T
+        o["mult"][:, pl.ds(places[f], face)] = signs[f] * mult[at, :].T
+        o["resid"][:, pl.ds(places[f], face)] = signs[f] * resid[at, :].T
 
 
 def body(sizes, residual_in, schur, modes, coarse_inv):
@@ -377,6 +396,11 @@
         n = lax.axis_size(axis)
         return lax.ppermute(x, axis, [(k, (k + by) % n) for k in range(n)])
 
+    def swap(x, axis, first):
+        n = lax.axis_size(axis)
+        side = lambda k: 1 if (k - first) % 2 == 0 else -1
+        return lax.ppermute(x, axis, [(k, (k + side(k)) % n) for k in range(n)])
+
     def far(x):
         pairs = []
         for a in range(nx):
@@ -393,11 +417,11 @@
     flops = 2 * width * width * 2 * loads * 2
 
     def z_out(extra):
-        return dict(y=sds((4 * face, loads)), zm=sds((face + PAD + extra, loads)),
-                    zp=sds((face + PAD + extra, loads)), z2=sds((PAD + min(extra, 2 * PAD), loads)))
+        return dict(y=sds((4 * face, loads)), za=sds((face + PAD + extra, loads)),
+                    zb=sds((face + PAD + extra, loads)), z2=sds((PAD + min(extra, 2 * PAD), loads)))
 
     def z_exchange(a, with_dots):
-        got = dict(zm=a["zm"], zp=a["zp"], y=a["y"], gzl=shift(a["zp"], "gz", 1), gzh=shift(a["zm"], "gz", -1))
+        got = dict(za=a["za"], zb=a["zb"], y=a["y"], gza=swap(a["za"], "gz", 0), gzb=swap(a["zb"], "gz", 1))
         if small:
             got["gz2"] = shift(a["z2"], "gz", 2)
         else:
@@ -407,27 +431,33 @@
         return got
 
     def value(stage, ins):
-        extra = 0 if stage == 2 else PAD
-        outs = dict(z=sds((2 * face, loads)), xb=sds((2 * face + extra, loads)),
-                    ym=sds((face + extra, loads)), yp=sds((face + extra, loads)))
+        extra = PAD if stage < 2 else 0
+        outs = dict(z=sds((2 * face, loads)), xab=sds((2 * face + extra, loads)),
+                    ya=sds((face + extra, loads)), yb=sds((face + extra, loads)))
         if stage == 0:
-            outs.update(mt_low=sds((face, 6 * PAD), BF16), mt_high=sds((face, 6 * PAD), BF16))
+            outs.update(mt_a=sds((face, 6 * PAD), BF16), mt_b=sds((face, 6 * PAD), BF16))
             if small:
                 outs["c_all"] = sds((nz * PAD, nz * PAD))
         if stage == 1:
             outs["known"] = rows
+        if stage == 3:
+            outs["dots"] = rows
         return call(functools.partial(value_kernel, face, stage), ins, outs, flops=2 * width * loads * 48)
 
+    def x_exchange(v):
+        got = dict(z=v["z"], xab=v["xab"])
+        if nx == 2:
+            got["gxab"] = swap(v["xab"], "gx", 0)
+        else:
+            a, b, rest = v["xab"][:face], v["xab"][face:2 * face], v["xab"][2 * face:]
+            got["gxab"] = jnp.concatenate([swap(a, "gx", 0), swap(b, "gx", 1), rest], axis=0)
+        return got
+
+    def y_exchange(v):
+        return dict(ya=v["ya"], yb=v["yb"], gya=swap(v["ya"], "gy", 0), gyb=swap(v["yb"], "gy", 1))
+
     def xy_exchange(v):
-        got = {name: v[name] for name in ("z", "xb", "ym", "yp")}
-        if nx == 2:
-            got["gxb"] = shift(v["xb"], "gx", 1)
-        else:
-            low, high, rest = v["xb"][:face], v["xb"][face:2 * face], v["xb"][2 * face:]
-            got["gxb"] = jnp.concatenate([shift(low, "gx", -1), shift(high, "gx", 1), rest], axis=0)
-        got["gyl"] = shift(v["yp"], "gy", 1)
-        got["gyh"] = shift(v["ym"], "gy", -1)
-        return got
+        return dict(x_exchange(v), **y_exchange(v))
 
     near = dict(near=rows) if small else {}
 
@@ -443,11 +473,11 @@
         scratch_shapes=[
             pltpu.VMEM(resid.shape, F32), pltpu.VMEM(matrix.shape, F32),
             pltpu.VMEM(mode_rows.shape, F32), pltpu.VMEM(coarse_rows.shape, F32),
-            pltpu.SemaphoreType.DMA((6,)),
+            pltpu.SemaphoreType.DMA((9,)),
         ],
         compiler_params=pltpu.CompilerParams(vmem_limit_bytes=VMEM_LIMIT),
         cost_estimate=pl.CostEstimate(flops=flops, bytes_accessed=4 * matrix.size, transcendentals=0),
-    )(resid, matrix, mode_rows, coarse_rows)
+    )(*[pltpu.with_memory_space_constraint(x, pltpu.HBM) for x in (resid, matrix, mode_rows, coarse_rows)])
     a = dict(zip(outs, res))
     r0, mt = a["r0"], a["mt"]
     fixed = dict(s_high=a["s_high"], s_low=a["s_low"], modes=a["modes"])
@@ -457,23 +487,23 @@
     else:
         c_own = a["c_own"]
         ins["c_all"] = jnp.concatenate([
-            c_own, shift(c_own, "gz", 1), shift(c_own, "gz", -1),
+            c_own, swap(c_own, "gz", 0), swap(c_own, "gz", 1),
             lax.all_gather(c_own, "gz", axis=0, tiled=True)], axis=0)
     v = value(0, ins)
-    column = dict(mt=mt, mt_low=v["mt_low"], mt_high=v["mt_high"], c_all=v["c_all"] if small else ins["c_all"])
+    column = dict(mt=mt, mt_a=v["mt_a"], mt_b=v["mt_b"], c_all=v["c_all"] if small else ins["c_all"])
     x = xy_exchange(v)
 
     a = call(functools.partial(second_kernel, face), dict(x, **fixed),
              dict(w0=vec, scale=rows, **near, **z_out(PAD)), flops=flops)
     w0 = a["w0"]
-    sums = dict(sum_near=a["near"], sum_far=far(a["near"])) if small else total(v["xb"][2 * face:])
+    sums = dict(sum_near=a["near"], sum_far=far(a["near"])) if small else total(v["xab"][2 * face:])
     v = value(1, dict(z_exchange(a, True), **column, **sums, scale=a["scale"]))
     known = v["known"]
     x = xy_exchange(v)
 
     a = call(functools.partial(third_kernel, face), dict(x, **fixed, w0=w0, known=known),
              dict(q=vec, w1=vec, **near, **z_out(0)), flops=flops)
-    sums = dict(sum_near=a["near"], sum_far=far(a["near"])) if small else total(v["xb"][2 * face:])
+    sums = dict(sum_near=a["near"], sum_far=far(a["near"])) if small else total(v["xab"][2 * face:])
     q, w1 = a["q"], a["w1"]
     v = value(2, dict(z_exchange(a, False), **column))
     x = xy_exchange(v)
@@ -483,12 +513,15 @@
              dict(x, **fixed, **sums, known=known, r0=r0, w0=w0, w1=w1, q=q),
              dict({name: vec for name in names}, known=rows, **z_out(PAD)), flops=flops)
     v = value(3, dict(z_exchange(a, True), **column))
-    x = xy_exchange(v)
     if small:
-        part = call(functools.partial(near_kernel, face), {name: x[name] for name in ("xb", "gxb", "gyl", "gyh")}, near)["near"]
-        sums = dict(sum_near=part, sum_far=far(part))
+        p = call(functools.partial(pair_kernel, face),
+                 dict(dots=v["dots"], gdots=swap(v["dots"], "gx", 0), ya=v["ya"], yb=v["yb"]),
+                 dict(pair=rows, ya=sds((face + PAD, loads)), yb=sds((face + PAD, loads))))
+        sums = dict(pair=p["pair"], gpair=shift(p["pair"], "gy", 2))
+        x = dict(x_exchange(v), **y_exchange(p))
     else:
-        sums = total(v["xb"][2 * face:])
+        sums = dict(sum=lax.psum(v["dots"], ("gx", "gy")))
+        x = xy_exchange(v)
     out = sds((loads, width))
     res = call(functools.partial(last_kernel, face),
                dict(x, **sums, known=a["known"], **{name: a[name] for name in names}),

time: 77.4 us -> 71.7 us (0.926)
  waiting for transfers between devices: 36 us -> 28.5 us
  starting transfers between devices: 27.2 us -> 32.8 us
  local copies, waits for them, and re-layouts: 4.06 us -> 0 us
    ppermute x0 -> x21, starting transfers between devices: none -> 26.4 us  [swap(): return lax.ppermute(x, axis, [(k, (k + side(k)) % n) for k in range(n)])]
    ppermute x24 -> x5, starting transfers between devices: 22.7 us -> 3.49 us  [shift(): return lax.ppermute(x, axis, [(k, (k + by) % n) for k in range(n)])]
    ppermute x24 -> x5, waiting for transfers between devices: 27 us -> 15 us  [shift(): return lax.ppermute(x, axis, [(k, (k + by) % n) for k in range(n)])]
    ppermute x0 -> x21, waiting for transfers between devices: none -> 7.43 us  [swap(): return lax.ppermute(x, axis, [(k, (k + side(k)) % n) for k in range(n)])]
    unnamed x8 -> x0, local copies, waits for them, and re-layouts: 4.06 us -> none
    ppermute x3 -> x2, waiting for transfers between devices: 9.04 us -> 6.1 us  [far(): return lax.ppermute(x, ('gx', 'gy'), pairs)]
    ppermute x3 -> x2, starting transfers between devices: 4.54 us -> 2.91 us  [far(): return lax.ppermute(x, ('gx', 'gy'), pairs)]
  transfers between devices with their start and end apart: 27 -> 28, of which waited for: 16 -> 9; matrix products, arithmetic and copies ran while one was open for 0% -> 0% of each run, Pallas kernels for 0% -> 0%
where the time goes in v3:
time: 71.7 us; the launch traced here: 71.6 us
  starting transfers between devices  32.8 us (46%)
  waiting for transfers between devices  28.5 us (40%)
  Pallas kernels  9.57 us (13%)
  between operations  0.73 us (1%)
    ppermute x21, starting transfers between devices, swap(): return lax.ppermute(x, axis, [(k, (k + side(k)) % n) for k in range(n)])  26.4 us
    ppermute x5, waiting for transfers between devices, shift(): return lax.ppermute(x, axis, [(k, (k + by) % n) for k in range(n)])  15 us
    ppermute x21, waiting for transfers between devices, swap(): return lax.ppermute(x, axis, [(k, (k + side(k)) % n) for k in range(n)])  7.43 us
    pallas_call x9, Pallas kernels, call(): pl.pallas_call(run, out_shape=[outs[n] for n in names_out], in_specs=[vme...  6.15 us
    ppermute x2, waiting for transfers between devices, far(): return lax.ppermute(x, ('gx', 'gy'), pairs)  6.1 us
    ppermute x5, starting transfers between devices, shift(): return lax.ppermute(x, axis, [(k, (k + by) % n) for k in range(n)])  3.49 us
    pallas_call x1, Pallas kernels, body(): pl.pallas_call(functools.partial(first_kernel, face, nz, n_modes, small),...  3.41 us
    ppermute x2, starting transfers between devices, far(): return lax.ppermute(x, ('gx', 'gy'), pairs)  2.91 us
  transfers between devices with their start and end apart: 28, of which 9 were waited for; matrix products, arithmetic and copies ran while one was open for 0% of the time, Pallas kernels for 0%

profile of v3, /device:TPU:0, one launch (start us, length us, event | category | flops | bytes accessed | tf_op | source)
XLA Modules:
  0.0 71.6 jit_solution(13129430568558600389)
XLA Ops:
  0.6 3.4 %shard_map.59 = (f32[768,128]{1,0:T(8,128)S(1)}, bf16[768,768]{1,0:T(8,128)(2,1)S(1)}, bf16[768,768]{1,0:T(8,128)(2,1)S(1)}, f32[8,768]{1,0:T(8,128)S(1)}, bf16[...) custom-call(f32[128,768]{1,0:T(8,128)} %bitcast.7, ...), custom_call_target="tpu_custom_call" | custom-call | flops 603979776 | bytes 2359296 | tf_op jit(solution)/shard_map/pallas_call | solution.py:468
  4.1 3.1 %collective-permute-start = (f32[160,128]{1,0:T(8,128)S(1)}, f32[160,128]{1,0:T(8,128)S(1)}, u32[]{:S(2)}, u32[]{:S(2)}) collective-permute-start(f32[160,128]{1,0:T(8,128)S(1)} %get-tuple-element.63.refs_0_), channel_id=1, source_target_pairs={{0,1},{1,0},{2,3},{3,2},{4,5},{5,4},{6,7},{7,6},{8,9},{9,8},{10,11... | collective-permute-start | bytes 245768 | tf_op jit(solution)/shard_map/ppermute | solution.py:402
  7.1 2.5 %collective-permute-start.1 = (f32[160,128]{1,0:T(8,128)S(1)}, f32[160,128]{1,0:T(8,128)S(1)}, u32[]{:S(2)}, u32[]{:S(2)}) collective-permute-start(f32[160,128]{1,0:T(8,128)S(1)} %get-tuple-element.64.refs_1_), channel_id=1, source_target_pairs={{0,3},{1,2},{2,1},{3,0},{4,7},{5,6},{6,5},{7,4},{8,11},{9,10},{10,... | collective-permute-start | bytes 245768 | tf_op jit(solution)/shard_map/ppermute | solution.py:402
  9.7 4.6 %collective-permute-done.2.refs_5_ = f32[24,128]{1,0:T(8,128)S(1)} collective-permute-done((f32[24,128]{1,0:T(8,128)S(1)}, f32[24,128]{1,0:T(8,128)S(1)}, u32[]{:S(2)}, u32[]{:S(2)}) %collective-permute-start.2) | collective-permute-done | bytes 12320 | tf_op jit(solution)/shard_map/ppermute | solution.py:397
  14.8 1.5 %collective-permute-start.3 = (f32[264,128]{1,0:T(8,128)S(1)}, f32[264,128]{1,0:T(8,128)S(1)}, u32[]{:S(2)}, u32[]{:S(2)}) collective-permute-start(f32[264,128]{1,0:T(8,128)S(1)} %get-tuple-element.70.refs_1_), channel_id=1, source_target_pairs={{0,16},{16,0},{1,17},{17,1},{2,18},{18,2},{3,19},{19,3},{4,20},{20... | collective-permute-start | bytes 405512 | tf_op jit(solution)/shard_map/ppermute | solution.py:402
  16.3 1.6 %collective-permute-start.5 = (f32[136,128]{1,0:T(8,128)S(1)}, f32[136,128]{1,0:T(8,128)S(1)}, u32[]{:S(2)}, u32[]{:S(2)}) collective-permute-start(f32[136,128]{1,0:T(8,128)S(1)} %get-tuple-element.72.refs_4_), channel_id=1, source_target_pairs={{0,12},{4,8},{8,4},{12,0},{1,13},{5,9},{9,5},{13,1},{2,14},{6,10},... | collective-permute-start | bytes 208904 | tf_op jit(solution)/shard_map/ppermute | solution.py:402
  18.0 2.2 %collective-permute-done.5.refs_6_ = f32[136,128]{1,0:T(8,128)S(1)} collective-permute-done((f32[136,128]{1,0:T(8,128)S(1)}, f32[136,128]{1,0:T(8,128)S(1)}, u32[]{:S(2)}, u32[]{:S(2)}) %collective-permute-start.5) | collective-permute-done | bytes 69664 | tf_op jit(solution)/shard_map/ppermute | solution.py:402
  21.8 2.4 %collective-permute-start.7 = (f32[144,128]{1,0:T(8,128)S(1)}, f32[144,128]{1,0:T(8,128)S(1)}, u32[]{:S(2)}, u32[]{:S(2)}) collective-permute-start(f32[144,128]{1,0:T(8,128)S(1)} %get-tuple-element.77.refs_1_), channel_id=1, source_target_pairs={{0,3},{1,2},{2,1},{3,0},{4,7},{5,6},{6,5},{7,4},{8,11},{9,10},{10,... | collective-permute-start | bytes 221192 | tf_op jit(solution)/shard_map/ppermute | solution.py:402
  24.7 2.1 %collective-permute-start.9 = (f32[8,128]{1,0:T(8,128)S(1)}, f32[8,128]{1,0:T(8,128)S(1)}, u32[]{:S(2)}, u32[]{:S(2)}) collective-permute-start(f32[8,128]{1,0:T(8,128)S(1)} %get-tuple-element.83.refs_10_), channel_id=1, source_target_pairs={{0,24},{4,28},{8,16},{12,20},{16,8},{20,12},{24,0},{28,4},{1,25},{... | collective-permute-start | bytes 12296 | tf_op jit(solution)/shard_map/ppermute | solution.py:409
  26.8 2.4 %collective-permute-done.9.refs_11_ = f32[8,128]{1,0:T(8,128)S(1)} collective-permute-done((f32[8,128]{1,0:T(8,128)S(1)}, f32[8,128]{1,0:T(8,128)S(1)}, u32[]{:S(2)}, u32[]{:S(2)}) %collective-permute-start.9) | collective-permute-done | bytes 4128 | tf_op jit(solution)/shard_map/ppermute | solution.py:409
  30.9 1.6 %collective-permute-start.12 = (f32[136,128]{1,0:T(8,128)S(1)}, f32[136,128]{1,0:T(8,128)S(1)}, u32[]{:S(2)}, u32[]{:S(2)}) collective-permute-start(f32[136,128]{1,0:T(8,128)S(1)} %get-tuple-element.88.refs_4_), channel_id=1, source_target_pairs={{0,12},{4,8},{8,4},{12,0},{1,13},{5,9},{9,5},{13,1},{2,14},{6,10},... | collective-permute-start | bytes 208904 | tf_op jit(solution)/shard_map/ppermute | solution.py:402
  32.5 2.2 %collective-permute-done.12.refs_6_ = f32[136,128]{1,0:T(8,128)S(1)} collective-permute-done((f32[136,128]{1,0:T(8,128)S(1)}, f32[136,128]{1,0:T(8,128)S(1)}, u32[]{:S(2)}, u32[]{:S(2)}) %collective-permute-start.12) | collective-permute-done | bytes 69664 | tf_op jit(solution)/shard_map/ppermute | solution.py:402
  35.7 1.5 %collective-permute-start.13 = (f32[136,128]{1,0:T(8,128)S(1)}, f32[136,128]{1,0:T(8,128)S(1)}, u32[]{:S(2)}, u32[]{:S(2)}) collective-permute-start(f32[136,128]{1,0:T(8,128)S(1)} %get-tuple-element.91.refs_0_), channel_id=1, source_target_pairs={{0,1},{1,0},{2,3},{3,2},{4,5},{5,4},{6,7},{7,6},{8,9},{9,8},{10,11... | collective-permute-start | bytes 208904 | tf_op jit(solution)/shard_map/ppermute | solution.py:402
  37.2 2.4 %collective-permute-start.14 = (f32[136,128]{1,0:T(8,128)S(1)}, f32[136,128]{1,0:T(8,128)S(1)}, u32[]{:S(2)}, u32[]{:S(2)}) collective-permute-start(f32[136,128]{1,0:T(8,128)S(1)} %get-tuple-element.92.refs_1_), channel_id=1, source_target_pairs={{0,3},{1,2},{2,1},{3,0},{4,7},{5,6},{6,5},{7,4},{8,11},{9,10},{10,... | collective-permute-start | bytes 208904 | tf_op jit(solution)/shard_map/ppermute | solution.py:402
  39.5 4.5 %collective-permute-done.15.refs_5_ = f32[8,128]{1,0:T(8,128)S(1)} collective-permute-done((f32[8,128]{1,0:T(8,128)S(1)}, f32[8,128]{1,0:T(8,128)S(1)}, u32[]{:S(2)}, u32[]{:S(2)}) %collective-permute-start.15) | collective-permute-done | bytes 4128 | tf_op jit(solution)/shard_map/ppermute | solution.py:397
  45.7 1.6 %collective-permute-start.18 = (f32[128,128]{1,0:T(8,128)S(1)}, f32[128,128]{1,0:T(8,128)S(1)}, u32[]{:S(2)}, u32[]{:S(2)}) collective-permute-start(f32[128,128]{1,0:T(8,128)S(1)} %get-tuple-element.98.refs_4_), channel_id=1, source_target_pairs={{0,12},{4,8},{8,4},{12,0},{1,13},{5,9},{9,5},{13,1},{2,14},{6,10},... | collective-permute-start | bytes 196616 | tf_op jit(solution)/shard_map/ppermute | solution.py:402
  48.1 3.7 %collective-permute-done.19.refs_11_ = f32[8,128]{1,0:T(8,128)S(1)} collective-permute-done((f32[8,128]{1,0:T(8,128)S(1)}, f32[8,128]{1,0:T(8,128)S(1)}, u32[]{:S(2)}, u32[]{:S(2)}) %collective-permute-start.19) | collective-permute-done | bytes 4128 | tf_op jit(solution)/shard_map/ppermute | solution.py:409
  51.8 1.3 %shard_map.65 = (f32[768,128]{1,0:T(8,128)S(1)}, f32[768,128]{1,0:T(8,128)S(1)}, f32[768,128]{1,0:T(8,128)S(1)}, f32[768,128]{1,0:T(8,128)S(1)}, f32[768,128]{1,...) custom-call(f32[256,128]{1,0:T(8,128)S(1)} %get-tuple-element.95.ref, ...), custom_call_target="tpu_custom_call" | custom-call | flops 603979776 | bytes 7405568 | tf_op jit(solution)/shard_map/pallas_call | solution.py:30
  53.3 2.2 %collective-permute-start.21 = (f32[144,128]{1,0:T(8,128)S(1)}, f32[144,128]{1,0:T(8,128)S(1)}, u32[]{:S(2)}, u32[]{:S(2)}) collective-permute-start(f32[144,128]{1,0:T(8,128)S(1)} %get-tuple-element.104.refs_1_), channel_id=1, source_target_pairs={{0,3},{1,2},{2,1},{3,0},{4,7},{5,6},{6,5},{7,4},{8,11},{9,10},{10,... | collective-permute-start | bytes 221192 | tf_op jit(solution)/shard_map/ppermute | solution.py:402
  55.5 1.3 %collective-permute-start.22 = (f32[16,128]{1,0:T(8,128)S(1)}, f32[16,128]{1,0:T(8,128)S(1)}, u32[]{:S(2)}, u32[]{:S(2)}) collective-permute-start(f32[16,128]{1,0:T(8,128)S(1)} %get-tuple-element.106), channel_id=1, source_target_pairs={{0,2},{1,3},{2,0},{3,1},{4,6},{5,7},{6,4},{7,5},{8,10},{9,11},{10,... | collective-permute-start | bytes 24584 | tf_op jit(solution)/shard_map/ppermute | solution.py:397
  56.7 3.4 %collective-permute-done.22.refs_5_ = f32[16,128]{1,0:T(8,128)S(1)} collective-permute-done((f32[16,128]{1,0:T(8,128)S(1)}, f32[16,128]{1,0:T(8,128)S(1)}, u32[]{:S(2)}, u32[]{:S(2)}) %collective-permute-start.22) | collective-permute-done | bytes 8224 | tf_op jit(solution)/shard_map/ppermute | solution.py:397
  62.6 3.0 %collective-permute-done.24.refs_1_ = f32[8,128]{1,0:T(8,128)S(1)} collective-permute-done((f32[8,128]{1,0:T(8,128)S(1)}, f32[8,128]{1,0:T(8,128)S(1)}, u32[]{:S(2)}, u32[]{:S(2)}) %collective-permute-start.24) | collective-permute-done | bytes 4128 | tf_op jit(solution)/shard_map/ppermute | solution.py:402
  66.3 1.5 %collective-permute-start.27 = (f32[8,128]{1,0:T(8,128)S(1)}, f32[8,128]{1,0:T(8,128)S(1)}, u32[]{:S(2)}, u32[]{:S(2)}) collective-permute-start(f32[8,128]{1,0:T(8,128)S(1)} %get-tuple-element.114.refs_7_), channel_id=1, source_target_pairs={{0,8},{4,12},{8,0},{12,4},{1,9},{5,13},{9,1},{13,5},{2,10},{6,14},... | collective-permute-start | bytes 12296 | tf_op jit(solution)/shard_map/ppermute | solution.py:397
  67.8 2.5 %collective-permute-done.27.refs_8_ = f32[8,128]{1,0:T(8,128)S(1)} collective-permute-done((f32[8,128]{1,0:T(8,128)S(1)}, f32[8,128]{1,0:T(8,128)S(1)}, u32[]{:S(2)}, u32[]{:S(2)}) %collective-permute-start.27) | collective-permute-done | bytes 4128 | tf_op jit(solution)/shard_map/ppermute | solution.py:397
  (42 shorter events, 12.3 us)
Async XLA Ops:
  4.1 10.3 %collective-permute-start = (f32[160,128]{1,0:T(8,128)S(1)}, f32[160,128]{1,0:T(8,128)S(1)}, u32[]{:S(2)}, u32[]{:S(2)}) collective-permute-start(f32[160,128]{1,0:T(8,128)S(1)} %get-tuple-element.63.refs_0_), channel_id=1, source_target_pairs={{0,1},{1,0},{2,3},{3,2},{4,5},{5,4},{6,7},{7,6},{8,9},{9,8},{10,11... | collective-permute-start | bytes 245768 | tf_op jit(solution)/shard_map/ppermute | solution.py:402
  7.1 7.2 %collective-permute-start.1 = (f32[160,128]{1,0:T(8,128)S(1)}, f32[160,128]{1,0:T(8,128)S(1)}, u32[]{:S(2)}, u32[]{:S(2)}) collective-permute-start(f32[160,128]{1,0:T(8,128)S(1)} %get-tuple-element.64.refs_1_), channel_id=1, source_target_pairs={{0,3},{1,2},{2,1},{3,0},{4,7},{5,6},{6,5},{7,4},{8,11},{9,10},{10,... | collective-permute-start | bytes 245768 | tf_op jit(solution)/shard_map/ppermute | solution.py:402
  9.6 4.7 %collective-permute-start.2 = (f32[24,128]{1,0:T(8,128)S(1)}, f32[24,128]{1,0:T(8,128)S(1)}, u32[]{:S(2)}, u32[]{:S(2)}) collective-permute-start(f32[24,128]{1,0:T(8,128)S(1)} %get-tuple-element.66), channel_id=1, source_target_pairs={{0,2},{1,3},{2,0},{3,1},{4,6},{5,7},{6,4},{7,5},{8,10},{9,11},{10,... | collective-permute-start | bytes 36872 | tf_op jit(solution)/shard_map/ppermute | solution.py:397
  14.8 5.4 %collective-permute-start.3 = (f32[264,128]{1,0:T(8,128)S(1)}, f32[264,128]{1,0:T(8,128)S(1)}, u32[]{:S(2)}, u32[]{:S(2)}) collective-permute-start(f32[264,128]{1,0:T(8,128)S(1)} %get-tuple-element.70.refs_1_), channel_id=1, source_target_pairs={{0,16},{16,0},{1,17},{17,1},{2,18},{18,2},{3,19},{19,3},{4,20},{20... | collective-permute-start | bytes 405512 | tf_op jit(solution)/shard_map/ppermute | solution.py:402
  21.2 8.1 %collective-permute-start.6 = (f32[144,128]{1,0:T(8,128)S(1)}, f32[144,128]{1,0:T(8,128)S(1)}, u32[]{:S(2)}, u32[]{:S(2)}) collective-permute-start(f32[144,128]{1,0:T(8,128)S(1)} %get-tuple-element.76.refs_0_), channel_id=1, source_target_pairs={{0,1},{1,0},{2,3},{3,2},{4,5},{5,4},{6,7},{7,6},{8,9},{9,8},{10,11... | collective-permute-start | bytes 221192 | tf_op jit(solution)/shard_map/ppermute | solution.py:402
  21.8 7.5 %collective-permute-start.7 = (f32[144,128]{1,0:T(8,128)S(1)}, f32[144,128]{1,0:T(8,128)S(1)}, u32[]{:S(2)}, u32[]{:S(2)}) collective-permute-start(f32[144,128]{1,0:T(8,128)S(1)} %get-tuple-element.77.refs_1_), channel_id=1, source_target_pairs={{0,3},{1,2},{2,1},{3,0},{4,7},{5,6},{6,5},{7,4},{8,11},{9,10},{10,... | collective-permute-start | bytes 221192 | tf_op jit(solution)/shard_map/ppermute | solution.py:402
  24.1 5.1 %collective-permute-start.8 = (f32[16,128]{1,0:T(8,128)S(1)}, f32[16,128]{1,0:T(8,128)S(1)}, u32[]{:S(2)}, u32[]{:S(2)}) collective-permute-start(f32[16,128]{1,0:T(8,128)S(1)} %get-tuple-element.79), channel_id=1, source_target_pairs={{0,2},{1,3},{2,0},{3,1},{4,6},{5,7},{6,4},{7,5},{8,10},{9,11},{10,... | collective-permute-start | bytes 24584 | tf_op jit(solution)/shard_map/ppermute | solution.py:397
  24.7 4.5 %collective-permute-start.9 = (f32[8,128]{1,0:T(8,128)S(1)}, f32[8,128]{1,0:T(8,128)S(1)}, u32[]{:S(2)}, u32[]{:S(2)}) collective-permute-start(f32[8,128]{1,0:T(8,128)S(1)} %get-tuple-element.83.refs_10_), channel_id=1, source_target_pairs={{0,24},{4,28},{8,16},{12,20},{16,8},{20,12},{24,0},{28,4},{1,25},{... | collective-permute-start | bytes 12296 | tf_op jit(solution)/shard_map/ppermute | solution.py:409
  29.6 5.1 %collective-permute-start.10 = (f32[264,128]{1,0:T(8,128)S(1)}, f32[264,128]{1,0:T(8,128)S(1)}, u32[]{:S(2)}, u32[]{:S(2)}) collective-permute-start(f32[264,128]{1,0:T(8,128)S(1)} %get-tuple-element.86.refs_1_), channel_id=1, source_target_pairs={{0,16},{16,0},{1,17},{17,1},{2,18},{18,2},{3,19},{19,3},{4,20},{20... | collective-permute-start | bytes 405512 | tf_op jit(solution)/shard_map/ppermute | solution.py:402
  35.7 8.4 %collective-permute-start.13 = (f32[136,128]{1,0:T(8,128)S(1)}, f32[136,128]{1,0:T(8,128)S(1)}, u32[]{:S(2)}, u32[]{:S(2)}) collective-permute-start(f32[136,128]{1,0:T(8,128)S(1)} %get-tuple-element.91.refs_0_), channel_id=1, source_target_pairs={{0,1},{1,0},{2,3},{3,2},{4,5},{5,4},{6,7},{7,6},{8,9},{9,8},{10,11... | collective-permute-start | bytes 208904 | tf_op jit(solution)/shard_map/ppermute | solution.py:402
  37.2 6.9 %collective-permute-start.14 = (f32[136,128]{1,0:T(8,128)S(1)}, f32[136,128]{1,0:T(8,128)S(1)}, u32[]{:S(2)}, u32[]{:S(2)}) collective-permute-start(f32[136,128]{1,0:T(8,128)S(1)} %get-tuple-element.92.refs_1_), channel_id=1, source_target_pairs={{0,3},{1,2},{2,1},{3,0},{4,7},{5,6},{6,5},{7,4},{8,11},{9,10},{10,... | collective-permute-start | bytes 208904 | tf_op jit(solution)/shard_map/ppermute | solution.py:402
  39.5 4.5 %collective-permute-start.15 = (f32[8,128]{1,0:T(8,128)S(1)}, f32[8,128]{1,0:T(8,128)S(1)}, u32[]{:S(2)}, u32[]{:S(2)}) collective-permute-start(f32[8,128]{1,0:T(8,128)S(1)} %get-tuple-element.94), channel_id=1, source_target_pairs={{0,2},{1,3},{2,0},{3,1},{4,6},{5,7},{6,4},{7,5},{8,10},{9,11},{10,... | collective-permute-start | bytes 12296 | tf_op jit(solution)/shard_map/ppermute | solution.py:397
  44.4 7.4 %collective-permute-start.16 = (f32[256,128]{1,0:T(8,128)S(1)}, f32[256,128]{1,0:T(8,128)S(1)}, u32[]{:S(2)}, u32[]{:S(2)}) collective-permute-start(f32[256,128]{1,0:T(8,128)S(1)} %get-tuple-element.96.refs_1_), channel_id=1, source_target_pairs={{0,16},{16,0},{1,17},{17,1},{2,18},{18,2},{3,19},{19,3},{4,20},{20... | collective-permute-start | bytes 393224 | tf_op jit(solution)/shard_map/ppermute | solution.py:402
  45.7 6.1 %collective-permute-start.17 = (f32[128,128]{1,0:T(8,128)S(1)}, f32[128,128]{1,0:T(8,128)S(1)}, u32[]{:S(2)}, u32[]{:S(2)}) collective-permute-start(f32[128,128]{1,0:T(8,128)S(1)} %get-tuple-element.97.refs_3_), channel_id=1, source_target_pairs={{0,4},{4,0},{8,12},{12,8},{1,5},{5,1},{9,13},{13,9},{2,6},{6,2},{1... | collective-permute-start | bytes 196616 | tf_op jit(solution)/shard_map/ppermute | solution.py:402
  45.7 6.1 %collective-permute-start.18 = (f32[128,128]{1,0:T(8,128)S(1)}, f32[128,128]{1,0:T(8,128)S(1)}, u32[]{:S(2)}, u32[]{:S(2)}) collective-permute-start(f32[128,128]{1,0:T(8,128)S(1)} %get-tuple-element.98.refs_4_), channel_id=1, source_target_pairs={{0,12},{4,8},{8,4},{12,0},{1,13},{5,9},{9,5},{13,1},{2,14},{6,10},... | collective-permute-start | bytes 196616 | tf_op jit(solution)/shard_map/ppermute | solution.py:402
  47.3 4.5 %collective-permute-start.19 = (f32[8,128]{1,0:T(8,128)S(1)}, f32[8,128]{1,0:T(8,128)S(1)}, u32[]{:S(2)}, u32[]{:S(2)}) collective-permute-start(f32[8,128]{1,0:T(8,128)S(1)} %get-tuple-element.99.refs_10_), channel_id=1, source_target_pairs={{0,24},{4,28},{8,16},{12,20},{16,8},{20,12},{24,0},{28,4},{1,25},{... | collective-permute-start | bytes 12296 | tf_op jit(solution)/shard_map/ppermute | solution.py:409
  53.2 6.9 %collective-permute-start.20 = (f32[144,128]{1,0:T(8,128)S(1)}, f32[144,128]{1,0:T(8,128)S(1)}, u32[]{:S(2)}, u32[]{:S(2)}) collective-permute-start(f32[144,128]{1,0:T(8,128)S(1)} %get-tuple-element.103.refs_0_), channel_id=1, source_target_pairs={{0,1},{1,0},{2,3},{3,2},{4,5},{5,4},{6,7},{7,6},{8,9},{9,8},{10,11... | collective-permute-start | bytes 221192 | tf_op jit(solution)/shard_map/ppermute | solution.py:402
  53.3 6.8 %collective-permute-start.21 = (f32[144,128]{1,0:T(8,128)S(1)}, f32[144,128]{1,0:T(8,128)S(1)}, u32[]{:S(2)}, u32[]{:S(2)}) collective-permute-start(f32[144,128]{1,0:T(8,128)S(1)} %get-tuple-element.104.refs_1_), channel_id=1, source_target_pairs={{0,3},{1,2},{2,1},{3,0},{4,7},{5,6},{6,5},{7,4},{8,11},{9,10},{10,... | collective-permute-start | bytes 221192 | tf_op jit(solution)/shard_map/ppermute | solution.py:402
  55.5 4.6 %collective-permute-start.22 = (f32[16,128]{1,0:T(8,128)S(1)}, f32[16,128]{1,0:T(8,128)S(1)}, u32[]{:S(2)}, u32[]{:S(2)}) collective-permute-start(f32[16,128]{1,0:T(8,128)S(1)} %get-tuple-element.106), channel_id=1, source_target_pairs={{0,2},{1,3},{2,0},{3,1},{4,6},{5,7},{6,4},{7,5},{8,10},{9,11},{10,... | collective-permute-start | bytes 24584 | tf_op jit(solution)/shard_map/ppermute | solution.py:397
  60.5 9.8 %collective-permute-start.23 = (f32[256,128]{1,0:T(8,128)S(1)}, f32[256,128]{1,0:T(8,128)S(1)}, u32[]{:S(2)}, u32[]{:S(2)}) collective-permute-start(f32[256,128]{1,0:T(8,128)S(1)} %get-tuple-element.108.refs_1_), channel_id=1, source_target_pairs={{0,16},{16,0},{1,17},{17,1},{2,18},{18,2},{3,19},{19,3},{4,20},{20... | collective-permute-start | bytes 393224 | tf_op jit(solution)/shard_map/ppermute | solution.py:402
  61.5 4.1 %collective-permute-start.24 = (f32[8,128]{1,0:T(8,128)S(1)}, f32[8,128]{1,0:T(8,128)S(1)}, u32[]{:S(2)}, u32[]{:S(2)}) collective-permute-start(f32[8,128]{1,0:T(8,128)S(1)} %get-tuple-element.109.refs_0_), channel_id=1, source_target_pairs={{0,16},{16,0},{1,17},{17,1},{2,18},{18,2},{3,19},{19,3},{4,20},{20... | collective-permute-start | bytes 12296 | tf_op jit(solution)/shard_map/ppermute | solution.py:402
  65.6 4.7 %collective-permute-start.25 = (f32[136,128]{1,0:T(8,128)S(1)}, f32[136,128]{1,0:T(8,128)S(1)}, u32[]{:S(2)}, u32[]{:S(2)}) collective-permute-start(f32[136,128]{1,0:T(8,128)S(1)} %get-tuple-element.112.refs_3_), channel_id=1, source_target_pairs={{0,4},{4,0},{8,12},{12,8},{1,5},{5,1},{9,13},{13,9},{2,6},{6,2},{1... | collective-permute-start | bytes 208904 | tf_op jit(solution)/shard_map/ppermute | solution.py:402
  65.7 4.6 %collective-permute-start.26 = (f32[136,128]{1,0:T(8,128)S(1)}, f32[136,128]{1,0:T(8,128)S(1)}, u32[]{:S(2)}, u32[]{:S(2)}) collective-permute-start(f32[136,128]{1,0:T(8,128)S(1)} %get-tuple-element.113.refs_4_), channel_id=1, source_target_pairs={{0,12},{4,8},{8,4},{12,0},{1,13},{5,9},{9,5},{13,1},{2,14},{6,10},... | collective-permute-start | bytes 208904 | tf_op jit(solution)/shard_map/ppermute | solution.py:402
  66.3 4.0 %collective-permute-start.27 = (f32[8,128]{1,0:T(8,128)S(1)}, f32[8,128]{1,0:T(8,128)S(1)}, u32[]{:S(2)}, u32[]{:S(2)}) collective-permute-start(f32[8,128]{1,0:T(8,128)S(1)} %get-tuple-element.114.refs_7_), channel_id=1, source_target_pairs={{0,8},{4,12},{8,0},{12,4},{1,9},{5,13},{9,1},{13,5},{2,10},{6,14},... | collective-permute-start | bytes 12296 | tf_op jit(solution)/shard_map/ppermute | solution.py:397
  (4 other events, 10.9 us)

commit v4 on v3

--- a/solution.py
+++ b/solution.py
@@ -264,10 +264,10 @@
     o["yb"][0:face, :] = xy[3 * face:]
     if stage == 3:
         o["dots"][...] = dots
-    elif stage != 2:
+    if stage != 2:
         o["xab"][2 * face:, :] = dots
-        o["ya"][face:, :] = dots
-        o["yb"][face:, :] = dots
+        o["ya"][face:face + PAD, :] = dots
+        o["yb"][face:face + PAD, :] = dots
 
 
 def assemble(face, i):
@@ -342,19 +342,13 @@
         half_dot(s1, s1), curv, half_dot(z1, vec), half_dot(s1, z1)], cols), PAD, o)
 
 
-def pair_kernel(face, i, o):
-    total = i["dots"][...] + i["gdots"][...]
-    o["pair"][...] = total
-    for name in ("ya", "yb"):
-        o[name][0:face, :] = i[name][...]
-        o[name][face:, :] = total
+def four_kernel(face, i, o):
+    near = i["dots"][...] + i["gxab"][2 * face:2 * face + PAD, :]
+    o["part"][...] = near + (i["across"][...] + i["gyb"][face:face + PAD, :])
 
 
 def last_kernel(face, i, o):
-    if "sum" in i:
-        d = i["sum"][...]
-    else:
-        d = (i["pair"][...] + i["gpair"][...]) + (i["gya"][face:, :] + i["gyb"][face:, :])
+    d = i["sum_near"][...] + i["sum_far"][...]
     rr, rw, ww, ws, ss, wc, sc, sz = (row(d, k) for k in range(8))
     norm1, alpha1 = row(i["known"], 0), row(i["known"], 1)
     beta2 = rr / norm1
@@ -401,12 +395,13 @@
         side = lambda k: 1 if (k - first) % 2 == 0 else -1
         return lax.ppermute(x, axis, [(k, (k + side(k)) % n) for k in range(n)])
 
+    def move(x, target):
+        places = [(a, b) for a in range(nx) for b in range(ny)]
+        pairs = [(a * ny + b, target(a, b)[0] * ny + target(a, b)[1]) for a, b in places]
+        return lax.ppermute(x, ("gx", "gy"), pairs)
+
     def far(x):
-        pairs = []
-        for a in range(nx):
-            for b in range(ny):
-                pairs.append((a * ny + b, (a + 1) % nx * ny + (b + 2) % ny))
-        return lax.ppermute(x, ("gx", "gy"), pairs)
+        return move(x, lambda a, b: ((a + 1) % nx, (b + 2) % ny))
 
     def total(x):
         return dict(sum_near=lax.psum(x, ("gx", "gy")), sum_far=jnp.zeros_like(x))
@@ -418,22 +413,23 @@
 
     def z_out(extra):
         return dict(y=sds((4 * face, loads)), za=sds((face + PAD + extra, loads)),
-                    zb=sds((face + PAD + extra, loads)), z2=sds((PAD + min(extra, 2 * PAD), loads)))
+                    zb=sds((face + PAD + extra + PAD, loads)), z2=sds((PAD + min(extra, 2 * PAD), loads)))
 
     def z_exchange(a, with_dots):
-        got = dict(za=a["za"], zb=a["zb"], y=a["y"], gza=swap(a["za"], "gz", 0), gzb=swap(a["zb"], "gz", 1))
+        got = dict(za=a["za"], zb=a["zb"], y=a["y"], gzb=swap(a["zb"], "gz", 1))
         if small:
             got["gz2"] = shift(a["z2"], "gz", 2)
-        else:
+        got["gza"] = swap(a["za"], "gz", 0)
+        if not small:
             got["g_all"] = lax.all_gather(a["z2"][0:PAD], "gz", axis=0, tiled=True)
             if with_dots:
                 got["d_all"] = lax.psum(a["z2"][PAD:2 * PAD], "gz")
         return got
 
     def value(stage, ins):
-        extra = PAD if stage < 2 else 0
+        extra = 0 if stage == 2 else PAD
         outs = dict(z=sds((2 * face, loads)), xab=sds((2 * face + extra, loads)),
-                    ya=sds((face + extra, loads)), yb=sds((face + extra, loads)))
+                    ya=sds((face + extra, loads)), yb=sds((face + extra + PAD, loads)))
         if stage == 0:
             outs.update(mt_a=sds((face, 6 * PAD), BF16), mt_b=sds((face, 6 * PAD), BF16))
             if small:
@@ -454,7 +450,8 @@
         return got
 
     def y_exchange(v):
-        return dict(ya=v["ya"], yb=v["yb"], gya=swap(v["ya"], "gy", 0), gyb=swap(v["yb"], "gy", 1))
+        gyb = swap(v["yb"], "gy", 1)
+        return dict(ya=v["ya"], yb=v["yb"], gya=swap(v["ya"], "gy", 0), gyb=gyb)
 
     def xy_exchange(v):
         return dict(x_exchange(v), **y_exchange(v))
@@ -503,10 +500,14 @@
 
     a = call(functools.partial(third_kernel, face), dict(x, **fixed, w0=w0, known=known),
              dict(q=vec, w1=vec, **near, **z_out(0)), flops=flops)
-    sums = dict(sum_near=a["near"], sum_far=far(a["near"])) if small else total(v["xab"][2 * face:])
+    if not small:
+        sums = total(v["xab"][2 * face:])
     q, w1 = a["q"], a["w1"]
     v = value(2, dict(z_exchange(a, False), **column))
-    x = xy_exchange(v)
+    x = x_exchange(v)
+    if small:
+        sums = dict(sum_near=a["near"], sum_far=far(a["near"]))
+    x.update(y_exchange(v))
 
     names = ("r2", "w2", "p1", "s1", "z1", "m2")
     a = call(functools.partial(fourth_kernel, face),
@@ -514,14 +515,15 @@
              dict({name: vec for name in names}, known=rows, **z_out(PAD)), flops=flops)
     v = value(3, dict(z_exchange(a, True), **column))
     if small:
-        p = call(functools.partial(pair_kernel, face),
-                 dict(dots=v["dots"], gdots=swap(v["dots"], "gx", 0), ya=v["ya"], yb=v["yb"]),
-                 dict(pair=rows, ya=sds((face + PAD, loads)), yb=sds((face + PAD, loads))))
-        sums = dict(pair=p["pair"], gpair=shift(p["pair"], "gy", 2))
-        x = dict(x_exchange(v), **y_exchange(p))
+        x = x_exchange(v)
+        across = move(v["dots"], lambda a, b: (1 - a, (b + (-1 if b % 2 == 0 else 1)) % ny))
+        x.update(y_exchange(v))
+        part = call(functools.partial(four_kernel, face),
+                    dict(dots=v["dots"], across=across, gxab=x["gxab"], gyb=x["gyb"]), dict(part=rows))["part"]
+        sums = dict(sum_near=part, sum_far=swap(part, "gy", 0))
     else:
-        sums = dict(sum=lax.psum(v["dots"], ("gx", "gy")))
         x = xy_exchange(v)
+        sums = total(v["dots"])
     out = sds((loads, width))
     res = call(functools.partial(last_kernel, face),
                dict(x, **sums, known=a["known"], **{name: a[name] for name in names}),

time: 71.7 us -> 69.5 us (0.969)
  waiting for transfers between devices: 28.5 us -> 25.8 us
    ppermute x5 -> x4, waiting for transfers between devices: 15 us -> 8.68 us  [shift(): return lax.ppermute(x, axis, [(k, (k + by) % n) for k in range(n)])]
    ppermute x21, starting transfers between devices: 26.4 us -> 22.3 us  [swap(): return lax.ppermute(x, axis, [(k, (k + side(k)) % n) for k in range(n)])]
    ppermute x5 -> x4, starting transfers between devices: 3.49 us -> 6.79 us  [shift(): return lax.ppermute(x, axis, [(k, (k + by) % n) for k in range(n)])]
    ppermute x2 -> x3, waiting for transfers between devices: 6.1 us -> 8.89 us  [move(): return lax.ppermute(x, ('gx', 'gy'), pairs)]
    ppermute x2 -> x3, starting transfers between devices: 2.91 us -> 4.05 us  [move(): return lax.ppermute(x, ('gx', 'gy'), pairs)]
    ppermute x21, waiting for transfers between devices: 7.43 us -> 8.24 us  [swap(): return lax.ppermute(x, axis, [(k, (k + side(k)) % n) for k in range(n)])]
  transfers between devices with their start and end apart: 28 -> 28, of which waited for: 9 -> 14; matrix products, arithmetic and copies ran while one was open for 0% -> 0% of each run, Pallas kernels for 0% -> 0%
where the time goes in v4:
time: 69.5 us; the launch traced here: 69.3 us
  starting transfers between devices  33.2 us (48%)
  waiting for transfers between devices  25.8 us (37%)
  Pallas kernels  9.63 us (14%)
  between operations  0.71 us (1%)
    ppermute x21, starting transfers between devices, swap(): return lax.ppermute(x, axis, [(k, (k + side(k)) % n) for k in range(n)])  22.3 us
    ppermute x3, waiting for transfers between devices, move(): return lax.ppermute(x, ('gx', 'gy'), pairs)  8.89 us
    ppermute x4, waiting for transfers between devices, shift(): return lax.ppermute(x, axis, [(k, (k + by) % n) for k in range(n)])  8.68 us
    ppermute x21, waiting for transfers between devices, swap(): return lax.ppermute(x, axis, [(k, (k + side(k)) % n) for k in range(n)])  8.24 us
    ppermute x4, starting transfers between devices, shift(): return lax.ppermute(x, axis, [(k, (k + by) % n) for k in range(n)])  6.79 us
    pallas_call x9, Pallas kernels, call(): pl.pallas_call(run, out_shape=[outs[n] for n in names_out], in_specs=[vme...  6.21 us
    ppermute x3, starting transfers between devices, move(): return lax.ppermute(x, ('gx', 'gy'), pairs)  4.05 us
    pallas_call x1, Pallas kernels, body(): pl.pallas_call(functools.partial(first_kernel, face, nz, n_modes, small),...  3.41 us
  transfers between devices with their start and end apart: 28, of which 14 were waited for; matrix products, arithmetic and copies ran while one was open for 0% of the time, Pallas kernels for 0%

profile of v4, /device:TPU:0, one launch (start us, length us, event | category | flops | bytes accessed | tf_op | source)
XLA Modules:
  0.0 69.3 jit_solution(211194601067995926)
XLA Ops:
  0.6 3.4 %shard_map.59 = (f32[768,128]{1,0:T(8,128)S(1)}, bf16[768,768]{1,0:T(8,128)(2,1)S(1)}, bf16[768,768]{1,0:T(8,128)(2,1)S(1)}, f32[8,768]{1,0:T(8,128)S(1)}, bf16[...) custom-call(f32[128,768]{1,0:T(8,128)} %bitcast.7, ...), custom_call_target="tpu_custom_call" | custom-call | flops 603979776 | bytes 2359296 | tf_op jit(solution)/shard_map/pallas_call | solution.py:465
  4.1 5.1 %collective-permute-start = (f32[168,128]{1,0:T(8,128)S(1)}, f32[168,128]{1,0:T(8,128)S(1)}, u32[]{:S(2)}, u32[]{:S(2)}) collective-permute-start(f32[168,128]{1,0:T(8,128)S(1)} %get-tuple-element.61.refs_1_), channel_id=1, source_target_pairs={{0,3},{1,2},{2,1},{3,0},{4,7},{5,6},{6,5},{7,4},{8,11},{9,10},{10,... | collective-permute-start | bytes 258056 | tf_op jit(solution)/shard_map/ppermute | solution.py:396
  9.8 4.1 %collective-permute-done.1.refs_4_ = f32[24,128]{1,0:T(8,128)S(1)} collective-permute-done((f32[24,128]{1,0:T(8,128)S(1)}, f32[24,128]{1,0:T(8,128)S(1)}, u32[]{:S(2)}, u32[]{:S(2)}) %collective-permute-start.1) | collective-permute-done | bytes 12320 | tf_op jit(solution)/shard_map/ppermute | solution.py:391
  14.4 1.7 %collective-permute-start.3 = (f32[264,128]{1,0:T(8,128)S(1)}, f32[264,128]{1,0:T(8,128)S(1)}, u32[]{:S(2)}, u32[]{:S(2)}) collective-permute-start(f32[264,128]{1,0:T(8,128)S(1)} %get-tuple-element.67.refs_1_), channel_id=1, source_target_pairs={{0,16},{16,0},{1,17},{17,1},{2,18},{18,2},{3,19},{19,3},{4,20},{20... | collective-permute-start | bytes 405512 | tf_op jit(solution)/shard_map/ppermute | solution.py:396
  16.2 1.5 %collective-permute-start.4 = (f32[136,128]{1,0:T(8,128)S(1)}, f32[136,128]{1,0:T(8,128)S(1)}, u32[]{:S(2)}, u32[]{:S(2)}) collective-permute-start(f32[136,128]{1,0:T(8,128)S(1)} %get-tuple-element.68.refs_3_), channel_id=1, source_target_pairs={{0,4},{4,0},{8,12},{12,8},{1,5},{5,1},{9,13},{13,9},{2,6},{6,2},{1... | collective-permute-start | bytes 208904 | tf_op jit(solution)/shard_map/ppermute | solution.py:396
  18.6 1.9 %collective-permute-done.5.refs_6_ = f32[144,128]{1,0:T(8,128)S(1)} collective-permute-done((f32[144,128]{1,0:T(8,128)S(1)}, f32[144,128]{1,0:T(8,128)S(1)}, u32[]{:S(2)}, u32[]{:S(2)}) %collective-permute-start.5) | collective-permute-done | bytes 73760 | tf_op jit(solution)/shard_map/ppermute | solution.py:396
  21.6 2.2 %collective-permute-start.6 = (f32[152,128]{1,0:T(8,128)S(1)}, f32[152,128]{1,0:T(8,128)S(1)}, u32[]{:S(2)}, u32[]{:S(2)}) collective-permute-start(f32[152,128]{1,0:T(8,128)S(1)} %get-tuple-element.74.refs_1_), channel_id=1, source_target_pairs={{0,3},{1,2},{2,1},{3,0},{4,7},{5,6},{6,5},{7,4},{8,11},{9,10},{10,... | collective-permute-start | bytes 233480 | tf_op jit(solution)/shard_map/ppermute | solution.py:396
  24.5 1.5 %collective-permute-start.7 = (f32[16,128]{1,0:T(8,128)S(1)}, f32[16,128]{1,0:T(8,128)S(1)}, u32[]{:S(2)}, u32[]{:S(2)}) collective-permute-start(f32[16,128]{1,0:T(8,128)S(1)} %get-tuple-element.76), channel_id=1, source_target_pairs={{0,2},{1,3},{2,0},{3,1},{4,6},{5,7},{6,4},{7,5},{8,10},{9,11},{10,... | collective-permute-start | bytes 24584 | tf_op jit(solution)/shard_map/ppermute | solution.py:391
  26.0 1.5 %collective-permute-start.9 = (f32[8,128]{1,0:T(8,128)S(1)}, f32[8,128]{1,0:T(8,128)S(1)}, u32[]{:S(2)}, u32[]{:S(2)}) collective-permute-start(f32[8,128]{1,0:T(8,128)S(1)} %get-tuple-element.80.refs_10_), channel_id=1, source_target_pairs={{0,24},{4,28},{8,16},{12,20},{16,8},{20,12},{24,0},{28,4},{1,25},{... | collective-permute-start | bytes 12296 | tf_op jit(solution)/shard_map/ppermute | solution.py:401
  27.5 3.0 %collective-permute-done.9.refs_11_ = f32[8,128]{1,0:T(8,128)S(1)} collective-permute-done((f32[8,128]{1,0:T(8,128)S(1)}, f32[8,128]{1,0:T(8,128)S(1)}, u32[]{:S(2)}, u32[]{:S(2)}) %collective-permute-start.9) | collective-permute-done | bytes 4128 | tf_op jit(solution)/shard_map/ppermute | solution.py:401
  31.5 1.6 %collective-permute-start.11 = (f32[136,128]{1,0:T(8,128)S(1)}, f32[136,128]{1,0:T(8,128)S(1)}, u32[]{:S(2)}, u32[]{:S(2)}) collective-permute-start(f32[136,128]{1,0:T(8,128)S(1)} %get-tuple-element.84.refs_3_), channel_id=1, source_target_pairs={{0,4},{4,0},{8,12},{12,8},{1,5},{5,1},{9,13},{13,9},{2,6},{6,2},{1... | collective-permute-start | bytes 208904 | tf_op jit(solution)/shard_map/ppermute | solution.py:396
  34.0 2.0 %collective-permute-done.12.refs_6_ = f32[144,128]{1,0:T(8,128)S(1)} collective-permute-done((f32[144,128]{1,0:T(8,128)S(1)}, f32[144,128]{1,0:T(8,128)S(1)}, u32[]{:S(2)}, u32[]{:S(2)}) %collective-permute-start.12) | collective-permute-done | bytes 73760 | tf_op jit(solution)/shard_map/ppermute | solution.py:396
  37.0 2.3 %collective-permute-start.13 = (f32[144,128]{1,0:T(8,128)S(1)}, f32[144,128]{1,0:T(8,128)S(1)}, u32[]{:S(2)}, u32[]{:S(2)}) collective-permute-start(f32[144,128]{1,0:T(8,128)S(1)} %get-tuple-element.89.refs_1_), channel_id=1, source_target_pairs={{0,3},{1,2},{2,1},{3,0},{4,7},{5,6},{6,5},{7,4},{8,11},{9,10},{10,... | collective-permute-start | bytes 221192 | tf_op jit(solution)/shard_map/ppermute | solution.py:396
  39.3 2.2 %collective-permute-start.14 = (f32[8,128]{1,0:T(8,128)S(1)}, f32[8,128]{1,0:T(8,128)S(1)}, u32[]{:S(2)}, u32[]{:S(2)}) collective-permute-start(f32[8,128]{1,0:T(8,128)S(1)} %get-tuple-element.91), channel_id=1, source_target_pairs={{0,2},{1,3},{2,0},{3,1},{4,6},{5,7},{6,4},{7,5},{8,10},{9,11},{10,... | collective-permute-start | bytes 12296 | tf_op jit(solution)/shard_map/ppermute | solution.py:391
  41.4 2.5 %collective-permute-done.14.refs_4_ = f32[8,128]{1,0:T(8,128)S(1)} collective-permute-done((f32[8,128]{1,0:T(8,128)S(1)}, f32[8,128]{1,0:T(8,128)S(1)}, u32[]{:S(2)}, u32[]{:S(2)}) %collective-permute-start.14) | collective-permute-done | bytes 4128 | tf_op jit(solution)/shard_map/ppermute | solution.py:391
  47.3 1.6 %collective-permute-start.19 = (f32[8,128]{1,0:T(8,128)S(1)}, f32[8,128]{1,0:T(8,128)S(1)}, u32[]{:S(2)}, u32[]{:S(2)}) collective-permute-start(f32[8,128]{1,0:T(8,128)S(1)} %get-tuple-element.96.refs_10_), channel_id=1, source_target_pairs={{0,24},{4,28},{8,16},{12,20},{16,8},{20,12},{24,0},{28,4},{1,25},{... | collective-permute-start | bytes 12296 | tf_op jit(solution)/shard_map/ppermute | solution.py:401
  48.9 2.9 %collective-permute-done.19.refs_11_ = f32[8,128]{1,0:T(8,128)S(1)} collective-permute-done((f32[8,128]{1,0:T(8,128)S(1)}, f32[8,128]{1,0:T(8,128)S(1)}, u32[]{:S(2)}, u32[]{:S(2)}) %collective-permute-start.19) | collective-permute-done | bytes 4128 | tf_op jit(solution)/shard_map/ppermute | solution.py:401
  51.8 1.3 %shard_map.65 = (f32[768,128]{1,0:T(8,128)S(1)}, f32[768,128]{1,0:T(8,128)S(1)}, f32[768,128]{1,0:T(8,128)S(1)}, f32[768,128]{1,0:T(8,128)S(1)}, f32[768,128]{1,...) custom-call(f32[256,128]{1,0:T(8,128)S(1)} %get-tuple-element.92.ref, ...), custom_call_target="tpu_custom_call" | custom-call | flops 603979776 | bytes 7417856 | tf_op jit(solution)/shard_map/pallas_call | solution.py:30
  53.2 1.8 %collective-permute-start.20 = (f32[152,128]{1,0:T(8,128)S(1)}, f32[152,128]{1,0:T(8,128)S(1)}, u32[]{:S(2)}, u32[]{:S(2)}) collective-permute-start(f32[152,128]{1,0:T(8,128)S(1)} %get-tuple-element.101.refs_1_), channel_id=1, source_target_pairs={{0,3},{1,2},{2,1},{3,0},{4,7},{5,6},{6,5},{7,4},{8,11},{9,10},{10,... | collective-permute-start | bytes 233480 | tf_op jit(solution)/shard_map/ppermute | solution.py:396
  55.2 2.4 %collective-permute-start.21 = (f32[16,128]{1,0:T(8,128)S(1)}, f32[16,128]{1,0:T(8,128)S(1)}, u32[]{:S(2)}, u32[]{:S(2)}) collective-permute-start(f32[16,128]{1,0:T(8,128)S(1)} %get-tuple-element.103), channel_id=1, source_target_pairs={{0,2},{1,3},{2,0},{3,1},{4,6},{5,7},{6,4},{7,5},{8,10},{9,11},{10,... | collective-permute-start | bytes 24584 | tf_op jit(solution)/shard_map/ppermute | solution.py:391
  57.6 2.1 %collective-permute-done.21.refs_4_ = f32[16,128]{1,0:T(8,128)S(1)} collective-permute-done((f32[16,128]{1,0:T(8,128)S(1)}, f32[16,128]{1,0:T(8,128)S(1)}, u32[]{:S(2)}, u32[]{:S(2)}) %collective-permute-start.21) | collective-permute-done | bytes 8224 | tf_op jit(solution)/shard_map/ppermute | solution.py:391
  61.0 1.9 %collective-permute-start.24 = (f32[136,128]{1,0:T(8,128)S(1)}, f32[136,128]{1,0:T(8,128)S(1)}, u32[]{:S(2)}, u32[]{:S(2)}) collective-permute-start(f32[136,128]{1,0:T(8,128)S(1)} %get-tuple-element.106.refs_3_), channel_id=1, source_target_pairs={{0,4},{4,0},{8,12},{12,8},{1,5},{5,1},{9,13},{13,9},{2,6},{6,2},{1... | collective-permute-start | bytes 208904 | tf_op jit(solution)/shard_map/ppermute | solution.py:396
  63.9 2.9 %collective-permute-done.26.refs_1_ = f32[8,128]{1,0:T(8,128)S(1)} collective-permute-done((f32[8,128]{1,0:T(8,128)S(1)}, f32[8,128]{1,0:T(8,128)S(1)}, u32[]{:S(2)}, u32[]{:S(2)}) %collective-permute-start.26) | collective-permute-done | bytes 4128 | tf_op jit(solution)/shard_map/ppermute | solution.py:401
  68.1 1.3 %shard_map.68 = (f32[128,768]{1,0:T(8,128)}, f32[128,768]{1,0:T(8,128)}) custom-call(f32[256,128]{1,0:T(8,128)S(1)} %get-tuple-element.104.refs_0_, f32[264,128]{1,0:T(8,128)S(1)} %get-tuple-element.105.refs_1_, f32[264,128]{1,0:T(8,128)S(1)} %collective-permute-done.23.refs_2_, f32[136,128]{1,0:T(8,128)S(1)} %get-tuple-element.106.refs_3_, ...), custom_call_target="tpu_custom_call" | custom-call | bytes 3846144 | tf_op jit(solution)/shard_map/pallas_call | solution.py:30
  (42 shorter events, 13.8 us)
Async XLA Ops:
  4.1 9.9 %collective-permute-start = (f32[168,128]{1,0:T(8,128)S(1)}, f32[168,128]{1,0:T(8,128)S(1)}, u32[]{:S(2)}, u32[]{:S(2)}) collective-permute-start(f32[168,128]{1,0:T(8,128)S(1)} %get-tuple-element.61.refs_1_), channel_id=1, source_target_pairs={{0,3},{1,2},{2,1},{3,0},{4,7},{5,6},{6,5},{7,4},{8,11},{9,10},{10,... | collective-permute-start | bytes 258056 | tf_op jit(solution)/shard_map/ppermute | solution.py:396
  9.2 4.8 %collective-permute-start.2 = (f32[160,128]{1,0:T(8,128)S(1)}, f32[160,128]{1,0:T(8,128)S(1)}, u32[]{:S(2)}, u32[]{:S(2)}) collective-permute-start(f32[160,128]{1,0:T(8,128)S(1)} %get-tuple-element.60.refs_0_), channel_id=1, source_target_pairs={{0,1},{1,0},{2,3},{3,2},{4,5},{5,4},{6,7},{7,6},{8,9},{9,8},{10,11... | collective-permute-start | bytes 245768 | tf_op jit(solution)/shard_map/ppermute | solution.py:396
  9.2 4.7 %collective-permute-start.1 = (f32[24,128]{1,0:T(8,128)S(1)}, f32[24,128]{1,0:T(8,128)S(1)}, u32[]{:S(2)}, u32[]{:S(2)}) collective-permute-start(f32[24,128]{1,0:T(8,128)S(1)} %get-tuple-element.63), channel_id=1, source_target_pairs={{0,2},{1,3},{2,0},{3,1},{4,6},{5,7},{6,4},{7,5},{8,10},{9,11},{10,... | collective-permute-start | bytes 36872 | tf_op jit(solution)/shard_map/ppermute | solution.py:391
  14.4 6.2 %collective-permute-start.3 = (f32[264,128]{1,0:T(8,128)S(1)}, f32[264,128]{1,0:T(8,128)S(1)}, u32[]{:S(2)}, u32[]{:S(2)}) collective-permute-start(f32[264,128]{1,0:T(8,128)S(1)} %get-tuple-element.67.refs_1_), channel_id=1, source_target_pairs={{0,16},{16,0},{1,17},{17,1},{2,18},{18,2},{3,19},{19,3},{4,20},{20... | collective-permute-start | bytes 405512 | tf_op jit(solution)/shard_map/ppermute | solution.py:396
  16.0 4.5 %collective-permute-start.5 = (f32[144,128]{1,0:T(8,128)S(1)}, f32[144,128]{1,0:T(8,128)S(1)}, u32[]{:S(2)}, u32[]{:S(2)}) collective-permute-start(f32[144,128]{1,0:T(8,128)S(1)} %get-tuple-element.69.refs_4_), channel_id=1, source_target_pairs={{0,12},{4,8},{8,4},{12,0},{1,13},{5,9},{9,5},{13,1},{2,14},{6,10},... | collective-permute-start | bytes 221192 | tf_op jit(solution)/shard_map/ppermute | solution.py:396
  21.6 9.0 %collective-permute-start.6 = (f32[152,128]{1,0:T(8,128)S(1)}, f32[152,128]{1,0:T(8,128)S(1)}, u32[]{:S(2)}, u32[]{:S(2)}) collective-permute-start(f32[152,128]{1,0:T(8,128)S(1)} %get-tuple-element.74.refs_1_), channel_id=1, source_target_pairs={{0,3},{1,2},{2,1},{3,0},{4,7},{5,6},{6,5},{7,4},{8,11},{9,10},{10,... | collective-permute-start | bytes 233480 | tf_op jit(solution)/shard_map/ppermute | solution.py:396
  23.8 6.7 %collective-permute-start.8 = (f32[144,128]{1,0:T(8,128)S(1)}, f32[144,128]{1,0:T(8,128)S(1)}, u32[]{:S(2)}, u32[]{:S(2)}) collective-permute-start(f32[144,128]{1,0:T(8,128)S(1)} %get-tuple-element.73.refs_0_), channel_id=1, source_target_pairs={{0,1},{1,0},{2,3},{3,2},{4,5},{5,4},{6,7},{7,6},{8,9},{9,8},{10,11... | collective-permute-start | bytes 221192 | tf_op jit(solution)/shard_map/ppermute | solution.py:396
  24.5 6.0 %collective-permute-start.7 = (f32[16,128]{1,0:T(8,128)S(1)}, f32[16,128]{1,0:T(8,128)S(1)}, u32[]{:S(2)}, u32[]{:S(2)}) collective-permute-start(f32[16,128]{1,0:T(8,128)S(1)} %get-tuple-element.76), channel_id=1, source_target_pairs={{0,2},{1,3},{2,0},{3,1},{4,6},{5,7},{6,4},{7,5},{8,10},{9,11},{10,... | collective-permute-start | bytes 24584 | tf_op jit(solution)/shard_map/ppermute | solution.py:391
  26.0 4.5 %collective-permute-start.9 = (f32[8,128]{1,0:T(8,128)S(1)}, f32[8,128]{1,0:T(8,128)S(1)}, u32[]{:S(2)}, u32[]{:S(2)}) collective-permute-start(f32[8,128]{1,0:T(8,128)S(1)} %get-tuple-element.80.refs_10_), channel_id=1, source_target_pairs={{0,24},{4,28},{8,16},{12,20},{16,8},{20,12},{24,0},{28,4},{1,25},{... | collective-permute-start | bytes 12296 | tf_op jit(solution)/shard_map/ppermute | solution.py:401
  30.9 5.1 %collective-permute-start.10 = (f32[264,128]{1,0:T(8,128)S(1)}, f32[264,128]{1,0:T(8,128)S(1)}, u32[]{:S(2)}, u32[]{:S(2)}) collective-permute-start(f32[264,128]{1,0:T(8,128)S(1)} %get-tuple-element.83.refs_1_), channel_id=1, source_target_pairs={{0,16},{16,0},{1,17},{17,1},{2,18},{18,2},{3,19},{19,3},{4,20},{20... | collective-permute-start | bytes 405512 | tf_op jit(solution)/shard_map/ppermute | solution.py:396
  31.5 4.5 %collective-permute-start.12 = (f32[144,128]{1,0:T(8,128)S(1)}, f32[144,128]{1,0:T(8,128)S(1)}, u32[]{:S(2)}, u32[]{:S(2)}) collective-permute-start(f32[144,128]{1,0:T(8,128)S(1)} %get-tuple-element.85.refs_4_), channel_id=1, source_target_pairs={{0,12},{4,8},{8,4},{12,0},{1,13},{5,9},{9,5},{13,1},{2,14},{6,10},... | collective-permute-start | bytes 221192 | tf_op jit(solution)/shard_map/ppermute | solution.py:396
  37.0 7.8 %collective-permute-start.13 = (f32[144,128]{1,0:T(8,128)S(1)}, f32[144,128]{1,0:T(8,128)S(1)}, u32[]{:S(2)}, u32[]{:S(2)}) collective-permute-start(f32[144,128]{1,0:T(8,128)S(1)} %get-tuple-element.89.refs_1_), channel_id=1, source_target_pairs={{0,3},{1,2},{2,1},{3,0},{4,7},{5,6},{6,5},{7,4},{8,11},{9,10},{10,... | collective-permute-start | bytes 221192 | tf_op jit(solution)/shard_map/ppermute | solution.py:396
  39.3 5.6 %collective-permute-start.15 = (f32[136,128]{1,0:T(8,128)S(1)}, f32[136,128]{1,0:T(8,128)S(1)}, u32[]{:S(2)}, u32[]{:S(2)}) collective-permute-start(f32[136,128]{1,0:T(8,128)S(1)} %get-tuple-element.88.refs_0_), channel_id=1, source_target_pairs={{0,1},{1,0},{2,3},{3,2},{4,5},{5,4},{6,7},{7,6},{8,9},{9,8},{10,11... | collective-permute-start | bytes 208904 | tf_op jit(solution)/shard_map/ppermute | solution.py:396
  39.3 4.7 %collective-permute-start.14 = (f32[8,128]{1,0:T(8,128)S(1)}, f32[8,128]{1,0:T(8,128)S(1)}, u32[]{:S(2)}, u32[]{:S(2)}) collective-permute-start(f32[8,128]{1,0:T(8,128)S(1)} %get-tuple-element.91), channel_id=1, source_target_pairs={{0,2},{1,3},{2,0},{3,1},{4,6},{5,7},{6,4},{7,5},{8,10},{9,11},{10,... | collective-permute-start | bytes 12296 | tf_op jit(solution)/shard_map/ppermute | solution.py:391
  45.2 6.6 %collective-permute-start.16 = (f32[256,128]{1,0:T(8,128)S(1)}, f32[256,128]{1,0:T(8,128)S(1)}, u32[]{:S(2)}, u32[]{:S(2)}) collective-permute-start(f32[256,128]{1,0:T(8,128)S(1)} %get-tuple-element.93.refs_1_), channel_id=1, source_target_pairs={{0,16},{16,0},{1,17},{17,1},{2,18},{18,2},{3,19},{19,3},{4,20},{20... | collective-permute-start | bytes 393224 | tf_op jit(solution)/shard_map/ppermute | solution.py:396
  45.6 6.2 %collective-permute-start.18 = (f32[136,128]{1,0:T(8,128)S(1)}, f32[136,128]{1,0:T(8,128)S(1)}, u32[]{:S(2)}, u32[]{:S(2)}) collective-permute-start(f32[136,128]{1,0:T(8,128)S(1)} %get-tuple-element.95.refs_4_), channel_id=1, source_target_pairs={{0,12},{4,8},{8,4},{12,0},{1,13},{5,9},{9,5},{13,1},{2,14},{6,10},... | collective-permute-start | bytes 208904 | tf_op jit(solution)/shard_map/ppermute | solution.py:396
  46.2 5.6 %collective-permute-start.17 = (f32[128,128]{1,0:T(8,128)S(1)}, f32[128,128]{1,0:T(8,128)S(1)}, u32[]{:S(2)}, u32[]{:S(2)}) collective-permute-start(f32[128,128]{1,0:T(8,128)S(1)} %get-tuple-element.94.refs_3_), channel_id=1, source_target_pairs={{0,4},{4,0},{8,12},{12,8},{1,5},{5,1},{9,13},{13,9},{2,6},{6,2},{1... | collective-permute-start | bytes 196616 | tf_op jit(solution)/shard_map/ppermute | solution.py:396
  47.3 4.5 %collective-permute-start.19 = (f32[8,128]{1,0:T(8,128)S(1)}, f32[8,128]{1,0:T(8,128)S(1)}, u32[]{:S(2)}, u32[]{:S(2)}) collective-permute-start(f32[8,128]{1,0:T(8,128)S(1)} %get-tuple-element.96.refs_10_), channel_id=1, source_target_pairs={{0,24},{4,28},{8,16},{12,20},{16,8},{20,12},{24,0},{28,4},{1,25},{... | collective-permute-start | bytes 12296 | tf_op jit(solution)/shard_map/ppermute | solution.py:401
  53.2 7.0 %collective-permute-start.20 = (f32[152,128]{1,0:T(8,128)S(1)}, f32[152,128]{1,0:T(8,128)S(1)}, u32[]{:S(2)}, u32[]{:S(2)}) collective-permute-start(f32[152,128]{1,0:T(8,128)S(1)} %get-tuple-element.101.refs_1_), channel_id=1, source_target_pairs={{0,3},{1,2},{2,1},{3,0},{4,7},{5,6},{6,5},{7,4},{8,11},{9,10},{10,... | collective-permute-start | bytes 233480 | tf_op jit(solution)/shard_map/ppermute | solution.py:396
  54.9 5.3 %collective-permute-start.22 = (f32[144,128]{1,0:T(8,128)S(1)}, f32[144,128]{1,0:T(8,128)S(1)}, u32[]{:S(2)}, u32[]{:S(2)}) collective-permute-start(f32[144,128]{1,0:T(8,128)S(1)} %get-tuple-element.100.refs_0_), channel_id=1, source_target_pairs={{0,1},{1,0},{2,3},{3,2},{4,5},{5,4},{6,7},{7,6},{8,9},{9,8},{10,11... | collective-permute-start | bytes 221192 | tf_op jit(solution)/shard_map/ppermute | solution.py:396
  55.2 4.6 %collective-permute-start.21 = (f32[16,128]{1,0:T(8,128)S(1)}, f32[16,128]{1,0:T(8,128)S(1)}, u32[]{:S(2)}, u32[]{:S(2)}) collective-permute-start(f32[16,128]{1,0:T(8,128)S(1)} %get-tuple-element.103), channel_id=1, source_target_pairs={{0,2},{1,3},{2,0},{3,1},{4,6},{5,7},{6,4},{7,5},{8,10},{9,11},{10,... | collective-permute-start | bytes 24584 | tf_op jit(solution)/shard_map/ppermute | solution.py:391
  60.6 6.2 %collective-permute-start.23 = (f32[264,128]{1,0:T(8,128)S(1)}, f32[264,128]{1,0:T(8,128)S(1)}, u32[]{:S(2)}, u32[]{:S(2)}) collective-permute-start(f32[264,128]{1,0:T(8,128)S(1)} %get-tuple-element.105.refs_1_), channel_id=1, source_target_pairs={{0,16},{16,0},{1,17},{17,1},{2,18},{18,2},{3,19},{19,3},{4,20},{20... | collective-permute-start | bytes 405512 | tf_op jit(solution)/shard_map/ppermute | solution.py:396
  61.0 5.8 %collective-permute-start.25 = (f32[144,128]{1,0:T(8,128)S(1)}, f32[144,128]{1,0:T(8,128)S(1)}, u32[]{:S(2)}, u32[]{:S(2)}) collective-permute-start(f32[144,128]{1,0:T(8,128)S(1)} %get-tuple-element.107.refs_4_), channel_id=1, source_target_pairs={{0,12},{4,8},{8,4},{12,0},{1,13},{5,9},{9,5},{13,1},{2,14},{6,10},... | collective-permute-start | bytes 221192 | tf_op jit(solution)/shard_map/ppermute | solution.py:396
  61.0 6.0 %collective-permute-start.24 = (f32[136,128]{1,0:T(8,128)S(1)}, f32[136,128]{1,0:T(8,128)S(1)}, u32[]{:S(2)}, u32[]{:S(2)}) collective-permute-start(f32[136,128]{1,0:T(8,128)S(1)} %get-tuple-element.106.refs_3_), channel_id=1, source_target_pairs={{0,4},{4,0},{8,12},{12,8},{1,5},{5,1},{9,13},{13,9},{2,6},{6,2},{1... | collective-permute-start | bytes 208904 | tf_op jit(solution)/shard_map/ppermute | solution.py:396
  (4 other events, 10.1 us)

commit v5 on v4

--- a/solution.py
+++ b/solution.py
@@ -90,13 +90,7 @@
     return places, signs
 
 
-def multiply(high, low, vec):
-    cols = vec.shape[1] // 2
-    both = dot16(high, vec) + dot16(low, vec)
-    return both[:, :cols] + both[:, cols:]
-
-
-def send_product(face, part, y, o):
+def store_product(face, part, y, o):
     if part < 2:
         o["y"][2 * part * face:2 * (part + 1) * face, :] = y
     else:
@@ -110,18 +104,18 @@
         o[name][start + at:start + at + n, :] = rows
 
 
-def product(face, vec, i, o, want_dot):
-    cols = vec.shape[1]
-    halves = jnp.concatenate(split(vec), axis=1)
-    total = None
+def product(face, vec, stack, o):
+    width, cols = vec.shape
+    both = dot16(stack[...], jnp.concatenate(split(vec), axis=1))
+    total = jnp.zeros((1, cols), F32)
     for part in range(3):
         at = slice(2 * part * face, 2 * (part + 1) * face)
-        y = multiply(i["s_high"][at, :], i["s_low"][at, :], halves)
-        send_product(face, part, y, o)
-        if want_dot:
-            dot = col_sum(vec[at] * y)
-            total = dot if total is None else total + dot
-    send_rows(face, dot32(i["modes"][...], vec), 0, o)
+        low = slice(width + 2 * part * face, width + 2 * (part + 1) * face)
+        y = (both[at, :cols] + both[at, cols:]) + (both[low, :cols] + both[low, cols:])
+        store_product(face, part, y, o)
+        total = total + col_sum(vec[at] * y)
+    loads = both[2 * width:, :cols] + both[2 * width:, cols:]
+    send_rows(face, (loads[0:PAD] + loads[PAD:2 * PAD]) + loads[2 * PAD:3 * PAD], 0, o)
     return total
 
 
@@ -131,7 +125,7 @@
 
 
 def first_kernel(face, nz, n_modes, turn, resid_hbm, schur_hbm, modes_hbm, coarse_hbm, *refs):
-    names = ["r0", "s_high", "s_low", "modes", "mt", "c_own", "y", "za", "zb", "z2"]
+    names = ["r0", "stack", "mt", "c_own", "y", "za", "zb", "z2"]
     o = dict(zip(names, refs[:len(names)]))
     resid, schur, mode_rows, coarse, sems = refs[len(names):]
     two = 2 * face
@@ -152,57 +146,51 @@
         jnp.concatenate([mode_rows[m, :, pl.ds(at, face)] for at in places], axis=1)
         for m in range(n_modes)], axis=0)
     modes = jnp.concatenate([modes, jnp.zeros((PAD - n_modes, modes.shape[1]), F32)], axis=0)
-    o["modes"][...] = modes
+    width = modes.shape[1]
     o["mt"][...] = mode_pieces(modes)
+    o["stack"][2 * width:, :] = jnp.concatenate(split3(modes) + (jnp.zeros(modes.shape, BF16),), axis=0)
 
     copies[1].wait()
     for f in range(6):
         o["r0"][f * face:(f + 1) * face, :] = signs[f] * resid[:, pl.ds(places[f], face)].T
     r0 = o["r0"][...]
     cols = r0.shape[1]
-    send_rows(face, dot32(modes, r0), 0, o)
 
     copies[2].wait()
     rows = jnp.concatenate([coarse[m] for m in range(n_modes)], axis=0)
     rows = jnp.concatenate([rows, jnp.zeros((PAD - n_modes, rows.shape[1]), F32)], axis=0)
-    wide = nz * PAD
+    wide = o["c_own"].shape[1]
     source = lax.broadcasted_iota(jnp.int32, (nz * n_modes, wide), 0)
     place = lax.broadcasted_iota(jnp.int32, (nz * n_modes, wide), 1)
     block, mode = place // PAD, place % PAD
 
-    def ordered(device):
-        pick = jnp.where((source == device * n_modes + mode) & (mode < n_modes), 1.0, 0.0)
-        return dot32(rows, pick)
-
-    def held_by(holder, side):
-        offset = jnp.where(block == 1, side, jnp.where(block == 2, -side, 2 * (block // 3)))
-        return ordered((holder + offset + 2 * nz) % nz)
-
     if turn:
         me = lax.axis_index("gz")
         side = 1 - 2 * lax.rem(me, 2)
-        o["c_own"][...] = held_by(me, side)
-        sent = (("za", me + side, -side, face + 3 * PAD), ("zb", me - side, -side, face + 3 * PAD), ("z2", me + 2, side, 2 * PAD))
-        for name, holder, holder_side, start in sent:
-            o[name][start:start + PAD, :] = jnp.zeros((PAD, cols), F32)
-            o[name][start:start + PAD, 0:wide] = held_by(holder, holder_side)
+        copy, block = block // nz, block % nz
+        holder = me + jnp.where(copy == 1, side, jnp.where(copy == 2, -side, 2 * (copy // 3)))
+        side = jnp.where((copy == 1) | (copy == 2), -side, side)
+        offset = jnp.where(block == 1, side, jnp.where(block == 2, -side, 2 * (block // 3)))
+        device = (holder + offset + 2 * nz) % nz
     else:
-        o["c_own"][...] = ordered(block)
+        device = block
+    pick = jnp.where((source == device * n_modes + mode) & (mode < n_modes), 1.0, 0.0)
+    ordered = dot32(rows, pick)
+    o["c_own"][...] = ordered
+    if turn:
+        for name, start in (("za", face + 3 * PAD), ("zb", face + 3 * PAD), ("z2", 2 * PAD)):
+            o[name][start:start + PAD, :] = ordered
     o["za"][face + 2 * PAD:face + 3 * PAD, :] = modes[:, 4 * face:5 * face]
     o["zb"][face + 2 * PAD:face + 3 * PAD, :] = modes[:, 5 * face:6 * face]
 
-    halves = jnp.concatenate(split(r0), axis=1)
-    curv = jnp.zeros((1, cols), F32)
     for part in range(3):
         at = slice(part * two, (part + 1) * two)
         copies[3 + 2 * part].wait()
         copies[4 + 2 * part].wait()
         high, low = split(jnp.concatenate([schur[at, pl.ds(start, face)] for start in places], axis=1))
-        o["s_high"][at, :] = high
-        o["s_low"][at, :] = low
-        y = multiply(high, low, halves)
-        send_product(face, part, y, o)
-        curv = curv + col_sum(r0[at] * y)
+        o["stack"][at, :] = high
+        o["stack"][width + part * two:width + (part + 1) * two, :] = low
+    curv = product(face, r0, o["stack"], o)
     send_rows(face, stack_rows([half_dot(r0, r0), curv], cols), PAD, o)
 
 
@@ -222,11 +210,11 @@
         if gathered:
             coarse = i["c_all"][...]
         else:
-            wide = i["c_own"].shape[1]
+            n = loads.shape[0]
             at = face + 3 * PAD
             coarse = jnp.concatenate([
-                i["c_own"][...], i["gza"][at:at + PAD, 0:wide], i["gzb"][at:at + PAD, 0:wide],
-                i["gz2"][2 * PAD:3 * PAD, 0:wide]], axis=0)
+                i["c_own"][:, 0:n], i["gza"][at:at + PAD, n:2 * n], i["gzb"][at:at + PAD, 2 * n:3 * n],
+                i["gz2"][2 * PAD:3 * PAD, 3 * n:4 * n]], axis=0)
             o["c_all"][...] = coarse
     else:
         mt_a, mt_b, coarse = i["mt_a"][...], i["mt_b"][...], i["c_all"][...]
@@ -251,12 +239,9 @@
         at = {0: 1, 1: 1, 3: 5}[stage]
         dots = jnp.concatenate([dots[0:at], row(dots, at) + quad, dots[at + 1:]], axis=0)
     if stage == 1:
-        sums = i["sum_near"][...] + i["sum_far"][...]
-        alpha0 = row(sums, 0) / row(sums, 1)
-        ratio = alpha0 / row(i["scale"], 0)
-        o["known"][...] = stack_rows([row(sums, 0), row(sums, 1), alpha0], cols)
-        dots = dots * (ratio * ratio)
-        xy, z_a, z_b = xy * ratio, z_a * ratio, z_b * ratio
+        dots = jnp.concatenate([i["first"][0:2, :], dots[0:2], dots[4:]], axis=0)
+    elif stage == 2 and "swapped" in i:
+        dots = six_columns(i, o)
     o["z"][0:face, :] = z_a
     o["z"][face:, :] = z_b
     o["xab"][0:2 * face, :] = xy[0:2 * face]
@@ -264,79 +249,96 @@
     o["yb"][0:face, :] = xy[3 * face:]
     if stage == 3:
         o["dots"][...] = dots
+    if stage != 2 or "swapped" in i:
+        o["xab"][2 * face:, :] = dots
     if stage != 2:
-        o["xab"][2 * face:, :] = dots
         o["ya"][face:face + PAD, :] = dots
         o["yb"][face:face + PAD, :] = dots
 
 
-def assemble(face, i):
+def assemble(face, i, rates=None):
     f = face
+    got = [i["gxab"][0:2 * f, :], i["gya"][0:f, :], i["gyb"][0:f, :]]
+    if rates is not None:
+        got = [rate * face_values for rate, face_values in zip(rates, got)]
     return jnp.concatenate([
-        i["xab"][0:2 * f, :] - i["gxab"][0:2 * f, :],
-        i["ya"][0:f, :] - i["gya"][0:f, :],
-        i["yb"][0:f, :] - i["gyb"][0:f, :],
-        i["z"][...],
+        i["xab"][0:2 * f, :] - got[0], i["ya"][0:f, :] - got[1], i["yb"][0:f, :] - got[2], i["z"][...],
     ], axis=0)
 
 
-def near_sum(face, i):
-    f = face
-    total = i["xab"][2 * f:2 * f + PAD, :] + i["gxab"][2 * f:2 * f + PAD, :]
-    return total + (i["gya"][f:f + PAD, :] + i["gyb"][f:f + PAD, :])
+def column_scale(dots):
+    norm, curv = row(dots, 0), row(dots, 1)
+    usable = (norm > 0.0) & (curv > 0.0)
+    return jnp.where(usable, norm / jnp.where(usable, curv, 1.0), 1.0)
+
+
+def rescale(dots, rate):
+    square = rate * rate
+    return stack_rows([row(dots, 0), row(dots, 1), square * row(dots, 2), square * row(dots, 3)], dots.shape[1])
 
 
 def second_kernel(face, i, o):
     w0 = assemble(face, i)
     o["w0"][...] = w0
-    own = i["xab"][2 * face:2 * face + PAD, :]
-    scale = row(own, 0) / row(own, 1)
+    first = i["xab"][2 * face:2 * face + PAD, :]
+    scale = column_scale(first)
     cols = w0.shape[1]
-    o["scale"][...] = stack_rows([scale], cols)
+    rates = [scale / column_scale(i[name][at:at + PAD, :])
+             for name, at in (("gxab", 2 * face), ("gya", face), ("gyb", face))]
+    o["first"][...] = stack_rows([row(first, 0), row(first, 1), scale] + rates, cols)
+    vec = scale * w0
+    curv = product(face, vec, i["stack"], o)
+    send_rows(face, stack_rows([half_dot(vec, vec), curv], cols), PAD, o)
+
+
+def third_kernel(face, i, o):
+    scale, *rates = (row(i["first"], k) for k in range(2, 6))
+    q = assemble(face, i, rates)
+    o["q"][...] = q
     if "near" in o:
-        o["near"][...] = near_sum(face, i)
-    vec = scale * w0
-    curv = product(face, vec, i, o, True)
-    send_rows(face, stack_rows([half_dot(vec, vec), curv], cols), PAD, o)
-
-
-def third_kernel(face, i, o):
-    q = assemble(face, i)
-    w1 = i["w0"][...] - q
-    o["q"][...] = q
-    o["w1"][...] = w1
-    if "near" in o:
-        o["near"][...] = near_sum(face, i)
-    product(face, row(i["known"], 2) * w1, i, o, False)
+        partners = [rescale(i[name][at:at + PAD, :], rate) for rate, name, at in zip(
+            rates, ("gxab", "gya", "gyb"), (2 * face, face, face))]
+        o["near"][...] = jnp.concatenate([partners[0], partners[2], partners[1] + i["xab"][2 * face:, :]], axis=0)
+    product(face, scale * q, i["stack"], o)
+
+
+def six_columns(i, o):
+    near = i["near"]
+    rate = row(i["first"], 4)
+    both = rescale(i["swapped"][0:PAD, :], rate), rescale(i["swapped"][PAD:2 * PAD, :], rate)
+    o["six"][...] = ((near[0:PAD, :] + near[PAD:2 * PAD, :]) + near[2 * PAD:, :]) + (both[0] + both[1])
+    return near[PAD:2 * PAD, :] + both[1]
 
 
 def fourth_kernel(face, i, o):
-    b = assemble(face, i)
-    m0, m1, alpha0 = (row(i["known"], k) for k in range(3))
-    sums = i["sum_near"][...] + i["sum_far"][...]
-    m2, m3 = row(sums, 0), row(sums, 1)
+    scale, *rates = (row(i["first"], k) for k in range(2, 6))
+    sums = i["six"][...]
+    if "whole" not in i:
+        sums = sums + rescale(i["gxab"][2 * face:, :], rates[0])
+    m0, m1 = row(sums, 0), row(sums, 1)
+    alpha0 = m0 / m1
+    ratio0 = alpha0 / scale
+    square = ratio0 * ratio0
+    m2, m3 = square * row(sums, 2), square * row(sums, 3)
     norm1 = m2 - m0
     curv1 = m1 - 2.0 * (m2 / alpha0) + m3
     beta1 = norm1 / m0
     alpha1 = norm1 / (curv1 - beta1 * norm1 / alpha0)
-    r0, w0, w1, q = i["r0"][...], i["w0"][...], i["w1"][...], i["q"][...]
-    ratio = alpha1 / alpha0
-    r1 = r0 - alpha0 * w0
-    p1 = r1 + beta1 * r0
+    r0, w0 = i["r0"][...], i["w0"][...]
+    q = ratio0 * i["q"][...]
+    b = q - square * assemble(face, i, [rate * rate for rate in rates])
+    w1 = w0 - q
     s1 = alpha1 * (w1 + beta1 * w0)
-    r2 = r1 - s1
-    z1 = ratio * (b + beta1 * q)
+    r2 = (r0 - alpha0 * w0) - s1
+    z1 = (alpha1 / alpha0) * (b + beta1 * q)
     w2 = w1 - z1
     vec = alpha1 * w2
     cols = w2.shape[1]
-    o["r2"][...] = r2
     o["w2"][...] = vec
-    o["p1"][...] = p1
     o["s1"][...] = s1
     o["z1"][...] = z1
-    o["m2"][...] = alpha0 * r0 + alpha1 * p1
-    o["known"][...] = stack_rows([norm1, alpha1], cols)
-    curv = product(face, vec, i, o, True)
+    o["known"][...] = stack_rows([norm1, alpha1, alpha0, beta1], cols)
+    curv = product(face, vec, i["stack"], o)
     send_rows(face, stack_rows([
         half_dot(r2, r2), half_dot(r2, w2), half_dot(vec, vec), half_dot(vec, s1),
         half_dot(s1, s1), curv, half_dot(z1, vec), half_dot(s1, z1)], cols), PAD, o)
@@ -350,7 +352,7 @@
 def last_kernel(face, i, o):
     d = i["sum_near"][...] + i["sum_far"][...]
     rr, rw, ww, ws, ss, wc, sc, sz = (row(d, k) for k in range(8))
-    norm1, alpha1 = row(i["known"], 0), row(i["known"], 1)
+    norm1, alpha1, alpha0, beta1 = (row(i["known"], k) for k in range(4))
     beta2 = rr / norm1
     alpha2 = rr / (rw - beta2 * rr / alpha1)
     ratio = alpha2 / alpha1
@@ -362,11 +364,15 @@
     alpha3 = norm3 / (curv3 - beta3 * norm3 / alpha2)
     c3 = assemble(face, i)
     w2, s1 = i["w2"][...], i["s1"][...]
-    p2 = i["r2"][...] + beta2 * i["p1"][...]
+    r0 = i["r0"][...]
+    r1 = r0 - alpha0 * i["w0"][...]
+    p1 = r1 + beta1 * r0
+    r2 = r1 - s1
+    p2 = r2 + beta2 * p1
     s2 = w2 + beta2 * s1
-    r3 = i["r2"][...] - ratio * s2
+    r3 = r2 - ratio * s2
     w3 = w2 / alpha1 - ratio * (c3 + beta2 * i["z1"][...])
-    mult = i["m2"][...] + alpha2 * p2 + alpha3 * (r3 + beta3 * p2)
+    mult = (alpha0 * r0 + alpha1 * p1) + alpha2 * p2 + alpha3 * (r3 + beta3 * p2)
     resid = r3 - alpha3 * (w3 + (beta3 / alpha1) * s2)
     places, signs = face_places(face)
     for f in range(6):
@@ -400,15 +406,15 @@
         pairs = [(a * ny + b, target(a, b)[0] * ny + target(a, b)[1]) for a, b in places]
         return lax.ppermute(x, ("gx", "gy"), pairs)
 
-    def far(x):
-        return move(x, lambda a, b: ((a + 1) % nx, (b + 2) % ny))
-
-    def total(x):
-        return dict(sum_near=lax.psum(x, ("gx", "gy")), sum_far=jnp.zeros_like(x))
+    def total(dots, scale):
+        rate = lax.pmin(scale, ("gx", "gy")) / scale
+        rates = jnp.concatenate([jnp.ones((2, loads), F32), rate * rate, rate * rate], axis=0)
+        sums = lax.psum(dots[0:4] * rates, ("gx", "gy")) / rates
+        return jnp.concatenate([sums, jnp.zeros((PAD - 4, loads), F32)], axis=0)
 
     vec = sds((width, loads))
     rows = sds((PAD, loads))
-    half = sds((width, width), BF16)
+    stack_shape = sds((2 * width + 4 * PAD, width), BF16)
     flops = 2 * width * width * 2 * loads * 2
 
     def z_out(extra):
@@ -428,14 +434,14 @@
 
     def value(stage, ins):
         extra = 0 if stage == 2 else PAD
-        outs = dict(z=sds((2 * face, loads)), xab=sds((2 * face + extra, loads)),
+        outs = dict(z=sds((2 * face, loads)), xab=sds((2 * face + (PAD if small else extra), loads)),
                     ya=sds((face + extra, loads)), yb=sds((face + extra + PAD, loads)))
         if stage == 0:
             outs.update(mt_a=sds((face, 6 * PAD), BF16), mt_b=sds((face, 6 * PAD), BF16))
             if small:
                 outs["c_all"] = sds((nz * PAD, nz * PAD))
-        if stage == 1:
-            outs["known"] = rows
+        if stage == 2 and small:
+            outs["six"] = rows
         if stage == 3:
             outs["dots"] = rows
         return call(functools.partial(value_kernel, face, stage), ins, outs, flops=2 * width * loads * 48)
@@ -456,12 +462,10 @@
     def xy_exchange(v):
         return dict(x_exchange(v), **y_exchange(v))
 
-    near = dict(near=rows) if small else {}
-
     hbm = pl.BlockSpec(memory_space=pltpu.HBM)
     vmem = pl.BlockSpec(memory_space=pltpu.VMEM)
-    outs = dict(r0=vec, s_high=half, s_low=half, modes=sds((PAD, width)), mt=sds((width, 6 * PAD), BF16),
-                c_own=sds((PAD, nz * PAD)), **z_out(3 * PAD))
+    outs = dict(r0=vec, stack=stack_shape, mt=sds((width, 6 * PAD), BF16),
+                c_own=sds((PAD, (4 if small else 1) * nz * PAD)), **z_out(3 * PAD))
     res = pl.pallas_call(
         functools.partial(first_kernel, face, nz, n_modes, small),
         out_shape=list(outs.values()),
@@ -476,8 +480,7 @@
         cost_estimate=pl.CostEstimate(flops=flops, bytes_accessed=4 * matrix.size, transcendentals=0),
     )(*[pltpu.with_memory_space_constraint(x, pltpu.HBM) for x in (resid, matrix, mode_rows, coarse_rows)])
     a = dict(zip(outs, res))
-    r0, mt = a["r0"], a["mt"]
-    fixed = dict(s_high=a["s_high"], s_low=a["s_low"], modes=a["modes"])
+    r0, mt, stack = a["r0"], a["mt"], a["stack"]
     ins = dict(z_exchange(a, True), mt=mt)
     if small:
         ins["c_own"] = a["c_own"]
@@ -490,29 +493,29 @@
     column = dict(mt=mt, mt_a=v["mt_a"], mt_b=v["mt_b"], c_all=v["c_all"] if small else ins["c_all"])
     x = xy_exchange(v)
 
-    a = call(functools.partial(second_kernel, face), dict(x, **fixed),
-             dict(w0=vec, scale=rows, **near, **z_out(PAD)), flops=flops)
-    w0 = a["w0"]
-    sums = dict(sum_near=a["near"], sum_far=far(a["near"])) if small else total(v["xab"][2 * face:])
-    v = value(1, dict(z_exchange(a, True), **column, **sums, scale=a["scale"]))
-    known = v["known"]
+    a = call(functools.partial(second_kernel, face), dict(x, stack=stack),
+             dict(w0=vec, first=rows, **z_out(PAD)), flops=flops)
+    w0, first = a["w0"], a["first"]
+    v = value(1, dict(z_exchange(a, True), **column, first=first))
     x = xy_exchange(v)
 
-    a = call(functools.partial(third_kernel, face), dict(x, **fixed, w0=w0, known=known),
-             dict(q=vec, w1=vec, **near, **z_out(0)), flops=flops)
-    if not small:
-        sums = total(v["xab"][2 * face:])
-    q, w1 = a["q"], a["w1"]
-    v = value(2, dict(z_exchange(a, False), **column))
-    x = x_exchange(v)
+    near = dict(near=sds((3 * PAD, loads))) if small else {}
+    a = call(functools.partial(third_kernel, face), dict(x, stack=stack, first=first),
+             dict(q=vec, **near, **z_out(0)), flops=flops)
+    q = a["q"]
+    ins = dict(z_exchange(a, False), **column)
     if small:
-        sums = dict(sum_near=a["near"], sum_far=far(a["near"]))
-    x.update(y_exchange(v))
-
-    names = ("r2", "w2", "p1", "s1", "z1", "m2")
+        ins.update(first=first, near=a["near"], swapped=swap(a["near"][0:2 * PAD], "gy", 0))
+        v = value(2, ins)
+        sums = dict(six=v["six"])
+    else:
+        sums = dict(six=total(v["xab"][2 * face:], first[2:3]), whole=first)
+        v = value(2, ins)
+    x = xy_exchange(v)
+
     a = call(functools.partial(fourth_kernel, face),
-             dict(x, **fixed, **sums, known=known, r0=r0, w0=w0, w1=w1, q=q),
-             dict({name: vec for name in names}, known=rows, **z_out(PAD)), flops=flops)
+             dict(x, stack=stack, **sums, first=first, r0=r0, w0=w0, q=q),
+             dict(w2=vec, s1=vec, z1=vec, known=rows, **z_out(PAD)), flops=flops)
     v = value(3, dict(z_exchange(a, True), **column))
     if small:
         x = x_exchange(v)
@@ -523,10 +526,10 @@
         sums = dict(sum_near=part, sum_far=swap(part, "gy", 0))
     else:
         x = xy_exchange(v)
-        sums = total(v["dots"])
+        sums = dict(sum_near=lax.psum(v["dots"], ("gx", "gy")), sum_far=jnp.zeros((PAD, loads), F32))
     out = sds((loads, width))
     res = call(functools.partial(last_kernel, face),
-               dict(x, **sums, known=a["known"], **{name: a[name] for name in names}),
+               dict(x, **sums, r0=r0, w0=w0, **{name: a[name] for name in ("known", "w2", "s1", "z1")}),
                dict(mult=out, resid=out))
     return (res["mult"][None, None, None], res["resid"][None, None, None])
 

time: 69.5 us -> 66 us (0.950)
  starting transfers between devices: 33.2 us -> 29.7 us
  Pallas kernels: 9.63 us -> 8.63 us
  waiting for transfers between devices: 25.8 us -> 26.8 us
    ppermute x3 -> x1, waiting for transfers between devices: 8.89 us -> 3.04 us  [move(): return lax.ppermute(x, ('gx', 'gy'), pairs)]
    ppermute x21 -> x22, waiting for transfers between devices: 8.24 us -> 11.9 us  [swap(): return lax.ppermute(x, axis, [(k, (k + side(k)) % n) for k in range(n)])]
    ppermute x4, waiting for transfers between devices: 8.68 us -> 11.9 us  [shift(): return lax.ppermute(x, axis, [(k, (k + by) % n) for k in range(n)])]
    ppermute x3 -> x1, starting transfers between devices: 4.05 us -> 0.9 us  [move(): return lax.ppermute(x, ('gx', 'gy'), pairs)]
    ppermute x21 -> x22, starting transfers between devices: 22.3 us -> 21.8 us  [swap(): return lax.ppermute(x, axis, [(k, (k + side(k)) % n) for k in range(n)])]
  transfers between devices with their start and end apart: 28 -> 27, of which waited for: 14 -> 16; matrix products, arithmetic and copies ran while one was open for 0% -> 0% of each run, Pallas kernels for 0% -> 0%
where the time goes in v5:
time: 66 us; the launch traced here: 65.9 us
  starting transfers between devices  29.7 us (45%)
  waiting for transfers between devices  26.8 us (41%)
  Pallas kernels  8.63 us (13%)
  between operations  0.72 us (1%)
    ppermute x22, starting transfers between devices, swap(): return lax.ppermute(x, axis, [(k, (k + side(k)) % n) for k in range(n)])  21.8 us
    ppermute x22, waiting for transfers between devices, swap(): return lax.ppermute(x, axis, [(k, (k + side(k)) % n) for k in range(n)])  11.9 us
    ppermute x4, waiting for transfers between devices, shift(): return lax.ppermute(x, axis, [(k, (k + by) % n) for k in range(n)])  11.9 us
    ppermute x4, starting transfers between devices, shift(): return lax.ppermute(x, axis, [(k, (k + by) % n) for k in range(n)])  7.01 us
    pallas_call x9, Pallas kernels, call(): pl.pallas_call(run, out_shape=[outs[n] for n in names_out], in_specs=[vme...  5.85 us
    ppermute x1, waiting for transfers between devices, move(): return lax.ppermute(x, ('gx', 'gy'), pairs)  3.04 us
    pallas_call x1, Pallas kernels, body(): pl.pallas_call(functools.partial(first_kernel, face, nz, n_modes, small),...  2.78 us
  transfers between devices with their start and end apart: 27, of which 16 were waited for; matrix products, arithmetic and copies ran while one was open for 0% of the time, Pallas kernels for 0%

profile of v5, /device:TPU:0, one launch (start us, length us, event | category | flops | bytes accessed | tf_op | source)
XLA Modules:
  0.0 65.9 jit_solution(18055186043510113960)
XLA Ops:
  0.6 2.8 %shard_map.59 = (f32[768,128]{1,0:T(8,128)S(1)}, bf16[1568,768]{1,0:T(8,128)(2,1)S(1)}, bf16[768,48]{1,0:T(8,128)(2,1)S(1)}, f32[8,128]{1,0:T(8,128)S(1)}, f32[5...) custom-call(f32[128,768]{1,0:T(8,128)} %bitcast.7, ...), custom_call_target="tpu_custom_call" | custom-call | flops 603979776 | bytes 2359296 | tf_op jit(solution)/shard_map/pallas_call | solution.py:469
  3.4 5.1 %collective-permute-start = (f32[168,128]{1,0:T(8,128)S(1)}, f32[168,128]{1,0:T(8,128)S(1)}, u32[]{:S(2)}, u32[]{:S(2)}) collective-permute-start(f32[168,128]{1,0:T(8,128)S(1)} %get-tuple-element.54.refs_1_), channel_id=1, source_target_pairs={{0,3},{1,2},{2,1},{3,0},{4,7},{5,6},{6,5},{7,4},{8,11},{9,10},{10,... | collective-permute-start | bytes 258056 | tf_op jit(solution)/shard_map/ppermute | solution.py:402
  9.2 4.1 %collective-permute-done.1.refs_4_ = f32[24,128]{1,0:T(8,128)S(1)} collective-permute-done((f32[24,128]{1,0:T(8,128)S(1)}, f32[24,128]{1,0:T(8,128)S(1)}, u32[]{:S(2)}, u32[]{:S(2)}) %collective-permute-start.1) | collective-permute-done | bytes 12320 | tf_op jit(solution)/shard_map/ppermute | solution.py:397
  13.8 1.7 %collective-permute-start.3 = (f32[264,128]{1,0:T(8,128)S(1)}, f32[264,128]{1,0:T(8,128)S(1)}, u32[]{:S(2)}, u32[]{:S(2)}) collective-permute-start(f32[264,128]{1,0:T(8,128)S(1)} %get-tuple-element.60.refs_1_), channel_id=1, source_target_pairs={{0,16},{16,0},{1,17},{17,1},{2,18},{18,2},{3,19},{19,3},{4,20},{20... | collective-permute-start | bytes 405512 | tf_op jit(solution)/shard_map/ppermute | solution.py:402
  15.6 1.5 %collective-permute-start.4 = (f32[136,128]{1,0:T(8,128)S(1)}, f32[136,128]{1,0:T(8,128)S(1)}, u32[]{:S(2)}, u32[]{:S(2)}) collective-permute-start(f32[136,128]{1,0:T(8,128)S(1)} %get-tuple-element.61.refs_3_), channel_id=1, source_target_pairs={{0,4},{4,0},{8,12},{12,8},{1,5},{5,1},{9,13},{13,9},{2,6},{6,2},{1... | collective-permute-start | bytes 208904 | tf_op jit(solution)/shard_map/ppermute | solution.py:402
  18.0 2.0 %collective-permute-done.5.refs_6_ = f32[144,128]{1,0:T(8,128)S(1)} collective-permute-done((f32[144,128]{1,0:T(8,128)S(1)}, f32[144,128]{1,0:T(8,128)S(1)}, u32[]{:S(2)}, u32[]{:S(2)}) %collective-permute-start.5) | collective-permute-done | bytes 73760 | tf_op jit(solution)/shard_map/ppermute | solution.py:402
  20.9 2.3 %collective-permute-start.6 = (f32[152,128]{1,0:T(8,128)S(1)}, f32[152,128]{1,0:T(8,128)S(1)}, u32[]{:S(2)}, u32[]{:S(2)}) collective-permute-start(f32[152,128]{1,0:T(8,128)S(1)} %get-tuple-element.65.refs_1_), channel_id=1, source_target_pairs={{0,3},{1,2},{2,1},{3,0},{4,7},{5,6},{6,5},{7,4},{8,11},{9,10},{10,... | collective-permute-start | bytes 233480 | tf_op jit(solution)/shard_map/ppermute | solution.py:402
  23.8 1.5 %collective-permute-start.7 = (f32[16,128]{1,0:T(8,128)S(1)}, f32[16,128]{1,0:T(8,128)S(1)}, u32[]{:S(2)}, u32[]{:S(2)}) collective-permute-start(f32[16,128]{1,0:T(8,128)S(1)} %get-tuple-element.67), channel_id=1, source_target_pairs={{0,2},{1,3},{2,0},{3,1},{4,6},{5,7},{6,4},{7,5},{8,10},{9,11},{10,... | collective-permute-start | bytes 24584 | tf_op jit(solution)/shard_map/ppermute | solution.py:397
  25.3 3.1 %collective-permute-done.7.refs_4_ = f32[16,128]{1,0:T(8,128)S(1)} collective-permute-done((f32[16,128]{1,0:T(8,128)S(1)}, f32[16,128]{1,0:T(8,128)S(1)}, u32[]{:S(2)}, u32[]{:S(2)}) %collective-permute-start.7) | collective-permute-done | bytes 8224 | tf_op jit(solution)/shard_map/ppermute | solution.py:397
  31.8 2.5 %collective-permute-done.11.refs_6_ = f32[144,128]{1,0:T(8,128)S(1)} collective-permute-done((f32[144,128]{1,0:T(8,128)S(1)}, f32[144,128]{1,0:T(8,128)S(1)}, u32[]{:S(2)}, u32[]{:S(2)}) %collective-permute-start.11) | collective-permute-done | bytes 73760 | tf_op jit(solution)/shard_map/ppermute | solution.py:402
  35.8 1.2 %collective-permute-start.12 = (f32[144,128]{1,0:T(8,128)S(1)}, f32[144,128]{1,0:T(8,128)S(1)}, u32[]{:S(2)}, u32[]{:S(2)}) collective-permute-start(f32[144,128]{1,0:T(8,128)S(1)} %get-tuple-element.77.refs_1_), channel_id=1, source_target_pairs={{0,3},{1,2},{2,1},{3,0},{4,7},{5,6},{6,5},{7,4},{8,11},{9,10},{10,... | collective-permute-start | bytes 221192 | tf_op jit(solution)/shard_map/ppermute | solution.py:402
  37.1 3.1 %collective-permute-start.13 = (f32[8,128]{1,0:T(8,128)S(1)}, f32[8,128]{1,0:T(8,128)S(1)}, u32[]{:S(2)}, u32[]{:S(2)}) collective-permute-start(f32[8,128]{1,0:T(8,128)S(1)} %get-tuple-element.79), channel_id=1, source_target_pairs={{0,2},{1,3},{2,0},{3,1},{4,6},{5,7},{6,4},{7,5},{8,10},{9,11},{10,... | collective-permute-start | bytes 12296 | tf_op jit(solution)/shard_map/ppermute | solution.py:397
  40.2 1.9 %collective-permute-done.13.refs_4_ = f32[8,128]{1,0:T(8,128)S(1)} collective-permute-done((f32[8,128]{1,0:T(8,128)S(1)}, f32[8,128]{1,0:T(8,128)S(1)}, u32[]{:S(2)}, u32[]{:S(2)}) %collective-permute-start.13) | collective-permute-done | bytes 4128 | tf_op jit(solution)/shard_map/ppermute | solution.py:397
  42.6 1.5 %collective-permute-start.16 = (f32[264,128]{1,0:T(8,128)S(1)}, f32[264,128]{1,0:T(8,128)S(1)}, u32[]{:S(2)}, u32[]{:S(2)}) collective-permute-start(f32[264,128]{1,0:T(8,128)S(1)} %get-tuple-element.82.refs_1_), channel_id=1, source_target_pairs={{0,16},{16,0},{1,17},{17,1},{2,18},{18,2},{3,19},{19,3},{4,20},{20... | collective-permute-start | bytes 405512 | tf_op jit(solution)/shard_map/ppermute | solution.py:402
  45.7 2.2 %collective-permute-done.18.refs_6_ = f32[136,128]{1,0:T(8,128)S(1)} collective-permute-done((f32[136,128]{1,0:T(8,128)S(1)}, f32[136,128]{1,0:T(8,128)S(1)}, u32[]{:S(2)}, u32[]{:S(2)}) %collective-permute-start.18) | collective-permute-done | bytes 69664 | tf_op jit(solution)/shard_map/ppermute | solution.py:402
  48.1 1.1 %shard_map.65 = (f32[768,128]{1,0:T(8,128)S(1)}, f32[768,128]{1,0:T(8,128)S(1)}, f32[768,128]{1,0:T(8,128)S(1)}, f32[8,128]{1,0:T(8,128)S(1)}, f32[512,128]{1,0:...) custom-call(f32[256,128]{1,0:T(8,128)S(1)} %get-tuple-element.81.refs_0_, ...), custom_call_target="tpu_custom_call" | custom-call | flops 603979776 | bytes 5873664 | tf_op jit(solution)/shard_map/pallas_call | solution.py:30
  49.3 1.7 %collective-permute-start.19 = (f32[152,128]{1,0:T(8,128)S(1)}, f32[152,128]{1,0:T(8,128)S(1)}, u32[]{:S(2)}, u32[]{:S(2)}) collective-permute-start(f32[152,128]{1,0:T(8,128)S(1)} %get-tuple-element.90.refs_1_), channel_id=1, source_target_pairs={{0,3},{1,2},{2,1},{3,0},{4,7},{5,6},{6,5},{7,4},{8,11},{9,10},{10,... | collective-permute-start | bytes 233480 | tf_op jit(solution)/shard_map/ppermute | solution.py:402
  52.0 1.7 %collective-permute-start.20 = (f32[16,128]{1,0:T(8,128)S(1)}, f32[16,128]{1,0:T(8,128)S(1)}, u32[]{:S(2)}, u32[]{:S(2)}) collective-permute-start(f32[16,128]{1,0:T(8,128)S(1)} %get-tuple-element.92), channel_id=1, source_target_pairs={{0,2},{1,3},{2,0},{3,1},{4,6},{5,7},{6,4},{7,5},{8,10},{9,11},{10,... | collective-permute-start | bytes 24584 | tf_op jit(solution)/shard_map/ppermute | solution.py:397
  53.7 2.8 %collective-permute-done.20.refs_4_ = f32[16,128]{1,0:T(8,128)S(1)} collective-permute-done((f32[16,128]{1,0:T(8,128)S(1)}, f32[16,128]{1,0:T(8,128)S(1)}, u32[]{:S(2)}, u32[]{:S(2)}) %collective-permute-start.20) | collective-permute-done | bytes 8224 | tf_op jit(solution)/shard_map/ppermute | solution.py:397
  56.9 1.1 %collective-permute-start.22 = (f32[264,128]{1,0:T(8,128)S(1)}, f32[264,128]{1,0:T(8,128)S(1)}, u32[]{:S(2)}, u32[]{:S(2)}) collective-permute-start(f32[264,128]{1,0:T(8,128)S(1)} %get-tuple-element.94.refs_1_), channel_id=1, source_target_pairs={{0,16},{16,0},{1,17},{17,1},{2,18},{18,2},{3,19},{19,3},{4,20},{20... | collective-permute-start | bytes 405512 | tf_op jit(solution)/shard_map/ppermute | solution.py:402
  58.2 1.1 %collective-permute-start.23 = (f32[136,128]{1,0:T(8,128)S(1)}, f32[136,128]{1,0:T(8,128)S(1)}, u32[]{:S(2)}, u32[]{:S(2)}) collective-permute-start(f32[136,128]{1,0:T(8,128)S(1)} %get-tuple-element.95.refs_3_), channel_id=1, source_target_pairs={{0,4},{4,0},{8,12},{12,8},{1,5},{5,1},{9,13},{13,9},{2,6},{6,2},{1... | collective-permute-start | bytes 208904 | tf_op jit(solution)/shard_map/ppermute | solution.py:402
  60.2 3.0 %collective-permute-done.25.refs_1_ = f32[8,128]{1,0:T(8,128)S(1)} collective-permute-done((f32[8,128]{1,0:T(8,128)S(1)}, f32[8,128]{1,0:T(8,128)S(1)}, u32[]{:S(2)}, u32[]{:S(2)}) %collective-permute-start.25) | collective-permute-done | bytes 4128 | tf_op jit(solution)/shard_map/ppermute | solution.py:407
  63.5 1.0 %collective-permute-done.26.refs_8_ = f32[8,128]{1,0:T(8,128)S(1)} collective-permute-done((f32[8,128]{1,0:T(8,128)S(1)}, f32[8,128]{1,0:T(8,128)S(1)}, u32[]{:S(2)}, u32[]{:S(2)}) %collective-permute-start.26) | collective-permute-done | bytes 4128 | tf_op jit(solution)/shard_map/ppermute | solution.py:402
  64.5 1.4 %shard_map.68 = (f32[128,768]{1,0:T(8,128)}, f32[128,768]{1,0:T(8,128)}) custom-call(f32[256,128]{1,0:T(8,128)S(1)} %get-tuple-element.93.refs_0_, f32[264,128]{1,0:T(8,128)S(1)} %get-tuple-element.94.refs_1_, f32[264,128]{1,0:T(8,128)S(1)} %collective-permute-done.22.refs_2_, f32[136,128]{1,0:T(8,128)S(1)} %get-tuple-element.95.refs_3_, ...), custom_call_target="tpu_custom_call" | custom-call | bytes 3452928 | tf_op jit(solution)/shard_map/pallas_call | solution.py:30
  (41 shorter events, 13.7 us)
Async XLA Ops:
  3.4 9.9 %collective-permute-start = (f32[168,128]{1,0:T(8,128)S(1)}, f32[168,128]{1,0:T(8,128)S(1)}, u32[]{:S(2)}, u32[]{:S(2)}) collective-permute-start(f32[168,128]{1,0:T(8,128)S(1)} %get-tuple-element.54.refs_1_), channel_id=1, source_target_pairs={{0,3},{1,2},{2,1},{3,0},{4,7},{5,6},{6,5},{7,4},{8,11},{9,10},{10,... | collective-permute-start | bytes 258056 | tf_op jit(solution)/shard_map/ppermute | solution.py:402
  8.5 4.8 %collective-permute-start.2 = (f32[160,128]{1,0:T(8,128)S(1)}, f32[160,128]{1,0:T(8,128)S(1)}, u32[]{:S(2)}, u32[]{:S(2)}) collective-permute-start(f32[160,128]{1,0:T(8,128)S(1)} %get-tuple-element.53.refs_0_), channel_id=1, source_target_pairs={{0,1},{1,0},{2,3},{3,2},{4,5},{5,4},{6,7},{7,6},{8,9},{9,8},{10,11... | collective-permute-start | bytes 245768 | tf_op jit(solution)/shard_map/ppermute | solution.py:402
  8.5 4.7 %collective-permute-start.1 = (f32[24,128]{1,0:T(8,128)S(1)}, f32[24,128]{1,0:T(8,128)S(1)}, u32[]{:S(2)}, u32[]{:S(2)}) collective-permute-start(f32[24,128]{1,0:T(8,128)S(1)} %get-tuple-element.56), channel_id=1, source_target_pairs={{0,2},{1,3},{2,0},{3,1},{4,6},{5,7},{6,4},{7,5},{8,10},{9,11},{10,... | collective-permute-start | bytes 36872 | tf_op jit(solution)/shard_map/ppermute | solution.py:397
  13.8 6.2 %collective-permute-start.3 = (f32[264,128]{1,0:T(8,128)S(1)}, f32[264,128]{1,0:T(8,128)S(1)}, u32[]{:S(2)}, u32[]{:S(2)}) collective-permute-start(f32[264,128]{1,0:T(8,128)S(1)} %get-tuple-element.60.refs_1_), channel_id=1, source_target_pairs={{0,16},{16,0},{1,17},{17,1},{2,18},{18,2},{3,19},{19,3},{4,20},{20... | collective-permute-start | bytes 405512 | tf_op jit(solution)/shard_map/ppermute | solution.py:402
  15.5 4.5 %collective-permute-start.5 = (f32[144,128]{1,0:T(8,128)S(1)}, f32[144,128]{1,0:T(8,128)S(1)}, u32[]{:S(2)}, u32[]{:S(2)}) collective-permute-start(f32[144,128]{1,0:T(8,128)S(1)} %get-tuple-element.62.refs_4_), channel_id=1, source_target_pairs={{0,12},{4,8},{8,4},{12,0},{1,13},{5,9},{9,5},{13,1},{2,14},{6,10},... | collective-permute-start | bytes 221192 | tf_op jit(solution)/shard_map/ppermute | solution.py:402
  15.6 2.4 %collective-permute-start.4 = (f32[136,128]{1,0:T(8,128)S(1)}, f32[136,128]{1,0:T(8,128)S(1)}, u32[]{:S(2)}, u32[]{:S(2)}) collective-permute-start(f32[136,128]{1,0:T(8,128)S(1)} %get-tuple-element.61.refs_3_), channel_id=1, source_target_pairs={{0,4},{4,0},{8,12},{12,8},{1,5},{5,1},{9,13},{13,9},{2,6},{6,2},{1... | collective-permute-start | bytes 208904 | tf_op jit(solution)/shard_map/ppermute | solution.py:402
  20.9 8.1 %collective-permute-start.6 = (f32[152,128]{1,0:T(8,128)S(1)}, f32[152,128]{1,0:T(8,128)S(1)}, u32[]{:S(2)}, u32[]{:S(2)}) collective-permute-start(f32[152,128]{1,0:T(8,128)S(1)} %get-tuple-element.65.refs_1_), channel_id=1, source_target_pairs={{0,3},{1,2},{2,1},{3,0},{4,7},{5,6},{6,5},{7,4},{8,11},{9,10},{10,... | collective-permute-start | bytes 233480 | tf_op jit(solution)/shard_map/ppermute | solution.py:402
  23.1 5.8 %collective-permute-start.8 = (f32[144,128]{1,0:T(8,128)S(1)}, f32[144,128]{1,0:T(8,128)S(1)}, u32[]{:S(2)}, u32[]{:S(2)}) collective-permute-start(f32[144,128]{1,0:T(8,128)S(1)} %get-tuple-element.64.refs_0_), channel_id=1, source_target_pairs={{0,1},{1,0},{2,3},{3,2},{4,5},{5,4},{6,7},{7,6},{8,9},{9,8},{10,11... | collective-permute-start | bytes 221192 | tf_op jit(solution)/shard_map/ppermute | solution.py:402
  23.8 4.6 %collective-permute-start.7 = (f32[16,128]{1,0:T(8,128)S(1)}, f32[16,128]{1,0:T(8,128)S(1)}, u32[]{:S(2)}, u32[]{:S(2)}) collective-permute-start(f32[16,128]{1,0:T(8,128)S(1)} %get-tuple-element.67), channel_id=1, source_target_pairs={{0,2},{1,3},{2,0},{3,1},{4,6},{5,7},{6,4},{7,5},{8,10},{9,11},{10,... | collective-permute-start | bytes 24584 | tf_op jit(solution)/shard_map/ppermute | solution.py:397
  29.4 5.6 %collective-permute-start.9 = (f32[264,128]{1,0:T(8,128)S(1)}, f32[264,128]{1,0:T(8,128)S(1)}, u32[]{:S(2)}, u32[]{:S(2)}) collective-permute-start(f32[264,128]{1,0:T(8,128)S(1)} %get-tuple-element.73.refs_1_), channel_id=1, source_target_pairs={{0,16},{16,0},{1,17},{17,1},{2,18},{18,2},{3,19},{19,3},{4,20},{20... | collective-permute-start | bytes 405512 | tf_op jit(solution)/shard_map/ppermute | solution.py:402
  29.9 4.4 %collective-permute-start.11 = (f32[144,128]{1,0:T(8,128)S(1)}, f32[144,128]{1,0:T(8,128)S(1)}, u32[]{:S(2)}, u32[]{:S(2)}) collective-permute-start(f32[144,128]{1,0:T(8,128)S(1)} %get-tuple-element.75.refs_4_), channel_id=1, source_target_pairs={{0,12},{4,8},{8,4},{12,0},{1,13},{5,9},{9,5},{13,1},{2,14},{6,10},... | collective-permute-start | bytes 221192 | tf_op jit(solution)/shard_map/ppermute | solution.py:402
  35.8 6.4 %collective-permute-start.12 = (f32[144,128]{1,0:T(8,128)S(1)}, f32[144,128]{1,0:T(8,128)S(1)}, u32[]{:S(2)}, u32[]{:S(2)}) collective-permute-start(f32[144,128]{1,0:T(8,128)S(1)} %get-tuple-element.77.refs_1_), channel_id=1, source_target_pairs={{0,3},{1,2},{2,1},{3,0},{4,7},{5,6},{6,5},{7,4},{8,11},{9,10},{10,... | collective-permute-start | bytes 221192 | tf_op jit(solution)/shard_map/ppermute | solution.py:402
  37.0 5.2 %collective-permute-start.14 = (f32[136,128]{1,0:T(8,128)S(1)}, f32[136,128]{1,0:T(8,128)S(1)}, u32[]{:S(2)}, u32[]{:S(2)}) collective-permute-start(f32[136,128]{1,0:T(8,128)S(1)} %get-tuple-element.76.refs_0_), channel_id=1, source_target_pairs={{0,1},{1,0},{2,3},{3,2},{4,5},{5,4},{6,7},{7,6},{8,9},{9,8},{10,11... | collective-permute-start | bytes 208904 | tf_op jit(solution)/shard_map/ppermute | solution.py:402
  37.1 5.1 %collective-permute-start.15 = (f32[16,128]{1,0:T(8,128)S(1)}, f32[16,128]{1,0:T(8,128)S(1)}, u32[]{:S(2)}, u32[]{:S(2)}) collective-permute-start(f32[16,128]{1,0:T(8,128)S(1)} %slice.3), channel_id=1, source_target_pairs={{0,4},{4,0},{8,12},{12,8},{1,5},{5,1},{9,13},{13,9},{2,6},{6,2},{1... | collective-permute-start | bytes 24584 | tf_op jit(solution)/shard_map/ppermute | solution.py:402
  37.1 5.1 %collective-permute-start.13 = (f32[8,128]{1,0:T(8,128)S(1)}, f32[8,128]{1,0:T(8,128)S(1)}, u32[]{:S(2)}, u32[]{:S(2)}) collective-permute-start(f32[8,128]{1,0:T(8,128)S(1)} %get-tuple-element.79), channel_id=1, source_target_pairs={{0,2},{1,3},{2,0},{3,1},{4,6},{5,7},{6,4},{7,5},{8,10},{9,11},{10,... | collective-permute-start | bytes 12296 | tf_op jit(solution)/shard_map/ppermute | solution.py:397
  42.6 5.6 %collective-permute-start.16 = (f32[264,128]{1,0:T(8,128)S(1)}, f32[264,128]{1,0:T(8,128)S(1)}, u32[]{:S(2)}, u32[]{:S(2)}) collective-permute-start(f32[264,128]{1,0:T(8,128)S(1)} %get-tuple-element.82.refs_1_), channel_id=1, source_target_pairs={{0,16},{16,0},{1,17},{17,1},{2,18},{18,2},{3,19},{19,3},{4,20},{20... | collective-permute-start | bytes 405512 | tf_op jit(solution)/shard_map/ppermute | solution.py:402
  44.1 3.7 %collective-permute-start.18 = (f32[136,128]{1,0:T(8,128)S(1)}, f32[136,128]{1,0:T(8,128)S(1)}, u32[]{:S(2)}, u32[]{:S(2)}) collective-permute-start(f32[136,128]{1,0:T(8,128)S(1)} %get-tuple-element.84.refs_4_), channel_id=1, source_target_pairs={{0,12},{4,8},{8,4},{12,0},{1,13},{5,9},{9,5},{13,1},{2,14},{6,10},... | collective-permute-start | bytes 208904 | tf_op jit(solution)/shard_map/ppermute | solution.py:402
  49.3 7.3 %collective-permute-start.19 = (f32[152,128]{1,0:T(8,128)S(1)}, f32[152,128]{1,0:T(8,128)S(1)}, u32[]{:S(2)}, u32[]{:S(2)}) collective-permute-start(f32[152,128]{1,0:T(8,128)S(1)} %get-tuple-element.90.refs_1_), channel_id=1, source_target_pairs={{0,3},{1,2},{2,1},{3,0},{4,7},{5,6},{6,5},{7,4},{8,11},{9,10},{10,... | collective-permute-start | bytes 233480 | tf_op jit(solution)/shard_map/ppermute | solution.py:402
  51.0 5.5 %collective-permute-start.21 = (f32[144,128]{1,0:T(8,128)S(1)}, f32[144,128]{1,0:T(8,128)S(1)}, u32[]{:S(2)}, u32[]{:S(2)}) collective-permute-start(f32[144,128]{1,0:T(8,128)S(1)} %get-tuple-element.89.refs_0_), channel_id=1, source_target_pairs={{0,1},{1,0},{2,3},{3,2},{4,5},{5,4},{6,7},{7,6},{8,9},{9,8},{10,11... | collective-permute-start | bytes 221192 | tf_op jit(solution)/shard_map/ppermute | solution.py:402
  52.0 4.5 %collective-permute-start.20 = (f32[16,128]{1,0:T(8,128)S(1)}, f32[16,128]{1,0:T(8,128)S(1)}, u32[]{:S(2)}, u32[]{:S(2)}) collective-permute-start(f32[16,128]{1,0:T(8,128)S(1)} %get-tuple-element.92), channel_id=1, source_target_pairs={{0,2},{1,3},{2,0},{3,1},{4,6},{5,7},{6,4},{7,5},{8,10},{9,11},{10,... | collective-permute-start | bytes 24584 | tf_op jit(solution)/shard_map/ppermute | solution.py:397
  56.9 6.3 %collective-permute-start.22 = (f32[264,128]{1,0:T(8,128)S(1)}, f32[264,128]{1,0:T(8,128)S(1)}, u32[]{:S(2)}, u32[]{:S(2)}) collective-permute-start(f32[264,128]{1,0:T(8,128)S(1)} %get-tuple-element.94.refs_1_), channel_id=1, source_target_pairs={{0,16},{16,0},{1,17},{17,1},{2,18},{18,2},{3,19},{19,3},{4,20},{20... | collective-permute-start | bytes 405512 | tf_op jit(solution)/shard_map/ppermute | solution.py:402
  58.0 5.2 %collective-permute-start.24 = (f32[144,128]{1,0:T(8,128)S(1)}, f32[144,128]{1,0:T(8,128)S(1)}, u32[]{:S(2)}, u32[]{:S(2)}) collective-permute-start(f32[144,128]{1,0:T(8,128)S(1)} %get-tuple-element.96.refs_4_), channel_id=1, source_target_pairs={{0,12},{4,8},{8,4},{12,0},{1,13},{5,9},{9,5},{13,1},{2,14},{6,10},... | collective-permute-start | bytes 221192 | tf_op jit(solution)/shard_map/ppermute | solution.py:402
  58.2 5.3 %collective-permute-start.23 = (f32[136,128]{1,0:T(8,128)S(1)}, f32[136,128]{1,0:T(8,128)S(1)}, u32[]{:S(2)}, u32[]{:S(2)}) collective-permute-start(f32[136,128]{1,0:T(8,128)S(1)} %get-tuple-element.95.refs_3_), channel_id=1, source_target_pairs={{0,4},{4,0},{8,12},{12,8},{1,5},{5,1},{9,13},{13,9},{2,6},{6,2},{1... | collective-permute-start | bytes 208904 | tf_op jit(solution)/shard_map/ppermute | solution.py:402
  59.3 3.9 %collective-permute-start.25 = (f32[8,128]{1,0:T(8,128)S(1)}, f32[8,128]{1,0:T(8,128)S(1)}, u32[]{:S(2)}, u32[]{:S(2)}) collective-permute-start(f32[8,128]{1,0:T(8,128)S(1)} %get-tuple-element.97.refs_0_), channel_id=1, source_target_pairs={{0,28},{4,24},{8,20},{12,16},{16,12},{20,8},{24,4},{28,0},{1,29},{... | collective-permute-start | bytes 12296 | tf_op jit(solution)/shard_map/ppermute | solution.py:407
  (3 other events, 4.7 us)

commit v6 on v5

--- a/solution.py
+++ b/solution.py
@@ -12,6 +12,7 @@
 HI = lax.Precision.HIGHEST
 PAD = 8
 VMEM_LIMIT = 24 * 1024 * 1024
+ROW_FLOPS = 5400000
 
 
 def sds(shape, dtype=F32):
@@ -197,6 +198,10 @@
 def column_rows(face, i, at):
     return [i["za"][face + at:face + at + PAD, :], i["gza"][face + at:face + at + PAD, :],
             i["gzb"][face + at:face + at + PAD, :], i["gz2"][at:at + PAD, :]]
+
+
+def copy_kernel(i, o):
+    o["z2"][...] = i["z2"][...]
 
 
 def value_kernel(face, stage, i, o):
@@ -424,7 +429,9 @@
     def z_exchange(a, with_dots):
         got = dict(za=a["za"], zb=a["zb"], y=a["y"], gzb=swap(a["zb"], "gz", 1))
         if small:
-            got["gz2"] = shift(a["z2"], "gz", 2)
+            rows_between = a["za"].shape[0] - a["z2"].shape[0] + PAD // 2
+            got["gz2"] = call(copy_kernel, dict(z2=shift(a["z2"], "gz", 2)), dict(z2=sds(a["z2"].shape)),
+                              flops=rows_between * ROW_FLOPS)["z2"]
         got["gza"] = swap(a["za"], "gz", 0)
         if not small:
             got["g_all"] = lax.all_gather(a["z2"][0:PAD], "gz", axis=0, tiled=True)

time: 66 us -> 67.4 us (1.021)
  waiting for transfers between devices: 26.8 us -> 27.8 us
    ppermute x22, starting transfers between devices: 21.8 us -> 29.1 us  [swap(): return lax.ppermute(x, axis, [(k, (k + side(k)) % n) for k in range(n)])]
    ppermute x4, starting transfers between devices: 7.01 us -> 0.01 us  [shift(): return lax.ppermute(x, axis, [(k, (k + by) % n) for k in range(n)])]
    ppermute x4, waiting for transfers between devices: 11.9 us -> 14.7 us  [shift(): return lax.ppermute(x, axis, [(k, (k + by) % n) for k in range(n)])]
    ppermute x22, waiting for transfers between devices: 11.9 us -> 10.2 us  [swap(): return lax.ppermute(x, axis, [(k, (k + side(k)) % n) for k in range(n)])]
    pallas_call x9 -> x13, Pallas kernels: 5.85 us -> 5.83 us  [call(): pl.pallas_call(run, out_shape=[outs[n] for n in names_out], in_specs=[vme...]
  transfers between devices with their start and end apart: 27 -> 27, of which waited for: 16 -> 14; matrix products, arithmetic and copies ran while one was open for 0% -> 0% of each run, Pallas kernels for 0% -> 0%
where the time goes in v6:
time: 67.4 us; the launch traced here: 67.2 us
  starting transfers between devices  30.1 us (45%)
  waiting for transfers between devices  27.8 us (41%)
  Pallas kernels  8.61 us (13%)
  between operations  0.73 us (1%)
    ppermute x22, starting transfers between devices, swap(): return lax.ppermute(x, axis, [(k, (k + side(k)) % n) for k in range(n)])  29.1 us
    ppermute x4, waiting for transfers between devices, shift(): return lax.ppermute(x, axis, [(k, (k + by) % n) for k in range(n)])  14.7 us
    ppermute x22, waiting for transfers between devices, swap(): return lax.ppermute(x, axis, [(k, (k + side(k)) % n) for k in range(n)])  10.2 us
    pallas_call x13, Pallas kernels, call(): pl.pallas_call(run, out_shape=[outs[n] for n in names_out], in_specs=[vme...  5.83 us
    ppermute x1, waiting for transfers between devices, move(): return lax.ppermute(x, ('gx', 'gy'), pairs)  2.96 us
    pallas_call x1, Pallas kernels, body(): pl.pallas_call(functools.partial(first_kernel, face, nz, n_modes, small),...  2.78 us
  transfers between devices with their start and end apart: 27, of which 14 were waited for; matrix products, arithmetic and copies ran while one was open for 0% of the time, Pallas kernels for 0%

profile of v6, /device:TPU:0, one launch (start us, length us, event | category | flops | bytes accessed | tf_op | source)
XLA Modules:
  0.0 67.2 jit_solution(9070265718756657522)
XLA Ops:
  0.6 2.8 %shard_map.59 = (f32[768,128]{1,0:T(8,128)S(1)}, bf16[1568,768]{1,0:T(8,128)(2,1)S(1)}, bf16[768,48]{1,0:T(8,128)(2,1)S(1)}, f32[8,128]{1,0:T(8,128)S(1)}, f32[5...) custom-call(f32[128,768]{1,0:T(8,128)} %bitcast.7, ...), custom_call_target="tpu_custom_call" | custom-call | flops 603979776 | bytes 2359296 | tf_op jit(solution)/shard_map/pallas_call | solution.py:476
  3.4 5.1 %collective-permute-start = (f32[168,128]{1,0:T(8,128)S(1)}, f32[168,128]{1,0:T(8,128)S(1)}, u32[]{:S(2)}, u32[]{:S(2)}) collective-permute-start(f32[168,128]{1,0:T(8,128)S(1)} %get-tuple-element.54.refs_1_), channel_id=1, source_target_pairs={{0,3},{1,2},{2,1},{3,0},{4,7},{5,6},{6,5},{7,4},{8,11},{9,10},{10,... | collective-permute-start | bytes 258056 | tf_op jit(solution)/shard_map/ppermute | solution.py:407
  9.2 4.1 %collective-permute-done.1.refs_0_ = f32[24,128]{1,0:T(8,128)S(1)} collective-permute-done((f32[24,128]{1,0:T(8,128)S(1)}, f32[24,128]{1,0:T(8,128)S(1)}, u32[]{:S(2)}, u32[]{:S(2)}) %collective-permute-start.1) | collective-permute-done | bytes 12320 | tf_op jit(solution)/shard_map/ppermute | solution.py:402
  13.7 1.6 %collective-permute-start.3 = (f32[264,128]{1,0:T(8,128)S(1)}, f32[264,128]{1,0:T(8,128)S(1)}, u32[]{:S(2)}, u32[]{:S(2)}) collective-permute-start(f32[264,128]{1,0:T(8,128)S(1)} %get-tuple-element.60.refs_1_), channel_id=1, source_target_pairs={{0,16},{16,0},{1,17},{17,1},{2,18},{18,2},{3,19},{19,3},{4,20},{20... | collective-permute-start | bytes 405512 | tf_op jit(solution)/shard_map/ppermute | solution.py:407
  15.4 1.5 %collective-permute-start.4 = (f32[136,128]{1,0:T(8,128)S(1)}, f32[136,128]{1,0:T(8,128)S(1)}, u32[]{:S(2)}, u32[]{:S(2)}) collective-permute-start(f32[136,128]{1,0:T(8,128)S(1)} %get-tuple-element.61.refs_3_), channel_id=1, source_target_pairs={{0,4},{4,0},{8,12},{12,8},{1,5},{5,1},{9,13},{13,9},{2,6},{6,2},{1... | collective-permute-start | bytes 208904 | tf_op jit(solution)/shard_map/ppermute | solution.py:407
  17.9 2.0 %collective-permute-done.5.refs_6_ = f32[144,128]{1,0:T(8,128)S(1)} collective-permute-done((f32[144,128]{1,0:T(8,128)S(1)}, f32[144,128]{1,0:T(8,128)S(1)}, u32[]{:S(2)}, u32[]{:S(2)}) %collective-permute-start.5) | collective-permute-done | bytes 73760 | tf_op jit(solution)/shard_map/ppermute | solution.py:407
  20.7 3.4 %collective-permute-start.6 = (f32[152,128]{1,0:T(8,128)S(1)}, f32[152,128]{1,0:T(8,128)S(1)}, u32[]{:S(2)}, u32[]{:S(2)}) collective-permute-start(f32[152,128]{1,0:T(8,128)S(1)} %get-tuple-element.65.refs_1_), channel_id=1, source_target_pairs={{0,3},{1,2},{2,1},{3,0},{4,7},{5,6},{6,5},{7,4},{8,11},{9,10},{10,... | collective-permute-start | bytes 233480 | tf_op jit(solution)/shard_map/ppermute | solution.py:407
  24.1 1.1 %collective-permute-start.8 = (f32[144,128]{1,0:T(8,128)S(1)}, f32[144,128]{1,0:T(8,128)S(1)}, u32[]{:S(2)}, u32[]{:S(2)}) collective-permute-start(f32[144,128]{1,0:T(8,128)S(1)} %get-tuple-element.64.refs_0_), channel_id=1, source_target_pairs={{0,1},{1,0},{2,3},{3,2},{4,5},{5,4},{6,7},{7,6},{8,9},{9,8},{10,11... | collective-permute-start | bytes 221192 | tf_op jit(solution)/shard_map/ppermute | solution.py:407
  25.2 3.6 %collective-permute-done.7.refs_0_ = f32[16,128]{1,0:T(8,128)S(1)} collective-permute-done((f32[16,128]{1,0:T(8,128)S(1)}, f32[16,128]{1,0:T(8,128)S(1)}, u32[]{:S(2)}, u32[]{:S(2)}) %collective-permute-start.7) | collective-permute-done | bytes 8224 | tf_op jit(solution)/shard_map/ppermute | solution.py:402
  29.9 1.6 %collective-permute-start.10 = (f32[136,128]{1,0:T(8,128)S(1)}, f32[136,128]{1,0:T(8,128)S(1)}, u32[]{:S(2)}, u32[]{:S(2)}) collective-permute-start(f32[136,128]{1,0:T(8,128)S(1)} %get-tuple-element.74.refs_3_), channel_id=1, source_target_pairs={{0,4},{4,0},{8,12},{12,8},{1,5},{5,1},{9,13},{13,9},{2,6},{6,2},{1... | collective-permute-start | bytes 208904 | tf_op jit(solution)/shard_map/ppermute | solution.py:407
  32.4 2.0 %collective-permute-done.11.refs_6_ = f32[144,128]{1,0:T(8,128)S(1)} collective-permute-done((f32[144,128]{1,0:T(8,128)S(1)}, f32[144,128]{1,0:T(8,128)S(1)}, u32[]{:S(2)}, u32[]{:S(2)}) %collective-permute-start.11) | collective-permute-done | bytes 73760 | tf_op jit(solution)/shard_map/ppermute | solution.py:407
  35.3 3.6 %collective-permute-start.12 = (f32[144,128]{1,0:T(8,128)S(1)}, f32[144,128]{1,0:T(8,128)S(1)}, u32[]{:S(2)}, u32[]{:S(2)}) collective-permute-start(f32[144,128]{1,0:T(8,128)S(1)} %get-tuple-element.77.refs_1_), channel_id=1, source_target_pairs={{0,3},{1,2},{2,1},{3,0},{4,7},{5,6},{6,5},{7,4},{8,11},{9,10},{10,... | collective-permute-start | bytes 221192 | tf_op jit(solution)/shard_map/ppermute | solution.py:407
  39.8 3.6 %collective-permute-done.13.refs_0_ = f32[8,128]{1,0:T(8,128)S(1)} collective-permute-done((f32[8,128]{1,0:T(8,128)S(1)}, f32[8,128]{1,0:T(8,128)S(1)}, u32[]{:S(2)}, u32[]{:S(2)}) %collective-permute-start.13) | collective-permute-done | bytes 4128 | tf_op jit(solution)/shard_map/ppermute | solution.py:402
  43.8 1.1 %collective-permute-start.16 = (f32[264,128]{1,0:T(8,128)S(1)}, f32[264,128]{1,0:T(8,128)S(1)}, u32[]{:S(2)}, u32[]{:S(2)}) collective-permute-start(f32[264,128]{1,0:T(8,128)S(1)} %get-tuple-element.82.refs_1_), channel_id=1, source_target_pairs={{0,16},{16,0},{1,17},{17,1},{2,18},{18,2},{3,19},{19,3},{4,20},{20... | collective-permute-start | bytes 405512 | tf_op jit(solution)/shard_map/ppermute | solution.py:407
  46.6 2.0 %collective-permute-done.18.refs_6_ = f32[136,128]{1,0:T(8,128)S(1)} collective-permute-done((f32[136,128]{1,0:T(8,128)S(1)}, f32[136,128]{1,0:T(8,128)S(1)}, u32[]{:S(2)}, u32[]{:S(2)}) %collective-permute-start.18) | collective-permute-done | bytes 69664 | tf_op jit(solution)/shard_map/ppermute | solution.py:407
  48.9 1.1 %shard_map.68 = (f32[768,128]{1,0:T(8,128)S(1)}, f32[768,128]{1,0:T(8,128)S(1)}, f32[768,128]{1,0:T(8,128)S(1)}, f32[8,128]{1,0:T(8,128)S(1)}, f32[512,128]{1,0:...) custom-call(f32[256,128]{1,0:T(8,128)S(1)} %get-tuple-element.81.refs_0_, ...), custom_call_target="tpu_custom_call" | custom-call | flops 603979776 | bytes 5873664 | tf_op jit(solution)/shard_map/pallas_call | solution.py:31
  50.0 3.3 %collective-permute-start.19 = (f32[152,128]{1,0:T(8,128)S(1)}, f32[152,128]{1,0:T(8,128)S(1)}, u32[]{:S(2)}, u32[]{:S(2)}) collective-permute-start(f32[152,128]{1,0:T(8,128)S(1)} %get-tuple-element.90.refs_1_), channel_id=1, source_target_pairs={{0,3},{1,2},{2,1},{3,0},{4,7},{5,6},{6,5},{7,4},{8,11},{9,10},{10,... | collective-permute-start | bytes 233480 | tf_op jit(solution)/shard_map/ppermute | solution.py:407
  53.3 1.2 %collective-permute-start.21 = (f32[144,128]{1,0:T(8,128)S(1)}, f32[144,128]{1,0:T(8,128)S(1)}, u32[]{:S(2)}, u32[]{:S(2)}) collective-permute-start(f32[144,128]{1,0:T(8,128)S(1)} %get-tuple-element.89.refs_0_), channel_id=1, source_target_pairs={{0,1},{1,0},{2,3},{3,2},{4,5},{5,4},{6,7},{7,6},{8,9},{9,8},{10,11... | collective-permute-start | bytes 221192 | tf_op jit(solution)/shard_map/ppermute | solution.py:407
  54.5 3.5 %collective-permute-done.20.refs_0_ = f32[16,128]{1,0:T(8,128)S(1)} collective-permute-done((f32[16,128]{1,0:T(8,128)S(1)}, f32[16,128]{1,0:T(8,128)S(1)}, u32[]{:S(2)}, u32[]{:S(2)}) %collective-permute-start.20) | collective-permute-done | bytes 8224 | tf_op jit(solution)/shard_map/ppermute | solution.py:402
  58.4 1.1 %collective-permute-start.22 = (f32[264,128]{1,0:T(8,128)S(1)}, f32[264,128]{1,0:T(8,128)S(1)}, u32[]{:S(2)}, u32[]{:S(2)}) collective-permute-start(f32[264,128]{1,0:T(8,128)S(1)} %get-tuple-element.94.refs_1_), channel_id=1, source_target_pairs={{0,16},{16,0},{1,17},{17,1},{2,18},{18,2},{3,19},{19,3},{4,20},{20... | collective-permute-start | bytes 405512 | tf_op jit(solution)/shard_map/ppermute | solution.py:407
  60.7 1.0 %collective-permute-start.25 = (f32[8,128]{1,0:T(8,128)S(1)}, f32[8,128]{1,0:T(8,128)S(1)}, u32[]{:S(2)}, u32[]{:S(2)}) collective-permute-start(f32[8,128]{1,0:T(8,128)S(1)} %get-tuple-element.97.refs_0_), channel_id=1, source_target_pairs={{0,28},{4,24},{8,20},{12,16},{16,12},{20,8},{24,4},{28,0},{1,29},{... | collective-permute-start | bytes 12296 | tf_op jit(solution)/shard_map/ppermute | solution.py:412
  61.6 3.0 %collective-permute-done.25.refs_1_ = f32[8,128]{1,0:T(8,128)S(1)} collective-permute-done((f32[8,128]{1,0:T(8,128)S(1)}, f32[8,128]{1,0:T(8,128)S(1)}, u32[]{:S(2)}, u32[]{:S(2)}) %collective-permute-start.25) | collective-permute-done | bytes 4128 | tf_op jit(solution)/shard_map/ppermute | solution.py:412
  64.8 1.0 %collective-permute-done.26.refs_8_ = f32[8,128]{1,0:T(8,128)S(1)} collective-permute-done((f32[8,128]{1,0:T(8,128)S(1)}, f32[8,128]{1,0:T(8,128)S(1)}, u32[]{:S(2)}, u32[]{:S(2)}) %collective-permute-start.26) | collective-permute-done | bytes 4128 | tf_op jit(solution)/shard_map/ppermute | solution.py:407
  65.8 1.4 %shard_map.72 = (f32[128,768]{1,0:T(8,128)}, f32[128,768]{1,0:T(8,128)}) custom-call(f32[256,128]{1,0:T(8,128)S(1)} %get-tuple-element.93.refs_0_, f32[264,128]{1,0:T(8,128)S(1)} %get-tuple-element.94.refs_1_, f32[264,128]{1,0:T(8,128)S(1)} %collective-permute-done.22.refs_2_, f32[136,128]{1,0:T(8,128)S(1)} %get-tuple-element.95.refs_3_, ...), custom_call_target="tpu_custom_call" | custom-call | bytes 3452928 | tf_op jit(solution)/shard_map/pallas_call | solution.py:31
  (45 shorter events, 11.1 us)
Async XLA Ops:
  3.4 9.8 %collective-permute-start = (f32[168,128]{1,0:T(8,128)S(1)}, f32[168,128]{1,0:T(8,128)S(1)}, u32[]{:S(2)}, u32[]{:S(2)}) collective-permute-start(f32[168,128]{1,0:T(8,128)S(1)} %get-tuple-element.54.refs_1_), channel_id=1, source_target_pairs={{0,3},{1,2},{2,1},{3,0},{4,7},{5,6},{6,5},{7,4},{8,11},{9,10},{10,... | collective-permute-start | bytes 258056 | tf_op jit(solution)/shard_map/ppermute | solution.py:407
  8.5 4.7 %collective-permute-start.1 = (f32[24,128]{1,0:T(8,128)S(1)}, f32[24,128]{1,0:T(8,128)S(1)}, u32[]{:S(2)}, u32[]{:S(2)}) collective-permute-start(f32[24,128]{1,0:T(8,128)S(1)} %get-tuple-element.56), channel_id=1, source_target_pairs={{0,2},{1,3},{2,0},{3,1},{4,6},{5,7},{6,4},{7,5},{8,10},{9,11},{10,... | collective-permute-start | bytes 36872 | tf_op jit(solution)/shard_map/ppermute | solution.py:402
  8.5 4.7 %collective-permute-start.2 = (f32[160,128]{1,0:T(8,128)S(1)}, f32[160,128]{1,0:T(8,128)S(1)}, u32[]{:S(2)}, u32[]{:S(2)}) collective-permute-start(f32[160,128]{1,0:T(8,128)S(1)} %get-tuple-element.53.refs_0_), channel_id=1, source_target_pairs={{0,1},{1,0},{2,3},{3,2},{4,5},{5,4},{6,7},{7,6},{8,9},{9,8},{10,11... | collective-permute-start | bytes 245768 | tf_op jit(solution)/shard_map/ppermute | solution.py:407
  13.7 6.2 %collective-permute-start.3 = (f32[264,128]{1,0:T(8,128)S(1)}, f32[264,128]{1,0:T(8,128)S(1)}, u32[]{:S(2)}, u32[]{:S(2)}) collective-permute-start(f32[264,128]{1,0:T(8,128)S(1)} %get-tuple-element.60.refs_1_), channel_id=1, source_target_pairs={{0,16},{16,0},{1,17},{17,1},{2,18},{18,2},{3,19},{19,3},{4,20},{20... | collective-permute-start | bytes 405512 | tf_op jit(solution)/shard_map/ppermute | solution.py:407
  15.3 4.5 %collective-permute-start.5 = (f32[144,128]{1,0:T(8,128)S(1)}, f32[144,128]{1,0:T(8,128)S(1)}, u32[]{:S(2)}, u32[]{:S(2)}) collective-permute-start(f32[144,128]{1,0:T(8,128)S(1)} %get-tuple-element.62.refs_4_), channel_id=1, source_target_pairs={{0,12},{4,8},{8,4},{12,0},{1,13},{5,9},{9,5},{13,1},{2,14},{6,10},... | collective-permute-start | bytes 221192 | tf_op jit(solution)/shard_map/ppermute | solution.py:407
  20.7 8.1 %collective-permute-start.6 = (f32[152,128]{1,0:T(8,128)S(1)}, f32[152,128]{1,0:T(8,128)S(1)}, u32[]{:S(2)}, u32[]{:S(2)}) collective-permute-start(f32[152,128]{1,0:T(8,128)S(1)} %get-tuple-element.65.refs_1_), channel_id=1, source_target_pairs={{0,3},{1,2},{2,1},{3,0},{4,7},{5,6},{6,5},{7,4},{8,11},{9,10},{10,... | collective-permute-start | bytes 233480 | tf_op jit(solution)/shard_map/ppermute | solution.py:407
  24.1 4.7 %collective-permute-start.7 = (f32[16,128]{1,0:T(8,128)S(1)}, f32[16,128]{1,0:T(8,128)S(1)}, u32[]{:S(2)}, u32[]{:S(2)}) collective-permute-start(f32[16,128]{1,0:T(8,128)S(1)} %get-tuple-element.67), channel_id=1, source_target_pairs={{0,2},{1,3},{2,0},{3,1},{4,6},{5,7},{6,4},{7,5},{8,10},{9,11},{10,... | collective-permute-start | bytes 24584 | tf_op jit(solution)/shard_map/ppermute | solution.py:402
  24.1 4.7 %collective-permute-start.8 = (f32[144,128]{1,0:T(8,128)S(1)}, f32[144,128]{1,0:T(8,128)S(1)}, u32[]{:S(2)}, u32[]{:S(2)}) collective-permute-start(f32[144,128]{1,0:T(8,128)S(1)} %get-tuple-element.64.refs_0_), channel_id=1, source_target_pairs={{0,1},{1,0},{2,3},{3,2},{4,5},{5,4},{6,7},{7,6},{8,9},{9,8},{10,11... | collective-permute-start | bytes 221192 | tf_op jit(solution)/shard_map/ppermute | solution.py:407
  29.2 5.2 %collective-permute-start.9 = (f32[264,128]{1,0:T(8,128)S(1)}, f32[264,128]{1,0:T(8,128)S(1)}, u32[]{:S(2)}, u32[]{:S(2)}) collective-permute-start(f32[264,128]{1,0:T(8,128)S(1)} %get-tuple-element.73.refs_1_), channel_id=1, source_target_pairs={{0,16},{16,0},{1,17},{17,1},{2,18},{18,2},{3,19},{19,3},{4,20},{20... | collective-permute-start | bytes 405512 | tf_op jit(solution)/shard_map/ppermute | solution.py:407
  29.9 4.5 %collective-permute-start.11 = (f32[144,128]{1,0:T(8,128)S(1)}, f32[144,128]{1,0:T(8,128)S(1)}, u32[]{:S(2)}, u32[]{:S(2)}) collective-permute-start(f32[144,128]{1,0:T(8,128)S(1)} %get-tuple-element.75.refs_4_), channel_id=1, source_target_pairs={{0,12},{4,8},{8,4},{12,0},{1,13},{5,9},{9,5},{13,1},{2,14},{6,10},... | collective-permute-start | bytes 221192 | tf_op jit(solution)/shard_map/ppermute | solution.py:407
  29.9 2.5 %collective-permute-start.10 = (f32[136,128]{1,0:T(8,128)S(1)}, f32[136,128]{1,0:T(8,128)S(1)}, u32[]{:S(2)}, u32[]{:S(2)}) collective-permute-start(f32[136,128]{1,0:T(8,128)S(1)} %get-tuple-element.74.refs_3_), channel_id=1, source_target_pairs={{0,4},{4,0},{8,12},{12,8},{1,5},{5,1},{9,13},{13,9},{2,6},{6,2},{1... | collective-permute-start | bytes 208904 | tf_op jit(solution)/shard_map/ppermute | solution.py:407
  35.3 8.1 %collective-permute-start.12 = (f32[144,128]{1,0:T(8,128)S(1)}, f32[144,128]{1,0:T(8,128)S(1)}, u32[]{:S(2)}, u32[]{:S(2)}) collective-permute-start(f32[144,128]{1,0:T(8,128)S(1)} %get-tuple-element.77.refs_1_), channel_id=1, source_target_pairs={{0,3},{1,2},{2,1},{3,0},{4,7},{5,6},{6,5},{7,4},{8,11},{9,10},{10,... | collective-permute-start | bytes 221192 | tf_op jit(solution)/shard_map/ppermute | solution.py:407
  38.9 4.5 %collective-permute-start.13 = (f32[8,128]{1,0:T(8,128)S(1)}, f32[8,128]{1,0:T(8,128)S(1)}, u32[]{:S(2)}, u32[]{:S(2)}) collective-permute-start(f32[8,128]{1,0:T(8,128)S(1)} %get-tuple-element.79), channel_id=1, source_target_pairs={{0,2},{1,3},{2,0},{3,1},{4,6},{5,7},{6,4},{7,5},{8,10},{9,11},{10,... | collective-permute-start | bytes 12296 | tf_op jit(solution)/shard_map/ppermute | solution.py:402
  38.9 4.5 %collective-permute-start.14 = (f32[136,128]{1,0:T(8,128)S(1)}, f32[136,128]{1,0:T(8,128)S(1)}, u32[]{:S(2)}, u32[]{:S(2)}) collective-permute-start(f32[136,128]{1,0:T(8,128)S(1)} %get-tuple-element.76.refs_0_), channel_id=1, source_target_pairs={{0,1},{1,0},{2,3},{3,2},{4,5},{5,4},{6,7},{7,6},{8,9},{9,8},{10,11... | collective-permute-start | bytes 208904 | tf_op jit(solution)/shard_map/ppermute | solution.py:407
  39.8 3.6 %collective-permute-start.15 = (f32[16,128]{1,0:T(8,128)S(1)}, f32[16,128]{1,0:T(8,128)S(1)}, u32[]{:S(2)}, u32[]{:S(2)}) collective-permute-start(f32[16,128]{1,0:T(8,128)S(1)} %slice.3), channel_id=1, source_target_pairs={{0,4},{4,0},{8,12},{12,8},{1,5},{5,1},{9,13},{13,9},{2,6},{6,2},{1... | collective-permute-start | bytes 24584 | tf_op jit(solution)/shard_map/ppermute | solution.py:407
  43.8 5.1 %collective-permute-start.16 = (f32[264,128]{1,0:T(8,128)S(1)}, f32[264,128]{1,0:T(8,128)S(1)}, u32[]{:S(2)}, u32[]{:S(2)}) collective-permute-start(f32[264,128]{1,0:T(8,128)S(1)} %get-tuple-element.82.refs_1_), channel_id=1, source_target_pairs={{0,16},{16,0},{1,17},{17,1},{2,18},{18,2},{3,19},{19,3},{4,20},{20... | collective-permute-start | bytes 405512 | tf_op jit(solution)/shard_map/ppermute | solution.py:407
  44.9 3.8 %collective-permute-start.18 = (f32[136,128]{1,0:T(8,128)S(1)}, f32[136,128]{1,0:T(8,128)S(1)}, u32[]{:S(2)}, u32[]{:S(2)}) collective-permute-start(f32[136,128]{1,0:T(8,128)S(1)} %get-tuple-element.84.refs_4_), channel_id=1, source_target_pairs={{0,12},{4,8},{8,4},{12,0},{1,13},{5,9},{9,5},{13,1},{2,14},{6,10},... | collective-permute-start | bytes 208904 | tf_op jit(solution)/shard_map/ppermute | solution.py:407
  50.0 8.0 %collective-permute-start.19 = (f32[152,128]{1,0:T(8,128)S(1)}, f32[152,128]{1,0:T(8,128)S(1)}, u32[]{:S(2)}, u32[]{:S(2)}) collective-permute-start(f32[152,128]{1,0:T(8,128)S(1)} %get-tuple-element.90.refs_1_), channel_id=1, source_target_pairs={{0,3},{1,2},{2,1},{3,0},{4,7},{5,6},{6,5},{7,4},{8,11},{9,10},{10,... | collective-permute-start | bytes 233480 | tf_op jit(solution)/shard_map/ppermute | solution.py:407
  53.3 4.7 %collective-permute-start.20 = (f32[16,128]{1,0:T(8,128)S(1)}, f32[16,128]{1,0:T(8,128)S(1)}, u32[]{:S(2)}, u32[]{:S(2)}) collective-permute-start(f32[16,128]{1,0:T(8,128)S(1)} %get-tuple-element.92), channel_id=1, source_target_pairs={{0,2},{1,3},{2,0},{3,1},{4,6},{5,7},{6,4},{7,5},{8,10},{9,11},{10,... | collective-permute-start | bytes 24584 | tf_op jit(solution)/shard_map/ppermute | solution.py:402
  53.3 4.7 %collective-permute-start.21 = (f32[144,128]{1,0:T(8,128)S(1)}, f32[144,128]{1,0:T(8,128)S(1)}, u32[]{:S(2)}, u32[]{:S(2)}) collective-permute-start(f32[144,128]{1,0:T(8,128)S(1)} %get-tuple-element.89.refs_0_), channel_id=1, source_target_pairs={{0,1},{1,0},{2,3},{3,2},{4,5},{5,4},{6,7},{7,6},{8,9},{9,8},{10,11... | collective-permute-start | bytes 221192 | tf_op jit(solution)/shard_map/ppermute | solution.py:407
  58.4 6.2 %collective-permute-start.22 = (f32[264,128]{1,0:T(8,128)S(1)}, f32[264,128]{1,0:T(8,128)S(1)}, u32[]{:S(2)}, u32[]{:S(2)}) collective-permute-start(f32[264,128]{1,0:T(8,128)S(1)} %get-tuple-element.94.refs_1_), channel_id=1, source_target_pairs={{0,16},{16,0},{1,17},{17,1},{2,18},{18,2},{3,19},{19,3},{4,20},{20... | collective-permute-start | bytes 405512 | tf_op jit(solution)/shard_map/ppermute | solution.py:407
  59.4 5.2 %collective-permute-start.24 = (f32[144,128]{1,0:T(8,128)S(1)}, f32[144,128]{1,0:T(8,128)S(1)}, u32[]{:S(2)}, u32[]{:S(2)}) collective-permute-start(f32[144,128]{1,0:T(8,128)S(1)} %get-tuple-element.96.refs_4_), channel_id=1, source_target_pairs={{0,12},{4,8},{8,4},{12,0},{1,13},{5,9},{9,5},{13,1},{2,14},{6,10},... | collective-permute-start | bytes 221192 | tf_op jit(solution)/shard_map/ppermute | solution.py:407
  59.9 4.9 %collective-permute-start.23 = (f32[136,128]{1,0:T(8,128)S(1)}, f32[136,128]{1,0:T(8,128)S(1)}, u32[]{:S(2)}, u32[]{:S(2)}) collective-permute-start(f32[136,128]{1,0:T(8,128)S(1)} %get-tuple-element.95.refs_3_), channel_id=1, source_target_pairs={{0,4},{4,0},{8,12},{12,8},{1,5},{5,1},{9,13},{13,9},{2,6},{6,2},{1... | collective-permute-start | bytes 208904 | tf_op jit(solution)/shard_map/ppermute | solution.py:407
  60.7 3.9 %collective-permute-start.25 = (f32[8,128]{1,0:T(8,128)S(1)}, f32[8,128]{1,0:T(8,128)S(1)}, u32[]{:S(2)}, u32[]{:S(2)}) collective-permute-start(f32[8,128]{1,0:T(8,128)S(1)} %get-tuple-element.97.refs_0_), channel_id=1, source_target_pairs={{0,28},{4,24},{8,20},{12,16},{16,12},{20,8},{24,4},{28,0},{1,29},{... | collective-permute-start | bytes 12296 | tf_op jit(solution)/shard_map/ppermute | solution.py:412
  (3 other events, 5.4 us)

commit v7 on v5

--- a/solution.py
+++ b/solution.py
@@ -12,6 +12,7 @@
 HI = lax.Precision.HIGHEST
 PAD = 8
 VMEM_LIMIT = 24 * 1024 * 1024
+Z_FLOPS = 770000000
 
 
 def sds(shape, dtype=F32):
@@ -96,12 +97,6 @@
     else:
         o["za"][0:face, :] = y[0:face]
         o["zb"][0:face, :] = y[face:]
-
-
-def send_rows(face, rows, at, o):
-    n = rows.shape[0]
-    for name, start in (("za", face), ("zb", face), ("z2", 0)):
-        o[name][start + at:start + at + n, :] = rows
 
 
 def product(face, vec, stack, o):
@@ -115,7 +110,7 @@
         store_product(face, part, y, o)
         total = total + col_sum(vec[at] * y)
     loads = both[2 * width:, :cols] + both[2 * width:, cols:]
-    send_rows(face, (loads[0:PAD] + loads[PAD:2 * PAD]) + loads[2 * PAD:3 * PAD], 0, o)
+    o["t"][0:PAD, :] = (loads[0:PAD] + loads[PAD:2 * PAD]) + loads[2 * PAD:3 * PAD]
     return total
 
 
@@ -125,7 +120,7 @@
 
 
 def first_kernel(face, nz, n_modes, turn, resid_hbm, schur_hbm, modes_hbm, coarse_hbm, *refs):
-    names = ["r0", "stack", "mt", "c_own", "y", "za", "zb", "z2"]
+    names = ["r0", "stack", "mt", "c_own", "y", "za", "zb", "t"]
     o = dict(zip(names, refs[:len(names)]))
     resid, schur, mode_rows, coarse, sems = refs[len(names):]
     two = 2 * face
@@ -178,10 +173,9 @@
     ordered = dot32(rows, pick)
     o["c_own"][...] = ordered
     if turn:
-        for name, start in (("za", face + 3 * PAD), ("zb", face + 3 * PAD), ("z2", 2 * PAD)):
-            o[name][start:start + PAD, :] = ordered
-    o["za"][face + 2 * PAD:face + 3 * PAD, :] = modes[:, 4 * face:5 * face]
-    o["zb"][face + 2 * PAD:face + 3 * PAD, :] = modes[:, 5 * face:6 * face]
+        o["t"][2 * PAD:3 * PAD, :] = ordered
+    o["za"][face:face + PAD, :] = modes[:, 4 * face:5 * face]
+    o["zb"][face:face + PAD, :] = modes[:, 5 * face:6 * face]
 
     for part in range(3):
         at = slice(part * two, (part + 1) * two)
@@ -191,41 +185,40 @@
         o["stack"][at, :] = high
         o["stack"][width + part * two:width + (part + 1) * two, :] = low
     curv = product(face, r0, o["stack"], o)
-    send_rows(face, stack_rows([half_dot(r0, r0), curv], cols), PAD, o)
-
-
-def column_rows(face, i, at):
-    return [i["za"][face + at:face + at + PAD, :], i["gza"][face + at:face + at + PAD, :],
-            i["gzb"][face + at:face + at + PAD, :], i["gz2"][at:at + PAD, :]]
+    o["t"][PAD:2 * PAD, :] = stack_rows([half_dot(r0, r0), curv], cols)
+
+
+def column_rows(i, at):
+    return [i[name][at:at + PAD, :] for name in ("t", "gta", "gtb", "gt2")]
+
+
+def z_kernel(face, i, o):
+    for k, name in enumerate(("a", "b")):
+        if "mt_" + name in o:
+            got_modes = mode_pieces(i["gz" + name][face:face + PAD, :])
+            o["mt_" + name][...] = got_modes
+        else:
+            got_modes = i["mt_" + name][...]
+        amp = i["amp"]
+        own = i["z" + name][0:face, :] + dot16(i["mt"][(4 + k) * face:(5 + k) * face, :], amp_pieces(amp[0:PAD, :]))
+        at = (1 + k) * PAD
+        got = i["gz" + name][0:face, :] + dot16(got_modes, amp_pieces(amp[at:at + PAD, :]))
+        o["z"][k * face:(k + 1) * face, :] = own - got
 
 
 def value_kernel(face, stage, i, o):
     gathered = "g_all" in i
-    loads = i["g_all"][...] if gathered else jnp.concatenate(column_rows(face, i, 0), axis=0)
-    if stage == 0:
-        mt_a = mode_pieces(i["gza"][face + 2 * PAD:face + 3 * PAD, :])
-        mt_b = mode_pieces(i["gzb"][face + 2 * PAD:face + 3 * PAD, :])
-        o["mt_a"][...] = mt_a
-        o["mt_b"][...] = mt_b
-        if gathered:
-            coarse = i["c_all"][...]
-        else:
-            n = loads.shape[0]
-            at = face + 3 * PAD
-            coarse = jnp.concatenate([
-                i["c_own"][:, 0:n], i["gza"][at:at + PAD, n:2 * n], i["gzb"][at:at + PAD, 2 * n:3 * n],
-                i["gz2"][2 * PAD:3 * PAD, 3 * n:4 * n]], axis=0)
-            o["c_all"][...] = coarse
+    loads = i["g_all"][...] if gathered else jnp.concatenate(column_rows(i, 0), axis=0)
+    if stage == 0 and not gathered:
+        n = loads.shape[0]
+        coarse = jnp.concatenate([part[:, k * n:(k + 1) * n] for k, part in enumerate(
+            [i["c_own"][...]] + column_rows(i, 2 * PAD)[1:])], axis=0)
+        o["c_all"][...] = coarse
     else:
-        mt_a, mt_b, coarse = i["mt_a"][...], i["mt_b"][...], i["c_all"][...]
+        coarse = i["c_all"][...]
     amp = dot32(coarse, loads)
-    own = amp_pieces(amp[0:PAD])
-    mt = i["mt"]
-    xy = i["y"][...] + dot16(mt[0:4 * face, :], own)
-    z_a = i["za"][0:face, :] + dot16(mt[4 * face:5 * face, :], own)
-    z_a = z_a - (i["gza"][0:face, :] + dot16(mt_a, amp_pieces(amp[PAD:2 * PAD])))
-    z_b = i["zb"][0:face, :] + dot16(mt[5 * face:6 * face, :], own)
-    z_b = z_b - (i["gzb"][0:face, :] + dot16(mt_b, amp_pieces(amp[2 * PAD:3 * PAD])))
+    o["amp"][...] = amp[0:3 * PAD]
+    xy = i["y"][...] + dot16(i["mt"][0:4 * face, :], amp_pieces(amp[0:PAD]))
     cols = loads.shape[1]
 
     if stage != 2:
@@ -233,7 +226,7 @@
             dots = i["d_all"][...]
             quad = col_sum(loads * amp[3 * PAD:])
         else:
-            parts = column_rows(face, i, PAD)
+            parts = column_rows(i, PAD)
             dots = (parts[0] + parts[1]) + (parts[2] + parts[3])
             quad = col_sum(loads * amp)
         at = {0: 1, 1: 1, 3: 5}[stage]
@@ -242,8 +235,6 @@
         dots = jnp.concatenate([i["first"][0:2, :], dots[0:2], dots[4:]], axis=0)
     elif stage == 2 and "swapped" in i:
         dots = six_columns(i, o)
-    o["z"][0:face, :] = z_a
-    o["z"][face:, :] = z_b
     o["xab"][0:2 * face, :] = xy[0:2 * face]
     o["ya"][0:face, :] = xy[2 * face:3 * face]
     o["yb"][0:face, :] = xy[3 * face:]
@@ -288,7 +279,7 @@
     o["first"][...] = stack_rows([row(first, 0), row(first, 1), scale] + rates, cols)
     vec = scale * w0
     curv = product(face, vec, i["stack"], o)
-    send_rows(face, stack_rows([half_dot(vec, vec), curv], cols), PAD, o)
+    o["t"][PAD:, :] = stack_rows([half_dot(vec, vec), curv], cols)
 
 
 def third_kernel(face, i, o):
@@ -339,9 +330,9 @@
     o["z1"][...] = z1
     o["known"][...] = stack_rows([norm1, alpha1, alpha0, beta1], cols)
     curv = product(face, vec, i["stack"], o)
-    send_rows(face, stack_rows([
+    o["t"][PAD:, :] = stack_rows([
         half_dot(r2, r2), half_dot(r2, w2), half_dot(vec, vec), half_dot(vec, s1),
-        half_dot(s1, s1), curv, half_dot(z1, vec), half_dot(s1, z1)], cols), PAD, o)
+        half_dot(s1, s1), curv, half_dot(z1, vec), half_dot(s1, z1)], cols)
 
 
 def four_kernel(face, i, o):
@@ -417,29 +408,35 @@
     stack_shape = sds((2 * width + 4 * PAD, width), BF16)
     flops = 2 * width * width * 2 * loads * 2
 
-    def z_out(extra):
-        return dict(y=sds((4 * face, loads)), za=sds((face + PAD + extra, loads)),
-                    zb=sds((face + PAD + extra + PAD, loads)), z2=sds((PAD + min(extra, 2 * PAD), loads)))
-
-    def z_exchange(a, with_dots):
-        got = dict(za=a["za"], zb=a["zb"], y=a["y"], gzb=swap(a["zb"], "gz", 1))
+    def z_out(tiny, extra=0):
+        return dict(y=sds((4 * face, loads)), za=sds((face + extra, loads)),
+                    zb=sds((face + extra, loads)), t=sds((tiny * PAD, loads)))
+
+    def t_exchange(a, with_dots):
+        got = dict(t=a["t"], y=a["y"])
         if small:
-            got["gz2"] = shift(a["z2"], "gz", 2)
-        got["gza"] = swap(a["za"], "gz", 0)
-        if not small:
-            got["g_all"] = lax.all_gather(a["z2"][0:PAD], "gz", axis=0, tiled=True)
+            got.update(gtb=swap(a["t"], "gz", 1), gt2=shift(a["t"], "gz", 2), gta=swap(a["t"], "gz", 0))
+        else:
+            got["g_all"] = lax.all_gather(a["t"][0:PAD], "gz", axis=0, tiled=True)
             if with_dots:
-                got["d_all"] = lax.psum(a["z2"][PAD:2 * PAD], "gz")
+                got["d_all"] = lax.psum(a["t"][PAD:2 * PAD], "gz")
         return got
+
+    def z_faces(a, v, modes=None):
+        ins = dict(za=a["za"], zb=a["zb"], gzb=swap(a["zb"], "gz", 1), gza=swap(a["za"], "gz", 0), mt=mt, amp=v["amp"])
+        outs = dict(z=sds((2 * face, loads)))
+        if modes is None:
+            outs.update(mt_a=sds((face, 6 * PAD), BF16), mt_b=sds((face, 6 * PAD), BF16))
+        else:
+            ins.update(modes)
+        return call(functools.partial(z_kernel, face), ins, outs, flops=Z_FLOPS)
 
     def value(stage, ins):
         extra = 0 if stage == 2 else PAD
-        outs = dict(z=sds((2 * face, loads)), xab=sds((2 * face + (PAD if small else extra), loads)),
+        outs = dict(amp=sds((3 * PAD, loads)), xab=sds((2 * face + (PAD if small else extra), loads)),
                     ya=sds((face + extra, loads)), yb=sds((face + extra + PAD, loads)))
-        if stage == 0:
-            outs.update(mt_a=sds((face, 6 * PAD), BF16), mt_b=sds((face, 6 * PAD), BF16))
-            if small:
-                outs["c_all"] = sds((nz * PAD, nz * PAD))
+        if stage == 0 and small:
+            outs["c_all"] = sds((nz * PAD, nz * PAD))
         if stage == 2 and small:
             outs["six"] = rows
         if stage == 3:
@@ -447,7 +444,7 @@
         return call(functools.partial(value_kernel, face, stage), ins, outs, flops=2 * width * loads * 48)
 
     def x_exchange(v):
-        got = dict(z=v["z"], xab=v["xab"])
+        got = dict(xab=v["xab"])
         if nx == 2:
             got["gxab"] = swap(v["xab"], "gx", 0)
         else:
@@ -465,7 +462,7 @@
     hbm = pl.BlockSpec(memory_space=pltpu.HBM)
     vmem = pl.BlockSpec(memory_space=pltpu.VMEM)
     outs = dict(r0=vec, stack=stack_shape, mt=sds((width, 6 * PAD), BF16),
-                c_own=sds((PAD, (4 if small else 1) * nz * PAD)), **z_out(3 * PAD))
+                c_own=sds((PAD, (4 if small else 1) * nz * PAD)), **z_out(3, PAD))
     res = pl.pallas_call(
         functools.partial(first_kernel, face, nz, n_modes, small),
         out_shape=list(outs.values()),
@@ -481,7 +478,7 @@
     )(*[pltpu.with_memory_space_constraint(x, pltpu.HBM) for x in (resid, matrix, mode_rows, coarse_rows)])
     a = dict(zip(outs, res))
     r0, mt, stack = a["r0"], a["mt"], a["stack"]
-    ins = dict(z_exchange(a, True), mt=mt)
+    ins = dict(t_exchange(a, True), mt=mt)
     if small:
         ins["c_own"] = a["c_own"]
     else:
@@ -490,20 +487,22 @@
             c_own, swap(c_own, "gz", 0), swap(c_own, "gz", 1),
             lax.all_gather(c_own, "gz", axis=0, tiled=True)], axis=0)
     v = value(0, ins)
-    column = dict(mt=mt, mt_a=v["mt_a"], mt_b=v["mt_b"], c_all=v["c_all"] if small else ins["c_all"])
-    x = xy_exchange(v)
+    column = dict(mt=mt, c_all=v["c_all"] if small else ins["c_all"])
+    z = z_faces(a, v)
+    got_modes = dict(mt_a=z["mt_a"], mt_b=z["mt_b"])
+    x = dict(xy_exchange(v), z=z["z"])
 
     a = call(functools.partial(second_kernel, face), dict(x, stack=stack),
-             dict(w0=vec, first=rows, **z_out(PAD)), flops=flops)
+             dict(w0=vec, first=rows, **z_out(2)), flops=flops)
     w0, first = a["w0"], a["first"]
-    v = value(1, dict(z_exchange(a, True), **column, first=first))
-    x = xy_exchange(v)
+    v = value(1, dict(t_exchange(a, True), **column, first=first))
+    x = dict(xy_exchange(v), z=z_faces(a, v, got_modes)["z"])
 
     near = dict(near=sds((3 * PAD, loads))) if small else {}
     a = call(functools.partial(third_kernel, face), dict(x, stack=stack, first=first),
-             dict(q=vec, **near, **z_out(0)), flops=flops)
+             dict(q=vec, **near, **z_out(1)), flops=flops)
     q = a["q"]
-    ins = dict(z_exchange(a, False), **column)
+    ins = dict(t_exchange(a, False), **column)
     if small:
         ins.update(first=first, near=a["near"], swapped=swap(a["near"][0:2 * PAD], "gy", 0))
         v = value(2, ins)
@@ -511,25 +510,26 @@
     else:
         sums = dict(six=total(v["xab"][2 * face:], first[2:3]), whole=first)
         v = value(2, ins)
-    x = xy_exchange(v)
+    x = dict(xy_exchange(v), z=z_faces(a, v, got_modes)["z"])
 
     a = call(functools.partial(fourth_kernel, face),
              dict(x, stack=stack, **sums, first=first, r0=r0, w0=w0, q=q),
-             dict(w2=vec, s1=vec, z1=vec, known=rows, **z_out(PAD)), flops=flops)
-    v = value(3, dict(z_exchange(a, True), **column))
+             dict(w2=vec, s1=vec, z1=vec, known=rows, **z_out(2)), flops=flops)
+    v = value(3, dict(t_exchange(a, True), **column))
+    z = z_faces(a, v, got_modes)["z"]
     if small:
         x = x_exchange(v)
         across = move(v["dots"], lambda a, b: (1 - a, (b + (-1 if b % 2 == 0 else 1)) % ny))
         x.update(y_exchange(v))
         part = call(functools.partial(four_kernel, face),
-                    dict(dots=v["dots"], across=across, gxab=x["gxab"], gyb=x["gyb"]), dict(part=rows))["part"]
+                    dict(dots=v["dots"], across=across, gxab=x["gxab"], gyb=x["gyb"], z=z), dict(part=rows))["part"]
         sums = dict(sum_near=part, sum_far=swap(part, "gy", 0))
     else:
         x = xy_exchange(v)
         sums = dict(sum_near=lax.psum(v["dots"], ("gx", "gy")), sum_far=jnp.zeros((PAD, loads), F32))
     out = sds((loads, width))
     res = call(functools.partial(last_kernel, face),
-               dict(x, **sums, r0=r0, w0=w0, **{name: a[name] for name in ("known", "w2", "s1", "z1")}),
+               dict(x, **sums, z=z, r0=r0, w0=w0, **{name: a[name] for name in ("known", "w2", "s1", "z1")}),
                dict(mult=out, resid=out))
     return (res["mult"][None, None, None], res["resid"][None, None, None])
 

time: 66 us -> 66.4 us (level)
  waiting for transfers between devices: 26.8 us -> 16.3 us
  starting transfers between devices: 29.7 us -> 39.9 us
    ppermute x4, waiting for transfers between devices: 11.9 us -> 0.01 us  [shift(): return lax.ppermute(x, axis, [(k, (k + by) % n) for k in range(n)])]
    ppermute x22 -> x30, starting transfers between devices: 21.8 us -> 29.7 us  [swap(): return lax.ppermute(x, axis, [(k, (k + side(k)) % n) for k in range(n)])]
    ppermute x22 -> x30, waiting for transfers between devices: 11.9 us -> 15.5 us  [swap(): return lax.ppermute(x, axis, [(k, (k + side(k)) % n) for k in range(n)])]
    ppermute x1, waiting for transfers between devices: 3.04 us -> 0.78 us  [move(): return lax.ppermute(x, ('gx', 'gy'), pairs)]
    ppermute x1, starting transfers between devices: 0.9 us -> 2.25 us  [move(): return lax.ppermute(x, ('gx', 'gy'), pairs)]
    ppermute x4, starting transfers between devices: 7.01 us -> 7.92 us  [shift(): return lax.ppermute(x, axis, [(k, (k + by) % n) for k in range(n)])]
    pallas_call x9 -> x13, Pallas kernels: 5.85 us -> 6.48 us  [call(): pl.pallas_call(run, out_shape=[outs[n] for n in names_out], in_specs=[vme...]
  transfers between devices with their start and end apart: 27 -> 35, of which waited for: 16 -> 16; matrix products, arithmetic and copies ran while one was open for 0% -> 0% of each run, Pallas kernels for 0% -> 3%
where the time goes in v7:
time: 66.4 us; the launch traced here: 66.2 us
  starting transfers between devices  39.9 us (60%)
  waiting for transfers between devices  16.3 us (25%)
  Pallas kernels  9.26 us (14%)
  between operations  0.79 us (1%)
    ppermute x30, starting transfers between devices, swap(): return lax.ppermute(x, axis, [(k, (k + side(k)) % n) for k in range(n)])  29.7 us
    ppermute x30, waiting for transfers between devices, swap(): return lax.ppermute(x, axis, [(k, (k + side(k)) % n) for k in range(n)])  15.5 us
    ppermute x4, starting transfers between devices, shift(): return lax.ppermute(x, axis, [(k, (k + by) % n) for k in range(n)])  7.92 us
    pallas_call x13, Pallas kernels, call(): pl.pallas_call(run, out_shape=[outs[n] for n in names_out], in_specs=[vme...  6.48 us
    pallas_call x1, Pallas kernels, body(): pl.pallas_call(functools.partial(first_kernel, face, nz, n_modes, small),...  2.78 us
    ppermute x1, starting transfers between devices, move(): return lax.ppermute(x, ('gx', 'gy'), pairs)  2.25 us
  transfers between devices with their start and end apart: 35, of which 16 were waited for; matrix products, arithmetic and copies ran while one was open for 0% of the time, Pallas kernels for 3%

profile of v7, /device:TPU:0, one launch (start us, length us, event | category | flops | bytes accessed | tf_op | source)
XLA Modules:
  0.0 66.2 jit_solution(2628875605618842536)
XLA Ops:
  0.6 2.8 %shard_map.59 = (f32[768,128]{1,0:T(8,128)S(1)}, bf16[1568,768]{1,0:T(8,128)(2,1)S(1)}, bf16[768,48]{1,0:T(8,128)(2,1)S(1)}, f32[8,128]{1,0:T(8,128)S(1)}, f32[5...) custom-call(f32[128,768]{1,0:T(8,128)} %bitcast.7, ...), custom_call_target="tpu_custom_call" | custom-call | flops 603979776 | bytes 2359296 | tf_op jit(solution)/shard_map/pallas_call | solution.py:466
  3.4 3.1 %collective-permute-start.2 = (f32[24,128]{1,0:T(8,128)S(1)}, f32[24,128]{1,0:T(8,128)S(1)}, u32[]{:S(2)}, u32[]{:S(2)}) collective-permute-start(f32[24,128]{1,0:T(8,128)S(1)} %get-tuple-element.54.refs_0_), channel_id=1, source_target_pairs={{0,1},{1,0},{2,3},{3,2},{4,5},{5,4},{6,7},{7,6},{8,9},{9,8},{10,11... | collective-permute-start | bytes 36872 | tf_op jit(solution)/shard_map/ppermute | solution.py:393
  6.5 2.6 %collective-permute-start.1 = (f32[24,128]{1,0:T(8,128)S(1)}, f32[24,128]{1,0:T(8,128)S(1)}, u32[]{:S(2)}, u32[]{:S(2)}) collective-permute-start(f32[24,128]{1,0:T(8,128)S(1)} %get-tuple-element.54.refs_0_), channel_id=1, source_target_pairs={{0,2},{1,3},{2,0},{3,1},{4,6},{5,7},{6,4},{7,5},{8,10},{9,11},{10,... | collective-permute-start | bytes 36872 | tf_op jit(solution)/shard_map/ppermute | solution.py:388
  10.0 2.9 %collective-permute-start.6 = (f32[136,128]{1,0:T(8,128)S(1)}, f32[136,128]{1,0:T(8,128)S(1)}, u32[]{:S(2)}, u32[]{:S(2)}) collective-permute-start(f32[136,128]{1,0:T(8,128)S(1)} %get-tuple-element.62.refs_1_), channel_id=1, source_target_pairs={{0,3},{1,2},{2,1},{3,0},{4,7},{5,6},{6,5},{7,4},{8,11},{9,10},{10,... | collective-permute-start | bytes 208904 | tf_op jit(solution)/shard_map/ppermute | solution.py:393
  12.9 1.7 %collective-permute-done.refs_2_ = f32[24,128]{1,0:T(8,128)S(1)} collective-permute-done((f32[24,128]{1,0:T(8,128)S(1)}, f32[24,128]{1,0:T(8,128)S(1)}, u32[]{:S(2)}, u32[]{:S(2)}) %collective-permute-start) | collective-permute-done | bytes 12320 | tf_op jit(solution)/shard_map/ppermute | solution.py:393
  15.0 1.6 %collective-permute-start.3 = (f32[264,128]{1,0:T(8,128)S(1)}, f32[264,128]{1,0:T(8,128)S(1)}, u32[]{:S(2)}, u32[]{:S(2)}) collective-permute-start(f32[264,128]{1,0:T(8,128)S(1)} %get-tuple-element.58.refs_0_), channel_id=1, source_target_pairs={{0,16},{16,0},{1,17},{17,1},{2,18},{18,2},{3,19},{19,3},{4,20},{20... | collective-permute-start | bytes 405512 | tf_op jit(solution)/shard_map/ppermute | solution.py:393
  16.6 1.6 %collective-permute-start.4 = (f32[136,128]{1,0:T(8,128)S(1)}, f32[136,128]{1,0:T(8,128)S(1)}, u32[]{:S(2)}, u32[]{:S(2)}) collective-permute-start(f32[136,128]{1,0:T(8,128)S(1)} %get-tuple-element.59.refs_2_), channel_id=1, source_target_pairs={{0,4},{4,0},{8,12},{12,8},{1,5},{5,1},{9,13},{13,9},{2,6},{6,2},{1... | collective-permute-start | bytes 208904 | tf_op jit(solution)/shard_map/ppermute | solution.py:393
  19.1 2.0 %collective-permute-done.5.refs_5_ = f32[144,128]{1,0:T(8,128)S(1)} collective-permute-done((f32[144,128]{1,0:T(8,128)S(1)}, f32[144,128]{1,0:T(8,128)S(1)}, u32[]{:S(2)}, u32[]{:S(2)}) %collective-permute-start.5) | collective-permute-done | bytes 73760 | tf_op jit(solution)/shard_map/ppermute | solution.py:393
  22.9 3.5 %collective-permute-start.8 = (f32[16,128]{1,0:T(8,128)S(1)}, f32[16,128]{1,0:T(8,128)S(1)}, u32[]{:S(2)}, u32[]{:S(2)}) collective-permute-start(f32[16,128]{1,0:T(8,128)S(1)} %get-tuple-element.66.refs_0_), channel_id=1, source_target_pairs={{0,3},{1,2},{2,1},{3,0},{4,7},{5,6},{6,5},{7,4},{8,11},{9,10},{10,... | collective-permute-start | bytes 24584 | tf_op jit(solution)/shard_map/ppermute | solution.py:393
  27.0 1.3 %collective-permute-done.8.refs_2_ = f32[16,128]{1,0:T(8,128)S(1)} collective-permute-done((f32[16,128]{1,0:T(8,128)S(1)}, f32[16,128]{1,0:T(8,128)S(1)}, u32[]{:S(2)}, u32[]{:S(2)}) %collective-permute-start.8) | collective-permute-done | bytes 8224 | tf_op jit(solution)/shard_map/ppermute | solution.py:393
  29.2 1.7 %collective-permute-start.12 = (f32[136,128]{1,0:T(8,128)S(1)}, f32[136,128]{1,0:T(8,128)S(1)}, u32[]{:S(2)}, u32[]{:S(2)}) collective-permute-start(f32[136,128]{1,0:T(8,128)S(1)} %get-tuple-element.71.refs_2_), channel_id=1, source_target_pairs={{0,4},{4,0},{8,12},{12,8},{1,5},{5,1},{9,13},{13,9},{2,6},{6,2},{1... | collective-permute-start | bytes 208904 | tf_op jit(solution)/shard_map/ppermute | solution.py:393
  31.4 1.2 %collective-permute-done.14.refs_2_ = f32[128,128]{1,0:T(8,128)S(1)} collective-permute-done((f32[128,128]{1,0:T(8,128)S(1)}, f32[128,128]{1,0:T(8,128)S(1)}, u32[]{:S(2)}, u32[]{:S(2)}) %collective-permute-start.14) | collective-permute-done | bytes 65568 | tf_op jit(solution)/shard_map/ppermute | solution.py:393
  35.1 3.9 %collective-permute-start.17 = (f32[8,128]{1,0:T(8,128)S(1)}, f32[8,128]{1,0:T(8,128)S(1)}, u32[]{:S(2)}, u32[]{:S(2)}) collective-permute-start(f32[8,128]{1,0:T(8,128)S(1)} %get-tuple-element.78.refs_0_), channel_id=1, source_target_pairs={{0,2},{1,3},{2,0},{3,1},{4,6},{5,7},{6,4},{7,5},{8,10},{9,11},{10,... | collective-permute-start | bytes 12296 | tf_op jit(solution)/shard_map/ppermute | solution.py:388
  39.6 3.3 %collective-permute-start.23 = (f32[128,128]{1,0:T(8,128)S(1)}, f32[128,128]{1,0:T(8,128)S(1)}, u32[]{:S(2)}, u32[]{:S(2)}) collective-permute-start(f32[128,128]{1,0:T(8,128)S(1)} %get-tuple-element.85.refs_1_), channel_id=1, source_target_pairs={{0,3},{1,2},{2,1},{3,0},{4,7},{5,6},{6,5},{7,4},{8,11},{9,10},{10,... | collective-permute-start | bytes 196616 | tf_op jit(solution)/shard_map/ppermute | solution.py:393
  42.9 1.7 %collective-permute-done.16.refs_2_ = f32[8,128]{1,0:T(8,128)S(1)} collective-permute-done((f32[8,128]{1,0:T(8,128)S(1)}, f32[8,128]{1,0:T(8,128)S(1)}, u32[]{:S(2)}, u32[]{:S(2)}) %collective-permute-start.16) | collective-permute-done | bytes 4128 | tf_op jit(solution)/shard_map/ppermute | solution.py:393
  45.8 1.5 %collective-permute-start.22 = (f32[136,128]{1,0:T(8,128)S(1)}, f32[136,128]{1,0:T(8,128)S(1)}, u32[]{:S(2)}, u32[]{:S(2)}) collective-permute-start(f32[136,128]{1,0:T(8,128)S(1)} %get-tuple-element.83.refs_3_), channel_id=1, source_target_pairs={{0,12},{4,8},{8,4},{12,0},{1,13},{5,9},{9,5},{13,1},{2,14},{6,10},... | collective-permute-start | bytes 208904 | tf_op jit(solution)/shard_map/ppermute | solution.py:393
  47.5 2.2 %collective-permute-done.22.refs_5_ = f32[136,128]{1,0:T(8,128)S(1)} collective-permute-done((f32[136,128]{1,0:T(8,128)S(1)}, f32[136,128]{1,0:T(8,128)S(1)}, u32[]{:S(2)}, u32[]{:S(2)}) %collective-permute-start.22) | collective-permute-done | bytes 69664 | tf_op jit(solution)/shard_map/ppermute | solution.py:393
  50.0 1.1 %shard_map.68 = (f32[768,128]{1,0:T(8,128)S(1)}, f32[768,128]{1,0:T(8,128)S(1)}, f32[768,128]{1,0:T(8,128)S(1)}, f32[8,128]{1,0:T(8,128)S(1)}, f32[512,128]{1,0:...) custom-call(f32[264,128]{1,0:T(8,128)S(1)} %get-tuple-element.81.refs_0_, ...), custom_call_target="tpu_custom_call" | custom-call | flops 603979776 | bytes 5853184 | tf_op jit(solution)/shard_map/pallas_call | solution.py:31
  51.8 3.8 %collective-permute-start.25 = (f32[16,128]{1,0:T(8,128)S(1)}, f32[16,128]{1,0:T(8,128)S(1)}, u32[]{:S(2)}, u32[]{:S(2)}) collective-permute-start(f32[16,128]{1,0:T(8,128)S(1)} %get-tuple-element.91.refs_0_), channel_id=1, source_target_pairs={{0,3},{1,2},{2,1},{3,0},{4,7},{5,6},{6,5},{7,4},{8,11},{9,10},{10,... | collective-permute-start | bytes 24584 | tf_op jit(solution)/shard_map/ppermute | solution.py:393
  56.2 1.1 %collective-permute-done.25.refs_2_ = f32[16,128]{1,0:T(8,128)S(1)} collective-permute-done((f32[16,128]{1,0:T(8,128)S(1)}, f32[16,128]{1,0:T(8,128)S(1)}, u32[]{:S(2)}, u32[]{:S(2)}) %collective-permute-start.25) | collective-permute-done | bytes 8224 | tf_op jit(solution)/shard_map/ppermute | solution.py:393
  57.7 1.0 %collective-permute-start.28 = (f32[264,128]{1,0:T(8,128)S(1)}, f32[264,128]{1,0:T(8,128)S(1)}, u32[]{:S(2)}, u32[]{:S(2)}) collective-permute-start(f32[264,128]{1,0:T(8,128)S(1)} %get-tuple-element.93.refs_0_), channel_id=1, source_target_pairs={{0,16},{16,0},{1,17},{17,1},{2,18},{18,2},{3,19},{19,3},{4,20},{20... | collective-permute-start | bytes 405512 | tf_op jit(solution)/shard_map/ppermute | solution.py:393
  58.7 2.2 %collective-permute-start.31 = (f32[8,128]{1,0:T(8,128)S(1)}, f32[8,128]{1,0:T(8,128)S(1)}, u32[]{:S(2)}, u32[]{:S(2)}) collective-permute-start(f32[8,128]{1,0:T(8,128)S(1)} %get-tuple-element.96.refs_0_), channel_id=1, source_target_pairs={{0,28},{4,24},{8,20},{12,16},{16,12},{20,8},{24,4},{28,0},{1,29},{... | collective-permute-start | bytes 12296 | tf_op jit(solution)/shard_map/ppermute | solution.py:398
  63.1 1.0 %collective-permute-start.34 = (f32[8,128]{1,0:T(8,128)S(1)}, f32[8,128]{1,0:T(8,128)S(1)}, u32[]{:S(2)}, u32[]{:S(2)}) collective-permute-start(f32[8,128]{1,0:T(8,128)S(1)} %shard_map.71.refs_6_), channel_id=1, source_target_pairs={{0,4},{4,0},{8,12},{12,8},{1,5},{5,1},{9,13},{13,9},{2,6},{6,2},{1... | collective-permute-start | bytes 12296 | tf_op jit(solution)/shard_map/ppermute | solution.py:393
  64.8 1.4 %shard_map.72 = (f32[128,768]{1,0:T(8,128)}, f32[128,768]{1,0:T(8,128)}) custom-call(f32[264,128]{1,0:T(8,128)S(1)} %get-tuple-element.93.refs_0_, f32[264,128]{1,0:T(8,128)S(1)} %collective-permute-done.28.refs_2_.refs_1_, f32[136,128]{1,0:T(8,128)S(1)} %get-tuple-element.94.refs_2_, f32[144,128]{1,0:T(8,128)S(1)} %get-tuple-element.95.refs_3_, ...), custom_call_target="tpu_custom_call" | custom-call | bytes 3452928 | tf_op jit(solution)/shard_map/pallas_call | solution.py:31
  (61 shorter events, 15.2 us)
Async XLA Ops:
  3.4 9.5 %collective-permute-start.2 = (f32[24,128]{1,0:T(8,128)S(1)}, f32[24,128]{1,0:T(8,128)S(1)}, u32[]{:S(2)}, u32[]{:S(2)}) collective-permute-start(f32[24,128]{1,0:T(8,128)S(1)} %get-tuple-element.54.refs_0_), channel_id=1, source_target_pairs={{0,1},{1,0},{2,3},{3,2},{4,5},{5,4},{6,7},{7,6},{8,9},{9,8},{10,11... | collective-permute-start | bytes 36872 | tf_op jit(solution)/shard_map/ppermute | solution.py:393
  6.5 6.4 %collective-permute-start.1 = (f32[24,128]{1,0:T(8,128)S(1)}, f32[24,128]{1,0:T(8,128)S(1)}, u32[]{:S(2)}, u32[]{:S(2)}) collective-permute-start(f32[24,128]{1,0:T(8,128)S(1)} %get-tuple-element.54.refs_0_), channel_id=1, source_target_pairs={{0,2},{1,3},{2,0},{3,1},{4,6},{5,7},{6,4},{7,5},{8,10},{9,11},{10,... | collective-permute-start | bytes 36872 | tf_op jit(solution)/shard_map/ppermute | solution.py:388
  9.1 5.6 %collective-permute-start = (f32[24,128]{1,0:T(8,128)S(1)}, f32[24,128]{1,0:T(8,128)S(1)}, u32[]{:S(2)}, u32[]{:S(2)}) collective-permute-start(f32[24,128]{1,0:T(8,128)S(1)} %get-tuple-element.54.refs_0_), channel_id=1, source_target_pairs={{0,3},{1,2},{2,1},{3,0},{4,7},{5,6},{6,5},{7,4},{8,11},{9,10},{10,... | collective-permute-start | bytes 36872 | tf_op jit(solution)/shard_map/ppermute | solution.py:393
  9.1 9.1 %collective-permute-start.7 = (f32[136,128]{1,0:T(8,128)S(1)}, f32[136,128]{1,0:T(8,128)S(1)}, u32[]{:S(2)}, u32[]{:S(2)}) collective-permute-start(f32[136,128]{1,0:T(8,128)S(1)} %get-tuple-element.61.refs_0_), channel_id=1, source_target_pairs={{0,1},{1,0},{2,3},{3,2},{4,5},{5,4},{6,7},{7,6},{8,9},{9,8},{10,11... | collective-permute-start | bytes 208904 | tf_op jit(solution)/shard_map/ppermute | solution.py:393
  10.0 8.3 %collective-permute-start.6 = (f32[136,128]{1,0:T(8,128)S(1)}, f32[136,128]{1,0:T(8,128)S(1)}, u32[]{:S(2)}, u32[]{:S(2)}) collective-permute-start(f32[136,128]{1,0:T(8,128)S(1)} %get-tuple-element.62.refs_1_), channel_id=1, source_target_pairs={{0,3},{1,2},{2,1},{3,0},{4,7},{5,6},{6,5},{7,4},{8,11},{9,10},{10,... | collective-permute-start | bytes 208904 | tf_op jit(solution)/shard_map/ppermute | solution.py:393
  15.0 6.1 %collective-permute-start.3 = (f32[264,128]{1,0:T(8,128)S(1)}, f32[264,128]{1,0:T(8,128)S(1)}, u32[]{:S(2)}, u32[]{:S(2)}) collective-permute-start(f32[264,128]{1,0:T(8,128)S(1)} %get-tuple-element.58.refs_0_), channel_id=1, source_target_pairs={{0,16},{16,0},{1,17},{17,1},{2,18},{18,2},{3,19},{19,3},{4,20},{20... | collective-permute-start | bytes 405512 | tf_op jit(solution)/shard_map/ppermute | solution.py:393
  22.0 5.0 %collective-permute-start.10 = (f32[16,128]{1,0:T(8,128)S(1)}, f32[16,128]{1,0:T(8,128)S(1)}, u32[]{:S(2)}, u32[]{:S(2)}) collective-permute-start(f32[16,128]{1,0:T(8,128)S(1)} %get-tuple-element.66.refs_0_), channel_id=1, source_target_pairs={{0,1},{1,0},{2,3},{3,2},{4,5},{5,4},{6,7},{7,6},{8,9},{9,8},{10,11... | collective-permute-start | bytes 24584 | tf_op jit(solution)/shard_map/ppermute | solution.py:393
  22.0 4.9 %collective-permute-start.9 = (f32[16,128]{1,0:T(8,128)S(1)}, f32[16,128]{1,0:T(8,128)S(1)}, u32[]{:S(2)}, u32[]{:S(2)}) collective-permute-start(f32[16,128]{1,0:T(8,128)S(1)} %get-tuple-element.66.refs_0_), channel_id=1, source_target_pairs={{0,2},{1,3},{2,0},{3,1},{4,6},{5,7},{6,4},{7,5},{8,10},{9,11},{10,... | collective-permute-start | bytes 24584 | tf_op jit(solution)/shard_map/ppermute | solution.py:388
  22.9 5.4 %collective-permute-start.8 = (f32[16,128]{1,0:T(8,128)S(1)}, f32[16,128]{1,0:T(8,128)S(1)}, u32[]{:S(2)}, u32[]{:S(2)}) collective-permute-start(f32[16,128]{1,0:T(8,128)S(1)} %get-tuple-element.66.refs_0_), channel_id=1, source_target_pairs={{0,3},{1,2},{2,1},{3,0},{4,7},{5,6},{6,5},{7,4},{8,11},{9,10},{10,... | collective-permute-start | bytes 24584 | tf_op jit(solution)/shard_map/ppermute | solution.py:393
  26.4 5.0 %collective-permute-start.15 = (f32[128,128]{1,0:T(8,128)S(1)}, f32[128,128]{1,0:T(8,128)S(1)}, u32[]{:S(2)}, u32[]{:S(2)}) collective-permute-start(f32[128,128]{1,0:T(8,128)S(1)} %get-tuple-element.73.refs_0_), channel_id=1, source_target_pairs={{0,1},{1,0},{2,3},{3,2},{4,5},{5,4},{6,7},{7,6},{8,9},{9,8},{10,11... | collective-permute-start | bytes 196616 | tf_op jit(solution)/shard_map/ppermute | solution.py:393
  26.4 6.2 %collective-permute-start.14 = (f32[128,128]{1,0:T(8,128)S(1)}, f32[128,128]{1,0:T(8,128)S(1)}, u32[]{:S(2)}, u32[]{:S(2)}) collective-permute-start(f32[128,128]{1,0:T(8,128)S(1)} %get-tuple-element.74.refs_1_), channel_id=1, source_target_pairs={{0,3},{1,2},{2,1},{3,0},{4,7},{5,6},{6,5},{7,4},{8,11},{9,10},{10,... | collective-permute-start | bytes 196616 | tf_op jit(solution)/shard_map/ppermute | solution.py:393
  28.7 5.1 %collective-permute-start.11 = (f32[264,128]{1,0:T(8,128)S(1)}, f32[264,128]{1,0:T(8,128)S(1)}, u32[]{:S(2)}, u32[]{:S(2)}) collective-permute-start(f32[264,128]{1,0:T(8,128)S(1)} %get-tuple-element.70.refs_0_), channel_id=1, source_target_pairs={{0,16},{16,0},{1,17},{17,1},{2,18},{18,2},{3,19},{19,3},{4,20},{20... | collective-permute-start | bytes 405512 | tf_op jit(solution)/shard_map/ppermute | solution.py:393
  34.6 10.0 %collective-permute-start.19 = (f32[16,128]{1,0:T(8,128)S(1)}, f32[16,128]{1,0:T(8,128)S(1)}, u32[]{:S(2)}, u32[]{:S(2)}) collective-permute-start(f32[16,128]{1,0:T(8,128)S(1)} %slice.3), channel_id=1, source_target_pairs={{0,4},{4,0},{8,12},{12,8},{1,5},{5,1},{9,13},{13,9},{2,6},{6,2},{1... | collective-permute-start | bytes 24584 | tf_op jit(solution)/shard_map/ppermute | solution.py:393
  35.1 7.8 %collective-permute-start.17 = (f32[8,128]{1,0:T(8,128)S(1)}, f32[8,128]{1,0:T(8,128)S(1)}, u32[]{:S(2)}, u32[]{:S(2)}) collective-permute-start(f32[8,128]{1,0:T(8,128)S(1)} %get-tuple-element.78.refs_0_), channel_id=1, source_target_pairs={{0,2},{1,3},{2,0},{3,1},{4,6},{5,7},{6,4},{7,5},{8,10},{9,11},{10,... | collective-permute-start | bytes 12296 | tf_op jit(solution)/shard_map/ppermute | solution.py:388
  39.0 5.6 %collective-permute-start.16 = (f32[8,128]{1,0:T(8,128)S(1)}, f32[8,128]{1,0:T(8,128)S(1)}, u32[]{:S(2)}, u32[]{:S(2)}) collective-permute-start(f32[8,128]{1,0:T(8,128)S(1)} %get-tuple-element.78.refs_0_), channel_id=1, source_target_pairs={{0,3},{1,2},{2,1},{3,0},{4,7},{5,6},{6,5},{7,4},{8,11},{9,10},{10,... | collective-permute-start | bytes 12296 | tf_op jit(solution)/shard_map/ppermute | solution.py:393
  39.2 8.1 %collective-permute-start.24 = (f32[128,128]{1,0:T(8,128)S(1)}, f32[128,128]{1,0:T(8,128)S(1)}, u32[]{:S(2)}, u32[]{:S(2)}) collective-permute-start(f32[128,128]{1,0:T(8,128)S(1)} %get-tuple-element.84.refs_0_), channel_id=1, source_target_pairs={{0,1},{1,0},{2,3},{3,2},{4,5},{5,4},{6,7},{7,6},{8,9},{9,8},{10,11... | collective-permute-start | bytes 196616 | tf_op jit(solution)/shard_map/ppermute | solution.py:393
  39.6 7.7 %collective-permute-start.23 = (f32[128,128]{1,0:T(8,128)S(1)}, f32[128,128]{1,0:T(8,128)S(1)}, u32[]{:S(2)}, u32[]{:S(2)}) collective-permute-start(f32[128,128]{1,0:T(8,128)S(1)} %get-tuple-element.85.refs_1_), channel_id=1, source_target_pairs={{0,3},{1,2},{2,1},{3,0},{4,7},{5,6},{6,5},{7,4},{8,11},{9,10},{10,... | collective-permute-start | bytes 196616 | tf_op jit(solution)/shard_map/ppermute | solution.py:393
  45.0 5.1 %collective-permute-start.20 = (f32[264,128]{1,0:T(8,128)S(1)}, f32[264,128]{1,0:T(8,128)S(1)}, u32[]{:S(2)}, u32[]{:S(2)}) collective-permute-start(f32[264,128]{1,0:T(8,128)S(1)} %get-tuple-element.81.refs_0_), channel_id=1, source_target_pairs={{0,16},{16,0},{1,17},{17,1},{2,18},{18,2},{3,19},{19,3},{4,20},{20... | collective-permute-start | bytes 405512 | tf_op jit(solution)/shard_map/ppermute | solution.py:393
  51.1 5.0 %collective-permute-start.27 = (f32[16,128]{1,0:T(8,128)S(1)}, f32[16,128]{1,0:T(8,128)S(1)}, u32[]{:S(2)}, u32[]{:S(2)}) collective-permute-start(f32[16,128]{1,0:T(8,128)S(1)} %get-tuple-element.91.refs_0_), channel_id=1, source_target_pairs={{0,1},{1,0},{2,3},{3,2},{4,5},{5,4},{6,7},{7,6},{8,9},{9,8},{10,11... | collective-permute-start | bytes 24584 | tf_op jit(solution)/shard_map/ppermute | solution.py:393
  51.2 4.9 %collective-permute-start.26 = (f32[16,128]{1,0:T(8,128)S(1)}, f32[16,128]{1,0:T(8,128)S(1)}, u32[]{:S(2)}, u32[]{:S(2)}) collective-permute-start(f32[16,128]{1,0:T(8,128)S(1)} %get-tuple-element.91.refs_0_), channel_id=1, source_target_pairs={{0,2},{1,3},{2,0},{3,1},{4,6},{5,7},{6,4},{7,5},{8,10},{9,11},{10,... | collective-permute-start | bytes 24584 | tf_op jit(solution)/shard_map/ppermute | solution.py:388
  51.8 5.5 %collective-permute-start.25 = (f32[16,128]{1,0:T(8,128)S(1)}, f32[16,128]{1,0:T(8,128)S(1)}, u32[]{:S(2)}, u32[]{:S(2)}) collective-permute-start(f32[16,128]{1,0:T(8,128)S(1)} %get-tuple-element.91.refs_0_), channel_id=1, source_target_pairs={{0,3},{1,2},{2,1},{3,0},{4,7},{5,6},{6,5},{7,4},{8,11},{9,10},{10,... | collective-permute-start | bytes 24584 | tf_op jit(solution)/shard_map/ppermute | solution.py:393
  55.6 5.3 %collective-permute-start.33 = (f32[128,128]{1,0:T(8,128)S(1)}, f32[128,128]{1,0:T(8,128)S(1)}, u32[]{:S(2)}, u32[]{:S(2)}) collective-permute-start(f32[128,128]{1,0:T(8,128)S(1)} %get-tuple-element.97.refs_0_), channel_id=1, source_target_pairs={{0,1},{1,0},{2,3},{3,2},{4,5},{5,4},{6,7},{7,6},{8,9},{9,8},{10,11... | collective-permute-start | bytes 196616 | tf_op jit(solution)/shard_map/ppermute | solution.py:393
  55.6 6.2 %collective-permute-start.32 = (f32[128,128]{1,0:T(8,128)S(1)}, f32[128,128]{1,0:T(8,128)S(1)}, u32[]{:S(2)}, u32[]{:S(2)}) collective-permute-start(f32[128,128]{1,0:T(8,128)S(1)} %get-tuple-element.98.refs_1_), channel_id=1, source_target_pairs={{0,3},{1,2},{2,1},{3,0},{4,7},{5,6},{6,5},{7,4},{8,11},{9,10},{10,... | collective-permute-start | bytes 196616 | tf_op jit(solution)/shard_map/ppermute | solution.py:393
  57.7 5.4 %collective-permute-start.28 = (f32[264,128]{1,0:T(8,128)S(1)}, f32[264,128]{1,0:T(8,128)S(1)}, u32[]{:S(2)}, u32[]{:S(2)}) collective-permute-start(f32[264,128]{1,0:T(8,128)S(1)} %get-tuple-element.93.refs_0_), channel_id=1, source_target_pairs={{0,16},{16,0},{1,17},{17,1},{2,18},{18,2},{3,19},{19,3},{4,20},{20... | collective-permute-start | bytes 405512 | tf_op jit(solution)/shard_map/ppermute | solution.py:393
  (11 other events, 38.5 us)

commit v8 on v7

--- a/solution.py
+++ b/solution.py
@@ -97,6 +97,12 @@
     else:
         o["za"][0:face, :] = y[0:face]
         o["zb"][0:face, :] = y[face:]
+
+
+def send_rows(face, rows, at, o):
+    n = rows.shape[0]
+    o["t"][at:at + n, :] = rows
+    o["zb"][face + at:face + at + n, :] = rows
 
 
 def product(face, vec, stack, o):
@@ -110,7 +116,7 @@
         store_product(face, part, y, o)
         total = total + col_sum(vec[at] * y)
     loads = both[2 * width:, :cols] + both[2 * width:, cols:]
-    o["t"][0:PAD, :] = (loads[0:PAD] + loads[PAD:2 * PAD]) + loads[2 * PAD:3 * PAD]
+    send_rows(face, (loads[0:PAD] + loads[PAD:2 * PAD]) + loads[2 * PAD:3 * PAD], 0, o)
     return total
 
 
@@ -173,9 +179,9 @@
     ordered = dot32(rows, pick)
     o["c_own"][...] = ordered
     if turn:
-        o["t"][2 * PAD:3 * PAD, :] = ordered
+        send_rows(face, ordered, 2 * PAD, o)
     o["za"][face:face + PAD, :] = modes[:, 4 * face:5 * face]
-    o["zb"][face:face + PAD, :] = modes[:, 5 * face:6 * face]
+    o["zb"][face + 3 * PAD:face + 4 * PAD, :] = modes[:, 5 * face:6 * face]
 
     for part in range(3):
         at = slice(part * two, (part + 1) * two)
@@ -185,17 +191,18 @@
         o["stack"][at, :] = high
         o["stack"][width + part * two:width + (part + 1) * two, :] = low
     curv = product(face, r0, o["stack"], o)
-    o["t"][PAD:2 * PAD, :] = stack_rows([half_dot(r0, r0), curv], cols)
-
-
-def column_rows(i, at):
-    return [i[name][at:at + PAD, :] for name in ("t", "gta", "gtb", "gt2")]
+    send_rows(face, stack_rows([half_dot(r0, r0), curv], cols), PAD, o)
+
+
+def column_rows(face, i, at):
+    return [i["t"][at:at + PAD, :], i["gta"][at:at + PAD, :],
+            i["gzb"][face + at:face + at + PAD, :], i["gt2"][at:at + PAD, :]]
 
 
 def z_kernel(face, i, o):
     for k, name in enumerate(("a", "b")):
         if "mt_" + name in o:
-            got_modes = mode_pieces(i["gz" + name][face:face + PAD, :])
+            got_modes = mode_pieces(i["gz" + name][-PAD:, :])
             o["mt_" + name][...] = got_modes
         else:
             got_modes = i["mt_" + name][...]
@@ -208,11 +215,11 @@
 
 def value_kernel(face, stage, i, o):
     gathered = "g_all" in i
-    loads = i["g_all"][...] if gathered else jnp.concatenate(column_rows(i, 0), axis=0)
+    loads = i["g_all"][...] if gathered else jnp.concatenate(column_rows(face, i, 0), axis=0)
     if stage == 0 and not gathered:
         n = loads.shape[0]
         coarse = jnp.concatenate([part[:, k * n:(k + 1) * n] for k, part in enumerate(
-            [i["c_own"][...]] + column_rows(i, 2 * PAD)[1:])], axis=0)
+            [i["c_own"][...]] + column_rows(face, i, 2 * PAD)[1:])], axis=0)
         o["c_all"][...] = coarse
     else:
         coarse = i["c_all"][...]
@@ -226,7 +233,7 @@
             dots = i["d_all"][...]
             quad = col_sum(loads * amp[3 * PAD:])
         else:
-            parts = column_rows(i, PAD)
+            parts = column_rows(face, i, PAD)
             dots = (parts[0] + parts[1]) + (parts[2] + parts[3])
             quad = col_sum(loads * amp)
         at = {0: 1, 1: 1, 3: 5}[stage]
@@ -279,7 +286,7 @@
     o["first"][...] = stack_rows([row(first, 0), row(first, 1), scale] + rates, cols)
     vec = scale * w0
     curv = product(face, vec, i["stack"], o)
-    o["t"][PAD:, :] = stack_rows([half_dot(vec, vec), curv], cols)
+    send_rows(face, stack_rows([half_dot(vec, vec), curv], cols), PAD, o)
 
 
 def third_kernel(face, i, o):
@@ -330,9 +337,9 @@
     o["z1"][...] = z1
     o["known"][...] = stack_rows([norm1, alpha1, alpha0, beta1], cols)
     curv = product(face, vec, i["stack"], o)
-    o["t"][PAD:, :] = stack_rows([
+    send_rows(face, stack_rows([
         half_dot(r2, r2), half_dot(r2, w2), half_dot(vec, vec), half_dot(vec, s1),
-        half_dot(s1, s1), curv, half_dot(z1, vec), half_dot(s1, z1)], cols)
+        half_dot(s1, s1), curv, half_dot(z1, vec), half_dot(s1, z1)], cols), PAD, o)
 
 
 def four_kernel(face, i, o):
@@ -410,20 +417,21 @@
 
     def z_out(tiny, extra=0):
         return dict(y=sds((4 * face, loads)), za=sds((face + extra, loads)),
-                    zb=sds((face + extra, loads)), t=sds((tiny * PAD, loads)))
+                    zb=sds((face + tiny * PAD + extra, loads)), t=sds((tiny * PAD, loads)))
 
     def t_exchange(a, with_dots):
         got = dict(t=a["t"], y=a["y"])
         if small:
-            got.update(gtb=swap(a["t"], "gz", 1), gt2=shift(a["t"], "gz", 2), gta=swap(a["t"], "gz", 0))
+            got.update(gzb=swap(a["zb"], "gz", 1), gt2=shift(a["t"], "gz", 2), gta=swap(a["t"], "gz", 0))
         else:
             got["g_all"] = lax.all_gather(a["t"][0:PAD], "gz", axis=0, tiled=True)
             if with_dots:
                 got["d_all"] = lax.psum(a["t"][PAD:2 * PAD], "gz")
         return got
 
-    def z_faces(a, v, modes=None):
-        ins = dict(za=a["za"], zb=a["zb"], gzb=swap(a["zb"], "gz", 1), gza=swap(a["za"], "gz", 0), mt=mt, amp=v["amp"])
+    def z_faces(a, v, t, modes=None):
+        ins = dict(za=a["za"], zb=a["zb"], gzb=t["gzb"] if small else swap(a["zb"], "gz", 1),
+                   gza=swap(a["za"], "gz", 0), mt=mt, amp=v["amp"])
         outs = dict(z=sds((2 * face, loads)))
         if modes is None:
             outs.update(mt_a=sds((face, 6 * PAD), BF16), mt_b=sds((face, 6 * PAD), BF16))
@@ -434,7 +442,7 @@
     def value(stage, ins):
         extra = 0 if stage == 2 else PAD
         outs = dict(amp=sds((3 * PAD, loads)), xab=sds((2 * face + (PAD if small else extra), loads)),
-                    ya=sds((face + extra, loads)), yb=sds((face + extra + PAD, loads)))
+                    ya=sds((face + extra, loads)), yb=sds((face + 2 * PAD, loads)))
         if stage == 0 and small:
             outs["c_all"] = sds((nz * PAD, nz * PAD))
         if stage == 2 and small:
@@ -486,23 +494,26 @@
         ins["c_all"] = jnp.concatenate([
             c_own, swap(c_own, "gz", 0), swap(c_own, "gz", 1),
             lax.all_gather(c_own, "gz", axis=0, tiled=True)], axis=0)
+    t = ins
     v = value(0, ins)
     column = dict(mt=mt, c_all=v["c_all"] if small else ins["c_all"])
-    z = z_faces(a, v)
+    z = z_faces(a, v, t)
     got_modes = dict(mt_a=z["mt_a"], mt_b=z["mt_b"])
     x = dict(xy_exchange(v), z=z["z"])
 
     a = call(functools.partial(second_kernel, face), dict(x, stack=stack),
              dict(w0=vec, first=rows, **z_out(2)), flops=flops)
     w0, first = a["w0"], a["first"]
-    v = value(1, dict(t_exchange(a, True), **column, first=first))
-    x = dict(xy_exchange(v), z=z_faces(a, v, got_modes)["z"])
+    t = t_exchange(a, True)
+    v = value(1, dict(t, **column, first=first))
+    x = dict(xy_exchange(v), z=z_faces(a, v, t, got_modes)["z"])
 
     near = dict(near=sds((3 * PAD, loads))) if small else {}
     a = call(functools.partial(third_kernel, face), dict(x, stack=stack, first=first),
              dict(q=vec, **near, **z_out(1)), flops=flops)
     q = a["q"]
-    ins = dict(t_exchange(a, False), **column)
+    t = t_exchange(a, False)
+    ins = dict(t, **column)
     if small:
         ins.update(first=first, near=a["near"], swapped=swap(a["near"][0:2 * PAD], "gy", 0))
         v = value(2, ins)
@@ -510,13 +521,14 @@
     else:
         sums = dict(six=total(v["xab"][2 * face:], first[2:3]), whole=first)
         v = value(2, ins)
-    x = dict(xy_exchange(v), z=z_faces(a, v, got_modes)["z"])
+    x = dict(xy_exchange(v), z=z_faces(a, v, t, got_modes)["z"])
 
     a = call(functools.partial(fourth_kernel, face),
              dict(x, stack=stack, **sums, first=first, r0=r0, w0=w0, q=q),
              dict(w2=vec, s1=vec, z1=vec, known=rows, **z_out(2)), flops=flops)
-    v = value(3, dict(t_exchange(a, True), **column))
-    z = z_faces(a, v, got_modes)["z"]
+    t = t_exchange(a, True)
+    v = value(3, dict(t, **column))
+    z = z_faces(a, v, t, got_modes)["z"]
     if small:
         x = x_exchange(v)
         across = move(v["dots"], lambda a, b: (1 - a, (b + (-1 if b % 2 == 0 else 1)) % ny))

time: 66.4 us -> 64.1 us (0.965)
  starting transfers between devices: 39.9 us -> 34.1 us
  waiting for transfers between devices: 16.3 us -> 19.9 us
    ppermute x30 -> x26, starting transfers between devices: 29.7 us -> 24.7 us  [swap(): return lax.ppermute(x, axis, [(k, (k + side(k)) % n) for k in range(n)])]
    ppermute x4, waiting for transfers between devices: 0.01 us -> 3.55 us  [shift(): return lax.ppermute(x, axis, [(k, (k + by) % n) for k in range(n)])]
    ppermute x4, starting transfers between devices: 7.92 us -> 6.94 us  [shift(): return lax.ppermute(x, axis, [(k, (k + by) % n) for k in range(n)])]
    ppermute x30 -> x26, waiting for transfers between devices: 15.5 us -> 14.9 us  [swap(): return lax.ppermute(x, axis, [(k, (k + side(k)) % n) for k in range(n)])]
  transfers between devices with their start and end apart: 35 -> 31, of which waited for: 16 -> 18; matrix products, arithmetic and copies ran while one was open for 0% -> 0% of each run, Pallas kernels for 3% -> 4%
where the time goes in v8:
time: 64.1 us; the launch traced here: 64 us
  starting transfers between devices  34.1 us (53%)
  waiting for transfers between devices  19.9 us (31%)
  Pallas kernels  9.24 us (14%)
  between operations  0.75 us (1%)
    ppermute x26, starting transfers between devices, swap(): return lax.ppermute(x, axis, [(k, (k + side(k)) % n) for k in range(n)])  24.7 us
    ppermute x26, waiting for transfers between devices, swap(): return lax.ppermute(x, axis, [(k, (k + side(k)) % n) for k in range(n)])  14.9 us
    ppermute x4, starting transfers between devices, shift(): return lax.ppermute(x, axis, [(k, (k + by) % n) for k in range(n)])  6.94 us
    pallas_call x13, Pallas kernels, call(): pl.pallas_call(run, out_shape=[outs[n] for n in names_out], in_specs=[vme...  6.47 us
    ppermute x4, waiting for transfers between devices, shift(): return lax.ppermute(x, axis, [(k, (k + by) % n) for k in range(n)])  3.55 us
    pallas_call x1, Pallas kernels, body(): pl.pallas_call(functools.partial(first_kernel, face, nz, n_modes, small),...  2.78 us
    ppermute x1, starting transfers between devices, move(): return lax.ppermute(x, ('gx', 'gy'), pairs)  2.45 us
    ppermute x1, waiting for transfers between devices, move(): return lax.ppermute(x, ('gx', 'gy'), pairs)  1.41 us
  transfers between devices with their start and end apart: 31, of which 18 were waited for; matrix products, arithmetic and copies ran while one was open for 0% of the time, Pallas kernels for 4%

profile of v8, /device:TPU:0, one launch (start us, length us, event | category | flops | bytes accessed | tf_op | source)
XLA Modules:
  0.0 64.0 jit_solution(6911848951379711859)
XLA Ops:
  0.6 2.8 %shard_map.59 = (f32[768,128]{1,0:T(8,128)S(1)}, bf16[1568,768]{1,0:T(8,128)(2,1)S(1)}, bf16[768,48]{1,0:T(8,128)(2,1)S(1)}, f32[8,128]{1,0:T(8,128)S(1)}, f32[5...) custom-call(f32[128,768]{1,0:T(8,128)} %bitcast.7, ...), custom_call_target="tpu_custom_call" | custom-call | flops 603979776 | bytes 2359296 | tf_op jit(solution)/shard_map/pallas_call | solution.py:474
  3.4 5.1 %collective-permute-start = (f32[160,128]{1,0:T(8,128)S(1)}, f32[160,128]{1,0:T(8,128)S(1)}, u32[]{:S(2)}, u32[]{:S(2)}) collective-permute-start(f32[160,128]{1,0:T(8,128)S(1)} %get-tuple-element.56.refs_1_), channel_id=1, source_target_pairs={{0,3},{1,2},{2,1},{3,0},{4,7},{5,6},{6,5},{7,4},{8,11},{9,10},{10,... | collective-permute-start | bytes 245768 | tf_op jit(solution)/shard_map/ppermute | solution.py:400
  9.2 1.4 %collective-permute-start.6 = (f32[136,128]{1,0:T(8,128)S(1)}, f32[136,128]{1,0:T(8,128)S(1)}, u32[]{:S(2)}, u32[]{:S(2)}) collective-permute-start(f32[136,128]{1,0:T(8,128)S(1)} %get-tuple-element.62.refs_0_), channel_id=1, source_target_pairs={{0,1},{1,0},{2,3},{3,2},{4,5},{5,4},{6,7},{7,6},{8,9},{9,8},{10,11... | collective-permute-start | bytes 208904 | tf_op jit(solution)/shard_map/ppermute | solution.py:400
  10.6 1.7 %collective-permute-done.2.refs_4_ = f32[24,128]{1,0:T(8,128)S(1)} collective-permute-done((f32[24,128]{1,0:T(8,128)S(1)}, f32[24,128]{1,0:T(8,128)S(1)}, u32[]{:S(2)}, u32[]{:S(2)}) %collective-permute-start.2) | collective-permute-done | bytes 12320 | tf_op jit(solution)/shard_map/ppermute | solution.py:400
  13.6 1.6 %collective-permute-start.3 = (f32[264,128]{1,0:T(8,128)S(1)}, f32[264,128]{1,0:T(8,128)S(1)}, u32[]{:S(2)}, u32[]{:S(2)}) collective-permute-start(f32[264,128]{1,0:T(8,128)S(1)} %get-tuple-element.59.refs_0_), channel_id=1, source_target_pairs={{0,16},{16,0},{1,17},{17,1},{2,18},{18,2},{3,19},{19,3},{4,20},{20... | collective-permute-start | bytes 405512 | tf_op jit(solution)/shard_map/ppermute | solution.py:400
  15.2 1.6 %collective-permute-start.4 = (f32[136,128]{1,0:T(8,128)S(1)}, f32[136,128]{1,0:T(8,128)S(1)}, u32[]{:S(2)}, u32[]{:S(2)}) collective-permute-start(f32[136,128]{1,0:T(8,128)S(1)} %get-tuple-element.60.refs_2_), channel_id=1, source_target_pairs={{0,4},{4,0},{8,12},{12,8},{1,5},{5,1},{9,13},{13,9},{2,6},{6,2},{1... | collective-permute-start | bytes 208904 | tf_op jit(solution)/shard_map/ppermute | solution.py:400
  17.7 1.9 %collective-permute-done.5.refs_5_ = f32[144,128]{1,0:T(8,128)S(1)} collective-permute-done((f32[144,128]{1,0:T(8,128)S(1)}, f32[144,128]{1,0:T(8,128)S(1)}, u32[]{:S(2)}, u32[]{:S(2)}) %collective-permute-start.5) | collective-permute-done | bytes 73760 | tf_op jit(solution)/shard_map/ppermute | solution.py:400
  20.6 2.2 %collective-permute-start.7 = (f32[144,128]{1,0:T(8,128)S(1)}, f32[144,128]{1,0:T(8,128)S(1)}, u32[]{:S(2)}, u32[]{:S(2)}) collective-permute-start(f32[144,128]{1,0:T(8,128)S(1)} %get-tuple-element.68.refs_1_), channel_id=1, source_target_pairs={{0,3},{1,2},{2,1},{3,0},{4,7},{5,6},{6,5},{7,4},{8,11},{9,10},{10,... | collective-permute-start | bytes 221192 | tf_op jit(solution)/shard_map/ppermute | solution.py:400
  22.9 2.1 %collective-permute-start.8 = (f32[16,128]{1,0:T(8,128)S(1)}, f32[16,128]{1,0:T(8,128)S(1)}, u32[]{:S(2)}, u32[]{:S(2)}) collective-permute-start(f32[16,128]{1,0:T(8,128)S(1)} %get-tuple-element.66.refs_0_), channel_id=1, source_target_pairs={{0,2},{1,3},{2,0},{3,1},{4,6},{5,7},{6,4},{7,5},{8,10},{9,11},{10,... | collective-permute-start | bytes 24584 | tf_op jit(solution)/shard_map/ppermute | solution.py:395
  25.0 1.0 %collective-permute-start.13 = (f32[128,128]{1,0:T(8,128)S(1)}, f32[128,128]{1,0:T(8,128)S(1)}, u32[]{:S(2)}, u32[]{:S(2)}) collective-permute-start(f32[128,128]{1,0:T(8,128)S(1)} %get-tuple-element.74.refs_0_), channel_id=1, source_target_pairs={{0,1},{1,0},{2,3},{3,2},{4,5},{5,4},{6,7},{7,6},{8,9},{9,8},{10,11... | collective-permute-start | bytes 196616 | tf_op jit(solution)/shard_map/ppermute | solution.py:400
  27.0 1.2 %collective-permute-done.8.refs_3_ = f32[16,128]{1,0:T(8,128)S(1)} collective-permute-done((f32[16,128]{1,0:T(8,128)S(1)}, f32[16,128]{1,0:T(8,128)S(1)}, u32[]{:S(2)}, u32[]{:S(2)}) %collective-permute-start.8) | collective-permute-done | bytes 8224 | tf_op jit(solution)/shard_map/ppermute | solution.py:395
  30.9 2.1 %collective-permute-done.12.refs_5_ = f32[144,128]{1,0:T(8,128)S(1)} collective-permute-done((f32[144,128]{1,0:T(8,128)S(1)}, f32[144,128]{1,0:T(8,128)S(1)}, u32[]{:S(2)}, u32[]{:S(2)}) %collective-permute-start.12) | collective-permute-done | bytes 73760 | tf_op jit(solution)/shard_map/ppermute | solution.py:400
  34.4 2.0 %collective-permute-start.14 = (f32[136,128]{1,0:T(8,128)S(1)}, f32[136,128]{1,0:T(8,128)S(1)}, u32[]{:S(2)}, u32[]{:S(2)}) collective-permute-start(f32[136,128]{1,0:T(8,128)S(1)} %get-tuple-element.80.refs_1_), channel_id=1, source_target_pairs={{0,3},{1,2},{2,1},{3,0},{4,7},{5,6},{6,5},{7,4},{8,11},{9,10},{10,... | collective-permute-start | bytes 208904 | tf_op jit(solution)/shard_map/ppermute | solution.py:400
  36.6 2.3 %collective-permute-start.15 = (f32[8,128]{1,0:T(8,128)S(1)}, f32[8,128]{1,0:T(8,128)S(1)}, u32[]{:S(2)}, u32[]{:S(2)}) collective-permute-start(f32[8,128]{1,0:T(8,128)S(1)} %get-tuple-element.78.refs_0_), channel_id=1, source_target_pairs={{0,2},{1,3},{2,0},{3,1},{4,6},{5,7},{6,4},{7,5},{8,10},{9,11},{10,... | collective-permute-start | bytes 12296 | tf_op jit(solution)/shard_map/ppermute | solution.py:395
  39.2 1.2 %collective-permute-done.16.refs_4_ = f32[8,128]{1,0:T(8,128)S(1)} collective-permute-done((f32[8,128]{1,0:T(8,128)S(1)}, f32[8,128]{1,0:T(8,128)S(1)}, u32[]{:S(2)}, u32[]{:S(2)}) %collective-permute-start.16) | collective-permute-done | bytes 4128 | tf_op jit(solution)/shard_map/ppermute | solution.py:400
  42.3 1.5 %collective-permute-start.19 = (f32[128,128]{1,0:T(8,128)S(1)}, f32[128,128]{1,0:T(8,128)S(1)}, u32[]{:S(2)}, u32[]{:S(2)}) collective-permute-start(f32[128,128]{1,0:T(8,128)S(1)} %get-tuple-element.83.refs_2_), channel_id=1, source_target_pairs={{0,4},{4,0},{8,12},{12,8},{1,5},{5,1},{9,13},{13,9},{2,6},{6,2},{1... | collective-permute-start | bytes 196616 | tf_op jit(solution)/shard_map/ppermute | solution.py:400
  44.7 2.1 %collective-permute-done.20.refs_5_ = f32[144,128]{1,0:T(8,128)S(1)} collective-permute-done((f32[144,128]{1,0:T(8,128)S(1)}, f32[144,128]{1,0:T(8,128)S(1)}, u32[]{:S(2)}, u32[]{:S(2)}) %collective-permute-start.20) | collective-permute-done | bytes 73760 | tf_op jit(solution)/shard_map/ppermute | solution.py:400
  46.8 1.1 %shard_map.68 = (f32[768,128]{1,0:T(8,128)S(1)}, f32[768,128]{1,0:T(8,128)S(1)}, f32[768,128]{1,0:T(8,128)S(1)}, f32[8,128]{1,0:T(8,128)S(1)}, f32[512,128]{1,0:...) custom-call(f32[264,128]{1,0:T(8,128)S(1)} %get-tuple-element.82.refs_0_, ...), custom_call_target="tpu_custom_call" | custom-call | flops 603979776 | bytes 5869568 | tf_op jit(solution)/shard_map/pallas_call | solution.py:31
  48.0 2.0 %collective-permute-start.22 = (f32[144,128]{1,0:T(8,128)S(1)}, f32[144,128]{1,0:T(8,128)S(1)}, u32[]{:S(2)}, u32[]{:S(2)}) collective-permute-start(f32[144,128]{1,0:T(8,128)S(1)} %get-tuple-element.93.refs_1_), channel_id=1, source_target_pairs={{0,3},{1,2},{2,1},{3,0},{4,7},{5,6},{6,5},{7,4},{8,11},{9,10},{10,... | collective-permute-start | bytes 221192 | tf_op jit(solution)/shard_map/ppermute | solution.py:400
  50.5 1.9 %collective-permute-start.23 = (f32[16,128]{1,0:T(8,128)S(1)}, f32[16,128]{1,0:T(8,128)S(1)}, u32[]{:S(2)}, u32[]{:S(2)}) collective-permute-start(f32[16,128]{1,0:T(8,128)S(1)} %get-tuple-element.91.refs_0_), channel_id=1, source_target_pairs={{0,2},{1,3},{2,0},{3,1},{4,6},{5,7},{6,4},{7,5},{8,10},{9,11},{10,... | collective-permute-start | bytes 24584 | tf_op jit(solution)/shard_map/ppermute | solution.py:395
  53.3 1.1 %collective-permute-done.24.refs_4_ = f32[16,128]{1,0:T(8,128)S(1)} collective-permute-done((f32[16,128]{1,0:T(8,128)S(1)}, f32[16,128]{1,0:T(8,128)S(1)}, u32[]{:S(2)}, u32[]{:S(2)}) %collective-permute-start.24) | collective-permute-done | bytes 8224 | tf_op jit(solution)/shard_map/ppermute | solution.py:400
  56.3 2.4 %collective-permute-start.28 = (f32[8,128]{1,0:T(8,128)S(1)}, f32[8,128]{1,0:T(8,128)S(1)}, u32[]{:S(2)}, u32[]{:S(2)}) collective-permute-start(f32[8,128]{1,0:T(8,128)S(1)} %get-tuple-element.97.refs_0_), channel_id=1, source_target_pairs={{0,28},{4,24},{8,20},{12,16},{16,12},{20,8},{24,4},{28,0},{1,29},{... | collective-permute-start | bytes 12296 | tf_op jit(solution)/shard_map/ppermute | solution.py:405
  58.9 1.4 %collective-permute-done.28.refs_1_ = f32[8,128]{1,0:T(8,128)S(1)} collective-permute-done((f32[8,128]{1,0:T(8,128)S(1)}, f32[8,128]{1,0:T(8,128)S(1)}, u32[]{:S(2)}, u32[]{:S(2)}) %collective-permute-start.28) | collective-permute-done | bytes 4128 | tf_op jit(solution)/shard_map/ppermute | solution.py:405
  62.6 1.4 %shard_map.72 = (f32[128,768]{1,0:T(8,128)}, f32[128,768]{1,0:T(8,128)}) custom-call(f32[264,128]{1,0:T(8,128)S(1)} %get-tuple-element.94.refs_0_, f32[264,128]{1,0:T(8,128)S(1)} %collective-permute-done.25.refs_2_.refs_1_, f32[136,128]{1,0:T(8,128)S(1)} %get-tuple-element.95.refs_2_, f32[144,128]{1,0:T(8,128)S(1)} %get-tuple-element.96.refs_3_, ...), custom_call_target="tpu_custom_call" | custom-call | bytes 3452928 | tf_op jit(solution)/shard_map/pallas_call | solution.py:31
  (53 shorter events, 18.1 us)
Async XLA Ops:
  3.4 9.8 %collective-permute-start = (f32[160,128]{1,0:T(8,128)S(1)}, f32[160,128]{1,0:T(8,128)S(1)}, u32[]{:S(2)}, u32[]{:S(2)}) collective-permute-start(f32[160,128]{1,0:T(8,128)S(1)} %get-tuple-element.56.refs_1_), channel_id=1, source_target_pairs={{0,3},{1,2},{2,1},{3,0},{4,7},{5,6},{6,5},{7,4},{8,11},{9,10},{10,... | collective-permute-start | bytes 245768 | tf_op jit(solution)/shard_map/ppermute | solution.py:400
  8.5 4.7 %collective-permute-start.1 = (f32[24,128]{1,0:T(8,128)S(1)}, f32[24,128]{1,0:T(8,128)S(1)}, u32[]{:S(2)}, u32[]{:S(2)}) collective-permute-start(f32[24,128]{1,0:T(8,128)S(1)} %get-tuple-element.54.refs_0_), channel_id=1, source_target_pairs={{0,2},{1,3},{2,0},{3,1},{4,6},{5,7},{6,4},{7,5},{8,10},{9,11},{10,... | collective-permute-start | bytes 36872 | tf_op jit(solution)/shard_map/ppermute | solution.py:395
  9.2 7.7 %collective-permute-start.6 = (f32[136,128]{1,0:T(8,128)S(1)}, f32[136,128]{1,0:T(8,128)S(1)}, u32[]{:S(2)}, u32[]{:S(2)}) collective-permute-start(f32[136,128]{1,0:T(8,128)S(1)} %get-tuple-element.62.refs_0_), channel_id=1, source_target_pairs={{0,1},{1,0},{2,3},{3,2},{4,5},{5,4},{6,7},{7,6},{8,9},{9,8},{10,11... | collective-permute-start | bytes 208904 | tf_op jit(solution)/shard_map/ppermute | solution.py:400
  13.6 6.1 %collective-permute-start.3 = (f32[264,128]{1,0:T(8,128)S(1)}, f32[264,128]{1,0:T(8,128)S(1)}, u32[]{:S(2)}, u32[]{:S(2)}) collective-permute-start(f32[264,128]{1,0:T(8,128)S(1)} %get-tuple-element.59.refs_0_), channel_id=1, source_target_pairs={{0,16},{16,0},{1,17},{17,1},{2,18},{18,2},{3,19},{19,3},{4,20},{20... | collective-permute-start | bytes 405512 | tf_op jit(solution)/shard_map/ppermute | solution.py:400
  15.2 4.5 %collective-permute-start.5 = (f32[144,128]{1,0:T(8,128)S(1)}, f32[144,128]{1,0:T(8,128)S(1)}, u32[]{:S(2)}, u32[]{:S(2)}) collective-permute-start(f32[144,128]{1,0:T(8,128)S(1)} %get-tuple-element.61.refs_3_), channel_id=1, source_target_pairs={{0,12},{4,8},{8,4},{12,0},{1,13},{5,9},{9,5},{13,1},{2,14},{6,10},... | collective-permute-start | bytes 221192 | tf_op jit(solution)/shard_map/ppermute | solution.py:400
  20.6 7.6 %collective-permute-start.7 = (f32[144,128]{1,0:T(8,128)S(1)}, f32[144,128]{1,0:T(8,128)S(1)}, u32[]{:S(2)}, u32[]{:S(2)}) collective-permute-start(f32[144,128]{1,0:T(8,128)S(1)} %get-tuple-element.68.refs_1_), channel_id=1, source_target_pairs={{0,3},{1,2},{2,1},{3,0},{4,7},{5,6},{6,5},{7,4},{8,11},{9,10},{10,... | collective-permute-start | bytes 221192 | tf_op jit(solution)/shard_map/ppermute | solution.py:400
  22.7 4.2 %collective-permute-start.9 = (f32[16,128]{1,0:T(8,128)S(1)}, f32[16,128]{1,0:T(8,128)S(1)}, u32[]{:S(2)}, u32[]{:S(2)}) collective-permute-start(f32[16,128]{1,0:T(8,128)S(1)} %get-tuple-element.66.refs_0_), channel_id=1, source_target_pairs={{0,1},{1,0},{2,3},{3,2},{4,5},{5,4},{6,7},{7,6},{8,9},{9,8},{10,11... | collective-permute-start | bytes 24584 | tf_op jit(solution)/shard_map/ppermute | solution.py:400
  22.9 5.2 %collective-permute-start.8 = (f32[16,128]{1,0:T(8,128)S(1)}, f32[16,128]{1,0:T(8,128)S(1)}, u32[]{:S(2)}, u32[]{:S(2)}) collective-permute-start(f32[16,128]{1,0:T(8,128)S(1)} %get-tuple-element.66.refs_0_), channel_id=1, source_target_pairs={{0,2},{1,3},{2,0},{3,1},{4,6},{5,7},{6,4},{7,5},{8,10},{9,11},{10,... | collective-permute-start | bytes 24584 | tf_op jit(solution)/shard_map/ppermute | solution.py:395
  25.0 5.0 %collective-permute-start.13 = (f32[128,128]{1,0:T(8,128)S(1)}, f32[128,128]{1,0:T(8,128)S(1)}, u32[]{:S(2)}, u32[]{:S(2)}) collective-permute-start(f32[128,128]{1,0:T(8,128)S(1)} %get-tuple-element.74.refs_0_), channel_id=1, source_target_pairs={{0,1},{1,0},{2,3},{3,2},{4,5},{5,4},{6,7},{7,6},{8,9},{9,8},{10,11... | collective-permute-start | bytes 196616 | tf_op jit(solution)/shard_map/ppermute | solution.py:400
  28.5 5.1 %collective-permute-start.10 = (f32[264,128]{1,0:T(8,128)S(1)}, f32[264,128]{1,0:T(8,128)S(1)}, u32[]{:S(2)}, u32[]{:S(2)}) collective-permute-start(f32[264,128]{1,0:T(8,128)S(1)} %get-tuple-element.71.refs_0_), channel_id=1, source_target_pairs={{0,16},{16,0},{1,17},{17,1},{2,18},{18,2},{3,19},{19,3},{4,20},{20... | collective-permute-start | bytes 405512 | tf_op jit(solution)/shard_map/ppermute | solution.py:400
  34.4 6.7 %collective-permute-start.14 = (f32[136,128]{1,0:T(8,128)S(1)}, f32[136,128]{1,0:T(8,128)S(1)}, u32[]{:S(2)}, u32[]{:S(2)}) collective-permute-start(f32[136,128]{1,0:T(8,128)S(1)} %get-tuple-element.80.refs_1_), channel_id=1, source_target_pairs={{0,3},{1,2},{2,1},{3,0},{4,7},{5,6},{6,5},{7,4},{8,11},{9,10},{10,... | collective-permute-start | bytes 208904 | tf_op jit(solution)/shard_map/ppermute | solution.py:400
  36.4 4.7 %collective-permute-start.17 = (f32[16,128]{1,0:T(8,128)S(1)}, f32[16,128]{1,0:T(8,128)S(1)}, u32[]{:S(2)}, u32[]{:S(2)}) collective-permute-start(f32[16,128]{1,0:T(8,128)S(1)} %slice.3), channel_id=1, source_target_pairs={{0,4},{4,0},{8,12},{12,8},{1,5},{5,1},{9,13},{13,9},{2,6},{6,2},{1... | collective-permute-start | bytes 24584 | tf_op jit(solution)/shard_map/ppermute | solution.py:400
  36.4 4.0 %collective-permute-start.16 = (f32[8,128]{1,0:T(8,128)S(1)}, f32[8,128]{1,0:T(8,128)S(1)}, u32[]{:S(2)}, u32[]{:S(2)}) collective-permute-start(f32[8,128]{1,0:T(8,128)S(1)} %get-tuple-element.78.refs_0_), channel_id=1, source_target_pairs={{0,1},{1,0},{2,3},{3,2},{4,5},{5,4},{6,7},{7,6},{8,9},{9,8},{10,11... | collective-permute-start | bytes 12296 | tf_op jit(solution)/shard_map/ppermute | solution.py:400
  36.6 4.5 %collective-permute-start.15 = (f32[8,128]{1,0:T(8,128)S(1)}, f32[8,128]{1,0:T(8,128)S(1)}, u32[]{:S(2)}, u32[]{:S(2)}) collective-permute-start(f32[8,128]{1,0:T(8,128)S(1)} %get-tuple-element.78.refs_0_), channel_id=1, source_target_pairs={{0,2},{1,3},{2,0},{3,1},{4,6},{5,7},{6,4},{7,5},{8,10},{9,11},{10,... | collective-permute-start | bytes 12296 | tf_op jit(solution)/shard_map/ppermute | solution.py:395
  38.8 5.0 %collective-permute-start.21 = (f32[128,128]{1,0:T(8,128)S(1)}, f32[128,128]{1,0:T(8,128)S(1)}, u32[]{:S(2)}, u32[]{:S(2)}) collective-permute-start(f32[128,128]{1,0:T(8,128)S(1)} %get-tuple-element.85.refs_0_), channel_id=1, source_target_pairs={{0,1},{1,0},{2,3},{3,2},{4,5},{5,4},{6,7},{7,6},{8,9},{9,8},{10,11... | collective-permute-start | bytes 196616 | tf_op jit(solution)/shard_map/ppermute | solution.py:400
  41.4 5.4 %collective-permute-start.18 = (f32[264,128]{1,0:T(8,128)S(1)}, f32[264,128]{1,0:T(8,128)S(1)}, u32[]{:S(2)}, u32[]{:S(2)}) collective-permute-start(f32[264,128]{1,0:T(8,128)S(1)} %get-tuple-element.82.refs_0_), channel_id=1, source_target_pairs={{0,16},{16,0},{1,17},{17,1},{2,18},{18,2},{3,19},{19,3},{4,20},{20... | collective-permute-start | bytes 405512 | tf_op jit(solution)/shard_map/ppermute | solution.py:400
  42.3 4.5 %collective-permute-start.20 = (f32[144,128]{1,0:T(8,128)S(1)}, f32[144,128]{1,0:T(8,128)S(1)}, u32[]{:S(2)}, u32[]{:S(2)}) collective-permute-start(f32[144,128]{1,0:T(8,128)S(1)} %get-tuple-element.84.refs_3_), channel_id=1, source_target_pairs={{0,12},{4,8},{8,4},{12,0},{1,13},{5,9},{9,5},{13,1},{2,14},{6,10},... | collective-permute-start | bytes 221192 | tf_op jit(solution)/shard_map/ppermute | solution.py:400
  48.0 7.2 %collective-permute-start.22 = (f32[144,128]{1,0:T(8,128)S(1)}, f32[144,128]{1,0:T(8,128)S(1)}, u32[]{:S(2)}, u32[]{:S(2)}) collective-permute-start(f32[144,128]{1,0:T(8,128)S(1)} %get-tuple-element.93.refs_1_), channel_id=1, source_target_pairs={{0,3},{1,2},{2,1},{3,0},{4,7},{5,6},{6,5},{7,4},{8,11},{9,10},{10,... | collective-permute-start | bytes 221192 | tf_op jit(solution)/shard_map/ppermute | solution.py:400
  50.0 4.4 %collective-permute-start.24 = (f32[16,128]{1,0:T(8,128)S(1)}, f32[16,128]{1,0:T(8,128)S(1)}, u32[]{:S(2)}, u32[]{:S(2)}) collective-permute-start(f32[16,128]{1,0:T(8,128)S(1)} %get-tuple-element.91.refs_0_), channel_id=1, source_target_pairs={{0,1},{1,0},{2,3},{3,2},{4,5},{5,4},{6,7},{7,6},{8,9},{9,8},{10,11... | collective-permute-start | bytes 24584 | tf_op jit(solution)/shard_map/ppermute | solution.py:400
  50.5 4.6 %collective-permute-start.23 = (f32[16,128]{1,0:T(8,128)S(1)}, f32[16,128]{1,0:T(8,128)S(1)}, u32[]{:S(2)}, u32[]{:S(2)}) collective-permute-start(f32[16,128]{1,0:T(8,128)S(1)} %get-tuple-element.91.refs_0_), channel_id=1, source_target_pairs={{0,2},{1,3},{2,0},{3,1},{4,6},{5,7},{6,4},{7,5},{8,10},{9,11},{10,... | collective-permute-start | bytes 24584 | tf_op jit(solution)/shard_map/ppermute | solution.py:395
  52.4 6.4 %collective-permute-start.29 = (f32[128,128]{1,0:T(8,128)S(1)}, f32[128,128]{1,0:T(8,128)S(1)}, u32[]{:S(2)}, u32[]{:S(2)}) collective-permute-start(f32[128,128]{1,0:T(8,128)S(1)} %get-tuple-element.98.refs_0_), channel_id=1, source_target_pairs={{0,1},{1,0},{2,3},{3,2},{4,5},{5,4},{6,7},{7,6},{8,9},{9,8},{10,11... | collective-permute-start | bytes 196616 | tf_op jit(solution)/shard_map/ppermute | solution.py:400
  55.5 5.3 %collective-permute-start.25 = (f32[264,128]{1,0:T(8,128)S(1)}, f32[264,128]{1,0:T(8,128)S(1)}, u32[]{:S(2)}, u32[]{:S(2)}) collective-permute-start(f32[264,128]{1,0:T(8,128)S(1)} %get-tuple-element.94.refs_0_), channel_id=1, source_target_pairs={{0,16},{16,0},{1,17},{17,1},{2,18},{18,2},{3,19},{19,3},{4,20},{20... | collective-permute-start | bytes 405512 | tf_op jit(solution)/shard_map/ppermute | solution.py:400
  56.3 4.5 %collective-permute-start.27 = (f32[144,128]{1,0:T(8,128)S(1)}, f32[144,128]{1,0:T(8,128)S(1)}, u32[]{:S(2)}, u32[]{:S(2)}) collective-permute-start(f32[144,128]{1,0:T(8,128)S(1)} %get-tuple-element.96.refs_3_), channel_id=1, source_target_pairs={{0,12},{4,8},{8,4},{12,0},{1,13},{5,9},{9,5},{13,1},{2,14},{6,10},... | collective-permute-start | bytes 221192 | tf_op jit(solution)/shard_map/ppermute | solution.py:400
  56.3 4.0 %collective-permute-start.28 = (f32[8,128]{1,0:T(8,128)S(1)}, f32[8,128]{1,0:T(8,128)S(1)}, u32[]{:S(2)}, u32[]{:S(2)}) collective-permute-start(f32[8,128]{1,0:T(8,128)S(1)} %get-tuple-element.97.refs_0_), channel_id=1, source_target_pairs={{0,28},{4,24},{8,20},{12,16},{16,12},{20,8},{24,4},{28,0},{1,29},{... | collective-permute-start | bytes 12296 | tf_op jit(solution)/shard_map/ppermute | solution.py:405
  (7 other events, 19.2 us)

commit v9 on v8

--- a/solution.py
+++ b/solution.py
@@ -102,6 +102,7 @@
 def send_rows(face, rows, at, o):
     n = rows.shape[0]
     o["t"][at:at + n, :] = rows
+    o["t2"][at:at + n, :] = rows
     o["zb"][face + at:face + at + n, :] = rows
 
 
@@ -126,7 +127,7 @@
 
 
 def first_kernel(face, nz, n_modes, turn, resid_hbm, schur_hbm, modes_hbm, coarse_hbm, *refs):
-    names = ["r0", "stack", "mt", "c_own", "y", "za", "zb", "t"]
+    names = ["r0", "stack", "mt", "c_own", "y", "za", "zb", "t", "t2"]
     o = dict(zip(names, refs[:len(names)]))
     resid, schur, mode_rows, coarse, sems = refs[len(names):]
     two = 2 * face
@@ -417,12 +418,13 @@
 
     def z_out(tiny, extra=0):
         return dict(y=sds((4 * face, loads)), za=sds((face + extra, loads)),
-                    zb=sds((face + tiny * PAD + extra, loads)), t=sds((tiny * PAD, loads)))
+                    zb=sds((face + tiny * PAD + extra, loads)), t=sds((tiny * PAD, loads)),
+                    t2=sds((tiny * PAD + PAD, loads)))
 
     def t_exchange(a, with_dots):
         got = dict(t=a["t"], y=a["y"])
         if small:
-            got.update(gzb=swap(a["zb"], "gz", 1), gt2=shift(a["t"], "gz", 2), gta=swap(a["t"], "gz", 0))
+            got.update(gzb=swap(a["zb"], "gz", 1), gt2=shift(a["t2"], "gz", 2), gta=swap(a["t"], "gz", 0))
         else:
             got["g_all"] = lax.all_gather(a["t"][0:PAD], "gz", axis=0, tiled=True)
             if with_dots:

time: 64.1 us -> 63.5 us (level)
  starting transfers between devices: 34.1 us -> 32.9 us
    ppermute x4, starting transfers between devices: 6.94 us -> 0.82 us  [shift(): return lax.ppermute(x, axis, [(k, (k + by) % n) for k in range(n)])]
    ppermute x26, starting transfers between devices: 24.7 us -> 29.7 us  [swap(): return lax.ppermute(x, axis, [(k, (k + side(k)) % n) for k in range(n)])]
    ppermute x26, waiting for transfers between devices: 14.9 us -> 16.5 us  [swap(): return lax.ppermute(x, axis, [(k, (k + side(k)) % n) for k in range(n)])]
    ppermute x4, waiting for transfers between devices: 3.55 us -> 2.52 us  [shift(): return lax.ppermute(x, axis, [(k, (k + by) % n) for k in range(n)])]
  transfers between devices with their start and end apart: 31 -> 31, of which waited for: 18 -> 17; matrix products, arithmetic and copies ran while one was open for 0% -> 0% of each run, Pallas kernels for 4% -> 4%
where the time goes in v9:
time: 63.5 us; the launch traced here: 63.3 us
  starting transfers between devices  32.9 us (52%)
  waiting for transfers between devices  20.5 us (32%)
  Pallas kernels  9.21 us (15%)
  between operations  0.75 us (1%)
    ppermute x26, starting transfers between devices, swap(): return lax.ppermute(x, axis, [(k, (k + side(k)) % n) for k in range(n)])  29.7 us
    ppermute x26, waiting for transfers between devices, swap(): return lax.ppermute(x, axis, [(k, (k + side(k)) % n) for k in range(n)])  16.5 us
    pallas_call x13, Pallas kernels, call(): pl.pallas_call(run, out_shape=[outs[n] for n in names_out], in_specs=[vme...  6.43 us
    pallas_call x1, Pallas kernels, body(): pl.pallas_call(functools.partial(first_kernel, face, nz, n_modes, small),...  2.78 us
    ppermute x4, waiting for transfers between devices, shift(): return lax.ppermute(x, axis, [(k, (k + by) % n) for k in range(n)])  2.52 us
    ppermute x1, starting transfers between devices, move(): return lax.ppermute(x, ('gx', 'gy'), pairs)  2.38 us
    ppermute x1, waiting for transfers between devices, move(): return lax.ppermute(x, ('gx', 'gy'), pairs)  1.48 us
  transfers between devices with their start and end apart: 31, of which 17 were waited for; matrix products, arithmetic and copies ran while one was open for 0% of the time, Pallas kernels for 4%

profile of v9, /device:TPU:0, one launch (start us, length us, event | category | flops | bytes accessed | tf_op | source)
XLA Modules:
  0.0 63.3 jit_solution(8100427274559803107)
XLA Ops:
  0.6 2.8 %shard_map.59 = (f32[768,128]{1,0:T(8,128)S(1)}, bf16[1568,768]{1,0:T(8,128)(2,1)S(1)}, bf16[768,48]{1,0:T(8,128)(2,1)S(1)}, f32[8,128]{1,0:T(8,128)S(1)}, f32[5...) custom-call(f32[128,768]{1,0:T(8,128)} %bitcast.7, ...), custom_call_target="tpu_custom_call" | custom-call | flops 603979776 | bytes 2359296 | tf_op jit(solution)/shard_map/pallas_call | solution.py:476
  3.4 5.1 %collective-permute-start = (f32[160,128]{1,0:T(8,128)S(1)}, f32[160,128]{1,0:T(8,128)S(1)}, u32[]{:S(2)}, u32[]{:S(2)}) collective-permute-start(f32[160,128]{1,0:T(8,128)S(1)} %get-tuple-element.60.refs_1_), channel_id=1, source_target_pairs={{0,3},{1,2},{2,1},{3,0},{4,7},{5,6},{6,5},{7,4},{8,11},{9,10},{10,... | collective-permute-start | bytes 245768 | tf_op jit(solution)/shard_map/ppermute | solution.py:401
  9.2 1.4 %collective-permute-start.6 = (f32[136,128]{1,0:T(8,128)S(1)}, f32[136,128]{1,0:T(8,128)S(1)}, u32[]{:S(2)}, u32[]{:S(2)}) collective-permute-start(f32[136,128]{1,0:T(8,128)S(1)} %get-tuple-element.67.refs_0_), channel_id=1, source_target_pairs={{0,1},{1,0},{2,3},{3,2},{4,5},{5,4},{6,7},{7,6},{8,9},{9,8},{10,11... | collective-permute-start | bytes 208904 | tf_op jit(solution)/shard_map/ppermute | solution.py:401
  10.6 1.8 %collective-permute-done.2.refs_4_ = f32[24,128]{1,0:T(8,128)S(1)} collective-permute-done((f32[24,128]{1,0:T(8,128)S(1)}, f32[24,128]{1,0:T(8,128)S(1)}, u32[]{:S(2)}, u32[]{:S(2)}) %collective-permute-start.2) | collective-permute-done | bytes 12320 | tf_op jit(solution)/shard_map/ppermute | solution.py:401
  13.7 1.6 %collective-permute-start.3 = (f32[264,128]{1,0:T(8,128)S(1)}, f32[264,128]{1,0:T(8,128)S(1)}, u32[]{:S(2)}, u32[]{:S(2)}) collective-permute-start(f32[264,128]{1,0:T(8,128)S(1)} %get-tuple-element.64.refs_0_), channel_id=1, source_target_pairs={{0,16},{16,0},{1,17},{17,1},{2,18},{18,2},{3,19},{19,3},{4,20},{20... | collective-permute-start | bytes 405512 | tf_op jit(solution)/shard_map/ppermute | solution.py:401
  15.3 1.6 %collective-permute-start.4 = (f32[136,128]{1,0:T(8,128)S(1)}, f32[136,128]{1,0:T(8,128)S(1)}, u32[]{:S(2)}, u32[]{:S(2)}) collective-permute-start(f32[136,128]{1,0:T(8,128)S(1)} %get-tuple-element.65.refs_2_), channel_id=1, source_target_pairs={{0,4},{4,0},{8,12},{12,8},{1,5},{5,1},{9,13},{13,9},{2,6},{6,2},{1... | collective-permute-start | bytes 208904 | tf_op jit(solution)/shard_map/ppermute | solution.py:401
  17.8 2.0 %collective-permute-done.5.refs_5_ = f32[144,128]{1,0:T(8,128)S(1)} collective-permute-done((f32[144,128]{1,0:T(8,128)S(1)}, f32[144,128]{1,0:T(8,128)S(1)}, u32[]{:S(2)}, u32[]{:S(2)}) %collective-permute-start.5) | collective-permute-done | bytes 73760 | tf_op jit(solution)/shard_map/ppermute | solution.py:401
  20.6 2.3 %collective-permute-start.7 = (f32[144,128]{1,0:T(8,128)S(1)}, f32[144,128]{1,0:T(8,128)S(1)}, u32[]{:S(2)}, u32[]{:S(2)}) collective-permute-start(f32[144,128]{1,0:T(8,128)S(1)} %get-tuple-element.73.refs_1_), channel_id=1, source_target_pairs={{0,3},{1,2},{2,1},{3,0},{4,7},{5,6},{6,5},{7,4},{8,11},{9,10},{10,... | collective-permute-start | bytes 221192 | tf_op jit(solution)/shard_map/ppermute | solution.py:401
  23.0 2.1 %collective-permute-start.9 = (f32[16,128]{1,0:T(8,128)S(1)}, f32[16,128]{1,0:T(8,128)S(1)}, u32[]{:S(2)}, u32[]{:S(2)}) collective-permute-start(f32[16,128]{1,0:T(8,128)S(1)} %get-tuple-element.71.refs_0_), channel_id=1, source_target_pairs={{0,1},{1,0},{2,3},{3,2},{4,5},{5,4},{6,7},{7,6},{8,9},{9,8},{10,11... | collective-permute-start | bytes 24584 | tf_op jit(solution)/shard_map/ppermute | solution.py:401
  25.1 2.0 %collective-permute-done.9.refs_4_ = f32[16,128]{1,0:T(8,128)S(1)} collective-permute-done((f32[16,128]{1,0:T(8,128)S(1)}, f32[16,128]{1,0:T(8,128)S(1)}, u32[]{:S(2)}, u32[]{:S(2)}) %collective-permute-start.9) | collective-permute-done | bytes 8224 | tf_op jit(solution)/shard_map/ppermute | solution.py:401
  28.5 1.6 %collective-permute-start.11 = (f32[136,128]{1,0:T(8,128)S(1)}, f32[136,128]{1,0:T(8,128)S(1)}, u32[]{:S(2)}, u32[]{:S(2)}) collective-permute-start(f32[136,128]{1,0:T(8,128)S(1)} %get-tuple-element.78.refs_2_), channel_id=1, source_target_pairs={{0,4},{4,0},{8,12},{12,8},{1,5},{5,1},{9,13},{13,9},{2,6},{6,2},{1... | collective-permute-start | bytes 208904 | tf_op jit(solution)/shard_map/ppermute | solution.py:401
  30.9 2.1 %collective-permute-done.12.refs_5_ = f32[144,128]{1,0:T(8,128)S(1)} collective-permute-done((f32[144,128]{1,0:T(8,128)S(1)}, f32[144,128]{1,0:T(8,128)S(1)}, u32[]{:S(2)}, u32[]{:S(2)}) %collective-permute-start.12) | collective-permute-done | bytes 73760 | tf_op jit(solution)/shard_map/ppermute | solution.py:401
  33.9 2.4 %collective-permute-start.14 = (f32[136,128]{1,0:T(8,128)S(1)}, f32[136,128]{1,0:T(8,128)S(1)}, u32[]{:S(2)}, u32[]{:S(2)}) collective-permute-start(f32[136,128]{1,0:T(8,128)S(1)} %get-tuple-element.86.refs_1_), channel_id=1, source_target_pairs={{0,3},{1,2},{2,1},{3,0},{4,7},{5,6},{6,5},{7,4},{8,11},{9,10},{10,... | collective-permute-start | bytes 208904 | tf_op jit(solution)/shard_map/ppermute | solution.py:401
  36.5 1.8 %collective-permute-start.16 = (f32[8,128]{1,0:T(8,128)S(1)}, f32[8,128]{1,0:T(8,128)S(1)}, u32[]{:S(2)}, u32[]{:S(2)}) collective-permute-start(f32[8,128]{1,0:T(8,128)S(1)} %get-tuple-element.84.refs_0_), channel_id=1, source_target_pairs={{0,1},{1,0},{2,3},{3,2},{4,5},{5,4},{6,7},{7,6},{8,9},{9,8},{10,11... | collective-permute-start | bytes 12296 | tf_op jit(solution)/shard_map/ppermute | solution.py:401
  38.6 1.6 %collective-permute-done.16.refs_4_ = f32[8,128]{1,0:T(8,128)S(1)} collective-permute-done((f32[8,128]{1,0:T(8,128)S(1)}, f32[8,128]{1,0:T(8,128)S(1)}, u32[]{:S(2)}, u32[]{:S(2)}) %collective-permute-start.16) | collective-permute-done | bytes 4128 | tf_op jit(solution)/shard_map/ppermute | solution.py:401
  42.2 1.3 %collective-permute-start.19 = (f32[128,128]{1,0:T(8,128)S(1)}, f32[128,128]{1,0:T(8,128)S(1)}, u32[]{:S(2)}, u32[]{:S(2)}) collective-permute-start(f32[128,128]{1,0:T(8,128)S(1)} %get-tuple-element.90.refs_2_), channel_id=1, source_target_pairs={{0,4},{4,0},{8,12},{12,8},{1,5},{5,1},{9,13},{13,9},{2,6},{6,2},{1... | collective-permute-start | bytes 196616 | tf_op jit(solution)/shard_map/ppermute | solution.py:401
  44.4 2.1 %collective-permute-done.20.refs_5_ = f32[144,128]{1,0:T(8,128)S(1)} collective-permute-done((f32[144,128]{1,0:T(8,128)S(1)}, f32[144,128]{1,0:T(8,128)S(1)}, u32[]{:S(2)}, u32[]{:S(2)}) %collective-permute-start.20) | collective-permute-done | bytes 73760 | tf_op jit(solution)/shard_map/ppermute | solution.py:401
  46.5 1.1 %shard_map.68 = (f32[768,128]{1,0:T(8,128)S(1)}, f32[768,128]{1,0:T(8,128)S(1)}, f32[768,128]{1,0:T(8,128)S(1)}, f32[8,128]{1,0:T(8,128)S(1)}, f32[512,128]{1,0:...) custom-call(f32[264,128]{1,0:T(8,128)S(1)} %get-tuple-element.89.ref, ...), custom_call_target="tpu_custom_call" | custom-call | flops 603979776 | bytes 5881856 | tf_op jit(solution)/shard_map/pallas_call | solution.py:31
  47.6 2.1 %collective-permute-start.22 = (f32[144,128]{1,0:T(8,128)S(1)}, f32[144,128]{1,0:T(8,128)S(1)}, u32[]{:S(2)}, u32[]{:S(2)}) collective-permute-start(f32[144,128]{1,0:T(8,128)S(1)} %get-tuple-element.100.refs_1_), channel_id=1, source_target_pairs={{0,3},{1,2},{2,1},{3,0},{4,7},{5,6},{6,5},{7,4},{8,11},{9,10},{10,... | collective-permute-start | bytes 221192 | tf_op jit(solution)/shard_map/ppermute | solution.py:401
  50.2 1.9 %collective-permute-start.24 = (f32[16,128]{1,0:T(8,128)S(1)}, f32[16,128]{1,0:T(8,128)S(1)}, u32[]{:S(2)}, u32[]{:S(2)}) collective-permute-start(f32[16,128]{1,0:T(8,128)S(1)} %get-tuple-element.98.refs_0_), channel_id=1, source_target_pairs={{0,1},{1,0},{2,3},{3,2},{4,5},{5,4},{6,7},{7,6},{8,9},{9,8},{10,11... | collective-permute-start | bytes 24584 | tf_op jit(solution)/shard_map/ppermute | solution.py:401
  52.2 1.9 %collective-permute-done.24.refs_4_ = f32[16,128]{1,0:T(8,128)S(1)} collective-permute-done((f32[16,128]{1,0:T(8,128)S(1)}, f32[16,128]{1,0:T(8,128)S(1)}, u32[]{:S(2)}, u32[]{:S(2)}) %collective-permute-start.24) | collective-permute-done | bytes 8224 | tf_op jit(solution)/shard_map/ppermute | solution.py:401
  55.9 2.4 %collective-permute-start.28 = (f32[8,128]{1,0:T(8,128)S(1)}, f32[8,128]{1,0:T(8,128)S(1)}, u32[]{:S(2)}, u32[]{:S(2)}) collective-permute-start(f32[8,128]{1,0:T(8,128)S(1)} %get-tuple-element.105.refs_0_), channel_id=1, source_target_pairs={{0,28},{4,24},{8,20},{12,16},{16,12},{20,8},{24,4},{28,0},{1,29},{... | collective-permute-start | bytes 12296 | tf_op jit(solution)/shard_map/ppermute | solution.py:406
  58.5 1.5 %collective-permute-done.28.refs_1_ = f32[8,128]{1,0:T(8,128)S(1)} collective-permute-done((f32[8,128]{1,0:T(8,128)S(1)}, f32[8,128]{1,0:T(8,128)S(1)}, u32[]{:S(2)}, u32[]{:S(2)}) %collective-permute-start.28) | collective-permute-done | bytes 4128 | tf_op jit(solution)/shard_map/ppermute | solution.py:406
  62.0 1.4 %shard_map.72 = (f32[128,768]{1,0:T(8,128)}, f32[128,768]{1,0:T(8,128)}) custom-call(f32[264,128]{1,0:T(8,128)S(1)} %get-tuple-element.102.refs_0_, f32[264,128]{1,0:T(8,128)S(1)} %collective-permute-done.25.refs_2_.refs_1_, f32[136,128]{1,0:T(8,128)S(1)} %get-tuple-element.103.refs_2_, f32[144,128]{1,0:T(8,128)S(1)} %get-tuple-element.104.refs_3_, ...), custom_call_target="tpu_custom_call" | custom-call | bytes 3452928 | tf_op jit(solution)/shard_map/pallas_call | solution.py:31
  (53 shorter events, 14.9 us)
Async XLA Ops:
  3.4 9.9 %collective-permute-start = (f32[160,128]{1,0:T(8,128)S(1)}, f32[160,128]{1,0:T(8,128)S(1)}, u32[]{:S(2)}, u32[]{:S(2)}) collective-permute-start(f32[160,128]{1,0:T(8,128)S(1)} %get-tuple-element.60.refs_1_), channel_id=1, source_target_pairs={{0,3},{1,2},{2,1},{3,0},{4,7},{5,6},{6,5},{7,4},{8,11},{9,10},{10,... | collective-permute-start | bytes 245768 | tf_op jit(solution)/shard_map/ppermute | solution.py:401
  8.5 4.7 %collective-permute-start.1 = (f32[32,128]{1,0:T(8,128)S(1)}, f32[32,128]{1,0:T(8,128)S(1)}, u32[]{:S(2)}, u32[]{:S(2)}) collective-permute-start(f32[32,128]{1,0:T(8,128)S(1)} %get-tuple-element.61), channel_id=1, source_target_pairs={{0,2},{1,3},{2,0},{3,1},{4,6},{5,7},{6,4},{7,5},{8,10},{9,11},{10,... | collective-permute-start | bytes 49160 | tf_op jit(solution)/shard_map/ppermute | solution.py:396
  9.2 7.7 %collective-permute-start.6 = (f32[136,128]{1,0:T(8,128)S(1)}, f32[136,128]{1,0:T(8,128)S(1)}, u32[]{:S(2)}, u32[]{:S(2)}) collective-permute-start(f32[136,128]{1,0:T(8,128)S(1)} %get-tuple-element.67.refs_0_), channel_id=1, source_target_pairs={{0,1},{1,0},{2,3},{3,2},{4,5},{5,4},{6,7},{7,6},{8,9},{9,8},{10,11... | collective-permute-start | bytes 208904 | tf_op jit(solution)/shard_map/ppermute | solution.py:401
  13.7 6.1 %collective-permute-start.3 = (f32[264,128]{1,0:T(8,128)S(1)}, f32[264,128]{1,0:T(8,128)S(1)}, u32[]{:S(2)}, u32[]{:S(2)}) collective-permute-start(f32[264,128]{1,0:T(8,128)S(1)} %get-tuple-element.64.refs_0_), channel_id=1, source_target_pairs={{0,16},{16,0},{1,17},{17,1},{2,18},{18,2},{3,19},{19,3},{4,20},{20... | collective-permute-start | bytes 405512 | tf_op jit(solution)/shard_map/ppermute | solution.py:401
  15.2 4.5 %collective-permute-start.5 = (f32[144,128]{1,0:T(8,128)S(1)}, f32[144,128]{1,0:T(8,128)S(1)}, u32[]{:S(2)}, u32[]{:S(2)}) collective-permute-start(f32[144,128]{1,0:T(8,128)S(1)} %get-tuple-element.66.refs_3_), channel_id=1, source_target_pairs={{0,12},{4,8},{8,4},{12,0},{1,13},{5,9},{9,5},{13,1},{2,14},{6,10},... | collective-permute-start | bytes 221192 | tf_op jit(solution)/shard_map/ppermute | solution.py:401
  20.6 6.9 %collective-permute-start.7 = (f32[144,128]{1,0:T(8,128)S(1)}, f32[144,128]{1,0:T(8,128)S(1)}, u32[]{:S(2)}, u32[]{:S(2)}) collective-permute-start(f32[144,128]{1,0:T(8,128)S(1)} %get-tuple-element.73.refs_1_), channel_id=1, source_target_pairs={{0,3},{1,2},{2,1},{3,0},{4,7},{5,6},{6,5},{7,4},{8,11},{9,10},{10,... | collective-permute-start | bytes 221192 | tf_op jit(solution)/shard_map/ppermute | solution.py:401
  22.9 4.6 %collective-permute-start.8 = (f32[24,128]{1,0:T(8,128)S(1)}, f32[24,128]{1,0:T(8,128)S(1)}, u32[]{:S(2)}, u32[]{:S(2)}) collective-permute-start(f32[24,128]{1,0:T(8,128)S(1)} %get-tuple-element.74), channel_id=1, source_target_pairs={{0,2},{1,3},{2,0},{3,1},{4,6},{5,7},{6,4},{7,5},{8,10},{9,11},{10,... | collective-permute-start | bytes 36872 | tf_op jit(solution)/shard_map/ppermute | solution.py:396
  23.0 4.2 %collective-permute-start.9 = (f32[16,128]{1,0:T(8,128)S(1)}, f32[16,128]{1,0:T(8,128)S(1)}, u32[]{:S(2)}, u32[]{:S(2)}) collective-permute-start(f32[16,128]{1,0:T(8,128)S(1)} %get-tuple-element.71.refs_0_), channel_id=1, source_target_pairs={{0,1},{1,0},{2,3},{3,2},{4,5},{5,4},{6,7},{7,6},{8,9},{9,8},{10,11... | collective-permute-start | bytes 24584 | tf_op jit(solution)/shard_map/ppermute | solution.py:401
  25.1 5.0 %collective-permute-start.13 = (f32[128,128]{1,0:T(8,128)S(1)}, f32[128,128]{1,0:T(8,128)S(1)}, u32[]{:S(2)}, u32[]{:S(2)}) collective-permute-start(f32[128,128]{1,0:T(8,128)S(1)} %get-tuple-element.80.refs_0_), channel_id=1, source_target_pairs={{0,1},{1,0},{2,3},{3,2},{4,5},{5,4},{6,7},{7,6},{8,9},{9,8},{10,11... | collective-permute-start | bytes 196616 | tf_op jit(solution)/shard_map/ppermute | solution.py:401
  27.8 5.2 %collective-permute-start.10 = (f32[264,128]{1,0:T(8,128)S(1)}, f32[264,128]{1,0:T(8,128)S(1)}, u32[]{:S(2)}, u32[]{:S(2)}) collective-permute-start(f32[264,128]{1,0:T(8,128)S(1)} %get-tuple-element.77.refs_0_), channel_id=1, source_target_pairs={{0,16},{16,0},{1,17},{17,1},{2,18},{18,2},{3,19},{19,3},{4,20},{20... | collective-permute-start | bytes 405512 | tf_op jit(solution)/shard_map/ppermute | solution.py:401
  28.5 4.6 %collective-permute-start.12 = (f32[144,128]{1,0:T(8,128)S(1)}, f32[144,128]{1,0:T(8,128)S(1)}, u32[]{:S(2)}, u32[]{:S(2)}) collective-permute-start(f32[144,128]{1,0:T(8,128)S(1)} %get-tuple-element.79.refs_3_), channel_id=1, source_target_pairs={{0,12},{4,8},{8,4},{12,0},{1,13},{5,9},{9,5},{13,1},{2,14},{6,10},... | collective-permute-start | bytes 221192 | tf_op jit(solution)/shard_map/ppermute | solution.py:401
  33.9 7.0 %collective-permute-start.14 = (f32[136,128]{1,0:T(8,128)S(1)}, f32[136,128]{1,0:T(8,128)S(1)}, u32[]{:S(2)}, u32[]{:S(2)}) collective-permute-start(f32[136,128]{1,0:T(8,128)S(1)} %get-tuple-element.86.refs_1_), channel_id=1, source_target_pairs={{0,3},{1,2},{2,1},{3,0},{4,7},{5,6},{6,5},{7,4},{8,11},{9,10},{10,... | collective-permute-start | bytes 208904 | tf_op jit(solution)/shard_map/ppermute | solution.py:401
  36.3 4.0 %collective-permute-start.17 = (f32[16,128]{1,0:T(8,128)S(1)}, f32[16,128]{1,0:T(8,128)S(1)}, u32[]{:S(2)}, u32[]{:S(2)}) collective-permute-start(f32[16,128]{1,0:T(8,128)S(1)} %slice.3), channel_id=1, source_target_pairs={{0,4},{4,0},{8,12},{12,8},{1,5},{5,1},{9,13},{13,9},{2,6},{6,2},{1... | collective-permute-start | bytes 24584 | tf_op jit(solution)/shard_map/ppermute | solution.py:401
  36.3 4.5 %collective-permute-start.15 = (f32[16,128]{1,0:T(8,128)S(1)}, f32[16,128]{1,0:T(8,128)S(1)}, u32[]{:S(2)}, u32[]{:S(2)}) collective-permute-start(f32[16,128]{1,0:T(8,128)S(1)} %get-tuple-element.87), channel_id=1, source_target_pairs={{0,2},{1,3},{2,0},{3,1},{4,6},{5,7},{6,4},{7,5},{8,10},{9,11},{10,... | collective-permute-start | bytes 24584 | tf_op jit(solution)/shard_map/ppermute | solution.py:396
  38.3 5.2 %collective-permute-start.21 = (f32[128,128]{1,0:T(8,128)S(1)}, f32[128,128]{1,0:T(8,128)S(1)}, u32[]{:S(2)}, u32[]{:S(2)}) collective-permute-start(f32[128,128]{1,0:T(8,128)S(1)} %get-tuple-element.92.refs_0_), channel_id=1, source_target_pairs={{0,1},{1,0},{2,3},{3,2},{4,5},{5,4},{6,7},{7,6},{8,9},{9,8},{10,11... | collective-permute-start | bytes 196616 | tf_op jit(solution)/shard_map/ppermute | solution.py:401
  41.2 5.4 %collective-permute-start.18 = (f32[264,128]{1,0:T(8,128)S(1)}, f32[264,128]{1,0:T(8,128)S(1)}, u32[]{:S(2)}, u32[]{:S(2)}) collective-permute-start(f32[264,128]{1,0:T(8,128)S(1)} %get-tuple-element.89.refs_0_), channel_id=1, source_target_pairs={{0,16},{16,0},{1,17},{17,1},{2,18},{18,2},{3,19},{19,3},{4,20},{20... | collective-permute-start | bytes 405512 | tf_op jit(solution)/shard_map/ppermute | solution.py:401
  42.2 4.3 %collective-permute-start.20 = (f32[144,128]{1,0:T(8,128)S(1)}, f32[144,128]{1,0:T(8,128)S(1)}, u32[]{:S(2)}, u32[]{:S(2)}) collective-permute-start(f32[144,128]{1,0:T(8,128)S(1)} %get-tuple-element.91.refs_3_), channel_id=1, source_target_pairs={{0,12},{4,8},{8,4},{12,0},{1,13},{5,9},{9,5},{13,1},{2,14},{6,10},... | collective-permute-start | bytes 221192 | tf_op jit(solution)/shard_map/ppermute | solution.py:401
  47.6 7.1 %collective-permute-start.22 = (f32[144,128]{1,0:T(8,128)S(1)}, f32[144,128]{1,0:T(8,128)S(1)}, u32[]{:S(2)}, u32[]{:S(2)}) collective-permute-start(f32[144,128]{1,0:T(8,128)S(1)} %get-tuple-element.100.refs_1_), channel_id=1, source_target_pairs={{0,3},{1,2},{2,1},{3,0},{4,7},{5,6},{6,5},{7,4},{8,11},{9,10},{10,... | collective-permute-start | bytes 221192 | tf_op jit(solution)/shard_map/ppermute | solution.py:401
  49.7 5.0 %collective-permute-start.23 = (f32[24,128]{1,0:T(8,128)S(1)}, f32[24,128]{1,0:T(8,128)S(1)}, u32[]{:S(2)}, u32[]{:S(2)}) collective-permute-start(f32[24,128]{1,0:T(8,128)S(1)} %get-tuple-element.101), channel_id=1, source_target_pairs={{0,2},{1,3},{2,0},{3,1},{4,6},{5,7},{6,4},{7,5},{8,10},{9,11},{10,... | collective-permute-start | bytes 36872 | tf_op jit(solution)/shard_map/ppermute | solution.py:396
  50.2 3.9 %collective-permute-start.24 = (f32[16,128]{1,0:T(8,128)S(1)}, f32[16,128]{1,0:T(8,128)S(1)}, u32[]{:S(2)}, u32[]{:S(2)}) collective-permute-start(f32[16,128]{1,0:T(8,128)S(1)} %get-tuple-element.98.refs_0_), channel_id=1, source_target_pairs={{0,1},{1,0},{2,3},{3,2},{4,5},{5,4},{6,7},{7,6},{8,9},{9,8},{10,11... | collective-permute-start | bytes 24584 | tf_op jit(solution)/shard_map/ppermute | solution.py:401
  52.1 6.3 %collective-permute-start.29 = (f32[128,128]{1,0:T(8,128)S(1)}, f32[128,128]{1,0:T(8,128)S(1)}, u32[]{:S(2)}, u32[]{:S(2)}) collective-permute-start(f32[128,128]{1,0:T(8,128)S(1)} %get-tuple-element.106.refs_0_), channel_id=1, source_target_pairs={{0,1},{1,0},{2,3},{3,2},{4,5},{5,4},{6,7},{7,6},{8,9},{9,8},{10,11... | collective-permute-start | bytes 196616 | tf_op jit(solution)/shard_map/ppermute | solution.py:401
  55.0 5.1 %collective-permute-start.25 = (f32[264,128]{1,0:T(8,128)S(1)}, f32[264,128]{1,0:T(8,128)S(1)}, u32[]{:S(2)}, u32[]{:S(2)}) collective-permute-start(f32[264,128]{1,0:T(8,128)S(1)} %get-tuple-element.102.refs_0_), channel_id=1, source_target_pairs={{0,16},{16,0},{1,17},{17,1},{2,18},{18,2},{3,19},{19,3},{4,20},{20... | collective-permute-start | bytes 405512 | tf_op jit(solution)/shard_map/ppermute | solution.py:401
  55.9 4.2 %collective-permute-start.27 = (f32[144,128]{1,0:T(8,128)S(1)}, f32[144,128]{1,0:T(8,128)S(1)}, u32[]{:S(2)}, u32[]{:S(2)}) collective-permute-start(f32[144,128]{1,0:T(8,128)S(1)} %get-tuple-element.104.refs_3_), channel_id=1, source_target_pairs={{0,12},{4,8},{8,4},{12,0},{1,13},{5,9},{9,5},{13,1},{2,14},{6,10},... | collective-permute-start | bytes 221192 | tf_op jit(solution)/shard_map/ppermute | solution.py:401
  55.9 4.0 %collective-permute-start.28 = (f32[8,128]{1,0:T(8,128)S(1)}, f32[8,128]{1,0:T(8,128)S(1)}, u32[]{:S(2)}, u32[]{:S(2)}) collective-permute-start(f32[8,128]{1,0:T(8,128)S(1)} %get-tuple-element.105.refs_0_), channel_id=1, source_target_pairs={{0,28},{4,24},{8,20},{12,16},{16,12},{20,8},{24,4},{28,0},{1,29},{... | collective-permute-start | bytes 12296 | tf_op jit(solution)/shard_map/ppermute | solution.py:406
  (7 other events, 19.3 us)

commit v10 on v9

--- a/solution.py
+++ b/solution.py
@@ -12,7 +12,7 @@
 HI = lax.Precision.HIGHEST
 PAD = 8
 VMEM_LIMIT = 24 * 1024 * 1024
-Z_FLOPS = 770000000
+EARLY_FLOPS = 150000000
 
 
 def sds(shape, dtype=F32):
@@ -92,8 +92,11 @@
 
 
 def store_product(face, part, y, o):
-    if part < 2:
-        o["y"][2 * part * face:2 * (part + 1) * face, :] = y
+    if part == 0:
+        o["xa"][0:face, :] = y[0:face]
+        o["y"][0:face, :] = y[face:]
+    elif part == 1:
+        o["y"][face:3 * face, :] = y
     else:
         o["za"][0:face, :] = y[0:face]
         o["zb"][0:face, :] = y[face:]
@@ -127,7 +130,7 @@
 
 
 def first_kernel(face, nz, n_modes, turn, resid_hbm, schur_hbm, modes_hbm, coarse_hbm, *refs):
-    names = ["r0", "stack", "mt", "c_own", "y", "za", "zb", "t", "t2"]
+    names = ["r0", "stack", "mt", "c_own", "y", "xa", "za", "zb", "t", "t2"]
     o = dict(zip(names, refs[:len(names)]))
     resid, schur, mode_rows, coarse, sems = refs[len(names):]
     two = 2 * face
@@ -181,6 +184,7 @@
     o["c_own"][...] = ordered
     if turn:
         send_rows(face, ordered, 2 * PAD, o)
+    o["xa"][face:face + PAD, :] = modes[:, 0:face]
     o["za"][face:face + PAD, :] = modes[:, 4 * face:5 * face]
     o["zb"][face + 3 * PAD:face + 4 * PAD, :] = modes[:, 5 * face:6 * face]
 
@@ -200,18 +204,24 @@
             i["gzb"][face + at:face + at + PAD, :], i["gt2"][at:at + PAD, :]]
 
 
-def z_kernel(face, i, o):
+def early_kernel(face, i, o):
+    amp, mt = i["amp"], i["mt"]
+    own = amp_pieces(amp[0:PAD, :])
+    got_modes = {}
+    for name in ("x", "a", "b"):
+        if "mt_" + name in o:
+            rows = i["gxa" if name == "x" else "gz" + name][-PAD:, :]
+            got_modes[name] = mode_pieces(rows)
+            o["mt_" + name][...] = got_modes[name]
+        else:
+            got_modes[name] = i["mt_" + name]
     for k, name in enumerate(("a", "b")):
-        if "mt_" + name in o:
-            got_modes = mode_pieces(i["gz" + name][-PAD:, :])
-            o["mt_" + name][...] = got_modes
-        else:
-            got_modes = i["mt_" + name][...]
-        amp = i["amp"]
-        own = i["z" + name][0:face, :] + dot16(i["mt"][(4 + k) * face:(5 + k) * face, :], amp_pieces(amp[0:PAD, :]))
+        mine = i["z" + name][0:face, :] + dot16(mt[(4 + k) * face:(5 + k) * face, :], own)
         at = (1 + k) * PAD
-        got = i["gz" + name][0:face, :] + dot16(got_modes, amp_pieces(amp[at:at + PAD, :]))
-        o["z"][k * face:(k + 1) * face, :] = own - got
+        got = i["gz" + name][0:face, :] + dot16(got_modes[name][...], amp_pieces(amp[at:at + PAD, :]))
+        o["z"][k * face:(k + 1) * face, :] = mine - got
+    o["xa"][...] = i["xa"][0:face, :] + dot16(mt[0:face, :], own)
+    o["gxa"][...] = i["gxa"][0:face, :]
 
 
 def value_kernel(face, stage, i, o):
@@ -226,7 +236,7 @@
         coarse = i["c_all"][...]
     amp = dot32(coarse, loads)
     o["amp"][...] = amp[0:3 * PAD]
-    xy = i["y"][...] + dot16(i["mt"][0:4 * face, :], amp_pieces(amp[0:PAD]))
+    xy = i["y"][...] + dot16(i["mt"][face:4 * face, :], amp_pieces(amp[0:PAD]))
     cols = loads.shape[1]
 
     if stage != 2:
@@ -243,13 +253,14 @@
         dots = jnp.concatenate([i["first"][0:2, :], dots[0:2], dots[4:]], axis=0)
     elif stage == 2 and "swapped" in i:
         dots = six_columns(i, o)
-    o["xab"][0:2 * face, :] = xy[0:2 * face]
-    o["ya"][0:face, :] = xy[2 * face:3 * face]
-    o["yb"][0:face, :] = xy[3 * face:]
+    o["xb"][0:face, :] = xy[0:face]
+    o["xb"][face:face + PAD, :] = amp[0:PAD]
+    o["ya"][0:face, :] = xy[face:2 * face]
+    o["yb"][0:face, :] = xy[2 * face:]
     if stage == 3:
         o["dots"][...] = dots
     if stage != 2 or "swapped" in i:
-        o["xab"][2 * face:, :] = dots
+        o["xb"][face + PAD:, :] = dots
     if stage != 2:
         o["ya"][face:face + PAD, :] = dots
         o["yb"][face:face + PAD, :] = dots
@@ -257,12 +268,12 @@
 
 def assemble(face, i, rates=None):
     f = face
-    got = [i["gxab"][0:2 * f, :], i["gya"][0:f, :], i["gyb"][0:f, :]]
+    amp = i["gamp"][...] if "gamp" in i else i["gxb"][f:f + PAD, :]
+    got = [i["gxa"][...] + dot16(i["mt_x"][...], amp_pieces(amp)), i["gxb"][0:f, :], i["gya"][0:f, :], i["gyb"][0:f, :]]
     if rates is not None:
-        got = [rate * face_values for rate, face_values in zip(rates, got)]
-    return jnp.concatenate([
-        i["xab"][0:2 * f, :] - got[0], i["ya"][0:f, :] - got[1], i["yb"][0:f, :] - got[2], i["z"][...],
-    ], axis=0)
+        got = [rate * values for rate, values in zip(rates[0:1] + rates, got)]
+    own = [i["xa"][...], i["xb"][0:f, :], i["ya"][0:f, :], i["yb"][0:f, :]]
+    return jnp.concatenate([mine - other for mine, other in zip(own, got)] + [i["z"][...]], axis=0)
 
 
 def column_scale(dots):
@@ -279,11 +290,11 @@
 def second_kernel(face, i, o):
     w0 = assemble(face, i)
     o["w0"][...] = w0
-    first = i["xab"][2 * face:2 * face + PAD, :]
+    first = i["xb"][face + PAD:face + 2 * PAD, :]
     scale = column_scale(first)
     cols = w0.shape[1]
     rates = [scale / column_scale(i[name][at:at + PAD, :])
-             for name, at in (("gxab", 2 * face), ("gya", face), ("gyb", face))]
+             for name, at in (("gxb", face + PAD), ("gya", face), ("gyb", face))]
     o["first"][...] = stack_rows([row(first, 0), row(first, 1), scale] + rates, cols)
     vec = scale * w0
     curv = product(face, vec, i["stack"], o)
@@ -296,8 +307,8 @@
     o["q"][...] = q
     if "near" in o:
         partners = [rescale(i[name][at:at + PAD, :], rate) for rate, name, at in zip(
-            rates, ("gxab", "gya", "gyb"), (2 * face, face, face))]
-        o["near"][...] = jnp.concatenate([partners[0], partners[2], partners[1] + i["xab"][2 * face:, :]], axis=0)
+            rates, ("gxb", "gya", "gyb"), (face + PAD, face, face))]
+        o["near"][...] = jnp.concatenate([partners[0], partners[2], partners[1] + i["xb"][face + PAD:, :]], axis=0)
     product(face, scale * q, i["stack"], o)
 
 
@@ -313,7 +324,7 @@
     scale, *rates = (row(i["first"], k) for k in range(2, 6))
     sums = i["six"][...]
     if "whole" not in i:
-        sums = sums + rescale(i["gxab"][2 * face:, :], rates[0])
+        sums = sums + rescale(i["gxb"][face + PAD:, :], rates[0])
     m0, m1 = row(sums, 0), row(sums, 1)
     alpha0 = m0 / m1
     ratio0 = alpha0 / scale
@@ -344,7 +355,7 @@
 
 
 def four_kernel(face, i, o):
-    near = i["dots"][...] + i["gxab"][2 * face:2 * face + PAD, :]
+    near = i["dots"][...] + i["gxb"][face + PAD:face + 2 * PAD, :]
     o["part"][...] = near + (i["across"][...] + i["gyb"][face:face + PAD, :])
 
 
@@ -417,7 +428,7 @@
     flops = 2 * width * width * 2 * loads * 2
 
     def z_out(tiny, extra=0):
-        return dict(y=sds((4 * face, loads)), za=sds((face + extra, loads)),
+        return dict(y=sds((3 * face, loads)), xa=sds((face + extra, loads)), za=sds((face + extra, loads)),
                     zb=sds((face + tiny * PAD + extra, loads)), t=sds((tiny * PAD, loads)),
                     t2=sds((tiny * PAD + PAD, loads)))
 
@@ -431,20 +442,20 @@
                 got["d_all"] = lax.psum(a["t"][PAD:2 * PAD], "gz")
         return got
 
-    def z_faces(a, v, t, modes=None):
+    def early_faces(a, v, t, modes=None):
         ins = dict(za=a["za"], zb=a["zb"], gzb=t["gzb"] if small else swap(a["zb"], "gz", 1),
-                   gza=swap(a["za"], "gz", 0), mt=mt, amp=v["amp"])
-        outs = dict(z=sds((2 * face, loads)))
+                   gza=swap(a["za"], "gz", 0), xa=a["xa"], gxa=swap(a["xa"], "gx", 0), mt=mt, amp=v["amp"])
+        outs = dict(z=sds((2 * face, loads)), xa=sds((face, loads)), gxa=sds((face, loads)))
         if modes is None:
-            outs.update(mt_a=sds((face, 6 * PAD), BF16), mt_b=sds((face, 6 * PAD), BF16))
+            outs.update({name: sds((face, 6 * PAD), BF16) for name in ("mt_x", "mt_a", "mt_b")})
         else:
             ins.update(modes)
-        return call(functools.partial(z_kernel, face), ins, outs, flops=Z_FLOPS)
+        return call(functools.partial(early_kernel, face), ins, outs, flops=EARLY_FLOPS)
 
     def value(stage, ins):
         extra = 0 if stage == 2 else PAD
-        outs = dict(amp=sds((3 * PAD, loads)), xab=sds((2 * face + (PAD if small else extra), loads)),
-                    ya=sds((face + extra, loads)), yb=sds((face + 2 * PAD, loads)))
+        outs = dict(amp=sds((3 * PAD, loads)), xb=sds((face + PAD + (PAD if small else extra), loads)),
+                    ya=sds((face + extra, loads)), yb=sds((face + 3 * PAD, loads)))
         if stage == 0 and small:
             outs["c_all"] = sds((nz * PAD, nz * PAD))
         if stage == 2 and small:
@@ -453,21 +464,19 @@
             outs["dots"] = rows
         return call(functools.partial(value_kernel, face, stage), ins, outs, flops=2 * width * loads * 48)
 
-    def x_exchange(v):
-        got = dict(xab=v["xab"])
-        if nx == 2:
-            got["gxab"] = swap(v["xab"], "gx", 0)
-        else:
-            a, b, rest = v["xab"][:face], v["xab"][face:2 * face], v["xab"][2 * face:]
-            got["gxab"] = jnp.concatenate([swap(a, "gx", 0), swap(b, "gx", 1), rest], axis=0)
+    def x_exchange(v, early):
+        got = dict(xb=v["xb"], gxb=swap(v["xb"], "gx", 0 if nx == 2 else 1), mt_x=got_modes["mt_x"])
+        got.update({name: early[name] for name in ("z", "xa", "gxa")})
+        if nx != 2:
+            got["gamp"] = swap(v["amp"][0:PAD], "gx", 0)
         return got
 
     def y_exchange(v):
         gyb = swap(v["yb"], "gy", 1)
         return dict(ya=v["ya"], yb=v["yb"], gya=swap(v["ya"], "gy", 0), gyb=gyb)
 
-    def xy_exchange(v):
-        return dict(x_exchange(v), **y_exchange(v))
+    def xy_exchange(v, early):
+        return dict(x_exchange(v, early), **y_exchange(v))
 
     hbm = pl.BlockSpec(memory_space=pltpu.HBM)
     vmem = pl.BlockSpec(memory_space=pltpu.VMEM)
@@ -499,16 +508,16 @@
     t = ins
     v = value(0, ins)
     column = dict(mt=mt, c_all=v["c_all"] if small else ins["c_all"])
-    z = z_faces(a, v, t)
-    got_modes = dict(mt_a=z["mt_a"], mt_b=z["mt_b"])
-    x = dict(xy_exchange(v), z=z["z"])
+    early = early_faces(a, v, t)
+    got_modes = {name: early[name] for name in ("mt_x", "mt_a", "mt_b")}
+    x = xy_exchange(v, early)
 
     a = call(functools.partial(second_kernel, face), dict(x, stack=stack),
              dict(w0=vec, first=rows, **z_out(2)), flops=flops)
     w0, first = a["w0"], a["first"]
     t = t_exchange(a, True)
     v = value(1, dict(t, **column, first=first))
-    x = dict(xy_exchange(v), z=z_faces(a, v, t, got_modes)["z"])
+    x = xy_exchange(v, early_faces(a, v, t, got_modes))
 
     near = dict(near=sds((3 * PAD, loads))) if small else {}
     a = call(functools.partial(third_kernel, face), dict(x, stack=stack, first=first),
@@ -521,29 +530,29 @@
         v = value(2, ins)
         sums = dict(six=v["six"])
     else:
-        sums = dict(six=total(v["xab"][2 * face:], first[2:3]), whole=first)
+        sums = dict(six=total(v["xb"][face + PAD:], first[2:3]), whole=first)
         v = value(2, ins)
-    x = dict(xy_exchange(v), z=z_faces(a, v, t, got_modes)["z"])
+    x = xy_exchange(v, early_faces(a, v, t, got_modes))
 
     a = call(functools.partial(fourth_kernel, face),
              dict(x, stack=stack, **sums, first=first, r0=r0, w0=w0, q=q),
              dict(w2=vec, s1=vec, z1=vec, known=rows, **z_out(2)), flops=flops)
     t = t_exchange(a, True)
     v = value(3, dict(t, **column))
-    z = z_faces(a, v, t, got_modes)["z"]
+    early = early_faces(a, v, t, got_modes)
     if small:
-        x = x_exchange(v)
+        x = x_exchange(v, early)
         across = move(v["dots"], lambda a, b: (1 - a, (b + (-1 if b % 2 == 0 else 1)) % ny))
         x.update(y_exchange(v))
         part = call(functools.partial(four_kernel, face),
-                    dict(dots=v["dots"], across=across, gxab=x["gxab"], gyb=x["gyb"], z=z), dict(part=rows))["part"]
+                    dict(dots=v["dots"], across=across, gxb=x["gxb"], gyb=x["gyb"], z=early["z"]), dict(part=rows))["part"]
         sums = dict(sum_near=part, sum_far=swap(part, "gy", 0))
     else:
-        x = xy_exchange(v)
+        x = xy_exchange(v, early)
         sums = dict(sum_near=lax.psum(v["dots"], ("gx", "gy")), sum_far=jnp.zeros((PAD, loads), F32))
     out = sds((loads, width))
     res = call(functools.partial(last_kernel, face),
-               dict(x, **sums, z=z, r0=r0, w0=w0, **{name: a[name] for name in ("known", "w2", "s1", "z1")}),
+               dict(x, **sums, r0=r0, w0=w0, **{name: a[name] for name in ("known", "w2", "s1", "z1")}),
                dict(mult=out, resid=out))
     return (res["mult"][None, None, None], res["resid"][None, None, None])
 

time: 63.5 us -> 64 us (level)
  starting transfers between devices: 32.9 us -> 36.7 us
  waiting for transfers between devices: 20.5 us -> 17 us
    ppermute x26 -> x30, starting transfers between devices: 29.7 us -> 34.2 us  [swap(): return lax.ppermute(x, axis, [(k, (k + side(k)) % n) for k in range(n)])]
    ppermute x26 -> x30, waiting for transfers between devices: 16.5 us -> 12.7 us  [swap(): return lax.ppermute(x, axis, [(k, (k + side(k)) % n) for k in range(n)])]
    ppermute x1, waiting for transfers between devices: 1.48 us -> 2.56 us  [move(): return lax.ppermute(x, ('gx', 'gy'), pairs)]
    ppermute x1, starting transfers between devices: 2.38 us -> 1.52 us  [move(): return lax.ppermute(x, ('gx', 'gy'), pairs)]
    ppermute x4, waiting for transfers between devices: 2.52 us -> 1.75 us  [shift(): return lax.ppermute(x, axis, [(k, (k + by) % n) for k in range(n)])]
  transfers between devices with their start and end apart: 31 -> 35, of which waited for: 17 -> 15; matrix products, arithmetic and copies ran while one was open for 0% -> 0% of each run, Pallas kernels for 4% -> 4%
where the time goes in v10:
time: 64 us; the launch traced here: 63.9 us
  starting transfers between devices  36.7 us (57%)
  waiting for transfers between devices  17 us (27%)
  Pallas kernels  9.47 us (15%)
  between operations  0.78 us (1%)
    ppermute x30, starting transfers between devices, swap(): return lax.ppermute(x, axis, [(k, (k + side(k)) % n) for k in range(n)])  34.2 us
    ppermute x30, waiting for transfers between devices, swap(): return lax.ppermute(x, axis, [(k, (k + side(k)) % n) for k in range(n)])  12.7 us
    pallas_call x13, Pallas kernels, call(): pl.pallas_call(run, out_shape=[outs[n] for n in names_out], in_specs=[vme...  6.68 us
    pallas_call x1, Pallas kernels, body(): pl.pallas_call(functools.partial(first_kernel, face, nz, n_modes, small),...  2.78 us
    ppermute x1, waiting for transfers between devices, move(): return lax.ppermute(x, ('gx', 'gy'), pairs)  2.56 us
    ppermute x4, waiting for transfers between devices, shift(): return lax.ppermute(x, axis, [(k, (k + by) % n) for k in range(n)])  1.75 us
    ppermute x1, starting transfers between devices, move(): return lax.ppermute(x, ('gx', 'gy'), pairs)  1.52 us
  transfers between devices with their start and end apart: 35, of which 15 were waited for; matrix products, arithmetic and copies ran while one was open for 0% of the time, Pallas kernels for 4%

profile of v10, /device:TPU:0, one launch (start us, length us, event | category | flops | bytes accessed | tf_op | source)
XLA Modules:
  0.0 63.9 jit_solution(4008973096457431361)
XLA Ops:
  0.6 2.8 %shard_map.59 = (f32[768,128]{1,0:T(8,128)S(1)}, bf16[1568,768]{1,0:T(8,128)(2,1)S(1)}, bf16[768,48]{1,0:T(8,128)(2,1)S(1)}, f32[8,128]{1,0:T(8,128)S(1)}, f32[3...) custom-call(f32[128,768]{1,0:T(8,128)} %bitcast.7, ...), custom_call_target="tpu_custom_call" | custom-call | flops 603979776 | bytes 2359296 | tf_op jit(solution)/shard_map/pallas_call | solution.py:485
  3.4 5.1 %collective-permute-start = (f32[160,128]{1,0:T(8,128)S(1)}, f32[160,128]{1,0:T(8,128)S(1)}, u32[]{:S(2)}, u32[]{:S(2)}) collective-permute-start(f32[160,128]{1,0:T(8,128)S(1)} %get-tuple-element.76.refs_1_), channel_id=1, source_target_pairs={{0,3},{1,2},{2,1},{3,0},{4,7},{5,6},{6,5},{7,4},{8,11},{9,10},{10,... | collective-permute-start | bytes 245768 | tf_op jit(solution)/shard_map/ppermute | solution.py:412
  9.2 1.4 %collective-permute-start.4 = (f32[136,128]{1,0:T(8,128)S(1)}, f32[136,128]{1,0:T(8,128)S(1)}, u32[]{:S(2)}, u32[]{:S(2)}) collective-permute-start(f32[136,128]{1,0:T(8,128)S(1)} %get-tuple-element.81.refs_0_), channel_id=1, source_target_pairs={{0,1},{1,0},{2,3},{3,2},{4,5},{5,4},{6,7},{7,6},{8,9},{9,8},{10,11... | collective-permute-start | bytes 208904 | tf_op jit(solution)/shard_map/ppermute | solution.py:412
  10.6 1.5 %collective-permute-start.5 = (f32[136,128]{1,0:T(8,128)S(1)}, f32[136,128]{1,0:T(8,128)S(1)}, u32[]{:S(2)}, u32[]{:S(2)}) collective-permute-start(f32[136,128]{1,0:T(8,128)S(1)} %get-tuple-element.82.refs_4_), channel_id=1, source_target_pairs={{0,16},{16,0},{1,17},{17,1},{2,18},{18,2},{3,19},{19,3},{4,20},{20... | collective-permute-start | bytes 208904 | tf_op jit(solution)/shard_map/ppermute | solution.py:412
  13.8 1.6 %collective-permute-start.3 = (f32[144,128]{1,0:T(8,128)S(1)}, f32[144,128]{1,0:T(8,128)S(1)}, u32[]{:S(2)}, u32[]{:S(2)}) collective-permute-start(f32[144,128]{1,0:T(8,128)S(1)} %get-tuple-element.80.refs_0_), channel_id=1, source_target_pairs={{0,16},{16,0},{1,17},{17,1},{2,18},{18,2},{3,19},{19,3},{4,20},{20... | collective-permute-start | bytes 221192 | tf_op jit(solution)/shard_map/ppermute | solution.py:412
  15.3 1.3 %collective-permute-start.6 = (f32[136,128]{1,0:T(8,128)S(1)}, f32[136,128]{1,0:T(8,128)S(1)}, u32[]{:S(2)}, u32[]{:S(2)}) collective-permute-start(f32[136,128]{1,0:T(8,128)S(1)} %get-tuple-element.88.refs_6_), channel_id=1, source_target_pairs={{0,4},{4,0},{8,12},{12,8},{1,5},{5,1},{9,13},{13,9},{2,6},{6,2},{1... | collective-permute-start | bytes 208904 | tf_op jit(solution)/shard_map/ppermute | solution.py:412
  19.4 2.3 %collective-permute-start.8 = (f32[144,128]{1,0:T(8,128)S(1)}, f32[144,128]{1,0:T(8,128)S(1)}, u32[]{:S(2)}, u32[]{:S(2)}) collective-permute-start(f32[144,128]{1,0:T(8,128)S(1)} %get-tuple-element.93.refs_1_), channel_id=1, source_target_pairs={{0,3},{1,2},{2,1},{3,0},{4,7},{5,6},{6,5},{7,4},{8,11},{9,10},{10,... | collective-permute-start | bytes 221192 | tf_op jit(solution)/shard_map/ppermute | solution.py:412
  21.8 2.1 %collective-permute-start.10 = (f32[16,128]{1,0:T(8,128)S(1)}, f32[16,128]{1,0:T(8,128)S(1)}, u32[]{:S(2)}, u32[]{:S(2)}) collective-permute-start(f32[16,128]{1,0:T(8,128)S(1)} %get-tuple-element.91.refs_0_), channel_id=1, source_target_pairs={{0,1},{1,0},{2,3},{3,2},{4,5},{5,4},{6,7},{7,6},{8,9},{9,8},{10,11... | collective-permute-start | bytes 24584 | tf_op jit(solution)/shard_map/ppermute | solution.py:412
  23.9 1.5 %collective-permute-start.13 = (f32[128,128]{1,0:T(8,128)S(1)}, f32[128,128]{1,0:T(8,128)S(1)}, u32[]{:S(2)}, u32[]{:S(2)}) collective-permute-start(f32[128,128]{1,0:T(8,128)S(1)} %get-tuple-element.99.refs_4_), channel_id=1, source_target_pairs={{0,16},{16,0},{1,17},{17,1},{2,18},{18,2},{3,19},{19,3},{4,20},{20... | collective-permute-start | bytes 196616 | tf_op jit(solution)/shard_map/ppermute | solution.py:412
  27.3 1.5 %collective-permute-start.11 = (f32[144,128]{1,0:T(8,128)S(1)}, f32[144,128]{1,0:T(8,128)S(1)}, u32[]{:S(2)}, u32[]{:S(2)}) collective-permute-start(f32[144,128]{1,0:T(8,128)S(1)} %get-tuple-element.97.refs_0_), channel_id=1, source_target_pairs={{0,16},{16,0},{1,17},{17,1},{2,18},{18,2},{3,19},{19,3},{4,20},{20... | collective-permute-start | bytes 221192 | tf_op jit(solution)/shard_map/ppermute | solution.py:412
  30.5 1.8 %collective-permute-done.11.refs_1_ = f32[144,128]{1,0:T(8,128)S(1)} collective-permute-done((f32[144,128]{1,0:T(8,128)S(1)}, f32[144,128]{1,0:T(8,128)S(1)}, u32[]{:S(2)}, u32[]{:S(2)}) %collective-permute-start.11) | collective-permute-done | bytes 73760 | tf_op jit(solution)/shard_map/ppermute | solution.py:412
  33.3 1.7 %collective-permute-start.16 = (f32[136,128]{1,0:T(8,128)S(1)}, f32[136,128]{1,0:T(8,128)S(1)}, u32[]{:S(2)}, u32[]{:S(2)}) collective-permute-start(f32[136,128]{1,0:T(8,128)S(1)} %get-tuple-element.110.refs_1_), channel_id=1, source_target_pairs={{0,3},{1,2},{2,1},{3,0},{4,7},{5,6},{6,5},{7,4},{8,11},{9,10},{10,... | collective-permute-start | bytes 208904 | tf_op jit(solution)/shard_map/ppermute | solution.py:412
  35.1 2.6 %collective-permute-start.18 = (f32[8,128]{1,0:T(8,128)S(1)}, f32[8,128]{1,0:T(8,128)S(1)}, u32[]{:S(2)}, u32[]{:S(2)}) collective-permute-start(f32[8,128]{1,0:T(8,128)S(1)} %get-tuple-element.108.refs_0_), channel_id=1, source_target_pairs={{0,1},{1,0},{2,3},{3,2},{4,5},{5,4},{6,7},{7,6},{8,9},{9,8},{10,11... | collective-permute-start | bytes 12296 | tf_op jit(solution)/shard_map/ppermute | solution.py:412
  37.8 1.8 %collective-permute-done.18.refs_4_ = f32[8,128]{1,0:T(8,128)S(1)} collective-permute-done((f32[8,128]{1,0:T(8,128)S(1)}, f32[8,128]{1,0:T(8,128)S(1)}, u32[]{:S(2)}, u32[]{:S(2)}) %collective-permute-start.18) | collective-permute-done | bytes 4128 | tf_op jit(solution)/shard_map/ppermute | solution.py:412
  39.6 1.5 %collective-permute-start.22 = (f32[128,128]{1,0:T(8,128)S(1)}, f32[128,128]{1,0:T(8,128)S(1)}, u32[]{:S(2)}, u32[]{:S(2)}) collective-permute-start(f32[128,128]{1,0:T(8,128)S(1)} %get-tuple-element.115.refs_4_), channel_id=1, source_target_pairs={{0,16},{16,0},{1,17},{17,1},{2,18},{18,2},{3,19},{19,3},{4,20},{20... | collective-permute-start | bytes 196616 | tf_op jit(solution)/shard_map/ppermute | solution.py:412
  44.1 2.6 %collective-permute-done.20.refs_1_ = f32[144,128]{1,0:T(8,128)S(1)} collective-permute-done((f32[144,128]{1,0:T(8,128)S(1)}, f32[144,128]{1,0:T(8,128)S(1)}, u32[]{:S(2)}, u32[]{:S(2)}) %collective-permute-start.20) | collective-permute-done | bytes 73760 | tf_op jit(solution)/shard_map/ppermute | solution.py:412
  46.6 1.1 %shard_map.68 = (f32[768,128]{1,0:T(8,128)S(1)}, f32[768,128]{1,0:T(8,128)S(1)}, f32[768,128]{1,0:T(8,128)S(1)}, f32[8,128]{1,0:T(8,128)S(1)}, f32[384,128]{1,0:...) custom-call(f32[144,128]{1,0:T(8,128)S(1)} %get-tuple-element.113.re, ...), custom_call_target="tpu_custom_call" | custom-call | flops 603979776 | bytes 5910528 | tf_op jit(solution)/shard_map/pallas_call | solution.py:31
  47.8 2.4 %collective-permute-start.25 = (f32[144,128]{1,0:T(8,128)S(1)}, f32[144,128]{1,0:T(8,128)S(1)}, u32[]{:S(2)}, u32[]{:S(2)}) collective-permute-start(f32[144,128]{1,0:T(8,128)S(1)} %get-tuple-element.128.refs_1_), channel_id=1, source_target_pairs={{0,3},{1,2},{2,1},{3,0},{4,7},{5,6},{6,5},{7,4},{8,11},{9,10},{10,... | collective-permute-start | bytes 221192 | tf_op jit(solution)/shard_map/ppermute | solution.py:412
  51.0 1.2 %collective-permute-start.27 = (f32[16,128]{1,0:T(8,128)S(1)}, f32[16,128]{1,0:T(8,128)S(1)}, u32[]{:S(2)}, u32[]{:S(2)}) collective-permute-start(f32[16,128]{1,0:T(8,128)S(1)} %get-tuple-element.126.refs_0_), channel_id=1, source_target_pairs={{0,1},{1,0},{2,3},{3,2},{4,5},{5,4},{6,7},{7,6},{8,9},{9,8},{10,11... | collective-permute-start | bytes 24584 | tf_op jit(solution)/shard_map/ppermute | solution.py:412
  53.5 1.2 %collective-permute-done.27.refs_4_ = f32[16,128]{1,0:T(8,128)S(1)} collective-permute-done((f32[16,128]{1,0:T(8,128)S(1)}, f32[16,128]{1,0:T(8,128)S(1)}, u32[]{:S(2)}, u32[]{:S(2)}) %collective-permute-start.27) | collective-permute-done | bytes 8224 | tf_op jit(solution)/shard_map/ppermute | solution.py:412
  56.9 1.5 %collective-permute-start.33 = (f32[8,128]{1,0:T(8,128)S(1)}, f32[8,128]{1,0:T(8,128)S(1)}, u32[]{:S(2)}, u32[]{:S(2)}) collective-permute-start(f32[8,128]{1,0:T(8,128)S(1)} %get-tuple-element.139.refs_0_), channel_id=1, source_target_pairs={{0,28},{4,24},{8,20},{12,16},{16,12},{20,8},{24,4},{28,0},{1,29},{... | collective-permute-start | bytes 12296 | tf_op jit(solution)/shard_map/ppermute | solution.py:417
  58.6 2.6 %collective-permute-done.33.refs_1_ = f32[8,128]{1,0:T(8,128)S(1)} collective-permute-done((f32[8,128]{1,0:T(8,128)S(1)}, f32[8,128]{1,0:T(8,128)S(1)}, u32[]{:S(2)}, u32[]{:S(2)}) %collective-permute-start.33) | collective-permute-done | bytes 4128 | tf_op jit(solution)/shard_map/ppermute | solution.py:417
  61.3 1.1 %collective-permute-done.34.refs_11_ = f32[8,128]{1,0:T(8,128)S(1)} collective-permute-done((f32[8,128]{1,0:T(8,128)S(1)}, f32[8,128]{1,0:T(8,128)S(1)}, u32[]{:S(2)}, u32[]{:S(2)}) %collective-permute-start.34) | collective-permute-done | bytes 4128 | tf_op jit(solution)/shard_map/ppermute | solution.py:412
  62.4 1.4 %shard_map.72 = (f32[128,768]{1,0:T(8,128)}, f32[128,768]{1,0:T(8,128)}) custom-call(f32[144,128]{1,0:T(8,128)S(1)} %get-tuple-element.130.refs_0_, f32[144,128]{1,0:T(8,128)S(1)} %collective-permute-done.28.refs_2_.refs_1_, bf16[128,48]{1,0:T(8,128)(2,1)S(1)} %get-tuple-element.84.refs_2_.refs_8_, f32[256,128]{1,0:T(8,128)S(1)} %get-tuple-element.134.refs_4_.refs_3_, ...), custom_call_target="tpu_custom_call" | custom-call | bytes 3481600 | tf_op jit(solution)/shard_map/pallas_call | solution.py:31
  (61 shorter events, 17.4 us)
Async XLA Ops:
  3.4 9.9 %collective-permute-start = (f32[160,128]{1,0:T(8,128)S(1)}, f32[160,128]{1,0:T(8,128)S(1)}, u32[]{:S(2)}, u32[]{:S(2)}) collective-permute-start(f32[160,128]{1,0:T(8,128)S(1)} %get-tuple-element.76.refs_1_), channel_id=1, source_target_pairs={{0,3},{1,2},{2,1},{3,0},{4,7},{5,6},{6,5},{7,4},{8,11},{9,10},{10,... | collective-permute-start | bytes 245768 | tf_op jit(solution)/shard_map/ppermute | solution.py:412
  8.5 4.7 %collective-permute-start.1 = (f32[32,128]{1,0:T(8,128)S(1)}, f32[32,128]{1,0:T(8,128)S(1)}, u32[]{:S(2)}, u32[]{:S(2)}) collective-permute-start(f32[32,128]{1,0:T(8,128)S(1)} %get-tuple-element.77), channel_id=1, source_target_pairs={{0,2},{1,3},{2,0},{3,1},{4,6},{5,7},{6,4},{7,5},{8,10},{9,11},{10,... | collective-permute-start | bytes 49160 | tf_op jit(solution)/shard_map/ppermute | solution.py:407
  9.2 7.4 %collective-permute-start.4 = (f32[136,128]{1,0:T(8,128)S(1)}, f32[136,128]{1,0:T(8,128)S(1)}, u32[]{:S(2)}, u32[]{:S(2)}) collective-permute-start(f32[136,128]{1,0:T(8,128)S(1)} %get-tuple-element.81.refs_0_), channel_id=1, source_target_pairs={{0,1},{1,0},{2,3},{3,2},{4,5},{5,4},{6,7},{7,6},{8,9},{9,8},{10,11... | collective-permute-start | bytes 208904 | tf_op jit(solution)/shard_map/ppermute | solution.py:412
  10.6 6.0 %collective-permute-start.5 = (f32[136,128]{1,0:T(8,128)S(1)}, f32[136,128]{1,0:T(8,128)S(1)}, u32[]{:S(2)}, u32[]{:S(2)}) collective-permute-start(f32[136,128]{1,0:T(8,128)S(1)} %get-tuple-element.82.refs_4_), channel_id=1, source_target_pairs={{0,16},{16,0},{1,17},{17,1},{2,18},{18,2},{3,19},{19,3},{4,20},{20... | collective-permute-start | bytes 208904 | tf_op jit(solution)/shard_map/ppermute | solution.py:412
  13.7 4.8 %collective-permute-start.7 = (f32[152,128]{1,0:T(8,128)S(1)}, f32[152,128]{1,0:T(8,128)S(1)}, u32[]{:S(2)}, u32[]{:S(2)}) collective-permute-start(f32[152,128]{1,0:T(8,128)S(1)} %get-tuple-element.89.refs_7_), channel_id=1, source_target_pairs={{0,12},{4,8},{8,4},{12,0},{1,13},{5,9},{9,5},{13,1},{2,14},{6,10},... | collective-permute-start | bytes 233480 | tf_op jit(solution)/shard_map/ppermute | solution.py:412
  19.4 7.0 %collective-permute-start.8 = (f32[144,128]{1,0:T(8,128)S(1)}, f32[144,128]{1,0:T(8,128)S(1)}, u32[]{:S(2)}, u32[]{:S(2)}) collective-permute-start(f32[144,128]{1,0:T(8,128)S(1)} %get-tuple-element.93.refs_1_), channel_id=1, source_target_pairs={{0,3},{1,2},{2,1},{3,0},{4,7},{5,6},{6,5},{7,4},{8,11},{9,10},{10,... | collective-permute-start | bytes 221192 | tf_op jit(solution)/shard_map/ppermute | solution.py:412
  21.7 4.7 %collective-permute-start.9 = (f32[24,128]{1,0:T(8,128)S(1)}, f32[24,128]{1,0:T(8,128)S(1)}, u32[]{:S(2)}, u32[]{:S(2)}) collective-permute-start(f32[24,128]{1,0:T(8,128)S(1)} %get-tuple-element.94), channel_id=1, source_target_pairs={{0,2},{1,3},{2,0},{3,1},{4,6},{5,7},{6,4},{7,5},{8,10},{9,11},{10,... | collective-permute-start | bytes 36872 | tf_op jit(solution)/shard_map/ppermute | solution.py:407
  23.8 5.8 %collective-permute-start.12 = (f32[128,128]{1,0:T(8,128)S(1)}, f32[128,128]{1,0:T(8,128)S(1)}, u32[]{:S(2)}, u32[]{:S(2)}) collective-permute-start(f32[128,128]{1,0:T(8,128)S(1)} %get-tuple-element.98.refs_0_), channel_id=1, source_target_pairs={{0,1},{1,0},{2,3},{3,2},{4,5},{5,4},{6,7},{7,6},{8,9},{9,8},{10,11... | collective-permute-start | bytes 196616 | tf_op jit(solution)/shard_map/ppermute | solution.py:412
  23.9 5.8 %collective-permute-start.13 = (f32[128,128]{1,0:T(8,128)S(1)}, f32[128,128]{1,0:T(8,128)S(1)}, u32[]{:S(2)}, u32[]{:S(2)}) collective-permute-start(f32[128,128]{1,0:T(8,128)S(1)} %get-tuple-element.99.refs_4_), channel_id=1, source_target_pairs={{0,16},{16,0},{1,17},{17,1},{2,18},{18,2},{3,19},{19,3},{4,20},{20... | collective-permute-start | bytes 196616 | tf_op jit(solution)/shard_map/ppermute | solution.py:412
  26.7 5.6 %collective-permute-start.15 = (f32[152,128]{1,0:T(8,128)S(1)}, f32[152,128]{1,0:T(8,128)S(1)}, u32[]{:S(2)}, u32[]{:S(2)}) collective-permute-start(f32[152,128]{1,0:T(8,128)S(1)} %get-tuple-element.107.refs_7_), channel_id=1, source_target_pairs={{0,12},{4,8},{8,4},{12,0},{1,13},{5,9},{9,5},{13,1},{2,14},{6,10},... | collective-permute-start | bytes 233480 | tf_op jit(solution)/shard_map/ppermute | solution.py:412
  27.3 5.0 %collective-permute-start.11 = (f32[144,128]{1,0:T(8,128)S(1)}, f32[144,128]{1,0:T(8,128)S(1)}, u32[]{:S(2)}, u32[]{:S(2)}) collective-permute-start(f32[144,128]{1,0:T(8,128)S(1)} %get-tuple-element.97.refs_0_), channel_id=1, source_target_pairs={{0,16},{16,0},{1,17},{17,1},{2,18},{18,2},{3,19},{19,3},{4,20},{20... | collective-permute-start | bytes 221192 | tf_op jit(solution)/shard_map/ppermute | solution.py:412
  33.3 7.8 %collective-permute-start.16 = (f32[136,128]{1,0:T(8,128)S(1)}, f32[136,128]{1,0:T(8,128)S(1)}, u32[]{:S(2)}, u32[]{:S(2)}) collective-permute-start(f32[136,128]{1,0:T(8,128)S(1)} %get-tuple-element.110.refs_1_), channel_id=1, source_target_pairs={{0,3},{1,2},{2,1},{3,0},{4,7},{5,6},{6,5},{7,4},{8,11},{9,10},{10,... | collective-permute-start | bytes 208904 | tf_op jit(solution)/shard_map/ppermute | solution.py:412
  35.0 6.1 %collective-permute-start.19 = (f32[16,128]{1,0:T(8,128)S(1)}, f32[16,128]{1,0:T(8,128)S(1)}, u32[]{:S(2)}, u32[]{:S(2)}) collective-permute-start(f32[16,128]{1,0:T(8,128)S(1)} %slice.3), channel_id=1, source_target_pairs={{0,4},{4,0},{8,12},{12,8},{1,5},{5,1},{9,13},{13,9},{2,6},{6,2},{1... | collective-permute-start | bytes 24584 | tf_op jit(solution)/shard_map/ppermute | solution.py:412
  35.0 6.1 %collective-permute-start.17 = (f32[16,128]{1,0:T(8,128)S(1)}, f32[16,128]{1,0:T(8,128)S(1)}, u32[]{:S(2)}, u32[]{:S(2)}) collective-permute-start(f32[16,128]{1,0:T(8,128)S(1)} %get-tuple-element.111), channel_id=1, source_target_pairs={{0,2},{1,3},{2,0},{3,1},{4,6},{5,7},{6,4},{7,5},{8,10},{9,11},{10,... | collective-permute-start | bytes 24584 | tf_op jit(solution)/shard_map/ppermute | solution.py:407
  37.8 5.1 %collective-permute-start.21 = (f32[128,128]{1,0:T(8,128)S(1)}, f32[128,128]{1,0:T(8,128)S(1)}, u32[]{:S(2)}, u32[]{:S(2)}) collective-permute-start(f32[128,128]{1,0:T(8,128)S(1)} %get-tuple-element.114.refs_0_), channel_id=1, source_target_pairs={{0,1},{1,0},{2,3},{3,2},{4,5},{5,4},{6,7},{7,6},{8,9},{9,8},{10,11... | collective-permute-start | bytes 196616 | tf_op jit(solution)/shard_map/ppermute | solution.py:412
  41.5 5.2 %collective-permute-start.24 = (f32[152,128]{1,0:T(8,128)S(1)}, f32[152,128]{1,0:T(8,128)S(1)}, u32[]{:S(2)}, u32[]{:S(2)}) collective-permute-start(f32[152,128]{1,0:T(8,128)S(1)} %get-tuple-element.121.refs_7_), channel_id=1, source_target_pairs={{0,12},{4,8},{8,4},{12,0},{1,13},{5,9},{9,5},{13,1},{2,14},{6,10},... | collective-permute-start | bytes 233480 | tf_op jit(solution)/shard_map/ppermute | solution.py:412
  41.6 5.1 %collective-permute-start.20 = (f32[144,128]{1,0:T(8,128)S(1)}, f32[144,128]{1,0:T(8,128)S(1)}, u32[]{:S(2)}, u32[]{:S(2)}) collective-permute-start(f32[144,128]{1,0:T(8,128)S(1)} %get-tuple-element.113.refs_0_), channel_id=1, source_target_pairs={{0,16},{16,0},{1,17},{17,1},{2,18},{18,2},{3,19},{19,3},{4,20},{20... | collective-permute-start | bytes 221192 | tf_op jit(solution)/shard_map/ppermute | solution.py:412
  47.8 7.4 %collective-permute-start.25 = (f32[144,128]{1,0:T(8,128)S(1)}, f32[144,128]{1,0:T(8,128)S(1)}, u32[]{:S(2)}, u32[]{:S(2)}) collective-permute-start(f32[144,128]{1,0:T(8,128)S(1)} %get-tuple-element.128.refs_1_), channel_id=1, source_target_pairs={{0,3},{1,2},{2,1},{3,0},{4,7},{5,6},{6,5},{7,4},{8,11},{9,10},{10,... | collective-permute-start | bytes 221192 | tf_op jit(solution)/shard_map/ppermute | solution.py:412
  50.2 4.9 %collective-permute-start.26 = (f32[24,128]{1,0:T(8,128)S(1)}, f32[24,128]{1,0:T(8,128)S(1)}, u32[]{:S(2)}, u32[]{:S(2)}) collective-permute-start(f32[24,128]{1,0:T(8,128)S(1)} %get-tuple-element.129), channel_id=1, source_target_pairs={{0,2},{1,3},{2,0},{3,1},{4,6},{5,7},{6,4},{7,5},{8,10},{9,11},{10,... | collective-permute-start | bytes 36872 | tf_op jit(solution)/shard_map/ppermute | solution.py:407
  52.2 4.7 %collective-permute-start.29 = (f32[128,128]{1,0:T(8,128)S(1)}, f32[128,128]{1,0:T(8,128)S(1)}, u32[]{:S(2)}, u32[]{:S(2)}) collective-permute-start(f32[128,128]{1,0:T(8,128)S(1)} %get-tuple-element.131.refs_0_), channel_id=1, source_target_pairs={{0,1},{1,0},{2,3},{3,2},{4,5},{5,4},{6,7},{7,6},{8,9},{9,8},{10,11... | collective-permute-start | bytes 196616 | tf_op jit(solution)/shard_map/ppermute | solution.py:412
  53.0 5.5 %collective-permute-start.30 = (f32[128,128]{1,0:T(8,128)S(1)}, f32[128,128]{1,0:T(8,128)S(1)}, u32[]{:S(2)}, u32[]{:S(2)}) collective-permute-start(f32[128,128]{1,0:T(8,128)S(1)} %get-tuple-element.132.refs_4_), channel_id=1, source_target_pairs={{0,16},{16,0},{1,17},{17,1},{2,18},{18,2},{3,19},{19,3},{4,20},{20... | collective-permute-start | bytes 196616 | tf_op jit(solution)/shard_map/ppermute | solution.py:412
  55.5 5.8 %collective-permute-start.32 = (f32[152,128]{1,0:T(8,128)S(1)}, f32[152,128]{1,0:T(8,128)S(1)}, u32[]{:S(2)}, u32[]{:S(2)}) collective-permute-start(f32[152,128]{1,0:T(8,128)S(1)} %get-tuple-element.138.refs_7_), channel_id=1, source_target_pairs={{0,12},{4,8},{8,4},{12,0},{1,13},{5,9},{9,5},{13,1},{2,14},{6,10},... | collective-permute-start | bytes 233480 | tf_op jit(solution)/shard_map/ppermute | solution.py:412
  55.5 5.7 %collective-permute-start.28 = (f32[144,128]{1,0:T(8,128)S(1)}, f32[144,128]{1,0:T(8,128)S(1)}, u32[]{:S(2)}, u32[]{:S(2)}) collective-permute-start(f32[144,128]{1,0:T(8,128)S(1)} %get-tuple-element.130.refs_0_), channel_id=1, source_target_pairs={{0,16},{16,0},{1,17},{17,1},{2,18},{18,2},{3,19},{19,3},{4,20},{20... | collective-permute-start | bytes 221192 | tf_op jit(solution)/shard_map/ppermute | solution.py:412
  56.3 5.0 %collective-permute-start.31 = (f32[136,128]{1,0:T(8,128)S(1)}, f32[136,128]{1,0:T(8,128)S(1)}, u32[]{:S(2)}, u32[]{:S(2)}) collective-permute-start(f32[136,128]{1,0:T(8,128)S(1)} %get-tuple-element.137.refs_6_), channel_id=1, source_target_pairs={{0,4},{4,0},{8,12},{12,8},{1,5},{5,1},{9,13},{13,9},{2,6},{6,2},{1... | collective-permute-start | bytes 208904 | tf_op jit(solution)/shard_map/ppermute | solution.py:412
  (11 other events, 36.5 us)

commit v11 on v9

--- a/solution.py
+++ b/solution.py
@@ -348,10 +348,23 @@
     o["part"][...] = near + (i["across"][...] + i["gyb"][face:face + PAD, :])
 
 
-def last_kernel(face, i, o):
+def ready_kernel(face, i, o):
+    alpha1, alpha0, beta1 = (row(i["known"], k) for k in range(1, 4))
+    r0 = i["r0"][...]
+    r1 = r0 - alpha0 * i["w0"][...]
+    p1 = r1 + beta1 * r0
+    o["c3"][...] = assemble(face, i)
+    o["r2"][...] = r1 - i["s1"][...]
+    o["p1"][...] = p1
+    o["m2"][...] = alpha0 * r0 + alpha1 * p1
+
+
+def last_kernel(face, names, *refs):
+    i = dict(zip(names, refs))
+    mult_hbm, resid_hbm, mult_out, resid_out, sems = refs[len(names):]
     d = i["sum_near"][...] + i["sum_far"][...]
     rr, rw, ww, ws, ss, wc, sc, sz = (row(d, k) for k in range(8))
-    norm1, alpha1, alpha0, beta1 = (row(i["known"], k) for k in range(4))
+    norm1, alpha1 = row(i["known"], 0), row(i["known"], 1)
     beta2 = rr / norm1
     alpha2 = rr / (rw - beta2 * rr / alpha1)
     ratio = alpha2 / alpha1
@@ -361,23 +374,24 @@
     curv3 = curv3 + ratio2 * (wc + 2.0 * beta2 * sc + beta2 * beta2 * sz)
     beta3 = norm3 / rr
     alpha3 = norm3 / (curv3 - beta3 * norm3 / alpha2)
-    c3 = assemble(face, i)
-    w2, s1 = i["w2"][...], i["s1"][...]
-    r0 = i["r0"][...]
-    r1 = r0 - alpha0 * i["w0"][...]
-    p1 = r1 + beta1 * r0
-    r2 = r1 - s1
-    p2 = r2 + beta2 * p1
-    s2 = w2 + beta2 * s1
-    r3 = r2 - ratio * s2
-    w3 = w2 / alpha1 - ratio * (c3 + beta2 * i["z1"][...])
-    mult = (alpha0 * r0 + alpha1 * p1) + alpha2 * p2 + alpha3 * (r3 + beta3 * p2)
-    resid = r3 - alpha3 * (w3 + (beta3 / alpha1) * s2)
     places, signs = face_places(face)
+    copies = []
     for f in range(6):
         at = slice(f * face, (f + 1) * face)
-        o["mult"][:, pl.ds(places[f], face)] = signs[f] * mult[at, :].T
-        o["resid"][:, pl.ds(places[f], face)] = signs[f] * resid[at, :].T
+        w2, s1 = i["w2"][at, :], i["s1"][at, :]
+        p2 = i["r2"][at, :] + beta2 * i["p1"][at, :]
+        s2 = w2 + beta2 * s1
+        r3 = i["r2"][at, :] - ratio * s2
+        w3 = w2 / alpha1 - ratio * (i["c3"][at, :] + beta2 * i["z1"][at, :])
+        mult = i["m2"][at, :] + alpha2 * p2 + alpha3 * (r3 + beta3 * p2)
+        resid = r3 - alpha3 * (w3 + (beta3 / alpha1) * s2)
+        for k, (value, out, hbm) in enumerate(((mult, mult_out, mult_hbm), (resid, resid_out, resid_hbm))):
+            out[f] = (signs[f] * value).T
+            copy = pltpu.make_async_copy(out.at[f], hbm.at[:, pl.ds(places[f], face)], sems.at[2 * f + k])
+            copy.start()
+            copies.append(copy)
+    for copy in copies:
+        copy.wait()
 
 
 def body(sizes, residual_in, schur, modes, coarse_inv):
@@ -541,11 +555,22 @@
     else:
         x = xy_exchange(v)
         sums = dict(sum_near=lax.psum(v["dots"], ("gx", "gy")), sum_far=jnp.zeros((PAD, loads), F32))
+    ready = call(functools.partial(ready_kernel, face),
+                 dict(x, z=z, known=a["known"], s1=a["s1"], r0=r0, w0=w0),
+                 {name: vec for name in ("c3", "r2", "p1", "m2")}, flops=10 * width * loads)
+    ins = dict(sums, **ready, **{name: a[name] for name in ("known", "w2", "s1", "z1")})
     out = sds((loads, width))
-    res = call(functools.partial(last_kernel, face),
-               dict(x, **sums, z=z, r0=r0, w0=w0, **{name: a[name] for name in ("known", "w2", "s1", "z1")}),
-               dict(mult=out, resid=out))
-    return (res["mult"][None, None, None], res["resid"][None, None, None])
+    mult, final = pl.pallas_call(
+        functools.partial(last_kernel, face, list(ins)),
+        out_shape=[out, out],
+        in_specs=[vmem] * len(ins),
+        out_specs=[hbm, hbm],
+        scratch_shapes=[pltpu.VMEM((6, loads, face), F32), pltpu.VMEM((6, loads, face), F32),
+                        pltpu.SemaphoreType.DMA((12,))],
+        compiler_params=pltpu.CompilerParams(vmem_limit_bytes=VMEM_LIMIT),
+        cost_estimate=pl.CostEstimate(flops=20 * width * loads, bytes_accessed=9 * 4 * width * loads, transcendentals=0),
+    )(*ins.values())
+    return (mult[None, None, None], final[None, None, None])
 
 
 def solution(mesh):

time: 63.5 us -> 63.3 us (level)
    pallas_call x13, Pallas kernels: 6.43 us -> 5.25 us  [call(): pl.pallas_call(run, out_shape=[outs[n] for n in names_out], in_specs=[vme...]
    pallas_call x0 -> x1, Pallas kernels: none -> 1.16 us  [body(): pl.pallas_call(functools.partial(last_kernel, face, list(ins)), out_shape...]
where the time goes in v11:
time: 63.3 us; the launch traced here: 63.1 us
  starting transfers between devices  32.9 us (52%)
  waiting for transfers between devices  20.3 us (32%)
  Pallas kernels  9.19 us (15%)
  between operations  0.76 us (1%)
    ppermute x26, starting transfers between devices, swap(): return lax.ppermute(x, axis, [(k, (k + side(k)) % n) for k in range(n)])  29.7 us
    ppermute x26, waiting for transfers between devices, swap(): return lax.ppermute(x, axis, [(k, (k + side(k)) % n) for k in range(n)])  16.3 us
    pallas_call x13, Pallas kernels, call(): pl.pallas_call(run, out_shape=[outs[n] for n in names_out], in_specs=[vme...  5.25 us
    pallas_call x1, Pallas kernels, body(): pl.pallas_call(functools.partial(first_kernel, face, nz, n_modes, small),...  2.78 us
    ppermute x4, waiting for transfers between devices, shift(): return lax.ppermute(x, axis, [(k, (k + by) % n) for k in range(n)])  2.52 us
    ppermute x1, starting transfers between devices, move(): return lax.ppermute(x, ('gx', 'gy'), pairs)  2.38 us
    ppermute x1, waiting for transfers between devices, move(): return lax.ppermute(x, ('gx', 'gy'), pairs)  1.48 us
  transfers between devices with their start and end apart: 31, of which 17 were waited for; matrix products, arithmetic and copies ran while one was open for 0% of the time, Pallas kernels for 4%

profile of v11, /device:TPU:0, one launch (start us, length us, event | category | flops | bytes accessed | tf_op | source)
XLA Modules:
  0.0 63.1 jit_solution(12014402985607475491)
XLA Ops:
  0.6 2.8 %shard_map.59 = (f32[768,128]{1,0:T(8,128)S(1)}, bf16[1568,768]{1,0:T(8,128)(2,1)S(1)}, bf16[768,48]{1,0:T(8,128)(2,1)S(1)}, f32[8,128]{1,0:T(8,128)S(1)}, f32[5...) custom-call(f32[128,768]{1,0:T(8,128)} %bitcast.7, ...), custom_call_target="tpu_custom_call" | custom-call | flops 603979776 | bytes 2359296 | tf_op jit(solution)/shard_map/pallas_call | solution.py:490
  3.4 5.1 %collective-permute-start = (f32[160,128]{1,0:T(8,128)S(1)}, f32[160,128]{1,0:T(8,128)S(1)}, u32[]{:S(2)}, u32[]{:S(2)}) collective-permute-start(f32[160,128]{1,0:T(8,128)S(1)} %get-tuple-element.64.refs_1_), channel_id=1, source_target_pairs={{0,3},{1,2},{2,1},{3,0},{4,7},{5,6},{6,5},{7,4},{8,11},{9,10},{10,... | collective-permute-start | bytes 245768 | tf_op jit(solution)/shard_map/ppermute | solution.py:415
  9.2 1.4 %collective-permute-start.6 = (f32[136,128]{1,0:T(8,128)S(1)}, f32[136,128]{1,0:T(8,128)S(1)}, u32[]{:S(2)}, u32[]{:S(2)}) collective-permute-start(f32[136,128]{1,0:T(8,128)S(1)} %get-tuple-element.71.refs_0_), channel_id=1, source_target_pairs={{0,1},{1,0},{2,3},{3,2},{4,5},{5,4},{6,7},{7,6},{8,9},{9,8},{10,11... | collective-permute-start | bytes 208904 | tf_op jit(solution)/shard_map/ppermute | solution.py:415
  10.6 1.8 %collective-permute-done.2.refs_4_ = f32[24,128]{1,0:T(8,128)S(1)} collective-permute-done((f32[24,128]{1,0:T(8,128)S(1)}, f32[24,128]{1,0:T(8,128)S(1)}, u32[]{:S(2)}, u32[]{:S(2)}) %collective-permute-start.2) | collective-permute-done | bytes 12320 | tf_op jit(solution)/shard_map/ppermute | solution.py:415
  13.7 1.6 %collective-permute-start.3 = (f32[264,128]{1,0:T(8,128)S(1)}, f32[264,128]{1,0:T(8,128)S(1)}, u32[]{:S(2)}, u32[]{:S(2)}) collective-permute-start(f32[264,128]{1,0:T(8,128)S(1)} %get-tuple-element.68.refs_0_), channel_id=1, source_target_pairs={{0,16},{16,0},{1,17},{17,1},{2,18},{18,2},{3,19},{19,3},{4,20},{20... | collective-permute-start | bytes 405512 | tf_op jit(solution)/shard_map/ppermute | solution.py:415
  15.3 1.6 %collective-permute-start.4 = (f32[136,128]{1,0:T(8,128)S(1)}, f32[136,128]{1,0:T(8,128)S(1)}, u32[]{:S(2)}, u32[]{:S(2)}) collective-permute-start(f32[136,128]{1,0:T(8,128)S(1)} %get-tuple-element.69.refs_2_), channel_id=1, source_target_pairs={{0,4},{4,0},{8,12},{12,8},{1,5},{5,1},{9,13},{13,9},{2,6},{6,2},{1... | collective-permute-start | bytes 208904 | tf_op jit(solution)/shard_map/ppermute | solution.py:415
  17.8 2.0 %collective-permute-done.5.refs_5_ = f32[144,128]{1,0:T(8,128)S(1)} collective-permute-done((f32[144,128]{1,0:T(8,128)S(1)}, f32[144,128]{1,0:T(8,128)S(1)}, u32[]{:S(2)}, u32[]{:S(2)}) %collective-permute-start.5) | collective-permute-done | bytes 73760 | tf_op jit(solution)/shard_map/ppermute | solution.py:415
  20.6 2.3 %collective-permute-start.7 = (f32[144,128]{1,0:T(8,128)S(1)}, f32[144,128]{1,0:T(8,128)S(1)}, u32[]{:S(2)}, u32[]{:S(2)}) collective-permute-start(f32[144,128]{1,0:T(8,128)S(1)} %get-tuple-element.77.refs_1_), channel_id=1, source_target_pairs={{0,3},{1,2},{2,1},{3,0},{4,7},{5,6},{6,5},{7,4},{8,11},{9,10},{10,... | collective-permute-start | bytes 221192 | tf_op jit(solution)/shard_map/ppermute | solution.py:415
  23.0 2.1 %collective-permute-start.9 = (f32[16,128]{1,0:T(8,128)S(1)}, f32[16,128]{1,0:T(8,128)S(1)}, u32[]{:S(2)}, u32[]{:S(2)}) collective-permute-start(f32[16,128]{1,0:T(8,128)S(1)} %get-tuple-element.75.refs_0_), channel_id=1, source_target_pairs={{0,1},{1,0},{2,3},{3,2},{4,5},{5,4},{6,7},{7,6},{8,9},{9,8},{10,11... | collective-permute-start | bytes 24584 | tf_op jit(solution)/shard_map/ppermute | solution.py:415
  25.1 2.0 %collective-permute-done.9.refs_4_ = f32[16,128]{1,0:T(8,128)S(1)} collective-permute-done((f32[16,128]{1,0:T(8,128)S(1)}, f32[16,128]{1,0:T(8,128)S(1)}, u32[]{:S(2)}, u32[]{:S(2)}) %collective-permute-start.9) | collective-permute-done | bytes 8224 | tf_op jit(solution)/shard_map/ppermute | solution.py:415
  28.5 1.6 %collective-permute-start.11 = (f32[136,128]{1,0:T(8,128)S(1)}, f32[136,128]{1,0:T(8,128)S(1)}, u32[]{:S(2)}, u32[]{:S(2)}) collective-permute-start(f32[136,128]{1,0:T(8,128)S(1)} %get-tuple-element.82.refs_2_), channel_id=1, source_target_pairs={{0,4},{4,0},{8,12},{12,8},{1,5},{5,1},{9,13},{13,9},{2,6},{6,2},{1... | collective-permute-start | bytes 208904 | tf_op jit(solution)/shard_map/ppermute | solution.py:415
  30.9 2.1 %collective-permute-done.12.refs_5_ = f32[144,128]{1,0:T(8,128)S(1)} collective-permute-done((f32[144,128]{1,0:T(8,128)S(1)}, f32[144,128]{1,0:T(8,128)S(1)}, u32[]{:S(2)}, u32[]{:S(2)}) %collective-permute-start.12) | collective-permute-done | bytes 73760 | tf_op jit(solution)/shard_map/ppermute | solution.py:415
  33.9 2.4 %collective-permute-start.14 = (f32[136,128]{1,0:T(8,128)S(1)}, f32[136,128]{1,0:T(8,128)S(1)}, u32[]{:S(2)}, u32[]{:S(2)}) collective-permute-start(f32[136,128]{1,0:T(8,128)S(1)} %get-tuple-element.90.refs_1_), channel_id=1, source_target_pairs={{0,3},{1,2},{2,1},{3,0},{4,7},{5,6},{6,5},{7,4},{8,11},{9,10},{10,... | collective-permute-start | bytes 208904 | tf_op jit(solution)/shard_map/ppermute | solution.py:415
  36.5 1.8 %collective-permute-start.16 = (f32[8,128]{1,0:T(8,128)S(1)}, f32[8,128]{1,0:T(8,128)S(1)}, u32[]{:S(2)}, u32[]{:S(2)}) collective-permute-start(f32[8,128]{1,0:T(8,128)S(1)} %get-tuple-element.88.refs_0_), channel_id=1, source_target_pairs={{0,1},{1,0},{2,3},{3,2},{4,5},{5,4},{6,7},{7,6},{8,9},{9,8},{10,11... | collective-permute-start | bytes 12296 | tf_op jit(solution)/shard_map/ppermute | solution.py:415
  38.6 1.6 %collective-permute-done.16.refs_4_ = f32[8,128]{1,0:T(8,128)S(1)} collective-permute-done((f32[8,128]{1,0:T(8,128)S(1)}, f32[8,128]{1,0:T(8,128)S(1)}, u32[]{:S(2)}, u32[]{:S(2)}) %collective-permute-start.16) | collective-permute-done | bytes 4128 | tf_op jit(solution)/shard_map/ppermute | solution.py:415
  42.2 1.3 %collective-permute-start.19 = (f32[128,128]{1,0:T(8,128)S(1)}, f32[128,128]{1,0:T(8,128)S(1)}, u32[]{:S(2)}, u32[]{:S(2)}) collective-permute-start(f32[128,128]{1,0:T(8,128)S(1)} %get-tuple-element.94.refs_2_), channel_id=1, source_target_pairs={{0,4},{4,0},{8,12},{12,8},{1,5},{5,1},{9,13},{13,9},{2,6},{6,2},{1... | collective-permute-start | bytes 196616 | tf_op jit(solution)/shard_map/ppermute | solution.py:415
  44.4 2.1 %collective-permute-done.20.refs_5_ = f32[144,128]{1,0:T(8,128)S(1)} collective-permute-done((f32[144,128]{1,0:T(8,128)S(1)}, f32[144,128]{1,0:T(8,128)S(1)}, u32[]{:S(2)}, u32[]{:S(2)}) %collective-permute-start.20) | collective-permute-done | bytes 73760 | tf_op jit(solution)/shard_map/ppermute | solution.py:415
  46.5 1.1 %shard_map.68 = (f32[768,128]{1,0:T(8,128)S(1)}, f32[768,128]{1,0:T(8,128)S(1)}, f32[768,128]{1,0:T(8,128)S(1)}, f32[8,128]{1,0:T(8,128)S(1)}, f32[512,128]{1,0:...) custom-call(f32[264,128]{1,0:T(8,128)S(1)} %get-tuple-element.93.ref, ...), custom_call_target="tpu_custom_call" | custom-call | flops 603979776 | bytes 5881856 | tf_op jit(solution)/shard_map/pallas_call | solution.py:31
  47.6 2.1 %collective-permute-start.22 = (f32[144,128]{1,0:T(8,128)S(1)}, f32[144,128]{1,0:T(8,128)S(1)}, u32[]{:S(2)}, u32[]{:S(2)}) collective-permute-start(f32[144,128]{1,0:T(8,128)S(1)} %get-tuple-element.104.refs_1_), channel_id=1, source_target_pairs={{0,3},{1,2},{2,1},{3,0},{4,7},{5,6},{6,5},{7,4},{8,11},{9,10},{10,... | collective-permute-start | bytes 221192 | tf_op jit(solution)/shard_map/ppermute | solution.py:415
  50.1 1.9 %collective-permute-start.24 = (f32[16,128]{1,0:T(8,128)S(1)}, f32[16,128]{1,0:T(8,128)S(1)}, u32[]{:S(2)}, u32[]{:S(2)}) collective-permute-start(f32[16,128]{1,0:T(8,128)S(1)} %get-tuple-element.102.refs_0_), channel_id=1, source_target_pairs={{0,1},{1,0},{2,3},{3,2},{4,5},{5,4},{6,7},{7,6},{8,9},{9,8},{10,11... | collective-permute-start | bytes 24584 | tf_op jit(solution)/shard_map/ppermute | solution.py:415
  52.2 1.9 %collective-permute-done.24.refs_4_ = f32[16,128]{1,0:T(8,128)S(1)} collective-permute-done((f32[16,128]{1,0:T(8,128)S(1)}, f32[16,128]{1,0:T(8,128)S(1)}, u32[]{:S(2)}, u32[]{:S(2)}) %collective-permute-start.24) | collective-permute-done | bytes 8224 | tf_op jit(solution)/shard_map/ppermute | solution.py:415
  55.9 2.4 %collective-permute-start.25 = (f32[8,128]{1,0:T(8,128)S(1)}, f32[8,128]{1,0:T(8,128)S(1)}, u32[]{:S(2)}, u32[]{:S(2)}) collective-permute-start(f32[8,128]{1,0:T(8,128)S(1)} %get-tuple-element.106.refs_0_), channel_id=1, source_target_pairs={{0,28},{4,24},{8,20},{12,16},{16,12},{20,8},{24,4},{28,0},{1,29},{... | collective-permute-start | bytes 12296 | tf_op jit(solution)/shard_map/ppermute | solution.py:420
  58.5 1.5 %collective-permute-done.25.refs_1_ = f32[8,128]{1,0:T(8,128)S(1)} collective-permute-done((f32[8,128]{1,0:T(8,128)S(1)}, f32[8,128]{1,0:T(8,128)S(1)}, u32[]{:S(2)}, u32[]{:S(2)}) %collective-permute-start.25) | collective-permute-done | bytes 4128 | tf_op jit(solution)/shard_map/ppermute | solution.py:420
  62.0 1.2 %shard_map.73 = (f32[128,768]{1,0:T(8,128)}, f32[128,768]{1,0:T(8,128)}) custom-call(f32[8,128]{1,0:T(8,128)S(1)} %shard_map.71.refs_0_, f32[8,128]{1,0:T(8,128)S(1)} %collective-permute-done.29.refs_1_, f32[768,128]{1,0:T(8,128)S(1)} %get-tuple-element.114.refs_2_, f32[768,128]{1,0:T(8,128)S(1)} %get-tuple-element.115.refs_3_, ...), custom_call_target="tpu_custom_call" | custom-call | flops 1966080 | bytes 3538944 | tf_op jit(solution)/shard_map/pallas_call | solution.py:563
  (54 shorter events, 14.9 us)
Async XLA Ops:
  3.4 9.9 %collective-permute-start = (f32[160,128]{1,0:T(8,128)S(1)}, f32[160,128]{1,0:T(8,128)S(1)}, u32[]{:S(2)}, u32[]{:S(2)}) collective-permute-start(f32[160,128]{1,0:T(8,128)S(1)} %get-tuple-element.64.refs_1_), channel_id=1, source_target_pairs={{0,3},{1,2},{2,1},{3,0},{4,7},{5,6},{6,5},{7,4},{8,11},{9,10},{10,... | collective-permute-start | bytes 245768 | tf_op jit(solution)/shard_map/ppermute | solution.py:415
  8.5 4.7 %collective-permute-start.1 = (f32[32,128]{1,0:T(8,128)S(1)}, f32[32,128]{1,0:T(8,128)S(1)}, u32[]{:S(2)}, u32[]{:S(2)}) collective-permute-start(f32[32,128]{1,0:T(8,128)S(1)} %get-tuple-element.65), channel_id=1, source_target_pairs={{0,2},{1,3},{2,0},{3,1},{4,6},{5,7},{6,4},{7,5},{8,10},{9,11},{10,... | collective-permute-start | bytes 49160 | tf_op jit(solution)/shard_map/ppermute | solution.py:410
  9.2 7.7 %collective-permute-start.6 = (f32[136,128]{1,0:T(8,128)S(1)}, f32[136,128]{1,0:T(8,128)S(1)}, u32[]{:S(2)}, u32[]{:S(2)}) collective-permute-start(f32[136,128]{1,0:T(8,128)S(1)} %get-tuple-element.71.refs_0_), channel_id=1, source_target_pairs={{0,1},{1,0},{2,3},{3,2},{4,5},{5,4},{6,7},{7,6},{8,9},{9,8},{10,11... | collective-permute-start | bytes 208904 | tf_op jit(solution)/shard_map/ppermute | solution.py:415
  13.7 6.1 %collective-permute-start.3 = (f32[264,128]{1,0:T(8,128)S(1)}, f32[264,128]{1,0:T(8,128)S(1)}, u32[]{:S(2)}, u32[]{:S(2)}) collective-permute-start(f32[264,128]{1,0:T(8,128)S(1)} %get-tuple-element.68.refs_0_), channel_id=1, source_target_pairs={{0,16},{16,0},{1,17},{17,1},{2,18},{18,2},{3,19},{19,3},{4,20},{20... | collective-permute-start | bytes 405512 | tf_op jit(solution)/shard_map/ppermute | solution.py:415
  15.2 4.5 %collective-permute-start.5 = (f32[144,128]{1,0:T(8,128)S(1)}, f32[144,128]{1,0:T(8,128)S(1)}, u32[]{:S(2)}, u32[]{:S(2)}) collective-permute-start(f32[144,128]{1,0:T(8,128)S(1)} %get-tuple-element.70.refs_3_), channel_id=1, source_target_pairs={{0,12},{4,8},{8,4},{12,0},{1,13},{5,9},{9,5},{13,1},{2,14},{6,10},... | collective-permute-start | bytes 221192 | tf_op jit(solution)/shard_map/ppermute | solution.py:415
  20.6 6.9 %collective-permute-start.7 = (f32[144,128]{1,0:T(8,128)S(1)}, f32[144,128]{1,0:T(8,128)S(1)}, u32[]{:S(2)}, u32[]{:S(2)}) collective-permute-start(f32[144,128]{1,0:T(8,128)S(1)} %get-tuple-element.77.refs_1_), channel_id=1, source_target_pairs={{0,3},{1,2},{2,1},{3,0},{4,7},{5,6},{6,5},{7,4},{8,11},{9,10},{10,... | collective-permute-start | bytes 221192 | tf_op jit(solution)/shard_map/ppermute | solution.py:415
  22.9 4.6 %collective-permute-start.8 = (f32[24,128]{1,0:T(8,128)S(1)}, f32[24,128]{1,0:T(8,128)S(1)}, u32[]{:S(2)}, u32[]{:S(2)}) collective-permute-start(f32[24,128]{1,0:T(8,128)S(1)} %get-tuple-element.78), channel_id=1, source_target_pairs={{0,2},{1,3},{2,0},{3,1},{4,6},{5,7},{6,4},{7,5},{8,10},{9,11},{10,... | collective-permute-start | bytes 36872 | tf_op jit(solution)/shard_map/ppermute | solution.py:410
  23.0 4.2 %collective-permute-start.9 = (f32[16,128]{1,0:T(8,128)S(1)}, f32[16,128]{1,0:T(8,128)S(1)}, u32[]{:S(2)}, u32[]{:S(2)}) collective-permute-start(f32[16,128]{1,0:T(8,128)S(1)} %get-tuple-element.75.refs_0_), channel_id=1, source_target_pairs={{0,1},{1,0},{2,3},{3,2},{4,5},{5,4},{6,7},{7,6},{8,9},{9,8},{10,11... | collective-permute-start | bytes 24584 | tf_op jit(solution)/shard_map/ppermute | solution.py:415
  25.1 5.0 %collective-permute-start.13 = (f32[128,128]{1,0:T(8,128)S(1)}, f32[128,128]{1,0:T(8,128)S(1)}, u32[]{:S(2)}, u32[]{:S(2)}) collective-permute-start(f32[128,128]{1,0:T(8,128)S(1)} %get-tuple-element.84.refs_0_), channel_id=1, source_target_pairs={{0,1},{1,0},{2,3},{3,2},{4,5},{5,4},{6,7},{7,6},{8,9},{9,8},{10,11... | collective-permute-start | bytes 196616 | tf_op jit(solution)/shard_map/ppermute | solution.py:415
  27.8 5.2 %collective-permute-start.10 = (f32[264,128]{1,0:T(8,128)S(1)}, f32[264,128]{1,0:T(8,128)S(1)}, u32[]{:S(2)}, u32[]{:S(2)}) collective-permute-start(f32[264,128]{1,0:T(8,128)S(1)} %get-tuple-element.81.refs_0_), channel_id=1, source_target_pairs={{0,16},{16,0},{1,17},{17,1},{2,18},{18,2},{3,19},{19,3},{4,20},{20... | collective-permute-start | bytes 405512 | tf_op jit(solution)/shard_map/ppermute | solution.py:415
  28.5 4.6 %collective-permute-start.12 = (f32[144,128]{1,0:T(8,128)S(1)}, f32[144,128]{1,0:T(8,128)S(1)}, u32[]{:S(2)}, u32[]{:S(2)}) collective-permute-start(f32[144,128]{1,0:T(8,128)S(1)} %get-tuple-element.83.refs_3_), channel_id=1, source_target_pairs={{0,12},{4,8},{8,4},{12,0},{1,13},{5,9},{9,5},{13,1},{2,14},{6,10},... | collective-permute-start | bytes 221192 | tf_op jit(solution)/shard_map/ppermute | solution.py:415
  33.9 7.0 %collective-permute-start.14 = (f32[136,128]{1,0:T(8,128)S(1)}, f32[136,128]{1,0:T(8,128)S(1)}, u32[]{:S(2)}, u32[]{:S(2)}) collective-permute-start(f32[136,128]{1,0:T(8,128)S(1)} %get-tuple-element.90.refs_1_), channel_id=1, source_target_pairs={{0,3},{1,2},{2,1},{3,0},{4,7},{5,6},{6,5},{7,4},{8,11},{9,10},{10,... | collective-permute-start | bytes 208904 | tf_op jit(solution)/shard_map/ppermute | solution.py:415
  36.3 4.0 %collective-permute-start.17 = (f32[16,128]{1,0:T(8,128)S(1)}, f32[16,128]{1,0:T(8,128)S(1)}, u32[]{:S(2)}, u32[]{:S(2)}) collective-permute-start(f32[16,128]{1,0:T(8,128)S(1)} %slice.3), channel_id=1, source_target_pairs={{0,4},{4,0},{8,12},{12,8},{1,5},{5,1},{9,13},{13,9},{2,6},{6,2},{1... | collective-permute-start | bytes 24584 | tf_op jit(solution)/shard_map/ppermute | solution.py:415
  36.3 4.5 %collective-permute-start.15 = (f32[16,128]{1,0:T(8,128)S(1)}, f32[16,128]{1,0:T(8,128)S(1)}, u32[]{:S(2)}, u32[]{:S(2)}) collective-permute-start(f32[16,128]{1,0:T(8,128)S(1)} %get-tuple-element.91), channel_id=1, source_target_pairs={{0,2},{1,3},{2,0},{3,1},{4,6},{5,7},{6,4},{7,5},{8,10},{9,11},{10,... | collective-permute-start | bytes 24584 | tf_op jit(solution)/shard_map/ppermute | solution.py:410
  38.3 5.2 %collective-permute-start.21 = (f32[128,128]{1,0:T(8,128)S(1)}, f32[128,128]{1,0:T(8,128)S(1)}, u32[]{:S(2)}, u32[]{:S(2)}) collective-permute-start(f32[128,128]{1,0:T(8,128)S(1)} %get-tuple-element.96.refs_0_), channel_id=1, source_target_pairs={{0,1},{1,0},{2,3},{3,2},{4,5},{5,4},{6,7},{7,6},{8,9},{9,8},{10,11... | collective-permute-start | bytes 196616 | tf_op jit(solution)/shard_map/ppermute | solution.py:415
  41.2 5.4 %collective-permute-start.18 = (f32[264,128]{1,0:T(8,128)S(1)}, f32[264,128]{1,0:T(8,128)S(1)}, u32[]{:S(2)}, u32[]{:S(2)}) collective-permute-start(f32[264,128]{1,0:T(8,128)S(1)} %get-tuple-element.93.refs_0_), channel_id=1, source_target_pairs={{0,16},{16,0},{1,17},{17,1},{2,18},{18,2},{3,19},{19,3},{4,20},{20... | collective-permute-start | bytes 405512 | tf_op jit(solution)/shard_map/ppermute | solution.py:415
  42.2 4.3 %collective-permute-start.20 = (f32[144,128]{1,0:T(8,128)S(1)}, f32[144,128]{1,0:T(8,128)S(1)}, u32[]{:S(2)}, u32[]{:S(2)}) collective-permute-start(f32[144,128]{1,0:T(8,128)S(1)} %get-tuple-element.95.refs_3_), channel_id=1, source_target_pairs={{0,12},{4,8},{8,4},{12,0},{1,13},{5,9},{9,5},{13,1},{2,14},{6,10},... | collective-permute-start | bytes 221192 | tf_op jit(solution)/shard_map/ppermute | solution.py:415
  47.6 7.1 %collective-permute-start.22 = (f32[144,128]{1,0:T(8,128)S(1)}, f32[144,128]{1,0:T(8,128)S(1)}, u32[]{:S(2)}, u32[]{:S(2)}) collective-permute-start(f32[144,128]{1,0:T(8,128)S(1)} %get-tuple-element.104.refs_1_), channel_id=1, source_target_pairs={{0,3},{1,2},{2,1},{3,0},{4,7},{5,6},{6,5},{7,4},{8,11},{9,10},{10,... | collective-permute-start | bytes 221192 | tf_op jit(solution)/shard_map/ppermute | solution.py:415
  49.7 5.0 %collective-permute-start.23 = (f32[24,128]{1,0:T(8,128)S(1)}, f32[24,128]{1,0:T(8,128)S(1)}, u32[]{:S(2)}, u32[]{:S(2)}) collective-permute-start(f32[24,128]{1,0:T(8,128)S(1)} %get-tuple-element.105), channel_id=1, source_target_pairs={{0,2},{1,3},{2,0},{3,1},{4,6},{5,7},{6,4},{7,5},{8,10},{9,11},{10,... | collective-permute-start | bytes 36872 | tf_op jit(solution)/shard_map/ppermute | solution.py:410
  50.1 3.9 %collective-permute-start.24 = (f32[16,128]{1,0:T(8,128)S(1)}, f32[16,128]{1,0:T(8,128)S(1)}, u32[]{:S(2)}, u32[]{:S(2)}) collective-permute-start(f32[16,128]{1,0:T(8,128)S(1)} %get-tuple-element.102.refs_0_), channel_id=1, source_target_pairs={{0,1},{1,0},{2,3},{3,2},{4,5},{5,4},{6,7},{7,6},{8,9},{9,8},{10,11... | collective-permute-start | bytes 24584 | tf_op jit(solution)/shard_map/ppermute | solution.py:415
  52.1 6.3 %collective-permute-start.28 = (f32[128,128]{1,0:T(8,128)S(1)}, f32[128,128]{1,0:T(8,128)S(1)}, u32[]{:S(2)}, u32[]{:S(2)}) collective-permute-start(f32[128,128]{1,0:T(8,128)S(1)} %get-tuple-element.109.refs_0_), channel_id=1, source_target_pairs={{0,1},{1,0},{2,3},{3,2},{4,5},{5,4},{6,7},{7,6},{8,9},{9,8},{10,11... | collective-permute-start | bytes 196616 | tf_op jit(solution)/shard_map/ppermute | solution.py:415
  55.0 5.1 %collective-permute-start.26 = (f32[264,128]{1,0:T(8,128)S(1)}, f32[264,128]{1,0:T(8,128)S(1)}, u32[]{:S(2)}, u32[]{:S(2)}) collective-permute-start(f32[264,128]{1,0:T(8,128)S(1)} %get-tuple-element.107.refs_0_), channel_id=1, source_target_pairs={{0,16},{16,0},{1,17},{17,1},{2,18},{18,2},{3,19},{19,3},{4,20},{20... | collective-permute-start | bytes 405512 | tf_op jit(solution)/shard_map/ppermute | solution.py:415
  55.9 4.2 %collective-permute-start.27 = (f32[144,128]{1,0:T(8,128)S(1)}, f32[144,128]{1,0:T(8,128)S(1)}, u32[]{:S(2)}, u32[]{:S(2)}) collective-permute-start(f32[144,128]{1,0:T(8,128)S(1)} %get-tuple-element.108.refs_3_), channel_id=1, source_target_pairs={{0,12},{4,8},{8,4},{12,0},{1,13},{5,9},{9,5},{13,1},{2,14},{6,10},... | collective-permute-start | bytes 221192 | tf_op jit(solution)/shard_map/ppermute | solution.py:415
  55.9 4.0 %collective-permute-start.25 = (f32[8,128]{1,0:T(8,128)S(1)}, f32[8,128]{1,0:T(8,128)S(1)}, u32[]{:S(2)}, u32[]{:S(2)}) collective-permute-start(f32[8,128]{1,0:T(8,128)S(1)} %get-tuple-element.106.refs_0_), channel_id=1, source_target_pairs={{0,28},{4,24},{8,20},{12,16},{16,12},{20,8},{24,4},{28,0},{1,29},{... | collective-permute-start | bytes 12296 | tf_op jit(solution)/shard_map/ppermute | solution.py:420
  (7 other events, 19.3 us)

commit v12 on v11

--- a/solution.py
+++ b/solution.py
@@ -106,19 +106,31 @@
     o["zb"][face + at:face + at + n, :] = rows
 
 
+def part_rows(face, part):
+    return slice(4 * part * face, 4 * (part + 1) * face if part < 3 else None)
+
+
+def send_loads(face, stack, halves, o):
+    cols = halves.shape[1] // 2
+    both = dot16(stack[part_rows(face, 3), :], halves)
+    loads = both[:, :cols] + both[:, cols:]
+    send_rows(face, (loads[0:PAD] + loads[PAD:2 * PAD]) + loads[2 * PAD:3 * PAD], 0, o)
+
+
+def product_part(face, part, vec, stack, halves, o):
+    cols = vec.shape[1]
+    both = dot16(stack[part_rows(face, part), :], halves)
+    both = both[:, :cols] + both[:, cols:]
+    y = both[0:2 * face] + both[2 * face:]
+    store_product(face, part, y, o)
+    return col_sum(vec[2 * part * face:2 * (part + 1) * face] * y)
+
+
 def product(face, vec, stack, o):
-    width, cols = vec.shape
-    both = dot16(stack[...], jnp.concatenate(split(vec), axis=1))
-    total = jnp.zeros((1, cols), F32)
-    for part in range(3):
-        at = slice(2 * part * face, 2 * (part + 1) * face)
-        low = slice(width + 2 * part * face, width + 2 * (part + 1) * face)
-        y = (both[at, :cols] + both[at, cols:]) + (both[low, :cols] + both[low, cols:])
-        store_product(face, part, y, o)
-        total = total + col_sum(vec[at] * y)
-    loads = both[2 * width:, :cols] + both[2 * width:, cols:]
-    send_rows(face, (loads[0:PAD] + loads[PAD:2 * PAD]) + loads[2 * PAD:3 * PAD], 0, o)
-    return total
+    halves = jnp.concatenate(split(vec), axis=1)
+    parts = [product_part(face, part, vec, stack, halves, o) for part in range(3)]
+    send_loads(face, stack, halves, o)
+    return (parts[0] + parts[1]) + parts[2]
 
 
 def stack_rows(rows, cols):
@@ -184,14 +196,17 @@
     o["za"][face:face + PAD, :] = modes[:, 4 * face:5 * face]
     o["zb"][face + 3 * PAD:face + 4 * PAD, :] = modes[:, 5 * face:6 * face]
 
+    halves = jnp.concatenate(split(r0), axis=1)
+    send_loads(face, o["stack"], halves, o)
+    curv = jnp.zeros((1, cols), F32)
     for part in range(3):
         at = slice(part * two, (part + 1) * two)
         copies[3 + 2 * part].wait()
         copies[4 + 2 * part].wait()
         high, low = split(jnp.concatenate([schur[at, pl.ds(start, face)] for start in places], axis=1))
-        o["stack"][at, :] = high
-        o["stack"][width + part * two:width + (part + 1) * two, :] = low
-    curv = product(face, r0, o["stack"], o)
+        o["stack"][2 * part * two:(2 * part + 1) * two, :] = high
+        o["stack"][(2 * part + 1) * two:2 * (part + 1) * two, :] = low
+        curv = curv + product_part(face, part, r0, o["stack"], halves, o)
     send_rows(face, stack_rows([half_dot(r0, r0), curv], cols), PAD, o)
 
 

time: 63.3 us -> 63.9 us (level)
  Pallas kernels: 9.19 us -> 9.84 us
where the time goes in v12:
time: 63.9 us; the launch traced here: 63.8 us
  starting transfers between devices  32.9 us (51%)
  waiting for transfers between devices  20.3 us (32%)
  Pallas kernels  9.84 us (15%)
  between operations  0.75 us (1%)
    ppermute x26, starting transfers between devices, swap(): return lax.ppermute(x, axis, [(k, (k + side(k)) % n) for k in range(n)])  29.9 us
    ppermute x26, waiting for transfers between devices, swap(): return lax.ppermute(x, axis, [(k, (k + side(k)) % n) for k in range(n)])  16.3 us
    pallas_call x13, Pallas kernels, call(): pl.pallas_call(run, out_shape=[outs[n] for n in names_out], in_specs=[vme...  5.44 us
    pallas_call x1, Pallas kernels, body(): pl.pallas_call(functools.partial(first_kernel, face, nz, n_modes, small),...  3.25 us
    ppermute x4, waiting for transfers between devices, shift(): return lax.ppermute(x, axis, [(k, (k + by) % n) for k in range(n)])  2.43 us
    ppermute x1, starting transfers between devices, move(): return lax.ppermute(x, ('gx', 'gy'), pairs)  2.3 us
    ppermute x1, waiting for transfers between devices, move(): return lax.ppermute(x, ('gx', 'gy'), pairs)  1.55 us
  transfers between devices with their start and end apart: 31, of which 17 were waited for; matrix products, arithmetic and copies ran while one was open for 0% of the time, Pallas kernels for 4%

profile of v12, /device:TPU:0, one launch (start us, length us, event | category | flops | bytes accessed | tf_op | source)
XLA Modules:
  0.0 63.8 jit_solution(8812879492733383264)
XLA Ops:
  0.6 3.2 %shard_map.59 = (f32[768,128]{1,0:T(8,128)S(1)}, bf16[1568,768]{1,0:T(8,128)(2,1)S(1)}, bf16[768,48]{1,0:T(8,128)(2,1)S(1)}, f32[8,128]{1,0:T(8,128)S(1)}, f32[5...) custom-call(f32[128,768]{1,0:T(8,128)} %bitcast.7, ...), custom_call_target="tpu_custom_call" | custom-call | flops 603979776 | bytes 2359296 | tf_op jit(solution)/shard_map/pallas_call | solution.py:505
  3.9 5.1 %collective-permute-start = (f32[160,128]{1,0:T(8,128)S(1)}, f32[160,128]{1,0:T(8,128)S(1)}, u32[]{:S(2)}, u32[]{:S(2)}) collective-permute-start(f32[160,128]{1,0:T(8,128)S(1)} %get-tuple-element.64.refs_1_), channel_id=1, source_target_pairs={{0,3},{1,2},{2,1},{3,0},{4,7},{5,6},{6,5},{7,4},{8,11},{9,10},{10,... | collective-permute-start | bytes 245768 | tf_op jit(solution)/shard_map/ppermute | solution.py:430
  9.6 1.4 %collective-permute-start.6 = (f32[136,128]{1,0:T(8,128)S(1)}, f32[136,128]{1,0:T(8,128)S(1)}, u32[]{:S(2)}, u32[]{:S(2)}) collective-permute-start(f32[136,128]{1,0:T(8,128)S(1)} %get-tuple-element.71.refs_0_), channel_id=1, source_target_pairs={{0,1},{1,0},{2,3},{3,2},{4,5},{5,4},{6,7},{7,6},{8,9},{9,8},{10,11... | collective-permute-start | bytes 208904 | tf_op jit(solution)/shard_map/ppermute | solution.py:430
  11.0 1.7 %collective-permute-done.2.refs_4_ = f32[24,128]{1,0:T(8,128)S(1)} collective-permute-done((f32[24,128]{1,0:T(8,128)S(1)}, f32[24,128]{1,0:T(8,128)S(1)}, u32[]{:S(2)}, u32[]{:S(2)}) %collective-permute-start.2) | collective-permute-done | bytes 12320 | tf_op jit(solution)/shard_map/ppermute | solution.py:430
  14.2 1.6 %collective-permute-start.3 = (f32[264,128]{1,0:T(8,128)S(1)}, f32[264,128]{1,0:T(8,128)S(1)}, u32[]{:S(2)}, u32[]{:S(2)}) collective-permute-start(f32[264,128]{1,0:T(8,128)S(1)} %get-tuple-element.68.refs_0_), channel_id=1, source_target_pairs={{0,16},{16,0},{1,17},{17,1},{2,18},{18,2},{3,19},{19,3},{4,20},{20... | collective-permute-start | bytes 405512 | tf_op jit(solution)/shard_map/ppermute | solution.py:430
  15.7 1.6 %collective-permute-start.4 = (f32[136,128]{1,0:T(8,128)S(1)}, f32[136,128]{1,0:T(8,128)S(1)}, u32[]{:S(2)}, u32[]{:S(2)}) collective-permute-start(f32[136,128]{1,0:T(8,128)S(1)} %get-tuple-element.69.refs_2_), channel_id=1, source_target_pairs={{0,4},{4,0},{8,12},{12,8},{1,5},{5,1},{9,13},{13,9},{2,6},{6,2},{1... | collective-permute-start | bytes 208904 | tf_op jit(solution)/shard_map/ppermute | solution.py:430
  18.3 1.9 %collective-permute-done.5.refs_5_ = f32[144,128]{1,0:T(8,128)S(1)} collective-permute-done((f32[144,128]{1,0:T(8,128)S(1)}, f32[144,128]{1,0:T(8,128)S(1)}, u32[]{:S(2)}, u32[]{:S(2)}) %collective-permute-start.5) | collective-permute-done | bytes 73760 | tf_op jit(solution)/shard_map/ppermute | solution.py:430
  21.1 2.3 %collective-permute-start.7 = (f32[144,128]{1,0:T(8,128)S(1)}, f32[144,128]{1,0:T(8,128)S(1)}, u32[]{:S(2)}, u32[]{:S(2)}) collective-permute-start(f32[144,128]{1,0:T(8,128)S(1)} %get-tuple-element.77.refs_1_), channel_id=1, source_target_pairs={{0,3},{1,2},{2,1},{3,0},{4,7},{5,6},{6,5},{7,4},{8,11},{9,10},{10,... | collective-permute-start | bytes 221192 | tf_op jit(solution)/shard_map/ppermute | solution.py:430
  23.5 2.1 %collective-permute-start.9 = (f32[16,128]{1,0:T(8,128)S(1)}, f32[16,128]{1,0:T(8,128)S(1)}, u32[]{:S(2)}, u32[]{:S(2)}) collective-permute-start(f32[16,128]{1,0:T(8,128)S(1)} %get-tuple-element.75.refs_0_), channel_id=1, source_target_pairs={{0,1},{1,0},{2,3},{3,2},{4,5},{5,4},{6,7},{7,6},{8,9},{9,8},{10,11... | collective-permute-start | bytes 24584 | tf_op jit(solution)/shard_map/ppermute | solution.py:430
  25.6 2.0 %collective-permute-done.9.refs_4_ = f32[16,128]{1,0:T(8,128)S(1)} collective-permute-done((f32[16,128]{1,0:T(8,128)S(1)}, f32[16,128]{1,0:T(8,128)S(1)}, u32[]{:S(2)}, u32[]{:S(2)}) %collective-permute-start.9) | collective-permute-done | bytes 8224 | tf_op jit(solution)/shard_map/ppermute | solution.py:430
  29.0 1.6 %collective-permute-start.11 = (f32[136,128]{1,0:T(8,128)S(1)}, f32[136,128]{1,0:T(8,128)S(1)}, u32[]{:S(2)}, u32[]{:S(2)}) collective-permute-start(f32[136,128]{1,0:T(8,128)S(1)} %get-tuple-element.82.refs_2_), channel_id=1, source_target_pairs={{0,4},{4,0},{8,12},{12,8},{1,5},{5,1},{9,13},{13,9},{2,6},{6,2},{1... | collective-permute-start | bytes 208904 | tf_op jit(solution)/shard_map/ppermute | solution.py:430
  31.5 2.0 %collective-permute-done.12.refs_5_ = f32[144,128]{1,0:T(8,128)S(1)} collective-permute-done((f32[144,128]{1,0:T(8,128)S(1)}, f32[144,128]{1,0:T(8,128)S(1)}, u32[]{:S(2)}, u32[]{:S(2)}) %collective-permute-start.12) | collective-permute-done | bytes 73760 | tf_op jit(solution)/shard_map/ppermute | solution.py:430
  34.4 2.4 %collective-permute-start.14 = (f32[136,128]{1,0:T(8,128)S(1)}, f32[136,128]{1,0:T(8,128)S(1)}, u32[]{:S(2)}, u32[]{:S(2)}) collective-permute-start(f32[136,128]{1,0:T(8,128)S(1)} %get-tuple-element.90.refs_1_), channel_id=1, source_target_pairs={{0,3},{1,2},{2,1},{3,0},{4,7},{5,6},{6,5},{7,4},{8,11},{9,10},{10,... | collective-permute-start | bytes 208904 | tf_op jit(solution)/shard_map/ppermute | solution.py:430
  37.1 1.8 %collective-permute-start.16 = (f32[8,128]{1,0:T(8,128)S(1)}, f32[8,128]{1,0:T(8,128)S(1)}, u32[]{:S(2)}, u32[]{:S(2)}) collective-permute-start(f32[8,128]{1,0:T(8,128)S(1)} %get-tuple-element.88.refs_0_), channel_id=1, source_target_pairs={{0,1},{1,0},{2,3},{3,2},{4,5},{5,4},{6,7},{7,6},{8,9},{9,8},{10,11... | collective-permute-start | bytes 12296 | tf_op jit(solution)/shard_map/ppermute | solution.py:430
  39.2 1.6 %collective-permute-done.16.refs_4_ = f32[8,128]{1,0:T(8,128)S(1)} collective-permute-done((f32[8,128]{1,0:T(8,128)S(1)}, f32[8,128]{1,0:T(8,128)S(1)}, u32[]{:S(2)}, u32[]{:S(2)}) %collective-permute-start.16) | collective-permute-done | bytes 4128 | tf_op jit(solution)/shard_map/ppermute | solution.py:430
  42.8 1.2 %collective-permute-start.19 = (f32[128,128]{1,0:T(8,128)S(1)}, f32[128,128]{1,0:T(8,128)S(1)}, u32[]{:S(2)}, u32[]{:S(2)}) collective-permute-start(f32[128,128]{1,0:T(8,128)S(1)} %get-tuple-element.94.refs_2_), channel_id=1, source_target_pairs={{0,4},{4,0},{8,12},{12,8},{1,5},{5,1},{9,13},{13,9},{2,6},{6,2},{1... | collective-permute-start | bytes 196616 | tf_op jit(solution)/shard_map/ppermute | solution.py:430
  45.0 2.1 %collective-permute-done.20.refs_5_ = f32[144,128]{1,0:T(8,128)S(1)} collective-permute-done((f32[144,128]{1,0:T(8,128)S(1)}, f32[144,128]{1,0:T(8,128)S(1)}, u32[]{:S(2)}, u32[]{:S(2)}) %collective-permute-start.20) | collective-permute-done | bytes 73760 | tf_op jit(solution)/shard_map/ppermute | solution.py:430
  47.1 1.1 %shard_map.68 = (f32[768,128]{1,0:T(8,128)S(1)}, f32[768,128]{1,0:T(8,128)S(1)}, f32[768,128]{1,0:T(8,128)S(1)}, f32[8,128]{1,0:T(8,128)S(1)}, f32[512,128]{1,0:...) custom-call(f32[264,128]{1,0:T(8,128)S(1)} %get-tuple-element.93.ref, ...), custom_call_target="tpu_custom_call" | custom-call | flops 603979776 | bytes 5881856 | tf_op jit(solution)/shard_map/pallas_call | solution.py:31
  48.2 2.3 %collective-permute-start.22 = (f32[144,128]{1,0:T(8,128)S(1)}, f32[144,128]{1,0:T(8,128)S(1)}, u32[]{:S(2)}, u32[]{:S(2)}) collective-permute-start(f32[144,128]{1,0:T(8,128)S(1)} %get-tuple-element.104.refs_1_), channel_id=1, source_target_pairs={{0,3},{1,2},{2,1},{3,0},{4,7},{5,6},{6,5},{7,4},{8,11},{9,10},{10,... | collective-permute-start | bytes 221192 | tf_op jit(solution)/shard_map/ppermute | solution.py:430
  50.8 1.9 %collective-permute-start.24 = (f32[16,128]{1,0:T(8,128)S(1)}, f32[16,128]{1,0:T(8,128)S(1)}, u32[]{:S(2)}, u32[]{:S(2)}) collective-permute-start(f32[16,128]{1,0:T(8,128)S(1)} %get-tuple-element.102.refs_0_), channel_id=1, source_target_pairs={{0,1},{1,0},{2,3},{3,2},{4,5},{5,4},{6,7},{7,6},{8,9},{9,8},{10,11... | collective-permute-start | bytes 24584 | tf_op jit(solution)/shard_map/ppermute | solution.py:430
  52.8 1.9 %collective-permute-done.24.refs_4_ = f32[16,128]{1,0:T(8,128)S(1)} collective-permute-done((f32[16,128]{1,0:T(8,128)S(1)}, f32[16,128]{1,0:T(8,128)S(1)}, u32[]{:S(2)}, u32[]{:S(2)}) %collective-permute-start.24) | collective-permute-done | bytes 8224 | tf_op jit(solution)/shard_map/ppermute | solution.py:430
  56.6 2.3 %collective-permute-start.25 = (f32[8,128]{1,0:T(8,128)S(1)}, f32[8,128]{1,0:T(8,128)S(1)}, u32[]{:S(2)}, u32[]{:S(2)}) collective-permute-start(f32[8,128]{1,0:T(8,128)S(1)} %get-tuple-element.106.refs_0_), channel_id=1, source_target_pairs={{0,28},{4,24},{8,20},{12,16},{16,12},{20,8},{24,4},{28,0},{1,29},{... | collective-permute-start | bytes 12296 | tf_op jit(solution)/shard_map/ppermute | solution.py:435
  59.1 1.6 %collective-permute-done.25.refs_1_ = f32[8,128]{1,0:T(8,128)S(1)} collective-permute-done((f32[8,128]{1,0:T(8,128)S(1)}, f32[8,128]{1,0:T(8,128)S(1)}, u32[]{:S(2)}, u32[]{:S(2)}) %collective-permute-start.25) | collective-permute-done | bytes 4128 | tf_op jit(solution)/shard_map/ppermute | solution.py:435
  62.6 1.2 %shard_map.73 = (f32[128,768]{1,0:T(8,128)}, f32[128,768]{1,0:T(8,128)}) custom-call(f32[8,128]{1,0:T(8,128)S(1)} %shard_map.71.refs_0_, f32[8,128]{1,0:T(8,128)S(1)} %collective-permute-done.29.refs_1_, f32[768,128]{1,0:T(8,128)S(1)} %get-tuple-element.114.refs_2_, f32[768,128]{1,0:T(8,128)S(1)} %get-tuple-element.115.refs_3_, ...), custom_call_target="tpu_custom_call" | custom-call | flops 1966080 | bytes 3538944 | tf_op jit(solution)/shard_map/pallas_call | solution.py:578
  (54 shorter events, 15.0 us)
Async XLA Ops:
  3.9 9.9 %collective-permute-start = (f32[160,128]{1,0:T(8,128)S(1)}, f32[160,128]{1,0:T(8,128)S(1)}, u32[]{:S(2)}, u32[]{:S(2)}) collective-permute-start(f32[160,128]{1,0:T(8,128)S(1)} %get-tuple-element.64.refs_1_), channel_id=1, source_target_pairs={{0,3},{1,2},{2,1},{3,0},{4,7},{5,6},{6,5},{7,4},{8,11},{9,10},{10,... | collective-permute-start | bytes 245768 | tf_op jit(solution)/shard_map/ppermute | solution.py:430
  9.0 4.7 %collective-permute-start.1 = (f32[32,128]{1,0:T(8,128)S(1)}, f32[32,128]{1,0:T(8,128)S(1)}, u32[]{:S(2)}, u32[]{:S(2)}) collective-permute-start(f32[32,128]{1,0:T(8,128)S(1)} %get-tuple-element.65), channel_id=1, source_target_pairs={{0,2},{1,3},{2,0},{3,1},{4,6},{5,7},{6,4},{7,5},{8,10},{9,11},{10,... | collective-permute-start | bytes 49160 | tf_op jit(solution)/shard_map/ppermute | solution.py:425
  9.6 7.7 %collective-permute-start.6 = (f32[136,128]{1,0:T(8,128)S(1)}, f32[136,128]{1,0:T(8,128)S(1)}, u32[]{:S(2)}, u32[]{:S(2)}) collective-permute-start(f32[136,128]{1,0:T(8,128)S(1)} %get-tuple-element.71.refs_0_), channel_id=1, source_target_pairs={{0,1},{1,0},{2,3},{3,2},{4,5},{5,4},{6,7},{7,6},{8,9},{9,8},{10,11... | collective-permute-start | bytes 208904 | tf_op jit(solution)/shard_map/ppermute | solution.py:430
  14.2 6.0 %collective-permute-start.3 = (f32[264,128]{1,0:T(8,128)S(1)}, f32[264,128]{1,0:T(8,128)S(1)}, u32[]{:S(2)}, u32[]{:S(2)}) collective-permute-start(f32[264,128]{1,0:T(8,128)S(1)} %get-tuple-element.68.refs_0_), channel_id=1, source_target_pairs={{0,16},{16,0},{1,17},{17,1},{2,18},{18,2},{3,19},{19,3},{4,20},{20... | collective-permute-start | bytes 405512 | tf_op jit(solution)/shard_map/ppermute | solution.py:430
  15.7 4.5 %collective-permute-start.5 = (f32[144,128]{1,0:T(8,128)S(1)}, f32[144,128]{1,0:T(8,128)S(1)}, u32[]{:S(2)}, u32[]{:S(2)}) collective-permute-start(f32[144,128]{1,0:T(8,128)S(1)} %get-tuple-element.70.refs_3_), channel_id=1, source_target_pairs={{0,12},{4,8},{8,4},{12,0},{1,13},{5,9},{9,5},{13,1},{2,14},{6,10},... | collective-permute-start | bytes 221192 | tf_op jit(solution)/shard_map/ppermute | solution.py:430
  21.1 6.9 %collective-permute-start.7 = (f32[144,128]{1,0:T(8,128)S(1)}, f32[144,128]{1,0:T(8,128)S(1)}, u32[]{:S(2)}, u32[]{:S(2)}) collective-permute-start(f32[144,128]{1,0:T(8,128)S(1)} %get-tuple-element.77.refs_1_), channel_id=1, source_target_pairs={{0,3},{1,2},{2,1},{3,0},{4,7},{5,6},{6,5},{7,4},{8,11},{9,10},{10,... | collective-permute-start | bytes 221192 | tf_op jit(solution)/shard_map/ppermute | solution.py:430
  23.4 4.6 %collective-permute-start.8 = (f32[24,128]{1,0:T(8,128)S(1)}, f32[24,128]{1,0:T(8,128)S(1)}, u32[]{:S(2)}, u32[]{:S(2)}) collective-permute-start(f32[24,128]{1,0:T(8,128)S(1)} %get-tuple-element.78), channel_id=1, source_target_pairs={{0,2},{1,3},{2,0},{3,1},{4,6},{5,7},{6,4},{7,5},{8,10},{9,11},{10,... | collective-permute-start | bytes 36872 | tf_op jit(solution)/shard_map/ppermute | solution.py:425
  23.5 4.1 %collective-permute-start.9 = (f32[16,128]{1,0:T(8,128)S(1)}, f32[16,128]{1,0:T(8,128)S(1)}, u32[]{:S(2)}, u32[]{:S(2)}) collective-permute-start(f32[16,128]{1,0:T(8,128)S(1)} %get-tuple-element.75.refs_0_), channel_id=1, source_target_pairs={{0,1},{1,0},{2,3},{3,2},{4,5},{5,4},{6,7},{7,6},{8,9},{9,8},{10,11... | collective-permute-start | bytes 24584 | tf_op jit(solution)/shard_map/ppermute | solution.py:430
  25.6 5.0 %collective-permute-start.13 = (f32[128,128]{1,0:T(8,128)S(1)}, f32[128,128]{1,0:T(8,128)S(1)}, u32[]{:S(2)}, u32[]{:S(2)}) collective-permute-start(f32[128,128]{1,0:T(8,128)S(1)} %get-tuple-element.84.refs_0_), channel_id=1, source_target_pairs={{0,1},{1,0},{2,3},{3,2},{4,5},{5,4},{6,7},{7,6},{8,9},{9,8},{10,11... | collective-permute-start | bytes 196616 | tf_op jit(solution)/shard_map/ppermute | solution.py:430
  28.4 5.2 %collective-permute-start.10 = (f32[264,128]{1,0:T(8,128)S(1)}, f32[264,128]{1,0:T(8,128)S(1)}, u32[]{:S(2)}, u32[]{:S(2)}) collective-permute-start(f32[264,128]{1,0:T(8,128)S(1)} %get-tuple-element.81.refs_0_), channel_id=1, source_target_pairs={{0,16},{16,0},{1,17},{17,1},{2,18},{18,2},{3,19},{19,3},{4,20},{20... | collective-permute-start | bytes 405512 | tf_op jit(solution)/shard_map/ppermute | solution.py:430
  29.0 4.5 %collective-permute-start.12 = (f32[144,128]{1,0:T(8,128)S(1)}, f32[144,128]{1,0:T(8,128)S(1)}, u32[]{:S(2)}, u32[]{:S(2)}) collective-permute-start(f32[144,128]{1,0:T(8,128)S(1)} %get-tuple-element.83.refs_3_), channel_id=1, source_target_pairs={{0,12},{4,8},{8,4},{12,0},{1,13},{5,9},{9,5},{13,1},{2,14},{6,10},... | collective-permute-start | bytes 221192 | tf_op jit(solution)/shard_map/ppermute | solution.py:430
  34.4 7.0 %collective-permute-start.14 = (f32[136,128]{1,0:T(8,128)S(1)}, f32[136,128]{1,0:T(8,128)S(1)}, u32[]{:S(2)}, u32[]{:S(2)}) collective-permute-start(f32[136,128]{1,0:T(8,128)S(1)} %get-tuple-element.90.refs_1_), channel_id=1, source_target_pairs={{0,3},{1,2},{2,1},{3,0},{4,7},{5,6},{6,5},{7,4},{8,11},{9,10},{10,... | collective-permute-start | bytes 208904 | tf_op jit(solution)/shard_map/ppermute | solution.py:430
  36.9 3.9 %collective-permute-start.17 = (f32[16,128]{1,0:T(8,128)S(1)}, f32[16,128]{1,0:T(8,128)S(1)}, u32[]{:S(2)}, u32[]{:S(2)}) collective-permute-start(f32[16,128]{1,0:T(8,128)S(1)} %slice.3), channel_id=1, source_target_pairs={{0,4},{4,0},{8,12},{12,8},{1,5},{5,1},{9,13},{13,9},{2,6},{6,2},{1... | collective-permute-start | bytes 24584 | tf_op jit(solution)/shard_map/ppermute | solution.py:430
  36.9 4.5 %collective-permute-start.15 = (f32[16,128]{1,0:T(8,128)S(1)}, f32[16,128]{1,0:T(8,128)S(1)}, u32[]{:S(2)}, u32[]{:S(2)}) collective-permute-start(f32[16,128]{1,0:T(8,128)S(1)} %get-tuple-element.91), channel_id=1, source_target_pairs={{0,2},{1,3},{2,0},{3,1},{4,6},{5,7},{6,4},{7,5},{8,10},{9,11},{10,... | collective-permute-start | bytes 24584 | tf_op jit(solution)/shard_map/ppermute | solution.py:425
  38.9 5.2 %collective-permute-start.21 = (f32[128,128]{1,0:T(8,128)S(1)}, f32[128,128]{1,0:T(8,128)S(1)}, u32[]{:S(2)}, u32[]{:S(2)}) collective-permute-start(f32[128,128]{1,0:T(8,128)S(1)} %get-tuple-element.96.refs_0_), channel_id=1, source_target_pairs={{0,1},{1,0},{2,3},{3,2},{4,5},{5,4},{6,7},{7,6},{8,9},{9,8},{10,11... | collective-permute-start | bytes 196616 | tf_op jit(solution)/shard_map/ppermute | solution.py:430
  41.8 5.3 %collective-permute-start.18 = (f32[264,128]{1,0:T(8,128)S(1)}, f32[264,128]{1,0:T(8,128)S(1)}, u32[]{:S(2)}, u32[]{:S(2)}) collective-permute-start(f32[264,128]{1,0:T(8,128)S(1)} %get-tuple-element.93.refs_0_), channel_id=1, source_target_pairs={{0,16},{16,0},{1,17},{17,1},{2,18},{18,2},{3,19},{19,3},{4,20},{20... | collective-permute-start | bytes 405512 | tf_op jit(solution)/shard_map/ppermute | solution.py:430
  42.8 4.3 %collective-permute-start.20 = (f32[144,128]{1,0:T(8,128)S(1)}, f32[144,128]{1,0:T(8,128)S(1)}, u32[]{:S(2)}, u32[]{:S(2)}) collective-permute-start(f32[144,128]{1,0:T(8,128)S(1)} %get-tuple-element.95.refs_3_), channel_id=1, source_target_pairs={{0,12},{4,8},{8,4},{12,0},{1,13},{5,9},{9,5},{13,1},{2,14},{6,10},... | collective-permute-start | bytes 221192 | tf_op jit(solution)/shard_map/ppermute | solution.py:430
  48.2 7.0 %collective-permute-start.22 = (f32[144,128]{1,0:T(8,128)S(1)}, f32[144,128]{1,0:T(8,128)S(1)}, u32[]{:S(2)}, u32[]{:S(2)}) collective-permute-start(f32[144,128]{1,0:T(8,128)S(1)} %get-tuple-element.104.refs_1_), channel_id=1, source_target_pairs={{0,3},{1,2},{2,1},{3,0},{4,7},{5,6},{6,5},{7,4},{8,11},{9,10},{10,... | collective-permute-start | bytes 221192 | tf_op jit(solution)/shard_map/ppermute | solution.py:430
  50.5 4.7 %collective-permute-start.23 = (f32[24,128]{1,0:T(8,128)S(1)}, f32[24,128]{1,0:T(8,128)S(1)}, u32[]{:S(2)}, u32[]{:S(2)}) collective-permute-start(f32[24,128]{1,0:T(8,128)S(1)} %get-tuple-element.105), channel_id=1, source_target_pairs={{0,2},{1,3},{2,0},{3,1},{4,6},{5,7},{6,4},{7,5},{8,10},{9,11},{10,... | collective-permute-start | bytes 36872 | tf_op jit(solution)/shard_map/ppermute | solution.py:425
  50.8 4.0 %collective-permute-start.24 = (f32[16,128]{1,0:T(8,128)S(1)}, f32[16,128]{1,0:T(8,128)S(1)}, u32[]{:S(2)}, u32[]{:S(2)}) collective-permute-start(f32[16,128]{1,0:T(8,128)S(1)} %get-tuple-element.102.refs_0_), channel_id=1, source_target_pairs={{0,1},{1,0},{2,3},{3,2},{4,5},{5,4},{6,7},{7,6},{8,9},{9,8},{10,11... | collective-permute-start | bytes 24584 | tf_op jit(solution)/shard_map/ppermute | solution.py:430
  52.7 6.2 %collective-permute-start.28 = (f32[128,128]{1,0:T(8,128)S(1)}, f32[128,128]{1,0:T(8,128)S(1)}, u32[]{:S(2)}, u32[]{:S(2)}) collective-permute-start(f32[128,128]{1,0:T(8,128)S(1)} %get-tuple-element.109.refs_0_), channel_id=1, source_target_pairs={{0,1},{1,0},{2,3},{3,2},{4,5},{5,4},{6,7},{7,6},{8,9},{9,8},{10,11... | collective-permute-start | bytes 196616 | tf_op jit(solution)/shard_map/ppermute | solution.py:430
  55.6 5.2 %collective-permute-start.26 = (f32[264,128]{1,0:T(8,128)S(1)}, f32[264,128]{1,0:T(8,128)S(1)}, u32[]{:S(2)}, u32[]{:S(2)}) collective-permute-start(f32[264,128]{1,0:T(8,128)S(1)} %get-tuple-element.107.refs_0_), channel_id=1, source_target_pairs={{0,16},{16,0},{1,17},{17,1},{2,18},{18,2},{3,19},{19,3},{4,20},{20... | collective-permute-start | bytes 405512 | tf_op jit(solution)/shard_map/ppermute | solution.py:430
  56.6 4.2 %collective-permute-start.27 = (f32[144,128]{1,0:T(8,128)S(1)}, f32[144,128]{1,0:T(8,128)S(1)}, u32[]{:S(2)}, u32[]{:S(2)}) collective-permute-start(f32[144,128]{1,0:T(8,128)S(1)} %get-tuple-element.108.refs_3_), channel_id=1, source_target_pairs={{0,12},{4,8},{8,4},{12,0},{1,13},{5,9},{9,5},{13,1},{2,14},{6,10},... | collective-permute-start | bytes 221192 | tf_op jit(solution)/shard_map/ppermute | solution.py:430
  56.6 4.0 %collective-permute-start.25 = (f32[8,128]{1,0:T(8,128)S(1)}, f32[8,128]{1,0:T(8,128)S(1)}, u32[]{:S(2)}, u32[]{:S(2)}) collective-permute-start(f32[8,128]{1,0:T(8,128)S(1)} %get-tuple-element.106.refs_0_), channel_id=1, source_target_pairs={{0,28},{4,24},{8,20},{12,16},{16,12},{20,8},{24,4},{28,0},{1,29},{... | collective-permute-start | bytes 12296 | tf_op jit(solution)/shard_map/ppermute | solution.py:435
  (7 other events, 19.3 us)

commit v13 on v11

--- a/solution.py
+++ b/solution.py
@@ -298,13 +298,17 @@
         partners = [rescale(i[name][at:at + PAD, :], rate) for rate, name, at in zip(
             rates, ("gxab", "gya", "gyb"), (2 * face, face, face))]
         o["near"][...] = jnp.concatenate([partners[0], partners[2], partners[1] + i["xab"][2 * face:, :]], axis=0)
+        half = PAD // 2
+        o["pair"][...] = jnp.concatenate([partners[0][0:half], partners[2][0:half]], axis=0)
     product(face, scale * q, i["stack"], o)
+    send_rows(face, jnp.zeros((PAD, q.shape[1]), F32), PAD, o)
 
 
 def six_columns(i, o):
     near = i["near"]
     rate = row(i["first"], 4)
-    both = rescale(i["swapped"][0:PAD, :], rate), rescale(i["swapped"][PAD:2 * PAD, :], rate)
+    half = PAD // 2
+    both = rescale(i["swapped"][0:half, :], rate), rescale(i["swapped"][half:, :], rate)
     o["six"][...] = ((near[0:PAD, :] + near[PAD:2 * PAD, :]) + near[2 * PAD:, :]) + (both[0] + both[1])
     return near[PAD:2 * PAD, :] + both[1]
 
@@ -524,14 +528,14 @@
     v = value(1, dict(t, **column, first=first))
     x = dict(xy_exchange(v), z=z_faces(a, v, t, got_modes)["z"])
 
-    near = dict(near=sds((3 * PAD, loads))) if small else {}
+    near = dict(near=sds((3 * PAD, loads)), pair=rows) if small else {}
     a = call(functools.partial(third_kernel, face), dict(x, stack=stack, first=first),
-             dict(q=vec, **near, **z_out(1)), flops=flops)
+             dict(q=vec, **near, **z_out(2)), flops=flops)
     q = a["q"]
     t = t_exchange(a, False)
     ins = dict(t, **column)
     if small:
-        ins.update(first=first, near=a["near"], swapped=swap(a["near"][0:2 * PAD], "gy", 0))
+        ins.update(first=first, near=a["near"], swapped=swap(a["pair"], "gy", 0))
         v = value(2, ins)
         sums = dict(six=v["six"])
     else:

time: 63.3 us -> 63.4 us (level)
  transfers between devices with their start and end apart: 31 -> 31, of which waited for: 17 -> 18; matrix products, arithmetic and copies ran while one was open for 0% -> 0% of each run, Pallas kernels for 4% -> 4%
where the time goes in v13:
time: 63.4 us; the launch traced here: 63.2 us
  starting transfers between devices  32.8 us (52%)
  waiting for transfers between devices  20.4 us (32%)
  Pallas kernels  9.21 us (15%)
  between operations  0.76 us (1%)
    ppermute x26, starting transfers between devices, swap(): return lax.ppermute(x, axis, [(k, (k + side(k)) % n) for k in range(n)])  29.8 us
    ppermute x26, waiting for transfers between devices, swap(): return lax.ppermute(x, axis, [(k, (k + side(k)) % n) for k in range(n)])  16.6 us
    pallas_call x13, Pallas kernels, call(): pl.pallas_call(run, out_shape=[outs[n] for n in names_out], in_specs=[vme...  5.26 us
    pallas_call x1, Pallas kernels, body(): pl.pallas_call(functools.partial(first_kernel, face, nz, n_modes, small),...  2.78 us
    ppermute x1, starting transfers between devices, move(): return lax.ppermute(x, ('gx', 'gy'), pairs)  2.37 us
    ppermute x4, waiting for transfers between devices, shift(): return lax.ppermute(x, axis, [(k, (k + by) % n) for k in range(n)])  2.35 us
    ppermute x1, waiting for transfers between devices, move(): return lax.ppermute(x, ('gx', 'gy'), pairs)  1.48 us
  transfers between devices with their start and end apart: 31, of which 18 were waited for; matrix products, arithmetic and copies ran while one was open for 0% of the time, Pallas kernels for 4%

profile of v13, /device:TPU:0, one launch (start us, length us, event | category | flops | bytes accessed | tf_op | source)
XLA Modules:
  0.0 63.2 jit_solution(6015013618535307017)
XLA Ops:
  0.6 2.8 %shard_map.59 = (f32[768,128]{1,0:T(8,128)S(1)}, bf16[1568,768]{1,0:T(8,128)(2,1)S(1)}, bf16[768,48]{1,0:T(8,128)(2,1)S(1)}, f32[8,128]{1,0:T(8,128)S(1)}, f32[5...) custom-call(f32[128,768]{1,0:T(8,128)} %bitcast.7, ...), custom_call_target="tpu_custom_call" | custom-call | flops 603979776 | bytes 2359296 | tf_op jit(solution)/shard_map/pallas_call | solution.py:494
  3.4 5.1 %collective-permute-start = (f32[160,128]{1,0:T(8,128)S(1)}, f32[160,128]{1,0:T(8,128)S(1)}, u32[]{:S(2)}, u32[]{:S(2)}) collective-permute-start(f32[160,128]{1,0:T(8,128)S(1)} %get-tuple-element.65.refs_1_), channel_id=1, source_target_pairs={{0,3},{1,2},{2,1},{3,0},{4,7},{5,6},{6,5},{7,4},{8,11},{9,10},{10,... | collective-permute-start | bytes 245768 | tf_op jit(solution)/shard_map/ppermute | solution.py:419
  9.2 1.4 %collective-permute-start.6 = (f32[136,128]{1,0:T(8,128)S(1)}, f32[136,128]{1,0:T(8,128)S(1)}, u32[]{:S(2)}, u32[]{:S(2)}) collective-permute-start(f32[136,128]{1,0:T(8,128)S(1)} %get-tuple-element.72.refs_0_), channel_id=1, source_target_pairs={{0,1},{1,0},{2,3},{3,2},{4,5},{5,4},{6,7},{7,6},{8,9},{9,8},{10,11... | collective-permute-start | bytes 208904 | tf_op jit(solution)/shard_map/ppermute | solution.py:419
  10.6 1.8 %collective-permute-done.2.refs_4_ = f32[24,128]{1,0:T(8,128)S(1)} collective-permute-done((f32[24,128]{1,0:T(8,128)S(1)}, f32[24,128]{1,0:T(8,128)S(1)}, u32[]{:S(2)}, u32[]{:S(2)}) %collective-permute-start.2) | collective-permute-done | bytes 12320 | tf_op jit(solution)/shard_map/ppermute | solution.py:419
  13.7 1.6 %collective-permute-start.3 = (f32[264,128]{1,0:T(8,128)S(1)}, f32[264,128]{1,0:T(8,128)S(1)}, u32[]{:S(2)}, u32[]{:S(2)}) collective-permute-start(f32[264,128]{1,0:T(8,128)S(1)} %get-tuple-element.69.refs_0_), channel_id=1, source_target_pairs={{0,16},{16,0},{1,17},{17,1},{2,18},{18,2},{3,19},{19,3},{4,20},{20... | collective-permute-start | bytes 405512 | tf_op jit(solution)/shard_map/ppermute | solution.py:419
  15.3 1.6 %collective-permute-start.4 = (f32[136,128]{1,0:T(8,128)S(1)}, f32[136,128]{1,0:T(8,128)S(1)}, u32[]{:S(2)}, u32[]{:S(2)}) collective-permute-start(f32[136,128]{1,0:T(8,128)S(1)} %get-tuple-element.70.refs_2_), channel_id=1, source_target_pairs={{0,4},{4,0},{8,12},{12,8},{1,5},{5,1},{9,13},{13,9},{2,6},{6,2},{1... | collective-permute-start | bytes 208904 | tf_op jit(solution)/shard_map/ppermute | solution.py:419
  17.8 2.0 %collective-permute-done.5.refs_5_ = f32[144,128]{1,0:T(8,128)S(1)} collective-permute-done((f32[144,128]{1,0:T(8,128)S(1)}, f32[144,128]{1,0:T(8,128)S(1)}, u32[]{:S(2)}, u32[]{:S(2)}) %collective-permute-start.5) | collective-permute-done | bytes 73760 | tf_op jit(solution)/shard_map/ppermute | solution.py:419
  20.6 2.3 %collective-permute-start.7 = (f32[144,128]{1,0:T(8,128)S(1)}, f32[144,128]{1,0:T(8,128)S(1)}, u32[]{:S(2)}, u32[]{:S(2)}) collective-permute-start(f32[144,128]{1,0:T(8,128)S(1)} %get-tuple-element.78.refs_1_), channel_id=1, source_target_pairs={{0,3},{1,2},{2,1},{3,0},{4,7},{5,6},{6,5},{7,4},{8,11},{9,10},{10,... | collective-permute-start | bytes 221192 | tf_op jit(solution)/shard_map/ppermute | solution.py:419
  23.0 2.1 %collective-permute-start.9 = (f32[16,128]{1,0:T(8,128)S(1)}, f32[16,128]{1,0:T(8,128)S(1)}, u32[]{:S(2)}, u32[]{:S(2)}) collective-permute-start(f32[16,128]{1,0:T(8,128)S(1)} %get-tuple-element.76.refs_0_), channel_id=1, source_target_pairs={{0,1},{1,0},{2,3},{3,2},{4,5},{5,4},{6,7},{7,6},{8,9},{9,8},{10,11... | collective-permute-start | bytes 24584 | tf_op jit(solution)/shard_map/ppermute | solution.py:419
  25.1 2.0 %collective-permute-done.9.refs_4_ = f32[16,128]{1,0:T(8,128)S(1)} collective-permute-done((f32[16,128]{1,0:T(8,128)S(1)}, f32[16,128]{1,0:T(8,128)S(1)}, u32[]{:S(2)}, u32[]{:S(2)}) %collective-permute-start.9) | collective-permute-done | bytes 8224 | tf_op jit(solution)/shard_map/ppermute | solution.py:419
  28.5 1.6 %collective-permute-start.11 = (f32[136,128]{1,0:T(8,128)S(1)}, f32[136,128]{1,0:T(8,128)S(1)}, u32[]{:S(2)}, u32[]{:S(2)}) collective-permute-start(f32[136,128]{1,0:T(8,128)S(1)} %get-tuple-element.83.refs_2_), channel_id=1, source_target_pairs={{0,4},{4,0},{8,12},{12,8},{1,5},{5,1},{9,13},{13,9},{2,6},{6,2},{1... | collective-permute-start | bytes 208904 | tf_op jit(solution)/shard_map/ppermute | solution.py:419
  30.9 2.1 %collective-permute-done.12.refs_5_ = f32[144,128]{1,0:T(8,128)S(1)} collective-permute-done((f32[144,128]{1,0:T(8,128)S(1)}, f32[144,128]{1,0:T(8,128)S(1)}, u32[]{:S(2)}, u32[]{:S(2)}) %collective-permute-start.12) | collective-permute-done | bytes 73760 | tf_op jit(solution)/shard_map/ppermute | solution.py:419
  33.9 2.4 %collective-permute-start.14 = (f32[144,128]{1,0:T(8,128)S(1)}, f32[144,128]{1,0:T(8,128)S(1)}, u32[]{:S(2)}, u32[]{:S(2)}) collective-permute-start(f32[144,128]{1,0:T(8,128)S(1)} %get-tuple-element.91.refs_1_), channel_id=1, source_target_pairs={{0,3},{1,2},{2,1},{3,0},{4,7},{5,6},{6,5},{7,4},{8,11},{9,10},{10,... | collective-permute-start | bytes 221192 | tf_op jit(solution)/shard_map/ppermute | solution.py:419
  36.5 1.8 %collective-permute-start.16 = (f32[16,128]{1,0:T(8,128)S(1)}, f32[16,128]{1,0:T(8,128)S(1)}, u32[]{:S(2)}, u32[]{:S(2)}) collective-permute-start(f32[16,128]{1,0:T(8,128)S(1)} %get-tuple-element.89.refs_0_), channel_id=1, source_target_pairs={{0,1},{1,0},{2,3},{3,2},{4,5},{5,4},{6,7},{7,6},{8,9},{9,8},{10,11... | collective-permute-start | bytes 24584 | tf_op jit(solution)/shard_map/ppermute | solution.py:419
  41.3 1.0 %collective-permute-start.18 = (f32[264,128]{1,0:T(8,128)S(1)}, f32[264,128]{1,0:T(8,128)S(1)}, u32[]{:S(2)}, u32[]{:S(2)}) collective-permute-start(f32[264,128]{1,0:T(8,128)S(1)} %get-tuple-element.95.refs_0_), channel_id=1, source_target_pairs={{0,16},{16,0},{1,17},{17,1},{2,18},{18,2},{3,19},{19,3},{4,20},{20... | collective-permute-start | bytes 405512 | tf_op jit(solution)/shard_map/ppermute | solution.py:419
  42.3 1.3 %collective-permute-start.19 = (f32[128,128]{1,0:T(8,128)S(1)}, f32[128,128]{1,0:T(8,128)S(1)}, u32[]{:S(2)}, u32[]{:S(2)}) collective-permute-start(f32[128,128]{1,0:T(8,128)S(1)} %get-tuple-element.96.refs_2_), channel_id=1, source_target_pairs={{0,4},{4,0},{8,12},{12,8},{1,5},{5,1},{9,13},{13,9},{2,6},{6,2},{1... | collective-permute-start | bytes 196616 | tf_op jit(solution)/shard_map/ppermute | solution.py:419
  44.5 2.1 %collective-permute-done.20.refs_5_ = f32[144,128]{1,0:T(8,128)S(1)} collective-permute-done((f32[144,128]{1,0:T(8,128)S(1)}, f32[144,128]{1,0:T(8,128)S(1)}, u32[]{:S(2)}, u32[]{:S(2)}) %collective-permute-start.20) | collective-permute-done | bytes 73760 | tf_op jit(solution)/shard_map/ppermute | solution.py:419
  46.6 1.1 %shard_map.68 = (f32[768,128]{1,0:T(8,128)S(1)}, f32[768,128]{1,0:T(8,128)S(1)}, f32[768,128]{1,0:T(8,128)S(1)}, f32[8,128]{1,0:T(8,128)S(1)}, f32[512,128]{1,0:...) custom-call(f32[264,128]{1,0:T(8,128)S(1)} %get-tuple-element.95.ref, ...), custom_call_target="tpu_custom_call" | custom-call | flops 603979776 | bytes 5881856 | tf_op jit(solution)/shard_map/pallas_call | solution.py:31
  47.7 2.3 %collective-permute-start.22 = (f32[144,128]{1,0:T(8,128)S(1)}, f32[144,128]{1,0:T(8,128)S(1)}, u32[]{:S(2)}, u32[]{:S(2)}) collective-permute-start(f32[144,128]{1,0:T(8,128)S(1)} %get-tuple-element.106.refs_1_), channel_id=1, source_target_pairs={{0,3},{1,2},{2,1},{3,0},{4,7},{5,6},{6,5},{7,4},{8,11},{9,10},{10,... | collective-permute-start | bytes 221192 | tf_op jit(solution)/shard_map/ppermute | solution.py:419
  50.3 1.9 %collective-permute-start.24 = (f32[16,128]{1,0:T(8,128)S(1)}, f32[16,128]{1,0:T(8,128)S(1)}, u32[]{:S(2)}, u32[]{:S(2)}) collective-permute-start(f32[16,128]{1,0:T(8,128)S(1)} %get-tuple-element.104.refs_0_), channel_id=1, source_target_pairs={{0,1},{1,0},{2,3},{3,2},{4,5},{5,4},{6,7},{7,6},{8,9},{9,8},{10,11... | collective-permute-start | bytes 24584 | tf_op jit(solution)/shard_map/ppermute | solution.py:419
  52.3 1.9 %collective-permute-done.24.refs_4_ = f32[16,128]{1,0:T(8,128)S(1)} collective-permute-done((f32[16,128]{1,0:T(8,128)S(1)}, f32[16,128]{1,0:T(8,128)S(1)}, u32[]{:S(2)}, u32[]{:S(2)}) %collective-permute-start.24) | collective-permute-done | bytes 8224 | tf_op jit(solution)/shard_map/ppermute | solution.py:419
  56.0 2.4 %collective-permute-start.25 = (f32[8,128]{1,0:T(8,128)S(1)}, f32[8,128]{1,0:T(8,128)S(1)}, u32[]{:S(2)}, u32[]{:S(2)}) collective-permute-start(f32[8,128]{1,0:T(8,128)S(1)} %get-tuple-element.108.refs_0_), channel_id=1, source_target_pairs={{0,28},{4,24},{8,20},{12,16},{16,12},{20,8},{24,4},{28,0},{1,29},{... | collective-permute-start | bytes 12296 | tf_op jit(solution)/shard_map/ppermute | solution.py:424
  58.5 1.5 %collective-permute-done.25.refs_1_ = f32[8,128]{1,0:T(8,128)S(1)} collective-permute-done((f32[8,128]{1,0:T(8,128)S(1)}, f32[8,128]{1,0:T(8,128)S(1)}, u32[]{:S(2)}, u32[]{:S(2)}) %collective-permute-start.25) | collective-permute-done | bytes 4128 | tf_op jit(solution)/shard_map/ppermute | solution.py:424
  62.1 1.2 %shard_map.73 = (f32[128,768]{1,0:T(8,128)}, f32[128,768]{1,0:T(8,128)}) custom-call(f32[8,128]{1,0:T(8,128)S(1)} %shard_map.71.refs_0_, f32[8,128]{1,0:T(8,128)S(1)} %collective-permute-done.29.refs_1_, f32[768,128]{1,0:T(8,128)S(1)} %get-tuple-element.116.refs_2_, f32[768,128]{1,0:T(8,128)S(1)} %get-tuple-element.117.refs_3_, ...), custom_call_target="tpu_custom_call" | custom-call | flops 1966080 | bytes 3538944 | tf_op jit(solution)/shard_map/pallas_call | solution.py:567
  (53 shorter events, 15.5 us)
Async XLA Ops:
  3.4 9.9 %collective-permute-start = (f32[160,128]{1,0:T(8,128)S(1)}, f32[160,128]{1,0:T(8,128)S(1)}, u32[]{:S(2)}, u32[]{:S(2)}) collective-permute-start(f32[160,128]{1,0:T(8,128)S(1)} %get-tuple-element.65.refs_1_), channel_id=1, source_target_pairs={{0,3},{1,2},{2,1},{3,0},{4,7},{5,6},{6,5},{7,4},{8,11},{9,10},{10,... | collective-permute-start | bytes 245768 | tf_op jit(solution)/shard_map/ppermute | solution.py:419
  8.5 4.7 %collective-permute-start.1 = (f32[32,128]{1,0:T(8,128)S(1)}, f32[32,128]{1,0:T(8,128)S(1)}, u32[]{:S(2)}, u32[]{:S(2)}) collective-permute-start(f32[32,128]{1,0:T(8,128)S(1)} %get-tuple-element.66), channel_id=1, source_target_pairs={{0,2},{1,3},{2,0},{3,1},{4,6},{5,7},{6,4},{7,5},{8,10},{9,11},{10,... | collective-permute-start | bytes 49160 | tf_op jit(solution)/shard_map/ppermute | solution.py:414
  9.2 7.7 %collective-permute-start.6 = (f32[136,128]{1,0:T(8,128)S(1)}, f32[136,128]{1,0:T(8,128)S(1)}, u32[]{:S(2)}, u32[]{:S(2)}) collective-permute-start(f32[136,128]{1,0:T(8,128)S(1)} %get-tuple-element.72.refs_0_), channel_id=1, source_target_pairs={{0,1},{1,0},{2,3},{3,2},{4,5},{5,4},{6,7},{7,6},{8,9},{9,8},{10,11... | collective-permute-start | bytes 208904 | tf_op jit(solution)/shard_map/ppermute | solution.py:419
  13.7 6.1 %collective-permute-start.3 = (f32[264,128]{1,0:T(8,128)S(1)}, f32[264,128]{1,0:T(8,128)S(1)}, u32[]{:S(2)}, u32[]{:S(2)}) collective-permute-start(f32[264,128]{1,0:T(8,128)S(1)} %get-tuple-element.69.refs_0_), channel_id=1, source_target_pairs={{0,16},{16,0},{1,17},{17,1},{2,18},{18,2},{3,19},{19,3},{4,20},{20... | collective-permute-start | bytes 405512 | tf_op jit(solution)/shard_map/ppermute | solution.py:419
  15.2 4.5 %collective-permute-start.5 = (f32[144,128]{1,0:T(8,128)S(1)}, f32[144,128]{1,0:T(8,128)S(1)}, u32[]{:S(2)}, u32[]{:S(2)}) collective-permute-start(f32[144,128]{1,0:T(8,128)S(1)} %get-tuple-element.71.refs_3_), channel_id=1, source_target_pairs={{0,12},{4,8},{8,4},{12,0},{1,13},{5,9},{9,5},{13,1},{2,14},{6,10},... | collective-permute-start | bytes 221192 | tf_op jit(solution)/shard_map/ppermute | solution.py:419
  20.6 6.9 %collective-permute-start.7 = (f32[144,128]{1,0:T(8,128)S(1)}, f32[144,128]{1,0:T(8,128)S(1)}, u32[]{:S(2)}, u32[]{:S(2)}) collective-permute-start(f32[144,128]{1,0:T(8,128)S(1)} %get-tuple-element.78.refs_1_), channel_id=1, source_target_pairs={{0,3},{1,2},{2,1},{3,0},{4,7},{5,6},{6,5},{7,4},{8,11},{9,10},{10,... | collective-permute-start | bytes 221192 | tf_op jit(solution)/shard_map/ppermute | solution.py:419
  22.9 4.6 %collective-permute-start.8 = (f32[24,128]{1,0:T(8,128)S(1)}, f32[24,128]{1,0:T(8,128)S(1)}, u32[]{:S(2)}, u32[]{:S(2)}) collective-permute-start(f32[24,128]{1,0:T(8,128)S(1)} %get-tuple-element.79), channel_id=1, source_target_pairs={{0,2},{1,3},{2,0},{3,1},{4,6},{5,7},{6,4},{7,5},{8,10},{9,11},{10,... | collective-permute-start | bytes 36872 | tf_op jit(solution)/shard_map/ppermute | solution.py:414
  23.0 4.2 %collective-permute-start.9 = (f32[16,128]{1,0:T(8,128)S(1)}, f32[16,128]{1,0:T(8,128)S(1)}, u32[]{:S(2)}, u32[]{:S(2)}) collective-permute-start(f32[16,128]{1,0:T(8,128)S(1)} %get-tuple-element.76.refs_0_), channel_id=1, source_target_pairs={{0,1},{1,0},{2,3},{3,2},{4,5},{5,4},{6,7},{7,6},{8,9},{9,8},{10,11... | collective-permute-start | bytes 24584 | tf_op jit(solution)/shard_map/ppermute | solution.py:419
  25.1 5.0 %collective-permute-start.13 = (f32[128,128]{1,0:T(8,128)S(1)}, f32[128,128]{1,0:T(8,128)S(1)}, u32[]{:S(2)}, u32[]{:S(2)}) collective-permute-start(f32[128,128]{1,0:T(8,128)S(1)} %get-tuple-element.85.refs_0_), channel_id=1, source_target_pairs={{0,1},{1,0},{2,3},{3,2},{4,5},{5,4},{6,7},{7,6},{8,9},{9,8},{10,11... | collective-permute-start | bytes 196616 | tf_op jit(solution)/shard_map/ppermute | solution.py:419
  27.8 5.2 %collective-permute-start.10 = (f32[264,128]{1,0:T(8,128)S(1)}, f32[264,128]{1,0:T(8,128)S(1)}, u32[]{:S(2)}, u32[]{:S(2)}) collective-permute-start(f32[264,128]{1,0:T(8,128)S(1)} %get-tuple-element.82.refs_0_), channel_id=1, source_target_pairs={{0,16},{16,0},{1,17},{17,1},{2,18},{18,2},{3,19},{19,3},{4,20},{20... | collective-permute-start | bytes 405512 | tf_op jit(solution)/shard_map/ppermute | solution.py:419
  28.5 4.6 %collective-permute-start.12 = (f32[144,128]{1,0:T(8,128)S(1)}, f32[144,128]{1,0:T(8,128)S(1)}, u32[]{:S(2)}, u32[]{:S(2)}) collective-permute-start(f32[144,128]{1,0:T(8,128)S(1)} %get-tuple-element.84.refs_3_), channel_id=1, source_target_pairs={{0,12},{4,8},{8,4},{12,0},{1,13},{5,9},{9,5},{13,1},{2,14},{6,10},... | collective-permute-start | bytes 221192 | tf_op jit(solution)/shard_map/ppermute | solution.py:419
  33.9 7.1 %collective-permute-start.14 = (f32[144,128]{1,0:T(8,128)S(1)}, f32[144,128]{1,0:T(8,128)S(1)}, u32[]{:S(2)}, u32[]{:S(2)}) collective-permute-start(f32[144,128]{1,0:T(8,128)S(1)} %get-tuple-element.91.refs_1_), channel_id=1, source_target_pairs={{0,3},{1,2},{2,1},{3,0},{4,7},{5,6},{6,5},{7,4},{8,11},{9,10},{10,... | collective-permute-start | bytes 221192 | tf_op jit(solution)/shard_map/ppermute | solution.py:419
  36.3 4.7 %collective-permute-start.15 = (f32[24,128]{1,0:T(8,128)S(1)}, f32[24,128]{1,0:T(8,128)S(1)}, u32[]{:S(2)}, u32[]{:S(2)}) collective-permute-start(f32[24,128]{1,0:T(8,128)S(1)} %get-tuple-element.92), channel_id=1, source_target_pairs={{0,2},{1,3},{2,0},{3,1},{4,6},{5,7},{6,4},{7,5},{8,10},{9,11},{10,... | collective-permute-start | bytes 36872 | tf_op jit(solution)/shard_map/ppermute | solution.py:414
  36.5 3.9 %collective-permute-start.16 = (f32[16,128]{1,0:T(8,128)S(1)}, f32[16,128]{1,0:T(8,128)S(1)}, u32[]{:S(2)}, u32[]{:S(2)}) collective-permute-start(f32[16,128]{1,0:T(8,128)S(1)} %get-tuple-element.89.refs_0_), channel_id=1, source_target_pairs={{0,1},{1,0},{2,3},{3,2},{4,5},{5,4},{6,7},{7,6},{8,9},{9,8},{10,11... | collective-permute-start | bytes 24584 | tf_op jit(solution)/shard_map/ppermute | solution.py:419
  38.3 5.3 %collective-permute-start.21 = (f32[128,128]{1,0:T(8,128)S(1)}, f32[128,128]{1,0:T(8,128)S(1)}, u32[]{:S(2)}, u32[]{:S(2)}) collective-permute-start(f32[128,128]{1,0:T(8,128)S(1)} %get-tuple-element.98.refs_0_), channel_id=1, source_target_pairs={{0,1},{1,0},{2,3},{3,2},{4,5},{5,4},{6,7},{7,6},{8,9},{9,8},{10,11... | collective-permute-start | bytes 196616 | tf_op jit(solution)/shard_map/ppermute | solution.py:419
  41.3 5.3 %collective-permute-start.18 = (f32[264,128]{1,0:T(8,128)S(1)}, f32[264,128]{1,0:T(8,128)S(1)}, u32[]{:S(2)}, u32[]{:S(2)}) collective-permute-start(f32[264,128]{1,0:T(8,128)S(1)} %get-tuple-element.95.refs_0_), channel_id=1, source_target_pairs={{0,16},{16,0},{1,17},{17,1},{2,18},{18,2},{3,19},{19,3},{4,20},{20... | collective-permute-start | bytes 405512 | tf_op jit(solution)/shard_map/ppermute | solution.py:419
  42.3 4.3 %collective-permute-start.20 = (f32[144,128]{1,0:T(8,128)S(1)}, f32[144,128]{1,0:T(8,128)S(1)}, u32[]{:S(2)}, u32[]{:S(2)}) collective-permute-start(f32[144,128]{1,0:T(8,128)S(1)} %get-tuple-element.97.refs_3_), channel_id=1, source_target_pairs={{0,12},{4,8},{8,4},{12,0},{1,13},{5,9},{9,5},{13,1},{2,14},{6,10},... | collective-permute-start | bytes 221192 | tf_op jit(solution)/shard_map/ppermute | solution.py:419
  47.7 7.0 %collective-permute-start.22 = (f32[144,128]{1,0:T(8,128)S(1)}, f32[144,128]{1,0:T(8,128)S(1)}, u32[]{:S(2)}, u32[]{:S(2)}) collective-permute-start(f32[144,128]{1,0:T(8,128)S(1)} %get-tuple-element.106.refs_1_), channel_id=1, source_target_pairs={{0,3},{1,2},{2,1},{3,0},{4,7},{5,6},{6,5},{7,4},{8,11},{9,10},{10,... | collective-permute-start | bytes 221192 | tf_op jit(solution)/shard_map/ppermute | solution.py:419
  50.0 4.7 %collective-permute-start.23 = (f32[24,128]{1,0:T(8,128)S(1)}, f32[24,128]{1,0:T(8,128)S(1)}, u32[]{:S(2)}, u32[]{:S(2)}) collective-permute-start(f32[24,128]{1,0:T(8,128)S(1)} %get-tuple-element.107), channel_id=1, source_target_pairs={{0,2},{1,3},{2,0},{3,1},{4,6},{5,7},{6,4},{7,5},{8,10},{9,11},{10,... | collective-permute-start | bytes 36872 | tf_op jit(solution)/shard_map/ppermute | solution.py:414
  50.3 4.0 %collective-permute-start.24 = (f32[16,128]{1,0:T(8,128)S(1)}, f32[16,128]{1,0:T(8,128)S(1)}, u32[]{:S(2)}, u32[]{:S(2)}) collective-permute-start(f32[16,128]{1,0:T(8,128)S(1)} %get-tuple-element.104.refs_0_), channel_id=1, source_target_pairs={{0,1},{1,0},{2,3},{3,2},{4,5},{5,4},{6,7},{7,6},{8,9},{9,8},{10,11... | collective-permute-start | bytes 24584 | tf_op jit(solution)/shard_map/ppermute | solution.py:419
  52.2 6.2 %collective-permute-start.28 = (f32[128,128]{1,0:T(8,128)S(1)}, f32[128,128]{1,0:T(8,128)S(1)}, u32[]{:S(2)}, u32[]{:S(2)}) collective-permute-start(f32[128,128]{1,0:T(8,128)S(1)} %get-tuple-element.111.refs_0_), channel_id=1, source_target_pairs={{0,1},{1,0},{2,3},{3,2},{4,5},{5,4},{6,7},{7,6},{8,9},{9,8},{10,11... | collective-permute-start | bytes 196616 | tf_op jit(solution)/shard_map/ppermute | solution.py:419
  55.1 5.2 %collective-permute-start.26 = (f32[264,128]{1,0:T(8,128)S(1)}, f32[264,128]{1,0:T(8,128)S(1)}, u32[]{:S(2)}, u32[]{:S(2)}) collective-permute-start(f32[264,128]{1,0:T(8,128)S(1)} %get-tuple-element.109.refs_0_), channel_id=1, source_target_pairs={{0,16},{16,0},{1,17},{17,1},{2,18},{18,2},{3,19},{19,3},{4,20},{20... | collective-permute-start | bytes 405512 | tf_op jit(solution)/shard_map/ppermute | solution.py:419
  55.7 4.5 %collective-permute-start.27 = (f32[144,128]{1,0:T(8,128)S(1)}, f32[144,128]{1,0:T(8,128)S(1)}, u32[]{:S(2)}, u32[]{:S(2)}) collective-permute-start(f32[144,128]{1,0:T(8,128)S(1)} %get-tuple-element.110.refs_3_), channel_id=1, source_target_pairs={{0,12},{4,8},{8,4},{12,0},{1,13},{5,9},{9,5},{13,1},{2,14},{6,10},... | collective-permute-start | bytes 221192 | tf_op jit(solution)/shard_map/ppermute | solution.py:419
  56.0 4.0 %collective-permute-start.25 = (f32[8,128]{1,0:T(8,128)S(1)}, f32[8,128]{1,0:T(8,128)S(1)}, u32[]{:S(2)}, u32[]{:S(2)}) collective-permute-start(f32[8,128]{1,0:T(8,128)S(1)} %get-tuple-element.108.refs_0_), channel_id=1, source_target_pairs={{0,28},{4,24},{8,20},{12,16},{16,12},{20,8},{24,4},{28,0},{1,29},{... | collective-permute-start | bytes 12296 | tf_op jit(solution)/shard_map/ppermute | solution.py:424
  (7 other events, 16.9 us)

commit v14 on v11

--- a/solution.py
+++ b/solution.py
@@ -51,9 +51,13 @@
     return high, mid, (rest - mid.astype(F32)).astype(BF16)
 
 
+def left_pieces(x):
+    high, mid, low = split3(x)
+    return jnp.concatenate([high, high, mid, mid, high, low], axis=1)
+
+
 def mode_pieces(modes):
-    high, mid, low = split3(modes.T)
-    return jnp.concatenate([high, high, mid, mid, high, low], axis=1)
+    return left_pieces(modes.T)
 
 
 def amp_pieces(amp):
@@ -221,10 +225,11 @@
         n = loads.shape[0]
         coarse = jnp.concatenate([part[:, k * n:(k + 1) * n] for k, part in enumerate(
             [i["c_own"][...]] + column_rows(face, i, 2 * PAD)[1:])], axis=0)
+        coarse = left_pieces(coarse)
         o["c_all"][...] = coarse
     else:
         coarse = i["c_all"][...]
-    amp = dot32(coarse, loads)
+    amp = dot32(coarse, loads) if gathered else dot16(coarse, amp_pieces(loads))
     o["amp"][...] = amp[0:3 * PAD]
     xy = i["y"][...] + dot16(i["mt"][0:4 * face, :], amp_pieces(amp[0:PAD]))
     cols = loads.shape[1]
@@ -460,7 +465,7 @@
         outs = dict(amp=sds((3 * PAD, loads)), xab=sds((2 * face + (PAD if small else extra), loads)),
                     ya=sds((face + extra, loads)), yb=sds((face + 2 * PAD, loads)))
         if stage == 0 and small:
-            outs["c_all"] = sds((nz * PAD, nz * PAD))
+            outs["c_all"] = sds((nz * PAD, 6 * nz * PAD), BF16)
         if stage == 2 and small:
             outs["six"] = rows
         if stage == 3:

time: 63.3 us -> 63.2 us (level)
  no operation moved by 1% of the time
where the time goes in v14:
time: 63.2 us; the launch traced here: 63.1 us
  starting transfers between devices  32.9 us (52%)
  waiting for transfers between devices  20.3 us (32%)
  Pallas kernels  9.18 us (15%)
  between operations  0.76 us (1%)
    ppermute x26, starting transfers between devices, swap(): return lax.ppermute(x, axis, [(k, (k + side(k)) % n) for k in range(n)])  30 us
    ppermute x26, waiting for transfers between devices, swap(): return lax.ppermute(x, axis, [(k, (k + side(k)) % n) for k in range(n)])  16.3 us
    pallas_call x13, Pallas kernels, call(): pl.pallas_call(run, out_shape=[outs[n] for n in names_out], in_specs=[vme...  5.23 us
    pallas_call x1, Pallas kernels, body(): pl.pallas_call(functools.partial(first_kernel, face, nz, n_modes, small),...  2.78 us
    ppermute x4, waiting for transfers between devices, shift(): return lax.ppermute(x, axis, [(k, (k + by) % n) for k in range(n)])  2.39 us
    ppermute x1, starting transfers between devices, move(): return lax.ppermute(x, ('gx', 'gy'), pairs)  2.25 us
    ppermute x1, waiting for transfers between devices, move(): return lax.ppermute(x, ('gx', 'gy'), pairs)  1.6 us
  transfers between devices with their start and end apart: 31, of which 17 were waited for; matrix products, arithmetic and copies ran while one was open for 0% of the time, Pallas kernels for 4%

profile of v14, /device:TPU:0, one launch (start us, length us, event | category | flops | bytes accessed | tf_op | source)
XLA Modules:
  0.0 63.1 jit_solution(2965577347208948507)
XLA Ops:
  0.6 2.8 %shard_map.59 = (f32[768,128]{1,0:T(8,128)S(1)}, bf16[1568,768]{1,0:T(8,128)(2,1)S(1)}, bf16[768,48]{1,0:T(8,128)(2,1)S(1)}, f32[8,128]{1,0:T(8,128)S(1)}, f32[5...) custom-call(f32[128,768]{1,0:T(8,128)} %bitcast.7, ...), custom_call_target="tpu_custom_call" | custom-call | flops 603979776 | bytes 2359296 | tf_op jit(solution)/shard_map/pallas_call | solution.py:495
  3.4 5.1 %collective-permute-start = (f32[160,128]{1,0:T(8,128)S(1)}, f32[160,128]{1,0:T(8,128)S(1)}, u32[]{:S(2)}, u32[]{:S(2)}) collective-permute-start(f32[160,128]{1,0:T(8,128)S(1)} %get-tuple-element.64.refs_1_), channel_id=1, source_target_pairs={{0,3},{1,2},{2,1},{3,0},{4,7},{5,6},{6,5},{7,4},{8,11},{9,10},{10,... | collective-permute-start | bytes 245768 | tf_op jit(solution)/shard_map/ppermute | solution.py:420
  9.2 1.4 %collective-permute-start.6 = (f32[136,128]{1,0:T(8,128)S(1)}, f32[136,128]{1,0:T(8,128)S(1)}, u32[]{:S(2)}, u32[]{:S(2)}) collective-permute-start(f32[136,128]{1,0:T(8,128)S(1)} %get-tuple-element.71.refs_0_), channel_id=1, source_target_pairs={{0,1},{1,0},{2,3},{3,2},{4,5},{5,4},{6,7},{7,6},{8,9},{9,8},{10,11... | collective-permute-start | bytes 208904 | tf_op jit(solution)/shard_map/ppermute | solution.py:420
  10.6 1.8 %collective-permute-done.2.refs_4_ = f32[24,128]{1,0:T(8,128)S(1)} collective-permute-done((f32[24,128]{1,0:T(8,128)S(1)}, f32[24,128]{1,0:T(8,128)S(1)}, u32[]{:S(2)}, u32[]{:S(2)}) %collective-permute-start.2) | collective-permute-done | bytes 12320 | tf_op jit(solution)/shard_map/ppermute | solution.py:420
  13.7 1.6 %collective-permute-start.3 = (f32[264,128]{1,0:T(8,128)S(1)}, f32[264,128]{1,0:T(8,128)S(1)}, u32[]{:S(2)}, u32[]{:S(2)}) collective-permute-start(f32[264,128]{1,0:T(8,128)S(1)} %get-tuple-element.68.refs_0_), channel_id=1, source_target_pairs={{0,16},{16,0},{1,17},{17,1},{2,18},{18,2},{3,19},{19,3},{4,20},{20... | collective-permute-start | bytes 405512 | tf_op jit(solution)/shard_map/ppermute | solution.py:420
  15.3 1.6 %collective-permute-start.4 = (f32[136,128]{1,0:T(8,128)S(1)}, f32[136,128]{1,0:T(8,128)S(1)}, u32[]{:S(2)}, u32[]{:S(2)}) collective-permute-start(f32[136,128]{1,0:T(8,128)S(1)} %get-tuple-element.69.refs_2_), channel_id=1, source_target_pairs={{0,4},{4,0},{8,12},{12,8},{1,5},{5,1},{9,13},{13,9},{2,6},{6,2},{1... | collective-permute-start | bytes 208904 | tf_op jit(solution)/shard_map/ppermute | solution.py:420
  17.8 2.0 %collective-permute-done.5.refs_5_ = f32[144,128]{1,0:T(8,128)S(1)} collective-permute-done((f32[144,128]{1,0:T(8,128)S(1)}, f32[144,128]{1,0:T(8,128)S(1)}, u32[]{:S(2)}, u32[]{:S(2)}) %collective-permute-start.5) | collective-permute-done | bytes 73760 | tf_op jit(solution)/shard_map/ppermute | solution.py:420
  20.6 2.3 %collective-permute-start.7 = (f32[144,128]{1,0:T(8,128)S(1)}, f32[144,128]{1,0:T(8,128)S(1)}, u32[]{:S(2)}, u32[]{:S(2)}) collective-permute-start(f32[144,128]{1,0:T(8,128)S(1)} %get-tuple-element.77.refs_1_), channel_id=1, source_target_pairs={{0,3},{1,2},{2,1},{3,0},{4,7},{5,6},{6,5},{7,4},{8,11},{9,10},{10,... | collective-permute-start | bytes 221192 | tf_op jit(solution)/shard_map/ppermute | solution.py:420
  23.0 2.1 %collective-permute-start.9 = (f32[16,128]{1,0:T(8,128)S(1)}, f32[16,128]{1,0:T(8,128)S(1)}, u32[]{:S(2)}, u32[]{:S(2)}) collective-permute-start(f32[16,128]{1,0:T(8,128)S(1)} %get-tuple-element.75.refs_0_), channel_id=1, source_target_pairs={{0,1},{1,0},{2,3},{3,2},{4,5},{5,4},{6,7},{7,6},{8,9},{9,8},{10,11... | collective-permute-start | bytes 24584 | tf_op jit(solution)/shard_map/ppermute | solution.py:420
  25.1 2.0 %collective-permute-done.9.refs_4_ = f32[16,128]{1,0:T(8,128)S(1)} collective-permute-done((f32[16,128]{1,0:T(8,128)S(1)}, f32[16,128]{1,0:T(8,128)S(1)}, u32[]{:S(2)}, u32[]{:S(2)}) %collective-permute-start.9) | collective-permute-done | bytes 8224 | tf_op jit(solution)/shard_map/ppermute | solution.py:420
  28.5 1.6 %collective-permute-start.11 = (f32[136,128]{1,0:T(8,128)S(1)}, f32[136,128]{1,0:T(8,128)S(1)}, u32[]{:S(2)}, u32[]{:S(2)}) collective-permute-start(f32[136,128]{1,0:T(8,128)S(1)} %get-tuple-element.82.refs_2_), channel_id=1, source_target_pairs={{0,4},{4,0},{8,12},{12,8},{1,5},{5,1},{9,13},{13,9},{2,6},{6,2},{1... | collective-permute-start | bytes 208904 | tf_op jit(solution)/shard_map/ppermute | solution.py:420
  31.0 2.1 %collective-permute-done.12.refs_5_ = f32[144,128]{1,0:T(8,128)S(1)} collective-permute-done((f32[144,128]{1,0:T(8,128)S(1)}, f32[144,128]{1,0:T(8,128)S(1)}, u32[]{:S(2)}, u32[]{:S(2)}) %collective-permute-start.12) | collective-permute-done | bytes 73760 | tf_op jit(solution)/shard_map/ppermute | solution.py:420
  33.9 2.4 %collective-permute-start.14 = (f32[136,128]{1,0:T(8,128)S(1)}, f32[136,128]{1,0:T(8,128)S(1)}, u32[]{:S(2)}, u32[]{:S(2)}) collective-permute-start(f32[136,128]{1,0:T(8,128)S(1)} %get-tuple-element.90.refs_1_), channel_id=1, source_target_pairs={{0,3},{1,2},{2,1},{3,0},{4,7},{5,6},{6,5},{7,4},{8,11},{9,10},{10,... | collective-permute-start | bytes 208904 | tf_op jit(solution)/shard_map/ppermute | solution.py:420
  36.6 1.8 %collective-permute-start.16 = (f32[8,128]{1,0:T(8,128)S(1)}, f32[8,128]{1,0:T(8,128)S(1)}, u32[]{:S(2)}, u32[]{:S(2)}) collective-permute-start(f32[8,128]{1,0:T(8,128)S(1)} %get-tuple-element.88.refs_0_), channel_id=1, source_target_pairs={{0,1},{1,0},{2,3},{3,2},{4,5},{5,4},{6,7},{7,6},{8,9},{9,8},{10,11... | collective-permute-start | bytes 12296 | tf_op jit(solution)/shard_map/ppermute | solution.py:420
  38.6 1.6 %collective-permute-done.16.refs_4_ = f32[8,128]{1,0:T(8,128)S(1)} collective-permute-done((f32[8,128]{1,0:T(8,128)S(1)}, f32[8,128]{1,0:T(8,128)S(1)}, u32[]{:S(2)}, u32[]{:S(2)}) %collective-permute-start.16) | collective-permute-done | bytes 4128 | tf_op jit(solution)/shard_map/ppermute | solution.py:420
  41.2 1.1 %collective-permute-start.18 = (f32[264,128]{1,0:T(8,128)S(1)}, f32[264,128]{1,0:T(8,128)S(1)}, u32[]{:S(2)}, u32[]{:S(2)}) collective-permute-start(f32[264,128]{1,0:T(8,128)S(1)} %get-tuple-element.93.refs_0_), channel_id=1, source_target_pairs={{0,16},{16,0},{1,17},{17,1},{2,18},{18,2},{3,19},{19,3},{4,20},{20... | collective-permute-start | bytes 405512 | tf_op jit(solution)/shard_map/ppermute | solution.py:420
  42.3 1.3 %collective-permute-start.19 = (f32[128,128]{1,0:T(8,128)S(1)}, f32[128,128]{1,0:T(8,128)S(1)}, u32[]{:S(2)}, u32[]{:S(2)}) collective-permute-start(f32[128,128]{1,0:T(8,128)S(1)} %get-tuple-element.94.refs_2_), channel_id=1, source_target_pairs={{0,4},{4,0},{8,12},{12,8},{1,5},{5,1},{9,13},{13,9},{2,6},{6,2},{1... | collective-permute-start | bytes 196616 | tf_op jit(solution)/shard_map/ppermute | solution.py:420
  44.4 2.1 %collective-permute-done.20.refs_5_ = f32[144,128]{1,0:T(8,128)S(1)} collective-permute-done((f32[144,128]{1,0:T(8,128)S(1)}, f32[144,128]{1,0:T(8,128)S(1)}, u32[]{:S(2)}, u32[]{:S(2)}) %collective-permute-start.20) | collective-permute-done | bytes 73760 | tf_op jit(solution)/shard_map/ppermute | solution.py:420
  47.6 2.3 %collective-permute-start.22 = (f32[144,128]{1,0:T(8,128)S(1)}, f32[144,128]{1,0:T(8,128)S(1)}, u32[]{:S(2)}, u32[]{:S(2)}) collective-permute-start(f32[144,128]{1,0:T(8,128)S(1)} %get-tuple-element.104.refs_1_), channel_id=1, source_target_pairs={{0,3},{1,2},{2,1},{3,0},{4,7},{5,6},{6,5},{7,4},{8,11},{9,10},{10,... | collective-permute-start | bytes 221192 | tf_op jit(solution)/shard_map/ppermute | solution.py:420
  50.2 1.9 %collective-permute-start.24 = (f32[16,128]{1,0:T(8,128)S(1)}, f32[16,128]{1,0:T(8,128)S(1)}, u32[]{:S(2)}, u32[]{:S(2)}) collective-permute-start(f32[16,128]{1,0:T(8,128)S(1)} %get-tuple-element.102.refs_0_), channel_id=1, source_target_pairs={{0,1},{1,0},{2,3},{3,2},{4,5},{5,4},{6,7},{7,6},{8,9},{9,8},{10,11... | collective-permute-start | bytes 24584 | tf_op jit(solution)/shard_map/ppermute | solution.py:420
  52.2 1.9 %collective-permute-done.24.refs_4_ = f32[16,128]{1,0:T(8,128)S(1)} collective-permute-done((f32[16,128]{1,0:T(8,128)S(1)}, f32[16,128]{1,0:T(8,128)S(1)}, u32[]{:S(2)}, u32[]{:S(2)}) %collective-permute-start.24) | collective-permute-done | bytes 8224 | tf_op jit(solution)/shard_map/ppermute | solution.py:420
  56.0 2.2 %collective-permute-start.25 = (f32[8,128]{1,0:T(8,128)S(1)}, f32[8,128]{1,0:T(8,128)S(1)}, u32[]{:S(2)}, u32[]{:S(2)}) collective-permute-start(f32[8,128]{1,0:T(8,128)S(1)} %get-tuple-element.106.refs_0_), channel_id=1, source_target_pairs={{0,28},{4,24},{8,20},{12,16},{16,12},{20,8},{24,4},{28,0},{1,29},{... | collective-permute-start | bytes 12296 | tf_op jit(solution)/shard_map/ppermute | solution.py:425
  58.4 1.6 %collective-permute-done.25.refs_1_ = f32[8,128]{1,0:T(8,128)S(1)} collective-permute-done((f32[8,128]{1,0:T(8,128)S(1)}, f32[8,128]{1,0:T(8,128)S(1)}, u32[]{:S(2)}, u32[]{:S(2)}) %collective-permute-start.25) | collective-permute-done | bytes 4128 | tf_op jit(solution)/shard_map/ppermute | solution.py:425
  61.9 1.2 %shard_map.73 = (f32[128,768]{1,0:T(8,128)}, f32[128,768]{1,0:T(8,128)}) custom-call(f32[8,128]{1,0:T(8,128)S(1)} %shard_map.71.refs_0_, f32[8,128]{1,0:T(8,128)S(1)} %collective-permute-done.29.refs_1_, f32[768,128]{1,0:T(8,128)S(1)} %get-tuple-element.114.refs_2_, f32[768,128]{1,0:T(8,128)S(1)} %get-tuple-element.115.refs_3_, ...), custom_call_target="tpu_custom_call" | custom-call | flops 1966080 | bytes 3538944 | tf_op jit(solution)/shard_map/pallas_call | solution.py:568
  (54 shorter events, 14.8 us)
Async XLA Ops:
  3.4 9.9 %collective-permute-start = (f32[160,128]{1,0:T(8,128)S(1)}, f32[160,128]{1,0:T(8,128)S(1)}, u32[]{:S(2)}, u32[]{:S(2)}) collective-permute-start(f32[160,128]{1,0:T(8,128)S(1)} %get-tuple-element.64.refs_1_), channel_id=1, source_target_pairs={{0,3},{1,2},{2,1},{3,0},{4,7},{5,6},{6,5},{7,4},{8,11},{9,10},{10,... | collective-permute-start | bytes 245768 | tf_op jit(solution)/shard_map/ppermute | solution.py:420
  8.5 4.7 %collective-permute-start.1 = (f32[32,128]{1,0:T(8,128)S(1)}, f32[32,128]{1,0:T(8,128)S(1)}, u32[]{:S(2)}, u32[]{:S(2)}) collective-permute-start(f32[32,128]{1,0:T(8,128)S(1)} %get-tuple-element.65), channel_id=1, source_target_pairs={{0,2},{1,3},{2,0},{3,1},{4,6},{5,7},{6,4},{7,5},{8,10},{9,11},{10,... | collective-permute-start | bytes 49160 | tf_op jit(solution)/shard_map/ppermute | solution.py:415
  9.2 7.8 %collective-permute-start.6 = (f32[136,128]{1,0:T(8,128)S(1)}, f32[136,128]{1,0:T(8,128)S(1)}, u32[]{:S(2)}, u32[]{:S(2)}) collective-permute-start(f32[136,128]{1,0:T(8,128)S(1)} %get-tuple-element.71.refs_0_), channel_id=1, source_target_pairs={{0,1},{1,0},{2,3},{3,2},{4,5},{5,4},{6,7},{7,6},{8,9},{9,8},{10,11... | collective-permute-start | bytes 208904 | tf_op jit(solution)/shard_map/ppermute | solution.py:420
  13.7 6.1 %collective-permute-start.3 = (f32[264,128]{1,0:T(8,128)S(1)}, f32[264,128]{1,0:T(8,128)S(1)}, u32[]{:S(2)}, u32[]{:S(2)}) collective-permute-start(f32[264,128]{1,0:T(8,128)S(1)} %get-tuple-element.68.refs_0_), channel_id=1, source_target_pairs={{0,16},{16,0},{1,17},{17,1},{2,18},{18,2},{3,19},{19,3},{4,20},{20... | collective-permute-start | bytes 405512 | tf_op jit(solution)/shard_map/ppermute | solution.py:420
  15.3 4.5 %collective-permute-start.5 = (f32[144,128]{1,0:T(8,128)S(1)}, f32[144,128]{1,0:T(8,128)S(1)}, u32[]{:S(2)}, u32[]{:S(2)}) collective-permute-start(f32[144,128]{1,0:T(8,128)S(1)} %get-tuple-element.70.refs_3_), channel_id=1, source_target_pairs={{0,12},{4,8},{8,4},{12,0},{1,13},{5,9},{9,5},{13,1},{2,14},{6,10},... | collective-permute-start | bytes 221192 | tf_op jit(solution)/shard_map/ppermute | solution.py:420
  20.6 6.9 %collective-permute-start.7 = (f32[144,128]{1,0:T(8,128)S(1)}, f32[144,128]{1,0:T(8,128)S(1)}, u32[]{:S(2)}, u32[]{:S(2)}) collective-permute-start(f32[144,128]{1,0:T(8,128)S(1)} %get-tuple-element.77.refs_1_), channel_id=1, source_target_pairs={{0,3},{1,2},{2,1},{3,0},{4,7},{5,6},{6,5},{7,4},{8,11},{9,10},{10,... | collective-permute-start | bytes 221192 | tf_op jit(solution)/shard_map/ppermute | solution.py:420
  22.9 4.6 %collective-permute-start.8 = (f32[24,128]{1,0:T(8,128)S(1)}, f32[24,128]{1,0:T(8,128)S(1)}, u32[]{:S(2)}, u32[]{:S(2)}) collective-permute-start(f32[24,128]{1,0:T(8,128)S(1)} %get-tuple-element.78), channel_id=1, source_target_pairs={{0,2},{1,3},{2,0},{3,1},{4,6},{5,7},{6,4},{7,5},{8,10},{9,11},{10,... | collective-permute-start | bytes 36872 | tf_op jit(solution)/shard_map/ppermute | solution.py:415
  23.0 4.2 %collective-permute-start.9 = (f32[16,128]{1,0:T(8,128)S(1)}, f32[16,128]{1,0:T(8,128)S(1)}, u32[]{:S(2)}, u32[]{:S(2)}) collective-permute-start(f32[16,128]{1,0:T(8,128)S(1)} %get-tuple-element.75.refs_0_), channel_id=1, source_target_pairs={{0,1},{1,0},{2,3},{3,2},{4,5},{5,4},{6,7},{7,6},{8,9},{9,8},{10,11... | collective-permute-start | bytes 24584 | tf_op jit(solution)/shard_map/ppermute | solution.py:420
  25.1 5.0 %collective-permute-start.13 = (f32[128,128]{1,0:T(8,128)S(1)}, f32[128,128]{1,0:T(8,128)S(1)}, u32[]{:S(2)}, u32[]{:S(2)}) collective-permute-start(f32[128,128]{1,0:T(8,128)S(1)} %get-tuple-element.84.refs_0_), channel_id=1, source_target_pairs={{0,1},{1,0},{2,3},{3,2},{4,5},{5,4},{6,7},{7,6},{8,9},{9,8},{10,11... | collective-permute-start | bytes 196616 | tf_op jit(solution)/shard_map/ppermute | solution.py:420
  27.9 5.2 %collective-permute-start.10 = (f32[264,128]{1,0:T(8,128)S(1)}, f32[264,128]{1,0:T(8,128)S(1)}, u32[]{:S(2)}, u32[]{:S(2)}) collective-permute-start(f32[264,128]{1,0:T(8,128)S(1)} %get-tuple-element.81.refs_0_), channel_id=1, source_target_pairs={{0,16},{16,0},{1,17},{17,1},{2,18},{18,2},{3,19},{19,3},{4,20},{20... | collective-permute-start | bytes 405512 | tf_op jit(solution)/shard_map/ppermute | solution.py:420
  28.5 4.5 %collective-permute-start.12 = (f32[144,128]{1,0:T(8,128)S(1)}, f32[144,128]{1,0:T(8,128)S(1)}, u32[]{:S(2)}, u32[]{:S(2)}) collective-permute-start(f32[144,128]{1,0:T(8,128)S(1)} %get-tuple-element.83.refs_3_), channel_id=1, source_target_pairs={{0,12},{4,8},{8,4},{12,0},{1,13},{5,9},{9,5},{13,1},{2,14},{6,10},... | collective-permute-start | bytes 221192 | tf_op jit(solution)/shard_map/ppermute | solution.py:420
  33.9 7.0 %collective-permute-start.14 = (f32[136,128]{1,0:T(8,128)S(1)}, f32[136,128]{1,0:T(8,128)S(1)}, u32[]{:S(2)}, u32[]{:S(2)}) collective-permute-start(f32[136,128]{1,0:T(8,128)S(1)} %get-tuple-element.90.refs_1_), channel_id=1, source_target_pairs={{0,3},{1,2},{2,1},{3,0},{4,7},{5,6},{6,5},{7,4},{8,11},{9,10},{10,... | collective-permute-start | bytes 208904 | tf_op jit(solution)/shard_map/ppermute | solution.py:420
  36.3 4.0 %collective-permute-start.17 = (f32[16,128]{1,0:T(8,128)S(1)}, f32[16,128]{1,0:T(8,128)S(1)}, u32[]{:S(2)}, u32[]{:S(2)}) collective-permute-start(f32[16,128]{1,0:T(8,128)S(1)} %slice.3), channel_id=1, source_target_pairs={{0,4},{4,0},{8,12},{12,8},{1,5},{5,1},{9,13},{13,9},{2,6},{6,2},{1... | collective-permute-start | bytes 24584 | tf_op jit(solution)/shard_map/ppermute | solution.py:420
  36.3 4.5 %collective-permute-start.15 = (f32[16,128]{1,0:T(8,128)S(1)}, f32[16,128]{1,0:T(8,128)S(1)}, u32[]{:S(2)}, u32[]{:S(2)}) collective-permute-start(f32[16,128]{1,0:T(8,128)S(1)} %get-tuple-element.91), channel_id=1, source_target_pairs={{0,2},{1,3},{2,0},{3,1},{4,6},{5,7},{6,4},{7,5},{8,10},{9,11},{10,... | collective-permute-start | bytes 24584 | tf_op jit(solution)/shard_map/ppermute | solution.py:415
  38.3 5.2 %collective-permute-start.21 = (f32[128,128]{1,0:T(8,128)S(1)}, f32[128,128]{1,0:T(8,128)S(1)}, u32[]{:S(2)}, u32[]{:S(2)}) collective-permute-start(f32[128,128]{1,0:T(8,128)S(1)} %get-tuple-element.96.refs_0_), channel_id=1, source_target_pairs={{0,1},{1,0},{2,3},{3,2},{4,5},{5,4},{6,7},{7,6},{8,9},{9,8},{10,11... | collective-permute-start | bytes 196616 | tf_op jit(solution)/shard_map/ppermute | solution.py:420
  41.2 5.4 %collective-permute-start.18 = (f32[264,128]{1,0:T(8,128)S(1)}, f32[264,128]{1,0:T(8,128)S(1)}, u32[]{:S(2)}, u32[]{:S(2)}) collective-permute-start(f32[264,128]{1,0:T(8,128)S(1)} %get-tuple-element.93.refs_0_), channel_id=1, source_target_pairs={{0,16},{16,0},{1,17},{17,1},{2,18},{18,2},{3,19},{19,3},{4,20},{20... | collective-permute-start | bytes 405512 | tf_op jit(solution)/shard_map/ppermute | solution.py:420
  42.2 4.3 %collective-permute-start.20 = (f32[144,128]{1,0:T(8,128)S(1)}, f32[144,128]{1,0:T(8,128)S(1)}, u32[]{:S(2)}, u32[]{:S(2)}) collective-permute-start(f32[144,128]{1,0:T(8,128)S(1)} %get-tuple-element.95.refs_3_), channel_id=1, source_target_pairs={{0,12},{4,8},{8,4},{12,0},{1,13},{5,9},{9,5},{13,1},{2,14},{6,10},... | collective-permute-start | bytes 221192 | tf_op jit(solution)/shard_map/ppermute | solution.py:420
  47.6 7.0 %collective-permute-start.22 = (f32[144,128]{1,0:T(8,128)S(1)}, f32[144,128]{1,0:T(8,128)S(1)}, u32[]{:S(2)}, u32[]{:S(2)}) collective-permute-start(f32[144,128]{1,0:T(8,128)S(1)} %get-tuple-element.104.refs_1_), channel_id=1, source_target_pairs={{0,3},{1,2},{2,1},{3,0},{4,7},{5,6},{6,5},{7,4},{8,11},{9,10},{10,... | collective-permute-start | bytes 221192 | tf_op jit(solution)/shard_map/ppermute | solution.py:420
  49.9 4.7 %collective-permute-start.23 = (f32[24,128]{1,0:T(8,128)S(1)}, f32[24,128]{1,0:T(8,128)S(1)}, u32[]{:S(2)}, u32[]{:S(2)}) collective-permute-start(f32[24,128]{1,0:T(8,128)S(1)} %get-tuple-element.105), channel_id=1, source_target_pairs={{0,2},{1,3},{2,0},{3,1},{4,6},{5,7},{6,4},{7,5},{8,10},{9,11},{10,... | collective-permute-start | bytes 36872 | tf_op jit(solution)/shard_map/ppermute | solution.py:415
  50.2 4.0 %collective-permute-start.24 = (f32[16,128]{1,0:T(8,128)S(1)}, f32[16,128]{1,0:T(8,128)S(1)}, u32[]{:S(2)}, u32[]{:S(2)}) collective-permute-start(f32[16,128]{1,0:T(8,128)S(1)} %get-tuple-element.102.refs_0_), channel_id=1, source_target_pairs={{0,1},{1,0},{2,3},{3,2},{4,5},{5,4},{6,7},{7,6},{8,9},{9,8},{10,11... | collective-permute-start | bytes 24584 | tf_op jit(solution)/shard_map/ppermute | solution.py:420
  52.1 6.2 %collective-permute-start.28 = (f32[128,128]{1,0:T(8,128)S(1)}, f32[128,128]{1,0:T(8,128)S(1)}, u32[]{:S(2)}, u32[]{:S(2)}) collective-permute-start(f32[128,128]{1,0:T(8,128)S(1)} %get-tuple-element.109.refs_0_), channel_id=1, source_target_pairs={{0,1},{1,0},{2,3},{3,2},{4,5},{5,4},{6,7},{7,6},{8,9},{9,8},{10,11... | collective-permute-start | bytes 196616 | tf_op jit(solution)/shard_map/ppermute | solution.py:420
  54.9 5.2 %collective-permute-start.26 = (f32[264,128]{1,0:T(8,128)S(1)}, f32[264,128]{1,0:T(8,128)S(1)}, u32[]{:S(2)}, u32[]{:S(2)}) collective-permute-start(f32[264,128]{1,0:T(8,128)S(1)} %get-tuple-element.107.refs_0_), channel_id=1, source_target_pairs={{0,16},{16,0},{1,17},{17,1},{2,18},{18,2},{3,19},{19,3},{4,20},{20... | collective-permute-start | bytes 405512 | tf_op jit(solution)/shard_map/ppermute | solution.py:420
  56.0 4.2 %collective-permute-start.27 = (f32[144,128]{1,0:T(8,128)S(1)}, f32[144,128]{1,0:T(8,128)S(1)}, u32[]{:S(2)}, u32[]{:S(2)}) collective-permute-start(f32[144,128]{1,0:T(8,128)S(1)} %get-tuple-element.108.refs_3_), channel_id=1, source_target_pairs={{0,12},{4,8},{8,4},{12,0},{1,13},{5,9},{9,5},{13,1},{2,14},{6,10},... | collective-permute-start | bytes 221192 | tf_op jit(solution)/shard_map/ppermute | solution.py:420
  56.0 4.0 %collective-permute-start.25 = (f32[8,128]{1,0:T(8,128)S(1)}, f32[8,128]{1,0:T(8,128)S(1)}, u32[]{:S(2)}, u32[]{:S(2)}) collective-permute-start(f32[8,128]{1,0:T(8,128)S(1)} %get-tuple-element.106.refs_0_), channel_id=1, source_target_pairs={{0,28},{4,24},{8,20},{12,16},{16,12},{20,8},{24,4},{28,0},{1,29},{... | collective-permute-start | bytes 12296 | tf_op jit(solution)/shard_map/ppermute | solution.py:425
  (7 other events, 19.3 us)

commit v15 on v14

--- a/solution.py
+++ b/solution.py
@@ -181,7 +181,8 @@
     else:
         device = block
     pick = jnp.where((source == device * n_modes + mode) & (mode < n_modes), 1.0, 0.0)
-    ordered = dot32(rows, pick)
+    picked = dot16(jnp.concatenate(split3(rows), axis=0), pick.astype(BF16))
+    ordered = (picked[0:PAD] + picked[PAD:2 * PAD]) + picked[2 * PAD:]
     o["c_own"][...] = ordered
     if turn:
         send_rows(face, ordered, 2 * PAD, o)

time: 63.2 us -> 63.2 us (level)
  no operation moved by 1% of the time
where the time goes in v15:
time: 63.2 us; the launch traced here: 63.1 us
  starting transfers between devices  32.9 us (52%)
  waiting for transfers between devices  20.3 us (32%)
  Pallas kernels  9.14 us (14%)
  between operations  0.76 us (1%)
    ppermute x26, starting transfers between devices, swap(): return lax.ppermute(x, axis, [(k, (k + side(k)) % n) for k in range(n)])  30 us
    ppermute x26, waiting for transfers between devices, swap(): return lax.ppermute(x, axis, [(k, (k + side(k)) % n) for k in range(n)])  16.4 us
    pallas_call x13, Pallas kernels, call(): pl.pallas_call(run, out_shape=[outs[n] for n in names_out], in_specs=[vme...  5.22 us
    pallas_call x1, Pallas kernels, body(): pl.pallas_call(functools.partial(first_kernel, face, nz, n_modes, small),...  2.76 us
    ppermute x4, waiting for transfers between devices, shift(): return lax.ppermute(x, axis, [(k, (k + by) % n) for k in range(n)])  2.31 us
    ppermute x1, starting transfers between devices, move(): return lax.ppermute(x, ('gx', 'gy'), pairs)  2.29 us
    ppermute x1, waiting for transfers between devices, move(): return lax.ppermute(x, ('gx', 'gy'), pairs)  1.57 us
  transfers between devices with their start and end apart: 31, of which 17 were waited for; matrix products, arithmetic and copies ran while one was open for 0% of the time, Pallas kernels for 4%

profile of v15, /device:TPU:0, one launch (start us, length us, event | category | flops | bytes accessed | tf_op | source)
XLA Modules:
  0.0 63.1 jit_solution(13970264856417198951)
XLA Ops:
  0.6 2.8 %shard_map.59 = (f32[768,128]{1,0:T(8,128)S(1)}, bf16[1568,768]{1,0:T(8,128)(2,1)S(1)}, bf16[768,48]{1,0:T(8,128)(2,1)S(1)}, f32[8,128]{1,0:T(8,128)S(1)}, f32[5...) custom-call(f32[128,768]{1,0:T(8,128)} %bitcast.7, ...), custom_call_target="tpu_custom_call" | custom-call | flops 603979776 | bytes 2359296 | tf_op jit(solution)/shard_map/pallas_call | solution.py:496
  3.4 5.1 %collective-permute-start = (f32[160,128]{1,0:T(8,128)S(1)}, f32[160,128]{1,0:T(8,128)S(1)}, u32[]{:S(2)}, u32[]{:S(2)}) collective-permute-start(f32[160,128]{1,0:T(8,128)S(1)} %get-tuple-element.64.refs_1_), channel_id=1, source_target_pairs={{0,3},{1,2},{2,1},{3,0},{4,7},{5,6},{6,5},{7,4},{8,11},{9,10},{10,... | collective-permute-start | bytes 245768 | tf_op jit(solution)/shard_map/ppermute | solution.py:421
  9.1 1.4 %collective-permute-start.6 = (f32[136,128]{1,0:T(8,128)S(1)}, f32[136,128]{1,0:T(8,128)S(1)}, u32[]{:S(2)}, u32[]{:S(2)}) collective-permute-start(f32[136,128]{1,0:T(8,128)S(1)} %get-tuple-element.71.refs_0_), channel_id=1, source_target_pairs={{0,1},{1,0},{2,3},{3,2},{4,5},{5,4},{6,7},{7,6},{8,9},{9,8},{10,11... | collective-permute-start | bytes 208904 | tf_op jit(solution)/shard_map/ppermute | solution.py:421
  10.5 1.8 %collective-permute-done.2.refs_4_ = f32[24,128]{1,0:T(8,128)S(1)} collective-permute-done((f32[24,128]{1,0:T(8,128)S(1)}, f32[24,128]{1,0:T(8,128)S(1)}, u32[]{:S(2)}, u32[]{:S(2)}) %collective-permute-start.2) | collective-permute-done | bytes 12320 | tf_op jit(solution)/shard_map/ppermute | solution.py:421
  13.7 1.6 %collective-permute-start.3 = (f32[264,128]{1,0:T(8,128)S(1)}, f32[264,128]{1,0:T(8,128)S(1)}, u32[]{:S(2)}, u32[]{:S(2)}) collective-permute-start(f32[264,128]{1,0:T(8,128)S(1)} %get-tuple-element.68.refs_0_), channel_id=1, source_target_pairs={{0,16},{16,0},{1,17},{17,1},{2,18},{18,2},{3,19},{19,3},{4,20},{20... | collective-permute-start | bytes 405512 | tf_op jit(solution)/shard_map/ppermute | solution.py:421
  15.3 1.6 %collective-permute-start.4 = (f32[136,128]{1,0:T(8,128)S(1)}, f32[136,128]{1,0:T(8,128)S(1)}, u32[]{:S(2)}, u32[]{:S(2)}) collective-permute-start(f32[136,128]{1,0:T(8,128)S(1)} %get-tuple-element.69.refs_2_), channel_id=1, source_target_pairs={{0,4},{4,0},{8,12},{12,8},{1,5},{5,1},{9,13},{13,9},{2,6},{6,2},{1... | collective-permute-start | bytes 208904 | tf_op jit(solution)/shard_map/ppermute | solution.py:421
  17.8 2.0 %collective-permute-done.5.refs_5_ = f32[144,128]{1,0:T(8,128)S(1)} collective-permute-done((f32[144,128]{1,0:T(8,128)S(1)}, f32[144,128]{1,0:T(8,128)S(1)}, u32[]{:S(2)}, u32[]{:S(2)}) %collective-permute-start.5) | collective-permute-done | bytes 73760 | tf_op jit(solution)/shard_map/ppermute | solution.py:421
  20.6 2.3 %collective-permute-start.7 = (f32[144,128]{1,0:T(8,128)S(1)}, f32[144,128]{1,0:T(8,128)S(1)}, u32[]{:S(2)}, u32[]{:S(2)}) collective-permute-start(f32[144,128]{1,0:T(8,128)S(1)} %get-tuple-element.77.refs_1_), channel_id=1, source_target_pairs={{0,3},{1,2},{2,1},{3,0},{4,7},{5,6},{6,5},{7,4},{8,11},{9,10},{10,... | collective-permute-start | bytes 221192 | tf_op jit(solution)/shard_map/ppermute | solution.py:421
  23.0 2.1 %collective-permute-start.9 = (f32[16,128]{1,0:T(8,128)S(1)}, f32[16,128]{1,0:T(8,128)S(1)}, u32[]{:S(2)}, u32[]{:S(2)}) collective-permute-start(f32[16,128]{1,0:T(8,128)S(1)} %get-tuple-element.75.refs_0_), channel_id=1, source_target_pairs={{0,1},{1,0},{2,3},{3,2},{4,5},{5,4},{6,7},{7,6},{8,9},{9,8},{10,11... | collective-permute-start | bytes 24584 | tf_op jit(solution)/shard_map/ppermute | solution.py:421
  25.1 2.1 %collective-permute-done.9.refs_4_ = f32[16,128]{1,0:T(8,128)S(1)} collective-permute-done((f32[16,128]{1,0:T(8,128)S(1)}, f32[16,128]{1,0:T(8,128)S(1)}, u32[]{:S(2)}, u32[]{:S(2)}) %collective-permute-start.9) | collective-permute-done | bytes 8224 | tf_op jit(solution)/shard_map/ppermute | solution.py:421
  28.4 1.6 %collective-permute-start.11 = (f32[136,128]{1,0:T(8,128)S(1)}, f32[136,128]{1,0:T(8,128)S(1)}, u32[]{:S(2)}, u32[]{:S(2)}) collective-permute-start(f32[136,128]{1,0:T(8,128)S(1)} %get-tuple-element.82.refs_2_), channel_id=1, source_target_pairs={{0,4},{4,0},{8,12},{12,8},{1,5},{5,1},{9,13},{13,9},{2,6},{6,2},{1... | collective-permute-start | bytes 208904 | tf_op jit(solution)/shard_map/ppermute | solution.py:421
  30.9 2.0 %collective-permute-done.12.refs_5_ = f32[144,128]{1,0:T(8,128)S(1)} collective-permute-done((f32[144,128]{1,0:T(8,128)S(1)}, f32[144,128]{1,0:T(8,128)S(1)}, u32[]{:S(2)}, u32[]{:S(2)}) %collective-permute-start.12) | collective-permute-done | bytes 73760 | tf_op jit(solution)/shard_map/ppermute | solution.py:421
  33.8 2.4 %collective-permute-start.14 = (f32[136,128]{1,0:T(8,128)S(1)}, f32[136,128]{1,0:T(8,128)S(1)}, u32[]{:S(2)}, u32[]{:S(2)}) collective-permute-start(f32[136,128]{1,0:T(8,128)S(1)} %get-tuple-element.90.refs_1_), channel_id=1, source_target_pairs={{0,3},{1,2},{2,1},{3,0},{4,7},{5,6},{6,5},{7,4},{8,11},{9,10},{10,... | collective-permute-start | bytes 208904 | tf_op jit(solution)/shard_map/ppermute | solution.py:421
  36.5 1.8 %collective-permute-start.16 = (f32[8,128]{1,0:T(8,128)S(1)}, f32[8,128]{1,0:T(8,128)S(1)}, u32[]{:S(2)}, u32[]{:S(2)}) collective-permute-start(f32[8,128]{1,0:T(8,128)S(1)} %get-tuple-element.88.refs_0_), channel_id=1, source_target_pairs={{0,1},{1,0},{2,3},{3,2},{4,5},{5,4},{6,7},{7,6},{8,9},{9,8},{10,11... | collective-permute-start | bytes 12296 | tf_op jit(solution)/shard_map/ppermute | solution.py:421
  38.6 1.6 %collective-permute-done.16.refs_4_ = f32[8,128]{1,0:T(8,128)S(1)} collective-permute-done((f32[8,128]{1,0:T(8,128)S(1)}, f32[8,128]{1,0:T(8,128)S(1)}, u32[]{:S(2)}, u32[]{:S(2)}) %collective-permute-start.16) | collective-permute-done | bytes 4128 | tf_op jit(solution)/shard_map/ppermute | solution.py:421
  42.2 1.3 %collective-permute-start.19 = (f32[128,128]{1,0:T(8,128)S(1)}, f32[128,128]{1,0:T(8,128)S(1)}, u32[]{:S(2)}, u32[]{:S(2)}) collective-permute-start(f32[128,128]{1,0:T(8,128)S(1)} %get-tuple-element.94.refs_2_), channel_id=1, source_target_pairs={{0,4},{4,0},{8,12},{12,8},{1,5},{5,1},{9,13},{13,9},{2,6},{6,2},{1... | collective-permute-start | bytes 196616 | tf_op jit(solution)/shard_map/ppermute | solution.py:421
  44.4 2.1 %collective-permute-done.20.refs_5_ = f32[144,128]{1,0:T(8,128)S(1)} collective-permute-done((f32[144,128]{1,0:T(8,128)S(1)}, f32[144,128]{1,0:T(8,128)S(1)}, u32[]{:S(2)}, u32[]{:S(2)}) %collective-permute-start.20) | collective-permute-done | bytes 73760 | tf_op jit(solution)/shard_map/ppermute | solution.py:421
  46.5 1.1 %shard_map.68 = (f32[768,128]{1,0:T(8,128)S(1)}, f32[768,128]{1,0:T(8,128)S(1)}, f32[768,128]{1,0:T(8,128)S(1)}, f32[8,128]{1,0:T(8,128)S(1)}, f32[512,128]{1,0:...) custom-call(f32[264,128]{1,0:T(8,128)S(1)} %get-tuple-element.93.ref, ...), custom_call_target="tpu_custom_call" | custom-call | flops 603979776 | bytes 5881856 | tf_op jit(solution)/shard_map/pallas_call | solution.py:31
  47.6 2.3 %collective-permute-start.22 = (f32[144,128]{1,0:T(8,128)S(1)}, f32[144,128]{1,0:T(8,128)S(1)}, u32[]{:S(2)}, u32[]{:S(2)}) collective-permute-start(f32[144,128]{1,0:T(8,128)S(1)} %get-tuple-element.104.refs_1_), channel_id=1, source_target_pairs={{0,3},{1,2},{2,1},{3,0},{4,7},{5,6},{6,5},{7,4},{8,11},{9,10},{10,... | collective-permute-start | bytes 221192 | tf_op jit(solution)/shard_map/ppermute | solution.py:421
  50.1 1.9 %collective-permute-start.24 = (f32[16,128]{1,0:T(8,128)S(1)}, f32[16,128]{1,0:T(8,128)S(1)}, u32[]{:S(2)}, u32[]{:S(2)}) collective-permute-start(f32[16,128]{1,0:T(8,128)S(1)} %get-tuple-element.102.refs_0_), channel_id=1, source_target_pairs={{0,1},{1,0},{2,3},{3,2},{4,5},{5,4},{6,7},{7,6},{8,9},{9,8},{10,11... | collective-permute-start | bytes 24584 | tf_op jit(solution)/shard_map/ppermute | solution.py:421
  52.2 2.0 %collective-permute-done.24.refs_4_ = f32[16,128]{1,0:T(8,128)S(1)} collective-permute-done((f32[16,128]{1,0:T(8,128)S(1)}, f32[16,128]{1,0:T(8,128)S(1)}, u32[]{:S(2)}, u32[]{:S(2)}) %collective-permute-start.24) | collective-permute-done | bytes 8224 | tf_op jit(solution)/shard_map/ppermute | solution.py:421
  55.9 2.3 %collective-permute-start.25 = (f32[8,128]{1,0:T(8,128)S(1)}, f32[8,128]{1,0:T(8,128)S(1)}, u32[]{:S(2)}, u32[]{:S(2)}) collective-permute-start(f32[8,128]{1,0:T(8,128)S(1)} %get-tuple-element.106.refs_0_), channel_id=1, source_target_pairs={{0,28},{4,24},{8,20},{12,16},{16,12},{20,8},{24,4},{28,0},{1,29},{... | collective-permute-start | bytes 12296 | tf_op jit(solution)/shard_map/ppermute | solution.py:426
  58.4 1.6 %collective-permute-done.25.refs_1_ = f32[8,128]{1,0:T(8,128)S(1)} collective-permute-done((f32[8,128]{1,0:T(8,128)S(1)}, f32[8,128]{1,0:T(8,128)S(1)}, u32[]{:S(2)}, u32[]{:S(2)}) %collective-permute-start.25) | collective-permute-done | bytes 4128 | tf_op jit(solution)/shard_map/ppermute | solution.py:426
  61.9 1.2 %shard_map.73 = (f32[128,768]{1,0:T(8,128)}, f32[128,768]{1,0:T(8,128)}) custom-call(f32[8,128]{1,0:T(8,128)S(1)} %shard_map.71.refs_0_, f32[8,128]{1,0:T(8,128)S(1)} %collective-permute-done.29.refs_1_, f32[768,128]{1,0:T(8,128)S(1)} %get-tuple-element.114.refs_2_, f32[768,128]{1,0:T(8,128)S(1)} %get-tuple-element.115.refs_3_, ...), custom_call_target="tpu_custom_call" | custom-call | flops 1966080 | bytes 3538944 | tf_op jit(solution)/shard_map/pallas_call | solution.py:569
  (54 shorter events, 14.6 us)
Async XLA Ops:
  3.4 9.9 %collective-permute-start = (f32[160,128]{1,0:T(8,128)S(1)}, f32[160,128]{1,0:T(8,128)S(1)}, u32[]{:S(2)}, u32[]{:S(2)}) collective-permute-start(f32[160,128]{1,0:T(8,128)S(1)} %get-tuple-element.64.refs_1_), channel_id=1, source_target_pairs={{0,3},{1,2},{2,1},{3,0},{4,7},{5,6},{6,5},{7,4},{8,11},{9,10},{10,... | collective-permute-start | bytes 245768 | tf_op jit(solution)/shard_map/ppermute | solution.py:421
  8.5 4.7 %collective-permute-start.1 = (f32[32,128]{1,0:T(8,128)S(1)}, f32[32,128]{1,0:T(8,128)S(1)}, u32[]{:S(2)}, u32[]{:S(2)}) collective-permute-start(f32[32,128]{1,0:T(8,128)S(1)} %get-tuple-element.65), channel_id=1, source_target_pairs={{0,2},{1,3},{2,0},{3,1},{4,6},{5,7},{6,4},{7,5},{8,10},{9,11},{10,... | collective-permute-start | bytes 49160 | tf_op jit(solution)/shard_map/ppermute | solution.py:416
  9.1 7.7 %collective-permute-start.6 = (f32[136,128]{1,0:T(8,128)S(1)}, f32[136,128]{1,0:T(8,128)S(1)}, u32[]{:S(2)}, u32[]{:S(2)}) collective-permute-start(f32[136,128]{1,0:T(8,128)S(1)} %get-tuple-element.71.refs_0_), channel_id=1, source_target_pairs={{0,1},{1,0},{2,3},{3,2},{4,5},{5,4},{6,7},{7,6},{8,9},{9,8},{10,11... | collective-permute-start | bytes 208904 | tf_op jit(solution)/shard_map/ppermute | solution.py:421
  13.7 6.1 %collective-permute-start.3 = (f32[264,128]{1,0:T(8,128)S(1)}, f32[264,128]{1,0:T(8,128)S(1)}, u32[]{:S(2)}, u32[]{:S(2)}) collective-permute-start(f32[264,128]{1,0:T(8,128)S(1)} %get-tuple-element.68.refs_0_), channel_id=1, source_target_pairs={{0,16},{16,0},{1,17},{17,1},{2,18},{18,2},{3,19},{19,3},{4,20},{20... | collective-permute-start | bytes 405512 | tf_op jit(solution)/shard_map/ppermute | solution.py:421
  15.3 4.5 %collective-permute-start.5 = (f32[144,128]{1,0:T(8,128)S(1)}, f32[144,128]{1,0:T(8,128)S(1)}, u32[]{:S(2)}, u32[]{:S(2)}) collective-permute-start(f32[144,128]{1,0:T(8,128)S(1)} %get-tuple-element.70.refs_3_), channel_id=1, source_target_pairs={{0,12},{4,8},{8,4},{12,0},{1,13},{5,9},{9,5},{13,1},{2,14},{6,10},... | collective-permute-start | bytes 221192 | tf_op jit(solution)/shard_map/ppermute | solution.py:421
  20.6 6.9 %collective-permute-start.7 = (f32[144,128]{1,0:T(8,128)S(1)}, f32[144,128]{1,0:T(8,128)S(1)}, u32[]{:S(2)}, u32[]{:S(2)}) collective-permute-start(f32[144,128]{1,0:T(8,128)S(1)} %get-tuple-element.77.refs_1_), channel_id=1, source_target_pairs={{0,3},{1,2},{2,1},{3,0},{4,7},{5,6},{6,5},{7,4},{8,11},{9,10},{10,... | collective-permute-start | bytes 221192 | tf_op jit(solution)/shard_map/ppermute | solution.py:421
  22.9 4.6 %collective-permute-start.8 = (f32[24,128]{1,0:T(8,128)S(1)}, f32[24,128]{1,0:T(8,128)S(1)}, u32[]{:S(2)}, u32[]{:S(2)}) collective-permute-start(f32[24,128]{1,0:T(8,128)S(1)} %get-tuple-element.78), channel_id=1, source_target_pairs={{0,2},{1,3},{2,0},{3,1},{4,6},{5,7},{6,4},{7,5},{8,10},{9,11},{10,... | collective-permute-start | bytes 36872 | tf_op jit(solution)/shard_map/ppermute | solution.py:416
  23.0 4.3 %collective-permute-start.9 = (f32[16,128]{1,0:T(8,128)S(1)}, f32[16,128]{1,0:T(8,128)S(1)}, u32[]{:S(2)}, u32[]{:S(2)}) collective-permute-start(f32[16,128]{1,0:T(8,128)S(1)} %get-tuple-element.75.refs_0_), channel_id=1, source_target_pairs={{0,1},{1,0},{2,3},{3,2},{4,5},{5,4},{6,7},{7,6},{8,9},{9,8},{10,11... | collective-permute-start | bytes 24584 | tf_op jit(solution)/shard_map/ppermute | solution.py:421
  25.1 4.9 %collective-permute-start.13 = (f32[128,128]{1,0:T(8,128)S(1)}, f32[128,128]{1,0:T(8,128)S(1)}, u32[]{:S(2)}, u32[]{:S(2)}) collective-permute-start(f32[128,128]{1,0:T(8,128)S(1)} %get-tuple-element.84.refs_0_), channel_id=1, source_target_pairs={{0,1},{1,0},{2,3},{3,2},{4,5},{5,4},{6,7},{7,6},{8,9},{9,8},{10,11... | collective-permute-start | bytes 196616 | tf_op jit(solution)/shard_map/ppermute | solution.py:421
  27.8 5.2 %collective-permute-start.10 = (f32[264,128]{1,0:T(8,128)S(1)}, f32[264,128]{1,0:T(8,128)S(1)}, u32[]{:S(2)}, u32[]{:S(2)}) collective-permute-start(f32[264,128]{1,0:T(8,128)S(1)} %get-tuple-element.81.refs_0_), channel_id=1, source_target_pairs={{0,16},{16,0},{1,17},{17,1},{2,18},{18,2},{3,19},{19,3},{4,20},{20... | collective-permute-start | bytes 405512 | tf_op jit(solution)/shard_map/ppermute | solution.py:421
  28.4 4.5 %collective-permute-start.12 = (f32[144,128]{1,0:T(8,128)S(1)}, f32[144,128]{1,0:T(8,128)S(1)}, u32[]{:S(2)}, u32[]{:S(2)}) collective-permute-start(f32[144,128]{1,0:T(8,128)S(1)} %get-tuple-element.83.refs_3_), channel_id=1, source_target_pairs={{0,12},{4,8},{8,4},{12,0},{1,13},{5,9},{9,5},{13,1},{2,14},{6,10},... | collective-permute-start | bytes 221192 | tf_op jit(solution)/shard_map/ppermute | solution.py:421
  33.8 7.0 %collective-permute-start.14 = (f32[136,128]{1,0:T(8,128)S(1)}, f32[136,128]{1,0:T(8,128)S(1)}, u32[]{:S(2)}, u32[]{:S(2)}) collective-permute-start(f32[136,128]{1,0:T(8,128)S(1)} %get-tuple-element.90.refs_1_), channel_id=1, source_target_pairs={{0,3},{1,2},{2,1},{3,0},{4,7},{5,6},{6,5},{7,4},{8,11},{9,10},{10,... | collective-permute-start | bytes 208904 | tf_op jit(solution)/shard_map/ppermute | solution.py:421
  36.3 3.9 %collective-permute-start.17 = (f32[16,128]{1,0:T(8,128)S(1)}, f32[16,128]{1,0:T(8,128)S(1)}, u32[]{:S(2)}, u32[]{:S(2)}) collective-permute-start(f32[16,128]{1,0:T(8,128)S(1)} %slice.3), channel_id=1, source_target_pairs={{0,4},{4,0},{8,12},{12,8},{1,5},{5,1},{9,13},{13,9},{2,6},{6,2},{1... | collective-permute-start | bytes 24584 | tf_op jit(solution)/shard_map/ppermute | solution.py:421
  36.3 4.5 %collective-permute-start.15 = (f32[16,128]{1,0:T(8,128)S(1)}, f32[16,128]{1,0:T(8,128)S(1)}, u32[]{:S(2)}, u32[]{:S(2)}) collective-permute-start(f32[16,128]{1,0:T(8,128)S(1)} %get-tuple-element.91), channel_id=1, source_target_pairs={{0,2},{1,3},{2,0},{3,1},{4,6},{5,7},{6,4},{7,5},{8,10},{9,11},{10,... | collective-permute-start | bytes 24584 | tf_op jit(solution)/shard_map/ppermute | solution.py:416
  38.3 5.2 %collective-permute-start.21 = (f32[128,128]{1,0:T(8,128)S(1)}, f32[128,128]{1,0:T(8,128)S(1)}, u32[]{:S(2)}, u32[]{:S(2)}) collective-permute-start(f32[128,128]{1,0:T(8,128)S(1)} %get-tuple-element.96.refs_0_), channel_id=1, source_target_pairs={{0,1},{1,0},{2,3},{3,2},{4,5},{5,4},{6,7},{7,6},{8,9},{9,8},{10,11... | collective-permute-start | bytes 196616 | tf_op jit(solution)/shard_map/ppermute | solution.py:421
  41.2 5.4 %collective-permute-start.18 = (f32[264,128]{1,0:T(8,128)S(1)}, f32[264,128]{1,0:T(8,128)S(1)}, u32[]{:S(2)}, u32[]{:S(2)}) collective-permute-start(f32[264,128]{1,0:T(8,128)S(1)} %get-tuple-element.93.refs_0_), channel_id=1, source_target_pairs={{0,16},{16,0},{1,17},{17,1},{2,18},{18,2},{3,19},{19,3},{4,20},{20... | collective-permute-start | bytes 405512 | tf_op jit(solution)/shard_map/ppermute | solution.py:421
  42.2 4.3 %collective-permute-start.20 = (f32[144,128]{1,0:T(8,128)S(1)}, f32[144,128]{1,0:T(8,128)S(1)}, u32[]{:S(2)}, u32[]{:S(2)}) collective-permute-start(f32[144,128]{1,0:T(8,128)S(1)} %get-tuple-element.95.refs_3_), channel_id=1, source_target_pairs={{0,12},{4,8},{8,4},{12,0},{1,13},{5,9},{9,5},{13,1},{2,14},{6,10},... | collective-permute-start | bytes 221192 | tf_op jit(solution)/shard_map/ppermute | solution.py:421
  47.6 7.0 %collective-permute-start.22 = (f32[144,128]{1,0:T(8,128)S(1)}, f32[144,128]{1,0:T(8,128)S(1)}, u32[]{:S(2)}, u32[]{:S(2)}) collective-permute-start(f32[144,128]{1,0:T(8,128)S(1)} %get-tuple-element.104.refs_1_), channel_id=1, source_target_pairs={{0,3},{1,2},{2,1},{3,0},{4,7},{5,6},{6,5},{7,4},{8,11},{9,10},{10,... | collective-permute-start | bytes 221192 | tf_op jit(solution)/shard_map/ppermute | solution.py:421
  49.9 4.7 %collective-permute-start.23 = (f32[24,128]{1,0:T(8,128)S(1)}, f32[24,128]{1,0:T(8,128)S(1)}, u32[]{:S(2)}, u32[]{:S(2)}) collective-permute-start(f32[24,128]{1,0:T(8,128)S(1)} %get-tuple-element.105), channel_id=1, source_target_pairs={{0,2},{1,3},{2,0},{3,1},{4,6},{5,7},{6,4},{7,5},{8,10},{9,11},{10,... | collective-permute-start | bytes 36872 | tf_op jit(solution)/shard_map/ppermute | solution.py:416
  50.1 4.0 %collective-permute-start.24 = (f32[16,128]{1,0:T(8,128)S(1)}, f32[16,128]{1,0:T(8,128)S(1)}, u32[]{:S(2)}, u32[]{:S(2)}) collective-permute-start(f32[16,128]{1,0:T(8,128)S(1)} %get-tuple-element.102.refs_0_), channel_id=1, source_target_pairs={{0,1},{1,0},{2,3},{3,2},{4,5},{5,4},{6,7},{7,6},{8,9},{9,8},{10,11... | collective-permute-start | bytes 24584 | tf_op jit(solution)/shard_map/ppermute | solution.py:421
  52.1 6.1 %collective-permute-start.28 = (f32[128,128]{1,0:T(8,128)S(1)}, f32[128,128]{1,0:T(8,128)S(1)}, u32[]{:S(2)}, u32[]{:S(2)}) collective-permute-start(f32[128,128]{1,0:T(8,128)S(1)} %get-tuple-element.109.refs_0_), channel_id=1, source_target_pairs={{0,1},{1,0},{2,3},{3,2},{4,5},{5,4},{6,7},{7,6},{8,9},{9,8},{10,11... | collective-permute-start | bytes 196616 | tf_op jit(solution)/shard_map/ppermute | solution.py:421
  54.9 5.2 %collective-permute-start.26 = (f32[264,128]{1,0:T(8,128)S(1)}, f32[264,128]{1,0:T(8,128)S(1)}, u32[]{:S(2)}, u32[]{:S(2)}) collective-permute-start(f32[264,128]{1,0:T(8,128)S(1)} %get-tuple-element.107.refs_0_), channel_id=1, source_target_pairs={{0,16},{16,0},{1,17},{17,1},{2,18},{18,2},{3,19},{19,3},{4,20},{20... | collective-permute-start | bytes 405512 | tf_op jit(solution)/shard_map/ppermute | solution.py:421
  55.9 4.2 %collective-permute-start.27 = (f32[144,128]{1,0:T(8,128)S(1)}, f32[144,128]{1,0:T(8,128)S(1)}, u32[]{:S(2)}, u32[]{:S(2)}) collective-permute-start(f32[144,128]{1,0:T(8,128)S(1)} %get-tuple-element.108.refs_3_), channel_id=1, source_target_pairs={{0,12},{4,8},{8,4},{12,0},{1,13},{5,9},{9,5},{13,1},{2,14},{6,10},... | collective-permute-start | bytes 221192 | tf_op jit(solution)/shard_map/ppermute | solution.py:421
  55.9 4.0 %collective-permute-start.25 = (f32[8,128]{1,0:T(8,128)S(1)}, f32[8,128]{1,0:T(8,128)S(1)}, u32[]{:S(2)}, u32[]{:S(2)}) collective-permute-start(f32[8,128]{1,0:T(8,128)S(1)} %get-tuple-element.106.refs_0_), channel_id=1, source_target_pairs={{0,28},{4,24},{8,20},{12,16},{16,12},{20,8},{24,4},{28,0},{1,29},{... | collective-permute-start | bytes 12296 | tf_op jit(solution)/shard_map/ppermute | solution.py:426
  (7 other events, 19.3 us)

commit v16 on v15

--- a/solution.py
+++ b/solution.py
@@ -380,6 +380,7 @@
     curv3 = curv3 + ratio2 * (wc + 2.0 * beta2 * sc + beta2 * beta2 * sz)
     beta3 = norm3 / rr
     alpha3 = norm3 / (curv3 - beta3 * norm3 / alpha2)
+    inverse1 = 1.0 / alpha1
     places, signs = face_places(face)
     copies = []
     for f in range(6):
@@ -388,7 +389,7 @@
         p2 = i["r2"][at, :] + beta2 * i["p1"][at, :]
         s2 = w2 + beta2 * s1
         r3 = i["r2"][at, :] - ratio * s2
-        w3 = w2 / alpha1 - ratio * (i["c3"][at, :] + beta2 * i["z1"][at, :])
+        w3 = w2 * inverse1 - ratio * (i["c3"][at, :] + beta2 * i["z1"][at, :])
         mult = i["m2"][at, :] + alpha2 * p2 + alpha3 * (r3 + beta3 * p2)
         resid = r3 - alpha3 * (w3 + (beta3 / alpha1) * s2)
         for k, (value, out, hbm) in enumerate(((mult, mult_out, mult_hbm), (resid, resid_out, resid_hbm))):

time: 63.2 us -> 63.2 us (level)
  no operation moved by 1% of the time
where the time goes in v16:
time: 63.2 us; the launch traced here: 63.1 us
  starting transfers between devices  32.9 us (52%)
  waiting for transfers between devices  20.3 us (32%)
  Pallas kernels  9.14 us (14%)
  between operations  0.76 us (1%)
    ppermute x26, starting transfers between devices, swap(): return lax.ppermute(x, axis, [(k, (k + side(k)) % n) for k in range(n)])  30 us
    ppermute x26, waiting for transfers between devices, swap(): return lax.ppermute(x, axis, [(k, (k + side(k)) % n) for k in range(n)])  16.4 us
    pallas_call x13, Pallas kernels, call(): pl.pallas_call(run, out_shape=[outs[n] for n in names_out], in_specs=[vme...  5.22 us
    pallas_call x1, Pallas kernels, body(): pl.pallas_call(functools.partial(first_kernel, face, nz, n_modes, small),...  2.76 us
    ppermute x4, waiting for transfers between devices, shift(): return lax.ppermute(x, axis, [(k, (k + by) % n) for k in range(n)])  2.31 us
    ppermute x1, starting transfers between devices, move(): return lax.ppermute(x, ('gx', 'gy'), pairs)  2.29 us
    ppermute x1, waiting for transfers between devices, move(): return lax.ppermute(x, ('gx', 'gy'), pairs)  1.57 us
  transfers between devices with their start and end apart: 31, of which 17 were waited for; matrix products, arithmetic and copies ran while one was open for 0% of the time, Pallas kernels for 4%

profile of v16, /device:TPU:0, one launch (start us, length us, event | category | flops | bytes accessed | tf_op | source)
XLA Modules:
  0.0 63.1 jit_solution(14579918014856313064)
XLA Ops:
  0.6 2.8 %shard_map.59 = (f32[768,128]{1,0:T(8,128)S(1)}, bf16[1568,768]{1,0:T(8,128)(2,1)S(1)}, bf16[768,48]{1,0:T(8,128)(2,1)S(1)}, f32[8,128]{1,0:T(8,128)S(1)}, f32[5...) custom-call(f32[128,768]{1,0:T(8,128)} %bitcast.7, ...), custom_call_target="tpu_custom_call" | custom-call | flops 603979776 | bytes 2359296 | tf_op jit(solution)/shard_map/pallas_call | solution.py:497
  3.4 5.1 %collective-permute-start = (f32[160,128]{1,0:T(8,128)S(1)}, f32[160,128]{1,0:T(8,128)S(1)}, u32[]{:S(2)}, u32[]{:S(2)}) collective-permute-start(f32[160,128]{1,0:T(8,128)S(1)} %get-tuple-element.64.refs_1_), channel_id=1, source_target_pairs={{0,3},{1,2},{2,1},{3,0},{4,7},{5,6},{6,5},{7,4},{8,11},{9,10},{10,... | collective-permute-start | bytes 245768 | tf_op jit(solution)/shard_map/ppermute | solution.py:422
  9.1 1.4 %collective-permute-start.6 = (f32[136,128]{1,0:T(8,128)S(1)}, f32[136,128]{1,0:T(8,128)S(1)}, u32[]{:S(2)}, u32[]{:S(2)}) collective-permute-start(f32[136,128]{1,0:T(8,128)S(1)} %get-tuple-element.71.refs_0_), channel_id=1, source_target_pairs={{0,1},{1,0},{2,3},{3,2},{4,5},{5,4},{6,7},{7,6},{8,9},{9,8},{10,11... | collective-permute-start | bytes 208904 | tf_op jit(solution)/shard_map/ppermute | solution.py:422
  10.5 1.8 %collective-permute-done.2.refs_4_ = f32[24,128]{1,0:T(8,128)S(1)} collective-permute-done((f32[24,128]{1,0:T(8,128)S(1)}, f32[24,128]{1,0:T(8,128)S(1)}, u32[]{:S(2)}, u32[]{:S(2)}) %collective-permute-start.2) | collective-permute-done | bytes 12320 | tf_op jit(solution)/shard_map/ppermute | solution.py:422
  13.7 1.6 %collective-permute-start.3 = (f32[264,128]{1,0:T(8,128)S(1)}, f32[264,128]{1,0:T(8,128)S(1)}, u32[]{:S(2)}, u32[]{:S(2)}) collective-permute-start(f32[264,128]{1,0:T(8,128)S(1)} %get-tuple-element.68.refs_0_), channel_id=1, source_target_pairs={{0,16},{16,0},{1,17},{17,1},{2,18},{18,2},{3,19},{19,3},{4,20},{20... | collective-permute-start | bytes 405512 | tf_op jit(solution)/shard_map/ppermute | solution.py:422
  15.3 1.6 %collective-permute-start.4 = (f32[136,128]{1,0:T(8,128)S(1)}, f32[136,128]{1,0:T(8,128)S(1)}, u32[]{:S(2)}, u32[]{:S(2)}) collective-permute-start(f32[136,128]{1,0:T(8,128)S(1)} %get-tuple-element.69.refs_2_), channel_id=1, source_target_pairs={{0,4},{4,0},{8,12},{12,8},{1,5},{5,1},{9,13},{13,9},{2,6},{6,2},{1... | collective-permute-start | bytes 208904 | tf_op jit(solution)/shard_map/ppermute | solution.py:422
  17.8 2.0 %collective-permute-done.5.refs_5_ = f32[144,128]{1,0:T(8,128)S(1)} collective-permute-done((f32[144,128]{1,0:T(8,128)S(1)}, f32[144,128]{1,0:T(8,128)S(1)}, u32[]{:S(2)}, u32[]{:S(2)}) %collective-permute-start.5) | collective-permute-done | bytes 73760 | tf_op jit(solution)/shard_map/ppermute | solution.py:422
  20.6 2.3 %collective-permute-start.7 = (f32[144,128]{1,0:T(8,128)S(1)}, f32[144,128]{1,0:T(8,128)S(1)}, u32[]{:S(2)}, u32[]{:S(2)}) collective-permute-start(f32[144,128]{1,0:T(8,128)S(1)} %get-tuple-element.77.refs_1_), channel_id=1, source_target_pairs={{0,3},{1,2},{2,1},{3,0},{4,7},{5,6},{6,5},{7,4},{8,11},{9,10},{10,... | collective-permute-start | bytes 221192 | tf_op jit(solution)/shard_map/ppermute | solution.py:422
  23.0 2.1 %collective-permute-start.9 = (f32[16,128]{1,0:T(8,128)S(1)}, f32[16,128]{1,0:T(8,128)S(1)}, u32[]{:S(2)}, u32[]{:S(2)}) collective-permute-start(f32[16,128]{1,0:T(8,128)S(1)} %get-tuple-element.75.refs_0_), channel_id=1, source_target_pairs={{0,1},{1,0},{2,3},{3,2},{4,5},{5,4},{6,7},{7,6},{8,9},{9,8},{10,11... | collective-permute-start | bytes 24584 | tf_op jit(solution)/shard_map/ppermute | solution.py:422
  25.1 2.1 %collective-permute-done.9.refs_4_ = f32[16,128]{1,0:T(8,128)S(1)} collective-permute-done((f32[16,128]{1,0:T(8,128)S(1)}, f32[16,128]{1,0:T(8,128)S(1)}, u32[]{:S(2)}, u32[]{:S(2)}) %collective-permute-start.9) | collective-permute-done | bytes 8224 | tf_op jit(solution)/shard_map/ppermute | solution.py:422
  28.4 1.6 %collective-permute-start.11 = (f32[136,128]{1,0:T(8,128)S(1)}, f32[136,128]{1,0:T(8,128)S(1)}, u32[]{:S(2)}, u32[]{:S(2)}) collective-permute-start(f32[136,128]{1,0:T(8,128)S(1)} %get-tuple-element.82.refs_2_), channel_id=1, source_target_pairs={{0,4},{4,0},{8,12},{12,8},{1,5},{5,1},{9,13},{13,9},{2,6},{6,2},{1... | collective-permute-start | bytes 208904 | tf_op jit(solution)/shard_map/ppermute | solution.py:422
  30.9 2.0 %collective-permute-done.12.refs_5_ = f32[144,128]{1,0:T(8,128)S(1)} collective-permute-done((f32[144,128]{1,0:T(8,128)S(1)}, f32[144,128]{1,0:T(8,128)S(1)}, u32[]{:S(2)}, u32[]{:S(2)}) %collective-permute-start.12) | collective-permute-done | bytes 73760 | tf_op jit(solution)/shard_map/ppermute | solution.py:422
  33.8 2.4 %collective-permute-start.14 = (f32[136,128]{1,0:T(8,128)S(1)}, f32[136,128]{1,0:T(8,128)S(1)}, u32[]{:S(2)}, u32[]{:S(2)}) collective-permute-start(f32[136,128]{1,0:T(8,128)S(1)} %get-tuple-element.90.refs_1_), channel_id=1, source_target_pairs={{0,3},{1,2},{2,1},{3,0},{4,7},{5,6},{6,5},{7,4},{8,11},{9,10},{10,... | collective-permute-start | bytes 208904 | tf_op jit(solution)/shard_map/ppermute | solution.py:422
  36.5 1.8 %collective-permute-start.16 = (f32[8,128]{1,0:T(8,128)S(1)}, f32[8,128]{1,0:T(8,128)S(1)}, u32[]{:S(2)}, u32[]{:S(2)}) collective-permute-start(f32[8,128]{1,0:T(8,128)S(1)} %get-tuple-element.88.refs_0_), channel_id=1, source_target_pairs={{0,1},{1,0},{2,3},{3,2},{4,5},{5,4},{6,7},{7,6},{8,9},{9,8},{10,11... | collective-permute-start | bytes 12296 | tf_op jit(solution)/shard_map/ppermute | solution.py:422
  38.6 1.6 %collective-permute-done.16.refs_4_ = f32[8,128]{1,0:T(8,128)S(1)} collective-permute-done((f32[8,128]{1,0:T(8,128)S(1)}, f32[8,128]{1,0:T(8,128)S(1)}, u32[]{:S(2)}, u32[]{:S(2)}) %collective-permute-start.16) | collective-permute-done | bytes 4128 | tf_op jit(solution)/shard_map/ppermute | solution.py:422
  42.2 1.3 %collective-permute-start.19 = (f32[128,128]{1,0:T(8,128)S(1)}, f32[128,128]{1,0:T(8,128)S(1)}, u32[]{:S(2)}, u32[]{:S(2)}) collective-permute-start(f32[128,128]{1,0:T(8,128)S(1)} %get-tuple-element.94.refs_2_), channel_id=1, source_target_pairs={{0,4},{4,0},{8,12},{12,8},{1,5},{5,1},{9,13},{13,9},{2,6},{6,2},{1... | collective-permute-start | bytes 196616 | tf_op jit(solution)/shard_map/ppermute | solution.py:422
  44.4 2.1 %collective-permute-done.20.refs_5_ = f32[144,128]{1,0:T(8,128)S(1)} collective-permute-done((f32[144,128]{1,0:T(8,128)S(1)}, f32[144,128]{1,0:T(8,128)S(1)}, u32[]{:S(2)}, u32[]{:S(2)}) %collective-permute-start.20) | collective-permute-done | bytes 73760 | tf_op jit(solution)/shard_map/ppermute | solution.py:422
  46.5 1.1 %shard_map.68 = (f32[768,128]{1,0:T(8,128)S(1)}, f32[768,128]{1,0:T(8,128)S(1)}, f32[768,128]{1,0:T(8,128)S(1)}, f32[8,128]{1,0:T(8,128)S(1)}, f32[512,128]{1,0:...) custom-call(f32[264,128]{1,0:T(8,128)S(1)} %get-tuple-element.93.ref, ...), custom_call_target="tpu_custom_call" | custom-call | flops 603979776 | bytes 5881856 | tf_op jit(solution)/shard_map/pallas_call | solution.py:31
  47.6 2.3 %collective-permute-start.22 = (f32[144,128]{1,0:T(8,128)S(1)}, f32[144,128]{1,0:T(8,128)S(1)}, u32[]{:S(2)}, u32[]{:S(2)}) collective-permute-start(f32[144,128]{1,0:T(8,128)S(1)} %get-tuple-element.104.refs_1_), channel_id=1, source_target_pairs={{0,3},{1,2},{2,1},{3,0},{4,7},{5,6},{6,5},{7,4},{8,11},{9,10},{10,... | collective-permute-start | bytes 221192 | tf_op jit(solution)/shard_map/ppermute | solution.py:422
  50.1 1.9 %collective-permute-start.24 = (f32[16,128]{1,0:T(8,128)S(1)}, f32[16,128]{1,0:T(8,128)S(1)}, u32[]{:S(2)}, u32[]{:S(2)}) collective-permute-start(f32[16,128]{1,0:T(8,128)S(1)} %get-tuple-element.102.refs_0_), channel_id=1, source_target_pairs={{0,1},{1,0},{2,3},{3,2},{4,5},{5,4},{6,7},{7,6},{8,9},{9,8},{10,11... | collective-permute-start | bytes 24584 | tf_op jit(solution)/shard_map/ppermute | solution.py:422
  52.2 2.0 %collective-permute-done.24.refs_4_ = f32[16,128]{1,0:T(8,128)S(1)} collective-permute-done((f32[16,128]{1,0:T(8,128)S(1)}, f32[16,128]{1,0:T(8,128)S(1)}, u32[]{:S(2)}, u32[]{:S(2)}) %collective-permute-start.24) | collective-permute-done | bytes 8224 | tf_op jit(solution)/shard_map/ppermute | solution.py:422
  55.9 2.3 %collective-permute-start.25 = (f32[8,128]{1,0:T(8,128)S(1)}, f32[8,128]{1,0:T(8,128)S(1)}, u32[]{:S(2)}, u32[]{:S(2)}) collective-permute-start(f32[8,128]{1,0:T(8,128)S(1)} %get-tuple-element.106.refs_0_), channel_id=1, source_target_pairs={{0,28},{4,24},{8,20},{12,16},{16,12},{20,8},{24,4},{28,0},{1,29},{... | collective-permute-start | bytes 12296 | tf_op jit(solution)/shard_map/ppermute | solution.py:427
  58.4 1.6 %collective-permute-done.25.refs_1_ = f32[8,128]{1,0:T(8,128)S(1)} collective-permute-done((f32[8,128]{1,0:T(8,128)S(1)}, f32[8,128]{1,0:T(8,128)S(1)}, u32[]{:S(2)}, u32[]{:S(2)}) %collective-permute-start.25) | collective-permute-done | bytes 4128 | tf_op jit(solution)/shard_map/ppermute | solution.py:427
  61.9 1.2 %shard_map.73 = (f32[128,768]{1,0:T(8,128)}, f32[128,768]{1,0:T(8,128)}) custom-call(f32[8,128]{1,0:T(8,128)S(1)} %shard_map.71.refs_0_, f32[8,128]{1,0:T(8,128)S(1)} %collective-permute-done.29.refs_1_, f32[768,128]{1,0:T(8,128)S(1)} %get-tuple-element.114.refs_2_, f32[768,128]{1,0:T(8,128)S(1)} %get-tuple-element.115.refs_3_, ...), custom_call_target="tpu_custom_call" | custom-call | flops 1966080 | bytes 3538944 | tf_op jit(solution)/shard_map/pallas_call | solution.py:570
  (54 shorter events, 14.6 us)
Async XLA Ops:
  3.4 9.9 %collective-permute-start = (f32[160,128]{1,0:T(8,128)S(1)}, f32[160,128]{1,0:T(8,128)S(1)}, u32[]{:S(2)}, u32[]{:S(2)}) collective-permute-start(f32[160,128]{1,0:T(8,128)S(1)} %get-tuple-element.64.refs_1_), channel_id=1, source_target_pairs={{0,3},{1,2},{2,1},{3,0},{4,7},{5,6},{6,5},{7,4},{8,11},{9,10},{10,... | collective-permute-start | bytes 245768 | tf_op jit(solution)/shard_map/ppermute | solution.py:422
  8.5 4.7 %collective-permute-start.1 = (f32[32,128]{1,0:T(8,128)S(1)}, f32[32,128]{1,0:T(8,128)S(1)}, u32[]{:S(2)}, u32[]{:S(2)}) collective-permute-start(f32[32,128]{1,0:T(8,128)S(1)} %get-tuple-element.65), channel_id=1, source_target_pairs={{0,2},{1,3},{2,0},{3,1},{4,6},{5,7},{6,4},{7,5},{8,10},{9,11},{10,... | collective-permute-start | bytes 49160 | tf_op jit(solution)/shard_map/ppermute | solution.py:417
  9.1 7.7 %collective-permute-start.6 = (f32[136,128]{1,0:T(8,128)S(1)}, f32[136,128]{1,0:T(8,128)S(1)}, u32[]{:S(2)}, u32[]{:S(2)}) collective-permute-start(f32[136,128]{1,0:T(8,128)S(1)} %get-tuple-element.71.refs_0_), channel_id=1, source_target_pairs={{0,1},{1,0},{2,3},{3,2},{4,5},{5,4},{6,7},{7,6},{8,9},{9,8},{10,11... | collective-permute-start | bytes 208904 | tf_op jit(solution)/shard_map/ppermute | solution.py:422
  13.7 6.1 %collective-permute-start.3 = (f32[264,128]{1,0:T(8,128)S(1)}, f32[264,128]{1,0:T(8,128)S(1)}, u32[]{:S(2)}, u32[]{:S(2)}) collective-permute-start(f32[264,128]{1,0:T(8,128)S(1)} %get-tuple-element.68.refs_0_), channel_id=1, source_target_pairs={{0,16},{16,0},{1,17},{17,1},{2,18},{18,2},{3,19},{19,3},{4,20},{20... | collective-permute-start | bytes 405512 | tf_op jit(solution)/shard_map/ppermute | solution.py:422
  15.3 4.5 %collective-permute-start.5 = (f32[144,128]{1,0:T(8,128)S(1)}, f32[144,128]{1,0:T(8,128)S(1)}, u32[]{:S(2)}, u32[]{:S(2)}) collective-permute-start(f32[144,128]{1,0:T(8,128)S(1)} %get-tuple-element.70.refs_3_), channel_id=1, source_target_pairs={{0,12},{4,8},{8,4},{12,0},{1,13},{5,9},{9,5},{13,1},{2,14},{6,10},... | collective-permute-start | bytes 221192 | tf_op jit(solution)/shard_map/ppermute | solution.py:422
  20.6 6.9 %collective-permute-start.7 = (f32[144,128]{1,0:T(8,128)S(1)}, f32[144,128]{1,0:T(8,128)S(1)}, u32[]{:S(2)}, u32[]{:S(2)}) collective-permute-start(f32[144,128]{1,0:T(8,128)S(1)} %get-tuple-element.77.refs_1_), channel_id=1, source_target_pairs={{0,3},{1,2},{2,1},{3,0},{4,7},{5,6},{6,5},{7,4},{8,11},{9,10},{10,... | collective-permute-start | bytes 221192 | tf_op jit(solution)/shard_map/ppermute | solution.py:422
  22.9 4.6 %collective-permute-start.8 = (f32[24,128]{1,0:T(8,128)S(1)}, f32[24,128]{1,0:T(8,128)S(1)}, u32[]{:S(2)}, u32[]{:S(2)}) collective-permute-start(f32[24,128]{1,0:T(8,128)S(1)} %get-tuple-element.78), channel_id=1, source_target_pairs={{0,2},{1,3},{2,0},{3,1},{4,6},{5,7},{6,4},{7,5},{8,10},{9,11},{10,... | collective-permute-start | bytes 36872 | tf_op jit(solution)/shard_map/ppermute | solution.py:417
  23.0 4.3 %collective-permute-start.9 = (f32[16,128]{1,0:T(8,128)S(1)}, f32[16,128]{1,0:T(8,128)S(1)}, u32[]{:S(2)}, u32[]{:S(2)}) collective-permute-start(f32[16,128]{1,0:T(8,128)S(1)} %get-tuple-element.75.refs_0_), channel_id=1, source_target_pairs={{0,1},{1,0},{2,3},{3,2},{4,5},{5,4},{6,7},{7,6},{8,9},{9,8},{10,11... | collective-permute-start | bytes 24584 | tf_op jit(solution)/shard_map/ppermute | solution.py:422
  25.1 4.9 %collective-permute-start.13 = (f32[128,128]{1,0:T(8,128)S(1)}, f32[128,128]{1,0:T(8,128)S(1)}, u32[]{:S(2)}, u32[]{:S(2)}) collective-permute-start(f32[128,128]{1,0:T(8,128)S(1)} %get-tuple-element.84.refs_0_), channel_id=1, source_target_pairs={{0,1},{1,0},{2,3},{3,2},{4,5},{5,4},{6,7},{7,6},{8,9},{9,8},{10,11... | collective-permute-start | bytes 196616 | tf_op jit(solution)/shard_map/ppermute | solution.py:422
  27.8 5.2 %collective-permute-start.10 = (f32[264,128]{1,0:T(8,128)S(1)}, f32[264,128]{1,0:T(8,128)S(1)}, u32[]{:S(2)}, u32[]{:S(2)}) collective-permute-start(f32[264,128]{1,0:T(8,128)S(1)} %get-tuple-element.81.refs_0_), channel_id=1, source_target_pairs={{0,16},{16,0},{1,17},{17,1},{2,18},{18,2},{3,19},{19,3},{4,20},{20... | collective-permute-start | bytes 405512 | tf_op jit(solution)/shard_map/ppermute | solution.py:422
  28.4 4.5 %collective-permute-start.12 = (f32[144,128]{1,0:T(8,128)S(1)}, f32[144,128]{1,0:T(8,128)S(1)}, u32[]{:S(2)}, u32[]{:S(2)}) collective-permute-start(f32[144,128]{1,0:T(8,128)S(1)} %get-tuple-element.83.refs_3_), channel_id=1, source_target_pairs={{0,12},{4,8},{8,4},{12,0},{1,13},{5,9},{9,5},{13,1},{2,14},{6,10},... | collective-permute-start | bytes 221192 | tf_op jit(solution)/shard_map/ppermute | solution.py:422
  33.8 7.0 %collective-permute-start.14 = (f32[136,128]{1,0:T(8,128)S(1)}, f32[136,128]{1,0:T(8,128)S(1)}, u32[]{:S(2)}, u32[]{:S(2)}) collective-permute-start(f32[136,128]{1,0:T(8,128)S(1)} %get-tuple-element.90.refs_1_), channel_id=1, source_target_pairs={{0,3},{1,2},{2,1},{3,0},{4,7},{5,6},{6,5},{7,4},{8,11},{9,10},{10,... | collective-permute-start | bytes 208904 | tf_op jit(solution)/shard_map/ppermute | solution.py:422
  36.3 3.9 %collective-permute-start.17 = (f32[16,128]{1,0:T(8,128)S(1)}, f32[16,128]{1,0:T(8,128)S(1)}, u32[]{:S(2)}, u32[]{:S(2)}) collective-permute-start(f32[16,128]{1,0:T(8,128)S(1)} %slice.3), channel_id=1, source_target_pairs={{0,4},{4,0},{8,12},{12,8},{1,5},{5,1},{9,13},{13,9},{2,6},{6,2},{1... | collective-permute-start | bytes 24584 | tf_op jit(solution)/shard_map/ppermute | solution.py:422
  36.3 4.5 %collective-permute-start.15 = (f32[16,128]{1,0:T(8,128)S(1)}, f32[16,128]{1,0:T(8,128)S(1)}, u32[]{:S(2)}, u32[]{:S(2)}) collective-permute-start(f32[16,128]{1,0:T(8,128)S(1)} %get-tuple-element.91), channel_id=1, source_target_pairs={{0,2},{1,3},{2,0},{3,1},{4,6},{5,7},{6,4},{7,5},{8,10},{9,11},{10,... | collective-permute-start | bytes 24584 | tf_op jit(solution)/shard_map/ppermute | solution.py:417
  38.3 5.2 %collective-permute-start.21 = (f32[128,128]{1,0:T(8,128)S(1)}, f32[128,128]{1,0:T(8,128)S(1)}, u32[]{:S(2)}, u32[]{:S(2)}) collective-permute-start(f32[128,128]{1,0:T(8,128)S(1)} %get-tuple-element.96.refs_0_), channel_id=1, source_target_pairs={{0,1},{1,0},{2,3},{3,2},{4,5},{5,4},{6,7},{7,6},{8,9},{9,8},{10,11... | collective-permute-start | bytes 196616 | tf_op jit(solution)/shard_map/ppermute | solution.py:422
  41.2 5.4 %collective-permute-start.18 = (f32[264,128]{1,0:T(8,128)S(1)}, f32[264,128]{1,0:T(8,128)S(1)}, u32[]{:S(2)}, u32[]{:S(2)}) collective-permute-start(f32[264,128]{1,0:T(8,128)S(1)} %get-tuple-element.93.refs_0_), channel_id=1, source_target_pairs={{0,16},{16,0},{1,17},{17,1},{2,18},{18,2},{3,19},{19,3},{4,20},{20... | collective-permute-start | bytes 405512 | tf_op jit(solution)/shard_map/ppermute | solution.py:422
  42.2 4.3 %collective-permute-start.20 = (f32[144,128]{1,0:T(8,128)S(1)}, f32[144,128]{1,0:T(8,128)S(1)}, u32[]{:S(2)}, u32[]{:S(2)}) collective-permute-start(f32[144,128]{1,0:T(8,128)S(1)} %get-tuple-element.95.refs_3_), channel_id=1, source_target_pairs={{0,12},{4,8},{8,4},{12,0},{1,13},{5,9},{9,5},{13,1},{2,14},{6,10},... | collective-permute-start | bytes 221192 | tf_op jit(solution)/shard_map/ppermute | solution.py:422
  47.6 7.0 %collective-permute-start.22 = (f32[144,128]{1,0:T(8,128)S(1)}, f32[144,128]{1,0:T(8,128)S(1)}, u32[]{:S(2)}, u32[]{:S(2)}) collective-permute-start(f32[144,128]{1,0:T(8,128)S(1)} %get-tuple-element.104.refs_1_), channel_id=1, source_target_pairs={{0,3},{1,2},{2,1},{3,0},{4,7},{5,6},{6,5},{7,4},{8,11},{9,10},{10,... | collective-permute-start | bytes 221192 | tf_op jit(solution)/shard_map/ppermute | solution.py:422
  49.9 4.7 %collective-permute-start.23 = (f32[24,128]{1,0:T(8,128)S(1)}, f32[24,128]{1,0:T(8,128)S(1)}, u32[]{:S(2)}, u32[]{:S(2)}) collective-permute-start(f32[24,128]{1,0:T(8,128)S(1)} %get-tuple-element.105), channel_id=1, source_target_pairs={{0,2},{1,3},{2,0},{3,1},{4,6},{5,7},{6,4},{7,5},{8,10},{9,11},{10,... | collective-permute-start | bytes 36872 | tf_op jit(solution)/shard_map/ppermute | solution.py:417
  50.1 4.0 %collective-permute-start.24 = (f32[16,128]{1,0:T(8,128)S(1)}, f32[16,128]{1,0:T(8,128)S(1)}, u32[]{:S(2)}, u32[]{:S(2)}) collective-permute-start(f32[16,128]{1,0:T(8,128)S(1)} %get-tuple-element.102.refs_0_), channel_id=1, source_target_pairs={{0,1},{1,0},{2,3},{3,2},{4,5},{5,4},{6,7},{7,6},{8,9},{9,8},{10,11... | collective-permute-start | bytes 24584 | tf_op jit(solution)/shard_map/ppermute | solution.py:422
  52.1 6.1 %collective-permute-start.28 = (f32[128,128]{1,0:T(8,128)S(1)}, f32[128,128]{1,0:T(8,128)S(1)}, u32[]{:S(2)}, u32[]{:S(2)}) collective-permute-start(f32[128,128]{1,0:T(8,128)S(1)} %get-tuple-element.109.refs_0_), channel_id=1, source_target_pairs={{0,1},{1,0},{2,3},{3,2},{4,5},{5,4},{6,7},{7,6},{8,9},{9,8},{10,11... | collective-permute-start | bytes 196616 | tf_op jit(solution)/shard_map/ppermute | solution.py:422
  54.9 5.2 %collective-permute-start.26 = (f32[264,128]{1,0:T(8,128)S(1)}, f32[264,128]{1,0:T(8,128)S(1)}, u32[]{:S(2)}, u32[]{:S(2)}) collective-permute-start(f32[264,128]{1,0:T(8,128)S(1)} %get-tuple-element.107.refs_0_), channel_id=1, source_target_pairs={{0,16},{16,0},{1,17},{17,1},{2,18},{18,2},{3,19},{19,3},{4,20},{20... | collective-permute-start | bytes 405512 | tf_op jit(solution)/shard_map/ppermute | solution.py:422
  55.9 4.2 %collective-permute-start.27 = (f32[144,128]{1,0:T(8,128)S(1)}, f32[144,128]{1,0:T(8,128)S(1)}, u32[]{:S(2)}, u32[]{:S(2)}) collective-permute-start(f32[144,128]{1,0:T(8,128)S(1)} %get-tuple-element.108.refs_3_), channel_id=1, source_target_pairs={{0,12},{4,8},{8,4},{12,0},{1,13},{5,9},{9,5},{13,1},{2,14},{6,10},... | collective-permute-start | bytes 221192 | tf_op jit(solution)/shard_map/ppermute | solution.py:422
  55.9 4.0 %collective-permute-start.25 = (f32[8,128]{1,0:T(8,128)S(1)}, f32[8,128]{1,0:T(8,128)S(1)}, u32[]{:S(2)}, u32[]{:S(2)}) collective-permute-start(f32[8,128]{1,0:T(8,128)S(1)} %get-tuple-element.106.refs_0_), channel_id=1, source_target_pairs={{0,28},{4,24},{8,20},{12,16},{16,12},{20,8},{24,4},{28,0},{1,29},{... | collective-permute-start | bytes 12296 | tf_op jit(solution)/shard_map/ppermute | solution.py:427
  (7 other events, 19.3 us)
